TPU v7x, 32 devices: a whole 2x2x4 slice. The times are simulated.
32 devices in a mesh: tri: 8 (over y, x, core), vp: 4 (over z).
Axes of the slice: x: 2, y: 2, z: 4, core: 2. Of those that a mesh axis runs over, the one named last changes fastest.
Arguments:
- amplitudes: bfloat16 [2, 7680, 512], P(None, 'tri', 'vp'), may hold values from -6 to 6
- integrals: bfloat16 [7680, 512], P('tri', 'vp'), may hold values from -0.0029296875 to 0.0029296875
- ladder_blocks: bfloat16 [56, 768, 768], P('tri'), may hold values from -0.0625 to 0.0625
- slot_block: int32 [56], P('tri'), may hold values from 0 to 55, each once
Outputs:
- section_amplitudes: bfloat16 [2, 7680, 512], P(None, 'tri', 'vp')
Inputs may be any that keep to these rules, and one draw needn't show every extreme that they name: `slot_block`: each value below 55 names a triangle block and stands exactly once; values of 55 or more mark empty slots.
All inputs are finite; a program needn't handle non-finite values.
Results may differ from a plain program's by a relative error of at most 0.0085.
Values may be sent and summed in bfloat16 or wider, within the bound.
No kernel may reach another device: no remote copies, remote signals or barrier semaphores. Data moves between devices by JAX's collectives and lax.ppermute only.
A program may use at most 128 MiB of HBM per device.

v0:
```python
import jax
import jax.numpy as jnp
import numpy as np
from jax import lax
from jax.sharding import PartitionSpec as P

NB = 10
BLOCK = 768
PAIRS = 7680
TRI_BLOCKS = 55


def triangle_tables(block_count):
    row_list = []
    column_list = []
    for row_index in range(block_count):
        for column_index in range(row_index, block_count):
            row_list.append(row_index)
            column_list.append(column_index)
    return (np.array(row_list, np.int32), np.array(column_list, np.int32))


def decode(code):
    row_table, column_table = triangle_tables(NB)
    match = code == jnp.arange(TRI_BLOCKS, dtype=jnp.int32)
    row_block = jnp.sum(jnp.where(match, jnp.asarray(row_table), 0)).astype(jnp.int32)
    column_block = jnp.sum(jnp.where(match, jnp.asarray(column_table), 0)).astype(jnp.int32)
    filled = (code < TRI_BLOCKS).astype(jnp.float32)
    return (row_block, column_block, filled)


def symmetrize(block, row_block, column_block):
    values = block.astype(jnp.float32)
    diagonal = (row_block == column_block).astype(jnp.float32)
    return (values + diagonal * (0.5 * (values + values.T) - values)).astype(jnp.bfloat16)


def apply_block(partial_value, ladder_real, amp_row, amp_column, row_block, column_block, filled):

    def mult(weights, vectors):
        return jnp.dot(weights, vectors, preferred_element_type=jnp.float32)

    to_row = jnp.stack([mult(ladder_real, amp_column[0]), mult(ladder_real, amp_column[1])])
    to_column = jnp.stack([mult(ladder_real.T, amp_row[0]), mult(ladder_real.T, amp_row[1])])
    off_diagonal = filled * (row_block < column_block).astype(jnp.float32)
    start_row = row_block * BLOCK
    current = lax.dynamic_slice_in_dim(partial_value, start_row, BLOCK, 1)
    partial_value = lax.dynamic_update_slice_in_dim(
        partial_value, current + filled * to_row, start_row, 1
    )
    start_column = column_block * BLOCK
    current = lax.dynamic_slice_in_dim(partial_value, start_column, BLOCK, 1)
    return lax.dynamic_update_slice_in_dim(
        partial_value, current + off_diagonal * to_column, start_column, 1
    )


def place_block(partial_value, ladder_real, amp_row, amp_column, row_block, column_block, filled):
    return apply_block(
        partial_value, ladder_real, amp_row, amp_column, row_block, column_block, filled
    )


def shards(amplitudes, integrals, ladder_blocks, slot_block):
    slots = slot_block.shape[0]
    columns = amplitudes.shape[2]
    every_amp = lax.all_gather(amplitudes, "tri", axis=1, tiled=True)
    wide_amp, wide_int = (
        lax.all_gather(amplitudes, "vp", axis=2, tiled=True),
        lax.all_gather(integrals, "vp", axis=1, tiled=True),
    )

    def inner(left, right):
        return jnp.dot(left.T, right, preferred_element_type=jnp.float32)

    contracted = lax.psum(
        jnp.stack([inner(wide_int, amplitudes[0]), inner(wide_int, amplitudes[1])]).astype(
            jnp.bfloat16
        ),
        "tri",
    )

    def mult(left, right):
        return jnp.dot(left, right, preferred_element_type=jnp.float32)

    quad_real = 0.5 * (mult(wide_amp[0], contracted[0]) - mult(wide_amp[1], contracted[1]))
    quad_imag = 0.5 * (mult(wide_amp[0], contracted[1]) + mult(wide_amp[1], contracted[0]))
    partial_value = jnp.zeros((2, PAIRS, columns), jnp.float32)
    for slot_index in range(slots):
        row_block, column_block, filled = decode(slot_block[slot_index])
        start_row = row_block * BLOCK
        start_column = column_block * BLOCK
        amp_row = lax.dynamic_slice_in_dim(every_amp, start_row, BLOCK, 1)
        amp_column = lax.dynamic_slice_in_dim(every_amp, start_column, BLOCK, 1)
        symmetric = symmetrize(ladder_blocks[slot_index], row_block, column_block)
        partial_value = place_block(
            partial_value, symmetric, amp_row, amp_column, row_block, column_block, filled
        )
    scattered = lax.psum_scatter(
        partial_value.astype(jnp.bfloat16), "tri", scatter_dimension=1, tiled=True
    ).astype(jnp.float32)
    ladder_term = scattered + jnp.stack([quad_real, quad_imag])
    start_values = amplitudes.astype(jnp.float32)
    section_real = start_values[0] + 0.5 * ladder_term[1]
    section_imag = start_values[1] - 0.5 * ladder_term[0]
    return jnp.stack([section_real, section_imag]).astype(jnp.bfloat16)


def solution(mesh):
    in_specs = (P(None, "tri", "vp"), P("tri", "vp"), P("tri", None, None), P("tri"))
    out_specs = P(None, "tri", "vp")
    return jax.shard_map(shards, mesh=mesh, in_specs=in_specs, out_specs=out_specs, check_vma=False)
```

profile of v0, /device:TPU:0, one launch (start us, length us, event | category | flops | bytes accessed | tf_op | source)
XLA Modules:
  0.0 210.1 jit_solution(5982307551254516120)
XLA Ops:
  6.5 0.7 all-gather.3.cloned.1.call-update
  7.3 22.7 %all_gather.10 = bf16[960,512]{1,0:T(8,128)(2,1)S(1)} all-gather(bf16[960,128]{1,0:T(8,128)(2,1)} %param.19), channel_id=1, replica_groups=mesh['tri'=8,'vp'=4] {'vp'}, dimensions={1}, use_global_device_ids=true | all-gather | bytes 1228800 | tf_op jit(solution)/shard_map/all_gather | solution.py:70
  30.0 1.4 fusion.39
  32.0 0.7 pad_maximum_fusion.1
  32.8 0.7 all-gather.5.cloned.1.call-update
  33.5 0.7 fusion.120
  34.2 5.2 %fusion.118 = (s32[]{:T(128)}, s32[]{:T(128)}, s32[]{:T(128)}, s32[]{:T(128)}, s32[]{:T(128)}, /*index=5*/s32[]{:T(128)}, s32[]{:T(128)}, s32[]{:T(128)}, s32[]{...) fusion(s32[55]{0:T(128)S(1)} %copy-done.10, s32[]{:T(128)} %bitcast.72, s32[]{:T(128)} %bitcast.48, ...), kind=kLoop, calls=%fused_computation.229 | loop fusion | flops 1911 | bytes 524 | tf_op jit(solution)/shard_map/reduce_sum | solution.py:26
  69.6 8.6 %bitcast_convert_fusion = (f32[768,768]{1,0:T(8,128)}, f32[768,768]{1,0:T(8,128)}, f32[768,768]{1,0:T(8,128)}, f32[768,768]{1,0:T(8,128)}, f32[768,768]{1,0:T(8,...) fusion(bf16[7,768,768]{2,1,0:T(8,128)(2,1)} %param.20), kind=kLoop, calls=%fused_computation.76 | loop fusion | flops 4128768 | bytes 24772608 | tf_op jit(solution)/shard_map/convert_element_type | solution.py:33
  78.2 3.1 %copy.20 = f32[768,768]{0,1:T(8,128)} copy(f32[768,768]{1,0:T(8,128)} %get-tuple-element.29) | data formatting | bytes 4718592 | tf_op jit(solution)/shard_map/convert_element_type | solution.py:33
  81.3 3.1 %copy.21 = f32[768,768]{0,1:T(8,128)} copy(f32[768,768]{1,0:T(8,128)} %get-tuple-element.28) | data formatting | bytes 4718592 | tf_op jit(solution)/shard_map/convert_element_type | solution.py:33
  84.3 3.1 %copy.22 = f32[768,768]{0,1:T(8,128)} copy(f32[768,768]{1,0:T(8,128)} %get-tuple-element.27) | data formatting | bytes 4718592 | tf_op jit(solution)/shard_map/convert_element_type | solution.py:33
  87.5 3.1 %copy.23 = f32[768,768]{0,1:T(8,128)} copy(f32[768,768]{1,0:T(8,128)} %get-tuple-element.26) | data formatting | bytes 4718592 | tf_op jit(solution)/shard_map/convert_element_type | solution.py:33
  90.6 3.1 %copy.24 = f32[768,768]{0,1:T(8,128)} copy(f32[768,768]{1,0:T(8,128)} %get-tuple-element.31) | data formatting | bytes 4718592 | tf_op jit(solution)/shard_map/convert_element_type | solution.py:33
  93.6 3.1 %copy.25 = f32[768,768]{0,1:T(8,128)} copy(f32[768,768]{1,0:T(8,128)} %get-tuple-element.25) | data formatting | bytes 4718592 | tf_op jit(solution)/shard_map/convert_element_type | solution.py:33
  96.7 2.0 copy.19
  98.7 3.5 %fusion.34 = bf16[768,768]{1,0:T(8,128)(2,1)} fusion(f32[768,768]{0,1:T(8,128)} %copy.19, f32[]{:T(128)S(6)} %convert_element_type.127, bf16[7,768,768]{2,1,0:T(8,128)(2,1)} %param.20), kind=kLoop, calls=%fused_computation.41 | loop fusion | flops 4128768 | bytes 4718596 | tf_op jit(solution)/shard_map/convert_element_type | solution.py:35
  102.2 10.2 %fusion.4 = (bf16[768,768]{1,0:T(8,128)(2,1)S(1)}, bf16[768,768]{1,0:T(8,128)(2,1)S(1)}, bf16[768,768]{1,0:T(8,128)(2,1)S(1)}, bf16[768,768]{1,0:T(8,128)(2,1)},...) fusion(f32[768,768]{0,1:T(8,128)} %copy.25, f32[]{:T(128)S(6)} %convert_element_type.157, ...), kind=kLoop, calls=%fused_computation.5 | loop fusion | flops 24772608 | bytes 28311576 | tf_op jit(solution)/shard_map/convert_element_type | solution.py:35
  112.5 1.8 convolution_bitcast_fusion.27
  114.3 1.8 convolution_bitcast_fusion.26
  116.7 0.7 copy-done.3
  117.3 1.2 copy-done.4
  122.6 0.6 copy-done.1
  125.5 0.6 copy-done
  132.3 0.7 convolution_bitcast_fusion.5
  135.4 2.4 %convert_element_type.159 = bf16[2,7680,128]{2,1,0:T(8,128)(2,1)} convert(f32[2,7680,128]{2,1,0:T(8,128)S(1)} %fusion.69) | non-fusion elementwise | flops 1966080 | bytes 11796480 | tf_op jit(solution)/shard_map/convert_element_type | solution.py:100
  137.8 1.0 copy-done.6
  138.9 10.5 %all-gather.5.cloned.1.call-done = bf16[2,960,512]{2,1,0:T(8,128)(2,1)} async-done(((bf16[2,960,128]{2,1,0:T(8,128)(2,1)}), bf16[2,960,512]{2,1,0:T(8,128)(2,1)}) %all-gather.5.cloned.1.call-update) | async-done | bytes 1966096 | tf_op jit(solution)/shard_map/all_gather | solution.py:69
  149.4 1.8 fusion.41
  151.2 1.6 fusion.38
  153.6 47.9 %reduce-scatter.2.cloned.1.call-done = bf16[2,960,128]{2,1,0:T(8,128)(2,1)} async-done(((bf16[2,7680,128]{2,1,0:T(8,128)(2,1)}), bf16[2,960,128]{2,1,0:T(8,128)(2,1)}) %reduce-scatter.2.cloned.1.call-update) | async-done | bytes 491536 | tf_op jit(solution)/shard_map/reduce_scatter | solution.py:99
  201.5 1.1 maximum_add_fusion
  202.7 0.8 pad_maximum_fusion
  (72 shorter events, 17.0 us)
Async XLA Ops:
  6.5 24.9 %copy-start.5 = (bf16[2,960,128]{2,1,0:T(8,128)(2,1)S(1)}, bf16[2,960,128]{2,1,0:T(8,128)(2,1)}, u32[]{:S(2)}) copy-start(bf16[2,960,128]{2,1,0:T(8,128)(2,1)} %param.18) | copy-start | bytes 1474564
  6.5 105.9 %all-gather.3.cloned.1.call-start = ((), (), s32[]{:S(2)}) async-start(), calls=%async_computation.1 | async-start | bytes 4423680 | tf_op jit(solution)/shard_map/all_gather | solution.py:67
  7.3 26.3 %copy-start.9 = (s32[7]{0:T(128)S(1)}, s32[7]{0:T(128)}, u32[]{:S(2)}) copy-start(s32[7]{0:T(128)} %param.21) | copy-start | bytes 88
  7.3 26.9 %copy-start.10 = (s32[55]{0:T(128)S(1)}, s32[55]{0:T(128)}, u32[]{:S(2)}) copy-start(s32[55]{0:T(128)} %constant.24.clone) | copy-start | bytes 664
  7.3 26.9 %copy-start.11 = (s32[55]{0:T(128)S(1)}, s32[55]{0:T(128)}, u32[]{:S(2)}) copy-start(s32[55]{0:T(128)} %constant.25.clone) | copy-start | bytes 664
  7.3 131.6 %all-reduce.2.cloned.1.call-start = ((), (), s32[]{:S(2)}) async-start(), calls=%async_computation.3 | async-start | bytes 524288 | tf_op jit(solution)/shard_map/psum | solution.py:76
  32.7 116.7 %all-gather.5.cloned.1.call-start = ((), (), s32[]{:S(2)}) async-start(), calls=%async_computation.4 | async-start | bytes 2457600 | tf_op jit(solution)/shard_map/all_gather | solution.py:69
  33.5 168.0 %reduce-scatter.2.cloned.1.call-start = ((), (), s32[]{:S(2)}) async-start(), calls=%async_computation.2 | async-start | bytes 4423680 | tf_op jit(solution)/shard_map/reduce_scatter | solution.py:99
  116.1 1.3 copy-start.3
  116.1 2.5 %copy-start.4 = (bf16[2,7680,128]{2,1,0:T(8,128)(2,1)S(1)}, bf16[2,7680,128]{2,1,0:T(8,128)(2,1)}, u32[]{:S(2)}) copy-start(bf16[2,7680,128]{2,1,0:T(8,128)(2,1)} %all-gather.3.cloned.1.call-done) | copy-start | bytes 11796484
  119.0 1.3 copy-start.2
  121.9 1.3 copy-start.1
  124.8 1.3 copy-start
  137.8 1.0 copy-start.6
  138.9 13.9 %copy-start.8 = (bf16[2,512,128]{2,1,0:T(8,128)(2,1)S(1)}, bf16[2,512,128]{2,1,0:T(8,128)(2,1)}, u32[]{:S(2)}) copy-start(bf16[2,512,128]{2,1,0:T(8,128)(2,1)} %all-reduce.2.cloned.1.call-done) | copy-start | bytes 786436
  149.4 3.4 %copy-start.7 = (bf16[2,960,512]{2,1,0:T(8,128)(2,1)S(1)}, bf16[2,960,512]{2,1,0:T(8,128)(2,1)}, u32[]{:S(2)}) copy-start(bf16[2,960,512]{2,1,0:T(8,128)(2,1)} %all-gather.5.cloned.1.call-done) | copy-start | bytes 5898244
Sparse Core Ops, SparseCore 0:
  9.3 38.3 all-gather.2
  50.7 53.5 all-reduce.1
  105.9 43.4 all-gather.4
  153.2 48.2 reduce-scatter.1
where the time goes:
time: 211 us; the launch traced here: 210 us
  waiting for transfers between devices  59.8 us (28%)
  between operations  43.7 us (21%)
  other arithmetic  34.6 us (16%)
  local copies, waits for them, and re-layouts  26.4 us (13%)
  matrix products  22.8 us (11%)
  blocking collectives  22.7 us (11%)
    reduce_scatter x1, waiting for transfers between devices, shards(): lax.psum_scatter(partial_value.astype(jnp.bfloat16), 'tri', scatter_dimen...  47.9 us
    all_gather x1, blocking collectives, shards(): lax.all_gather(integrals, 'vp', axis=1, tiled=True)  22.7 us
    convert_element_type x7, local copies, waits for them, and re-layouts, symmetrize(): values = block.astype(jnp.float32)  20.5 us
    dot_general x28, matrix products, mult(): return jnp.dot(weights, vectors, preferred_element_type=jnp.float32)  16.6 us
    convert_element_type x2, other arithmetic, symmetrize(): (values + diagonal * (0.5 * (values + values.T) - values)).astype(jnp.bfl...  13.8 us
    all_gather x1, waiting for transfers between devices, shards(): lax.all_gather(amplitudes, 'vp', axis=2, tiled=True)  10.5 us
    convert_element_type x1, other arithmetic, symmetrize(): values = block.astype(jnp.float32)  8.58 us
    reduce_sum x1, other arithmetic, decode(): jnp.sum(jnp.where(match, jnp.asarray(row_table), 0)).astype(jnp.int32)  5.21 us
  transfers between devices with their start and end apart: 4, of which 2 were waited for; matrix products, arithmetic and copies ran while one was open for 37% of the time, Pallas kernels for 0%

commit v1 on v0

v1 whole, which is shorter than its diff:
```python
import functools

import jax
import jax.numpy as jnp
from jax import lax
from jax.experimental import pallas as pl
from jax.experimental.pallas import tpu as pltpu
from jax.sharding import PartitionSpec as P

NB = 10
BLOCK = 768
PAIRS = NB * BLOCK
TRI_BLOCKS = NB * (NB + 1) // 2
F32 = jnp.float32
BF16 = jnp.bfloat16


def swap(value, axis_size, bit):
    pairs = [(i, i ^ (1 << bit)) for i in range(axis_size)]
    return lax.ppermute(value, "tri", pairs)


def bit_orders(bits):
    outer = list(range(1, bits))
    return outer, outer[1:] + outer[:1]


def place_index(mask, order):
    index = 0
    for bit in order:
        index = 2 * index + ((mask >> bit) & 1)
    return index


def gather_pieces(piece, axis_size, order):
    pieces = {0: piece}
    for bit in order:
        for mask in list(pieces):
            pieces[mask | (1 << bit)] = swap(pieces[mask], axis_size, bit)
    return pieces


def ladder_kernel(tri_size, orders, me_ref, code_ref, *refs):
    count = 2 * tri_size
    piece_refs = refs[:count]
    ladder_ref = refs[count]
    keep_refs = refs[count + 1:count + 3]
    send_refs = refs[count + 3:count + 5]
    amp, acc, sems = refs[count + 5:]
    rows, columns = piece_refs[0].shape
    step = pl.program_id(0)
    me = me_ref[0]

    def rows_of(mask):
        return pl.ds(pl.multiple_of((me ^ mask) * rows, rows), rows)

    @pl.when(step == 0)
    def _():
        copies = []
        for part in range(2):
            for mask in range(tri_size):
                index = part * tri_size + mask
                copy = pltpu.make_async_copy(
                    piece_refs[index],
                    amp.at[rows_of(mask), pl.ds(part * columns, columns)],
                    sems.at[index],
                )
                copy.start()
                copies.append(copy)
        acc[...] = jnp.zeros_like(acc)
        for copy in copies:
            copy.wait()

    code = code_ref[step]
    row_block = jnp.int32(0)
    start = jnp.int32(0)
    for row in range(1, NB):
        first = row * NB - row * (row - 1) // 2
        past = code >= first
        row_block = jnp.where(past, row, row_block)
        start = jnp.where(past, first, start)
    column_block = jnp.minimum(row_block + code - start, NB - 1)
    weight = jnp.where(row_block == column_block, 0.5, 1.0) * jnp.where(code < TRI_BLOCKS, 1.0, 0.0)
    at_row = pl.ds(pl.multiple_of(row_block * BLOCK, BLOCK), BLOCK)
    at_column = pl.ds(pl.multiple_of(column_block * BLOCK, BLOCK), BLOCK)
    block = ladder_ref[0]
    to_row = lax.dot_general(block, amp[at_column, :], (((1,), (0,)), ((), ())), preferred_element_type=F32)
    acc[at_row, :] += weight * to_row
    to_column = lax.dot_general(block, amp[at_row, :], (((0,), (0,)), ((), ())), preferred_element_type=F32)
    acc[at_column, :] += weight * to_column

    @pl.when(step == pl.num_programs(0) - 1)
    def _():
        for part in range(2):
            lanes = slice(part * columns, (part + 1) * columns)
            for mask in range(tri_size):
                target = send_refs[part] if mask & 1 else keep_refs[part]
                target[place_index(mask, orders[part])] = acc[rows_of(mask), lanes].astype(BF16)


def ladder(me, codes, pieces, ladder_blocks, tri_size, orders):
    slots = ladder_blocks.shape[0]
    rows, columns = pieces[0].shape
    half = jax.ShapeDtypeStruct((tri_size // 2, rows, columns), BF16)
    whole = pl.BlockSpec((tri_size // 2, rows, columns), lambda s, *_: (0, 0, 0))
    return pl.pallas_call(
        functools.partial(ladder_kernel, tri_size, orders),
        grid_spec=pltpu.PrefetchScalarGridSpec(
            num_scalar_prefetch=2,
            grid=(slots,),
            in_specs=[pl.BlockSpec(memory_space=pl.ANY)] * (2 * tri_size)
            + [pl.BlockSpec((1, BLOCK, BLOCK), lambda s, *_: (s, 0, 0))],
            out_specs=[whole] * 4,
            scratch_shapes=[
                pltpu.VMEM((PAIRS, 2 * columns), BF16),
                pltpu.VMEM((PAIRS, 2 * columns), F32),
                pltpu.SemaphoreType.DMA((2 * tri_size,)),
            ],
        ),
        out_shape=[half] * 4,
        compiler_params=pltpu.CompilerParams(
            dimension_semantics=("arbitrary",), vmem_limit_bytes=48 * 1024 * 1024
        ),
        cost_estimate=pl.CostEstimate(
            flops=slots * 8 * BLOCK * BLOCK * columns,
            bytes_accessed=slots * BLOCK * BLOCK * 2 + 8 * PAIRS * columns,
            transcendentals=0,
        ),
        name="ladder",
    )(me, codes, *pieces, ladder_blocks)


def add(*terms):
    total = terms[0].astype(F32)
    for term in terms[1:]:
        total = total + term.astype(F32)
    return total


def scatter_sum(keep, send, tri_size, order):
    terms = [keep, swap(send, tri_size, 0)]
    for bit in order:
        half = terms[0].shape[0] // 2
        outgoing = add(*[term[half:] for term in terms]).astype(BF16)
        terms = [term[:half] for term in terms] + [swap(outgoing, tri_size, bit)]
    return add(*[term[0] for term in terms])


def shards(tri_size, vp_size, amplitudes, integrals, ladder_blocks, slot_block):
    bits = tri_size.bit_length() - 1
    orders = bit_orders(bits)
    me = lax.axis_index("tri").astype(jnp.int32)

    pieces = []
    for part in range(2):
        got = gather_pieces(amplitudes[part], tri_size, orders[part] + [0])
        pieces += [got[mask] for mask in range(tri_size)]

    ring = [(i, (i + 1) % vp_size) for i in range(vp_size)]
    ints = [integrals]
    for _ in range(vp_size - 1):
        ints.append(lax.ppermute(ints[-1], "vp", ring))
    amps = [amplitudes]
    for _ in range(vp_size - 1):
        amps.append(lax.ppermute(amps[-1], "vp", ring))

    contracted = jnp.stack(
        [
            jnp.stack(
                [
                    lax.dot_general(value, amplitudes[part], (((0,), (0,)), ((), ())), preferred_element_type=F32)
                    for value in ints
                ]
            ).astype(BF16)
            for part in range(2)
        ]
    )
    summed = []
    for part in range(2):
        value = contracted[part]
        for bit in [0] + orders[part]:
            value = add(value, swap(value, tri_size, bit)).astype(BF16)
        summed.append(value)
    quad_real = jnp.zeros(amplitudes.shape[1:], F32)
    quad_imag = jnp.zeros(amplitudes.shape[1:], F32)

    def mult(left, right):
        return jnp.dot(left, right, preferred_element_type=F32)

    for step in range(vp_size):
        real, imag = amps[step][0], amps[step][1]
        c_real, c_imag = summed[0][step], summed[1][step]
        quad_real += mult(real, c_real) - mult(imag, c_imag)
        quad_imag += mult(real, c_imag) + mult(imag, c_real)

    keep_real, keep_imag, send_real, send_imag = ladder(
        me[None], slot_block, pieces, ladder_blocks, tri_size, orders
    )
    sum_real = scatter_sum(keep_real, send_real, tri_size, orders[0])
    sum_imag = scatter_sum(keep_imag, send_imag, tri_size, orders[1])
    section_real = amplitudes[0].astype(F32) + 0.5 * (sum_imag + 0.5 * quad_imag)
    section_imag = amplitudes[1].astype(F32) - 0.5 * (sum_real + 0.5 * quad_real)
    return jnp.stack([section_real, section_imag]).astype(BF16)


def solution(mesh):
    in_specs = (P(None, "tri", "vp"), P("tri", "vp"), P("tri", None, None), P("tri"))
    out_specs = P(None, "tri", "vp")
    body = functools.partial(shards, mesh.shape["tri"], mesh.shape["vp"])
    return jax.shard_map(body, mesh=mesh, in_specs=in_specs, out_specs=out_specs, check_vma=False)
```

time: 211 us -> 94.4 us (0.45)
  between operations: 43.7 us -> 0.35 us
  other arithmetic: 34.6 us -> 1.59 us
  starting transfers between devices: 0.12 us -> 25.6 us
  local copies, waits for them, and re-layouts: 26.4 us -> 1.75 us
  blocking collectives: 22.7 us -> 0 us
  waiting for transfers between devices: 59.8 us -> 40.6 us
  Pallas kernels: 0 us -> 12.5 us
  matrix products: 22.8 us -> 11.6 us
    reduce_scatter x1 -> x0, waiting for transfers between devices: 47.9 us -> none  [shards(): lax.psum_scatter(partial_value.astype(jnp.bfloat16), 'tri', scatter_dimen...]
    ppermute x0 -> x32, waiting for transfers between devices: none -> 40.6 us  [the longest x26 30.3 us: swap(): return lax.ppermute(value, 'tri', pairs)]
    ppermute x0 -> x32, starting transfers between devices: none -> 25.6 us  [the longest x26 18.9 us: swap(): return lax.ppermute(value, 'tri', pairs)]
    convert_element_type x5 -> x10, other arithmetic: 24.8 us -> 0.73 us  [the longest x4 0.46 us: scatter_sum(): outgoing = add(*[term[half:] for term in terms]).astype(BF16)]
    all_gather x1 -> x0, blocking collectives: 22.7 us -> none  [shards(): lax.all_gather(integrals, 'vp', axis=1, tiled=True)]
    convert_element_type x7 -> x0, local copies, waits for them, and re-layouts: 20.5 us -> none  [symmetrize(): values = block.astype(jnp.float32)]
    pallas_call x0 -> x1, Pallas kernels: none -> 12.5 us  [ladder(): pl.pallas_call(functools.partial(ladder_kernel, tri_size, orders), grid_s...]
    dot_general x34 -> x24, matrix products: 22.8 us -> 11.6 us  [the longest x8 8.08 us: shards(): lax.dot_general(value, amplitudes[part], (((0,), (0,)), ((), ())), prefer...]
  transfers between devices with their start and end apart: 4 -> 32, of which waited for: 2 -> 16; matrix products, arithmetic and copies ran while one was open for 37% -> 13% of each run, Pallas kernels for 0% -> 13%
where the time goes in v1:
time: 94.4 us; the launch traced here: 94 us
  waiting for transfers between devices  40.6 us (43%)
  starting transfers between devices  25.6 us (27%)
  Pallas kernels  12.5 us (13%)
  matrix products  11.6 us (12%)
  local copies, waits for them, and re-layouts  1.75 us (2%)
  other arithmetic  1.59 us (2%)
    ppermute x26, waiting for transfers between devices, swap(): return lax.ppermute(value, 'tri', pairs)  30.3 us
    ppermute x26, starting transfers between devices, swap(): return lax.ppermute(value, 'tri', pairs)  18.9 us
    pallas_call x1, Pallas kernels, ladder(): pl.pallas_call(functools.partial(ladder_kernel, tri_size, orders), grid_s...  12.5 us
    ppermute x3, waiting for transfers between devices, shards(): ints.append(lax.ppermute(ints[-1], 'vp', ring))  8.61 us
    dot_general x8, matrix products, shards(): lax.dot_general(value, amplitudes[part], (((0,), (0,)), ((), ())), prefer...  8.08 us
    dot_general x16, matrix products, mult(): return jnp.dot(left, right, preferred_element_type=F32)  3.54 us
    ppermute x3, starting transfers between devices, shards(): amps.append(lax.ppermute(amps[-1], 'vp', ring))  3.49 us
    ppermute x3, starting transfers between devices, shards(): ints.append(lax.ppermute(ints[-1], 'vp', ring))  3.21 us
  transfers between devices with their start and end apart: 32, of which 16 were waited for; matrix products, arithmetic and copies ran while one was open for 13% of the time, Pallas kernels for 13%

profile of v1, /device:TPU:0, one launch (start us, length us, event | category | flops | bytes accessed | tf_op | source)
XLA Modules:
  0.0 94.0 jit_solution(17385738869477746004)
XLA Ops:
  0.0 1.1 %slice_bitcast_fusion.6 = (bf16[960,128]{1,0:T(8,128)(2,1)S(1)}, bf16[960,128]{1,0:T(8,128)(2,1)S(1)}) fusion(bf16[2,960,128]{2,1,0:T(8,128)(2,1)} %param.4), kind=kLoop, calls=%fused_computation.61 | loop fusion | bytes 983040 | tf_op jit(solution)/shard_map/squeeze | solution.py:156
  1.1 3.0 %collective-permute-start.10 = (bf16[960,128]{1,0:T(8,128)(2,1)S(1)}, bf16[960,128]{1,0:T(8,128)(2,1)S(1)}, u32[]{:S(2)}, u32[]{:S(2)}) collective-permute-start(bf16[960,128]{1,0:T(8,128)(2,1)S(1)} %get-tuple-element.13.refs_8_), channel_id=1, source_target_pairs={{0,16},{4,20},{8,24},{12,28},{16,0},{20,4},{24,8},{28,12},{1,17},{... | collective-permute-start | bytes 737288 | tf_op jit(solution)/shard_map/ppermute | solution.py:20
  4.1 1.5 %collective-permute-start.1 = (bf16[960,128]{1,0:T(8,128)(2,1)S(1)}, bf16[960,128]{1,0:T(8,128)(2,1)S(1)}, u32[]{:S(2)}, u32[]{:S(2)}) collective-permute-start(bf16[960,128]{1,0:T(8,128)(2,1)S(1)} %get-tuple-element.14.refs_0_), channel_id=1, source_target_pairs={{0,8},{4,12},{8,0},{12,4},{16,24},{20,28},{24,16},{28,20},{1,9},{5... | collective-permute-start | bytes 737288 | tf_op jit(solution)/shard_map/ppermute | solution.py:20
  6.2 4.7 %collective-permute-done.10.refs_12_ = bf16[960,128]{1,0:T(8,128)(2,1)S(1)} collective-permute-done((bf16[960,128]{1,0:T(8,128)(2,1)S(1)}, bf16[960,128]{1,0:T(8,128)(2,1)S(1)}, u32[]{:S(2)}, u32[]{:S(2)}) %collective-permute-start.10) | collective-permute-done | bytes 245792 | tf_op jit(solution)/shard_map/ppermute | solution.py:20
  10.9 2.1 %collective-permute-done.1.refs_2_ = bf16[960,128]{1,0:T(8,128)(2,1)S(1)} collective-permute-done((bf16[960,128]{1,0:T(8,128)(2,1)S(1)}, bf16[960,128]{1,0:T(8,128)(2,1)S(1)}, u32[]{:S(2)}, u32[]{:S(2)}) %collective-permute-start.1) | collective-permute-done | bytes 245792 | tf_op jit(solution)/shard_map/ppermute | solution.py:20
  13.0 1.6 %collective-permute-start.17 = (bf16[960,128]{1,0:T(8,128)(2,1)}, bf16[960,128]{1,0:T(8,128)(2,1)S(1)}, u32[]{:S(2)}, u32[]{:S(2)}) collective-permute-start(bf16[960,128]{1,0:T(8,128)(2,1)} %param.5), channel_id=1, source_target_pairs={{0,1},{1,2},{2,3},{3,0},{4,5},{5,6},{6,7},{7,4},{8,9},{9,10},{10,1... | collective-permute-start | bytes 737288 | tf_op jit(solution)/shard_map/ppermute | solution.py:162
  15.4 1.7 %collective-permute-start.12 = (bf16[960,128]{1,0:T(8,128)(2,1)S(1)}, bf16[960,128]{1,0:T(8,128)(2,1)S(1)}, u32[]{:S(2)}, u32[]{:S(2)}) collective-permute-start(bf16[960,128]{1,0:T(8,128)(2,1)S(1)} %collective-permute-done.10.refs_12_), channel_id=1, source_target_pairs={{0,8},{4,12},{8,0},{12,4},{16,24},{20,28},{24,16},{28,20},{1,9},{5... | collective-permute-start | bytes 737288 | tf_op jit(solution)/shard_map/ppermute | solution.py:20
  17.1 1.3 %fusion.20 = bf16[1,128,128]{2,1,0:T(8,128)(2,1)S(1)} fusion(bf16[960,128]{1,0:T(8,128)(2,1)} %param.5, bf16[2,960,128]{2,1,0:T(8,128)(2,1)} %param.4), kind=kOutput, calls=%fused_computation.36 | convolution fusion | flops 31473664 | bytes 524288 | tf_op jit(solution)/shard_map/dot_general | solution.py:171
  18.4 1.3 %fusion.24 = bf16[1,128,128]{2,1,0:T(8,128)(2,1)S(1)} fusion(bf16[960,128]{1,0:T(8,128)(2,1)} %param.5, bf16[2,960,128]{2,1,0:T(8,128)(2,1)} %param.4), kind=kOutput, calls=%fused_computation.40 | convolution fusion | flops 31473664 | bytes 524288 | tf_op jit(solution)/shard_map/dot_general | solution.py:171
  19.7 1.6 %collective-permute-start.26 = (bf16[2,960,128]{2,1,0:T(8,128)(2,1)}, bf16[2,960,128]{2,1,0:T(8,128)(2,1)S(1)}, u32[]{:S(2)}, u32[]{:S(2)}) collective-permute-start(bf16[2,960,128]{2,1,0:T(8,128)(2,1)} %param.4), channel_id=1, source_target_pairs={{0,1},{1,2},{2,3},{3,0},{4,5},{5,6},{6,7},{7,4},{8,9},{9,10},{10,1... | collective-permute-start | bytes 1474568 | tf_op jit(solution)/shard_map/ppermute | solution.py:165
  21.4 1.6 %collective-permute-start.5 = (bf16[960,128]{1,0:T(8,128)(2,1)S(1)}, bf16[960,128]{1,0:T(8,128)(2,1)S(1)}, u32[]{:S(2)}, u32[]{:S(2)}) collective-permute-start(bf16[960,128]{1,0:T(8,128)(2,1)S(1)} %collective-permute-done.1.refs_2_), channel_id=1, source_target_pairs={{0,16},{4,20},{8,24},{12,28},{16,0},{20,4},{24,8},{28,12},{1,17},{... | collective-permute-start | bytes 737288 | tf_op jit(solution)/shard_map/ppermute | solution.py:20
  23.1 1.6 %collective-permute-start.18 = (bf16[960,128]{1,0:T(8,128)(2,1)S(1)}, bf16[960,128]{1,0:T(8,128)(2,1)S(1)}, u32[]{:S(2)}, u32[]{:S(2)}) collective-permute-start(bf16[960,128]{1,0:T(8,128)(2,1)S(1)} %collective-permute-done.17), channel_id=1, source_target_pairs={{0,1},{1,2},{2,3},{3,0},{4,5},{5,6},{6,7},{7,4},{8,9},{9,10},{10,1... | collective-permute-start | bytes 737288 | tf_op jit(solution)/shard_map/ppermute | solution.py:162
  24.7 1.2 %fusion.21 = bf16[1,128,128]{2,1,0:T(8,128)(2,1)S(1)} fusion(bf16[960,128]{1,0:T(8,128)(2,1)S(1)} %collective-permute-done.17, bf16[2,960,128]{2,1,0:T(8,128)(2,1)} %param.4), kind=kOutput, calls=%fused_computation.37 | convolution fusion | flops 31473664 | bytes 524288 | tf_op jit(solution)/shard_map/dot_general | solution.py:171
  25.9 1.2 %fusion.25 = bf16[1,128,128]{2,1,0:T(8,128)(2,1)S(1)} fusion(bf16[960,128]{1,0:T(8,128)(2,1)S(1)} %collective-permute-done.17, bf16[2,960,128]{2,1,0:T(8,128)(2,1)} %param.4), kind=kOutput, calls=%fused_computation.41 | convolution fusion | flops 31473664 | bytes 524288 | tf_op jit(solution)/shard_map/dot_general | solution.py:171
  27.2 2.6 %collective-permute-done.5.refs_6_ = bf16[960,128]{1,0:T(8,128)(2,1)S(1)} collective-permute-done((bf16[960,128]{1,0:T(8,128)(2,1)S(1)}, bf16[960,128]{1,0:T(8,128)(2,1)S(1)}, u32[]{:S(2)}, u32[]{:S(2)}) %collective-permute-start.5) | collective-permute-done | bytes 245792 | tf_op jit(solution)/shard_map/ppermute | solution.py:20
  30.3 8.6 %collective-permute-done.18 = bf16[960,128]{1,0:T(8,128)(2,1)S(1)} collective-permute-done((bf16[960,128]{1,0:T(8,128)(2,1)S(1)}, bf16[960,128]{1,0:T(8,128)(2,1)S(1)}, u32[]{:S(2)}, u32[]{:S(2)}) %collective-permute-start.18) | collective-permute-done | bytes 245792 | tf_op jit(solution)/shard_map/ppermute | solution.py:162
  39.0 1.2 %fusion.22 = bf16[1,128,128]{2,1,0:T(8,128)(2,1)S(1)} fusion(bf16[960,128]{1,0:T(8,128)(2,1)S(1)} %collective-permute-done.18, bf16[2,960,128]{2,1,0:T(8,128)(2,1)} %param.4), kind=kOutput, calls=%fused_computation.38 | convolution fusion | flops 31473664 | bytes 524288 | tf_op jit(solution)/shard_map/dot_general | solution.py:171
  40.2 1.2 %fusion.26 = bf16[1,128,128]{2,1,0:T(8,128)(2,1)S(1)} fusion(bf16[960,128]{1,0:T(8,128)(2,1)S(1)} %collective-permute-done.18, bf16[2,960,128]{2,1,0:T(8,128)(2,1)} %param.4), kind=kOutput, calls=%fused_computation.42 | convolution fusion | flops 31473664 | bytes 524288 | tf_op jit(solution)/shard_map/dot_general | solution.py:171
  41.5 1.3 %collective-permute-start.27 = (bf16[2,960,128]{2,1,0:T(8,128)(2,1)S(1)}, bf16[2,960,128]{2,1,0:T(8,128)(2,1)S(1)}, u32[]{:S(2)}, u32[]{:S(2)}) collective-permute-start(bf16[2,960,128]{2,1,0:T(8,128)(2,1)S(1)} %collective-permute-done.26), channel_id=1, source_target_pairs={{0,1},{1,2},{2,3},{3,0},{4,5},{5,6},{6,7},{7,4},{8,9},{9,10},{10,1... | collective-permute-start | bytes 1474568 | tf_op jit(solution)/shard_map/ppermute | solution.py:165
  43.4 12.5 %ladder.1 = (bf16[4,960,128]{2,1,0:T(8,128)(2,1)S(1)}, bf16[4,960,128]{2,1,0:T(8,128)(2,1)S(1)}, bf16[4,960,128]{2,1,0:T(8,128)(2,1)}, bf16[4,960,128]{2,1,0:T(8,128)(2,1)}) custom-call(s32[1]{0:T(128)} %bitcast.1.me_ref, s32[7]{0:T(128)S(1)} %copy-done, bf16[960,128]{1,0:T(8,128)(2,1)S(1)} %get-tuple-element.14.refs_0_, ...), custom_call_target="tpu_custom_call" | custom-call | flops 4227858432 | bytes 16121856 | tf_op jit(solution)/shard_map/ladder/pallas_call | solution.py:106
  57.7 1.2 %collective-permute-done.20 = bf16[4,128,128]{2,1,0:T(8,128)(2,1)S(1)} collective-permute-done((bf16[4,128,128]{2,1,0:T(8,128)(2,1)S(1)}, bf16[4,128,128]{2,1,0:T(8,128)(2,1)S(1)}, u32[]{:S(2)}, u32[]{:S(2)}) %collective-permute-start.20) | collective-permute-done | bytes 131104 | tf_op jit(solution)/shard_map/ppermute | solution.py:20
  59.0 1.6 %collective-permute-start.21 = (bf16[4,128,128]{2,1,0:T(8,128)(2,1)S(1)}, bf16[4,128,128]{2,1,0:T(8,128)(2,1)S(1)}, u32[]{:S(2)}, u32[]{:S(2)}) collective-permute-start(bf16[4,128,128]{2,1,0:T(8,128)(2,1)S(1)} %add_convert_fusion.9), channel_id=1, source_target_pairs={{0,16},{4,20},{8,24},{12,28},{16,0},{20,4},{24,8},{28,12},{1,17},{... | collective-permute-start | bytes 393224 | tf_op jit(solution)/shard_map/ppermute | solution.py:20
  61.2 1.0 %collective-permute-done.27 = bf16[2,960,128]{2,1,0:T(8,128)(2,1)S(1)} collective-permute-done((bf16[2,960,128]{2,1,0:T(8,128)(2,1)S(1)}, bf16[2,960,128]{2,1,0:T(8,128)(2,1)S(1)}, u32[]{:S(2)}, u32[]{:S(2)}) %collective-permute-start.27) | collective-permute-done | bytes 491552 | tf_op jit(solution)/shard_map/ppermute | solution.py:165
  62.8 1.8 %collective-permute-done.21 = bf16[4,128,128]{2,1,0:T(8,128)(2,1)S(1)} collective-permute-done((bf16[4,128,128]{2,1,0:T(8,128)(2,1)S(1)}, bf16[4,128,128]{2,1,0:T(8,128)(2,1)S(1)}, u32[]{:S(2)}, u32[]{:S(2)}) %collective-permute-start.21) | collective-permute-done | bytes 131104 | tf_op jit(solution)/shard_map/ppermute | solution.py:20
  66.9 2.8 %collective-permute-done.22 = bf16[4,128,128]{2,1,0:T(8,128)(2,1)S(1)} collective-permute-done((bf16[4,128,128]{2,1,0:T(8,128)(2,1)S(1)}, bf16[4,128,128]{2,1,0:T(8,128)(2,1)S(1)}, u32[]{:S(2)}, u32[]{:S(2)}) %collective-permute-start.22) | collective-permute-done | bytes 131104 | tf_op jit(solution)/shard_map/ppermute | solution.py:20
  69.9 1.1 %collective-permute-done.25 = bf16[4,128,128]{2,1,0:T(8,128)(2,1)S(1)} collective-permute-done((bf16[4,128,128]{2,1,0:T(8,128)(2,1)S(1)}, bf16[4,128,128]{2,1,0:T(8,128)(2,1)S(1)}, u32[]{:S(2)}, u32[]{:S(2)}) %collective-permute-start.25) | collective-permute-done | bytes 131104 | tf_op jit(solution)/shard_map/ppermute | solution.py:20
  74.6 1.6 %collective-permute-start.30 = (bf16[2,960,128]{2,1,0:T(8,128)(2,1)S(1)}, bf16[2,960,128]{2,1,0:T(8,128)(2,1)S(1)}, u32[]{:S(2)}, u32[]{:S(2)}) collective-permute-start(bf16[2,960,128]{2,1,0:T(8,128)(2,1)S(1)} %add_convert_fusion), channel_id=1, source_target_pairs={{0,8},{4,12},{8,0},{12,4},{16,24},{20,28},{24,16},{28,20},{1,9},{5... | collective-permute-start | bytes 1474568 | tf_op jit(solution)/shard_map/ppermute | solution.py:20
  77.1 7.8 %collective-permute-done.15 = bf16[2,960,128]{2,1,0:T(8,128)(2,1)S(1)} collective-permute-done((bf16[2,960,128]{2,1,0:T(8,128)(2,1)S(1)}, bf16[2,960,128]{2,1,0:T(8,128)(2,1)S(1)}, u32[]{:S(2)}, u32[]{:S(2)}) %collective-permute-start.15) | collective-permute-done | bytes 491552 | tf_op jit(solution)/shard_map/ppermute | solution.py:20
  85.0 0.9 collective-permute-start.16
  86.5 1.5 %collective-permute-start.31 = (bf16[1,960,128]{2,1,0:T(8,128)(2,1)S(1)}, bf16[1,960,128]{2,1,0:T(8,128)(2,1)S(1)}, u32[]{:S(2)}, u32[]{:S(2)}) collective-permute-start(bf16[1,960,128]{2,1,0:T(8,128)(2,1)S(1)} %add_convert_fusion.2), channel_id=1, source_target_pairs={{0,16},{4,20},{8,24},{12,28},{16,0},{20,4},{24,8},{28,12},{1,17},{... | collective-permute-start | bytes 737288 | tf_op jit(solution)/shard_map/ppermute | solution.py:20
  88.2 3.1 %collective-permute-done.16 = bf16[1,960,128]{2,1,0:T(8,128)(2,1)S(1)} collective-permute-done((bf16[1,960,128]{2,1,0:T(8,128)(2,1)S(1)}, bf16[1,960,128]{2,1,0:T(8,128)(2,1)S(1)}, u32[]{:S(2)}, u32[]{:S(2)}) %collective-permute-start.16) | collective-permute-done | bytes 245792 | tf_op jit(solution)/shard_map/ppermute | solution.py:20
  91.6 1.2 %collective-permute-done.31 = bf16[1,960,128]{2,1,0:T(8,128)(2,1)S(1)} collective-permute-done((bf16[1,960,128]{2,1,0:T(8,128)(2,1)S(1)}, bf16[1,960,128]{2,1,0:T(8,128)(2,1)S(1)}, u32[]{:S(2)}, u32[]{:S(2)}) %collective-permute-start.31) | collective-permute-done | bytes 245792 | tf_op jit(solution)/shard_map/ppermute | solution.py:20
  (75 shorter events, 15.3 us)
Async XLA Ops:
  1.1 9.8 %collective-permute-start.10 = (bf16[960,128]{1,0:T(8,128)(2,1)S(1)}, bf16[960,128]{1,0:T(8,128)(2,1)S(1)}, u32[]{:S(2)}, u32[]{:S(2)}) collective-permute-start(bf16[960,128]{1,0:T(8,128)(2,1)S(1)} %get-tuple-element.13.refs_8_), channel_id=1, source_target_pairs={{0,16},{4,20},{8,24},{12,28},{16,0},{20,4},{24,8},{28,12},{1,17},{... | collective-permute-start | bytes 737288 | tf_op jit(solution)/shard_map/ppermute | solution.py:20
  4.1 8.9 %collective-permute-start.1 = (bf16[960,128]{1,0:T(8,128)(2,1)S(1)}, bf16[960,128]{1,0:T(8,128)(2,1)S(1)}, u32[]{:S(2)}, u32[]{:S(2)}) collective-permute-start(bf16[960,128]{1,0:T(8,128)(2,1)S(1)} %get-tuple-element.14.refs_0_), channel_id=1, source_target_pairs={{0,8},{4,12},{8,0},{12,4},{16,24},{20,28},{24,16},{28,20},{1,9},{5... | collective-permute-start | bytes 737288 | tf_op jit(solution)/shard_map/ppermute | solution.py:20
  5.6 9.7 %collective-permute-start.3 = (bf16[960,128]{1,0:T(8,128)(2,1)S(1)}, bf16[960,128]{1,0:T(8,128)(2,1)S(1)}, u32[]{:S(2)}, u32[]{:S(2)}) collective-permute-start(bf16[960,128]{1,0:T(8,128)(2,1)S(1)} %get-tuple-element.14.refs_0_), channel_id=1, source_target_pairs={{0,16},{4,20},{8,24},{12,28},{16,0},{20,4},{24,8},{28,12},{1,17},{... | collective-permute-start | bytes 737288 | tf_op jit(solution)/shard_map/ppermute | solution.py:20
  6.1 13.6 %collective-permute-start.8 = (bf16[960,128]{1,0:T(8,128)(2,1)S(1)}, bf16[960,128]{1,0:T(8,128)(2,1)S(1)}, u32[]{:S(2)}, u32[]{:S(2)}) collective-permute-start(bf16[960,128]{1,0:T(8,128)(2,1)S(1)} %get-tuple-element.13.refs_8_), channel_id=1, source_target_pairs={{0,8},{4,12},{8,0},{12,4},{16,24},{20,28},{24,16},{28,20},{1,9},{5... | collective-permute-start | bytes 737288 | tf_op jit(solution)/shard_map/ppermute | solution.py:20
  6.2 15.1 %collective-permute-start = (bf16[960,128]{1,0:T(8,128)(2,1)S(1)}, bf16[960,128]{1,0:T(8,128)(2,1)S(1)}, u32[]{:S(2)}, u32[]{:S(2)}) collective-permute-start(bf16[960,128]{1,0:T(8,128)(2,1)S(1)} %get-tuple-element.14.refs_0_), channel_id=1, source_target_pairs={{0,4},{4,0},{8,12},{12,8},{16,20},{20,16},{24,28},{28,24},{1,5},{5... | collective-permute-start | bytes 737288 | tf_op jit(solution)/shard_map/ppermute | solution.py:20
  10.9 10.5 %collective-permute-start.7 = (bf16[960,128]{1,0:T(8,128)(2,1)S(1)}, bf16[960,128]{1,0:T(8,128)(2,1)S(1)}, u32[]{:S(2)}, u32[]{:S(2)}) collective-permute-start(bf16[960,128]{1,0:T(8,128)(2,1)S(1)} %get-tuple-element.13.refs_8_), channel_id=1, source_target_pairs={{0,4},{4,0},{8,12},{12,8},{16,20},{20,16},{24,28},{28,24},{1,5},{5... | collective-permute-start | bytes 737288 | tf_op jit(solution)/shard_map/ppermute | solution.py:20
  13.0 10.0 %collective-permute-start.17 = (bf16[960,128]{1,0:T(8,128)(2,1)}, bf16[960,128]{1,0:T(8,128)(2,1)S(1)}, u32[]{:S(2)}, u32[]{:S(2)}) collective-permute-start(bf16[960,128]{1,0:T(8,128)(2,1)} %param.5), channel_id=1, source_target_pairs={{0,1},{1,2},{2,3},{3,0},{4,5},{5,6},{6,7},{7,4},{8,9},{9,10},{10,1... | collective-permute-start | bytes 737288 | tf_op jit(solution)/shard_map/ppermute | solution.py:162
  15.4 7.8 %collective-permute-start.12 = (bf16[960,128]{1,0:T(8,128)(2,1)S(1)}, bf16[960,128]{1,0:T(8,128)(2,1)S(1)}, u32[]{:S(2)}, u32[]{:S(2)}) collective-permute-start(bf16[960,128]{1,0:T(8,128)(2,1)S(1)} %collective-permute-done.10.refs_12_), channel_id=1, source_target_pairs={{0,8},{4,12},{8,0},{12,4},{16,24},{20,28},{24,16},{28,20},{1,9},{5... | collective-permute-start | bytes 737288 | tf_op jit(solution)/shard_map/ppermute | solution.py:20
  19.7 21.7 %collective-permute-start.26 = (bf16[2,960,128]{2,1,0:T(8,128)(2,1)}, bf16[2,960,128]{2,1,0:T(8,128)(2,1)S(1)}, u32[]{:S(2)}, u32[]{:S(2)}) collective-permute-start(bf16[2,960,128]{2,1,0:T(8,128)(2,1)} %param.4), channel_id=1, source_target_pairs={{0,1},{1,2},{2,3},{3,0},{4,5},{5,6},{6,7},{7,4},{8,9},{9,10},{10,1... | collective-permute-start | bytes 1474568 | tf_op jit(solution)/shard_map/ppermute | solution.py:165
  21.4 8.4 %collective-permute-start.11 = (bf16[960,128]{1,0:T(8,128)(2,1)S(1)}, bf16[960,128]{1,0:T(8,128)(2,1)S(1)}, u32[]{:S(2)}, u32[]{:S(2)}) collective-permute-start(bf16[960,128]{1,0:T(8,128)(2,1)S(1)} %collective-permute-done.10.refs_12_), channel_id=1, source_target_pairs={{0,4},{4,0},{8,12},{12,8},{16,20},{20,16},{24,28},{28,24},{1,5},{5... | collective-permute-start | bytes 737288 | tf_op jit(solution)/shard_map/ppermute | solution.py:20
  21.4 8.4 %collective-permute-start.5 = (bf16[960,128]{1,0:T(8,128)(2,1)S(1)}, bf16[960,128]{1,0:T(8,128)(2,1)S(1)}, u32[]{:S(2)}, u32[]{:S(2)}) collective-permute-start(bf16[960,128]{1,0:T(8,128)(2,1)S(1)} %collective-permute-done.1.refs_2_), channel_id=1, source_target_pairs={{0,16},{4,20},{8,24},{12,28},{16,0},{20,4},{24,8},{28,12},{1,17},{... | collective-permute-start | bytes 737288 | tf_op jit(solution)/shard_map/ppermute | solution.py:20
  23.0 7.3 %collective-permute-start.2 = (bf16[960,128]{1,0:T(8,128)(2,1)S(1)}, bf16[960,128]{1,0:T(8,128)(2,1)S(1)}, u32[]{:S(2)}, u32[]{:S(2)}) collective-permute-start(bf16[960,128]{1,0:T(8,128)(2,1)S(1)} %collective-permute-done.1.refs_2_), channel_id=1, source_target_pairs={{0,4},{4,0},{8,12},{12,8},{16,20},{20,16},{24,28},{28,24},{1,5},{5... | collective-permute-start | bytes 737288 | tf_op jit(solution)/shard_map/ppermute | solution.py:20
  23.1 15.8 %collective-permute-start.18 = (bf16[960,128]{1,0:T(8,128)(2,1)S(1)}, bf16[960,128]{1,0:T(8,128)(2,1)S(1)}, u32[]{:S(2)}, u32[]{:S(2)}) collective-permute-start(bf16[960,128]{1,0:T(8,128)(2,1)S(1)} %collective-permute-done.17), channel_id=1, source_target_pairs={{0,1},{1,2},{2,3},{3,0},{4,5},{5,6},{6,7},{7,4},{8,9},{9,10},{10,1... | collective-permute-start | bytes 737288 | tf_op jit(solution)/shard_map/ppermute | solution.py:162
  29.8 11.7 %collective-permute-start.4 = (bf16[960,128]{1,0:T(8,128)(2,1)S(1)}, bf16[960,128]{1,0:T(8,128)(2,1)S(1)}, u32[]{:S(2)}, u32[]{:S(2)}) collective-permute-start(bf16[960,128]{1,0:T(8,128)(2,1)S(1)} %collective-permute-done.3.refs_4_), channel_id=1, source_target_pairs={{0,4},{4,0},{8,12},{12,8},{16,20},{20,16},{24,28},{28,24},{1,5},{5... | collective-permute-start | bytes 737288 | tf_op jit(solution)/shard_map/ppermute | solution.py:20
  29.8 13.0 %collective-permute-start.9 = (bf16[960,128]{1,0:T(8,128)(2,1)S(1)}, bf16[960,128]{1,0:T(8,128)(2,1)S(1)}, u32[]{:S(2)}, u32[]{:S(2)}) collective-permute-start(bf16[960,128]{1,0:T(8,128)(2,1)S(1)} %collective-permute-done.8.refs_10_), channel_id=1, source_target_pairs={{0,4},{4,0},{8,12},{12,8},{16,20},{20,16},{24,28},{28,24},{1,5},{5... | collective-permute-start | bytes 737288 | tf_op jit(solution)/shard_map/ppermute | solution.py:20
  30.3 12.5 %collective-permute-start.13 = (bf16[960,128]{1,0:T(8,128)(2,1)S(1)}, bf16[960,128]{1,0:T(8,128)(2,1)S(1)}, u32[]{:S(2)}, u32[]{:S(2)}) collective-permute-start(bf16[960,128]{1,0:T(8,128)(2,1)S(1)} %collective-permute-done.12.refs_14_), channel_id=1, source_target_pairs={{0,4},{4,0},{8,12},{12,8},{16,20},{20,16},{24,28},{28,24},{1,5},{5... | collective-permute-start | bytes 737288 | tf_op jit(solution)/shard_map/ppermute | solution.py:20
  39.0 3.8 %collective-permute-start.6 = (bf16[960,128]{1,0:T(8,128)(2,1)S(1)}, bf16[960,128]{1,0:T(8,128)(2,1)S(1)}, u32[]{:S(2)}, u32[]{:S(2)}) collective-permute-start(bf16[960,128]{1,0:T(8,128)(2,1)S(1)} %collective-permute-done.5.refs_6_), channel_id=1, source_target_pairs={{0,4},{4,0},{8,12},{12,8},{16,20},{20,16},{24,28},{28,24},{1,5},{5... | collective-permute-start | bytes 737288 | tf_op jit(solution)/shard_map/ppermute | solution.py:20
  41.4 14.6 %collective-permute-start.19 = (bf16[960,128]{1,0:T(8,128)(2,1)S(1)}, bf16[960,128]{1,0:T(8,128)(2,1)S(1)}, u32[]{:S(2)}, u32[]{:S(2)}) collective-permute-start(bf16[960,128]{1,0:T(8,128)(2,1)S(1)} %collective-permute-done.18), channel_id=1, source_target_pairs={{0,1},{1,2},{2,3},{3,0},{4,5},{5,6},{6,7},{7,4},{8,9},{9,10},{10,1... | collective-permute-start | bytes 737288 | tf_op jit(solution)/shard_map/ppermute | solution.py:162
  41.5 20.7 %collective-permute-start.27 = (bf16[2,960,128]{2,1,0:T(8,128)(2,1)S(1)}, bf16[2,960,128]{2,1,0:T(8,128)(2,1)S(1)}, u32[]{:S(2)}, u32[]{:S(2)}) collective-permute-start(bf16[2,960,128]{2,1,0:T(8,128)(2,1)S(1)} %collective-permute-done.26), channel_id=1, source_target_pairs={{0,1},{1,2},{2,3},{3,0},{4,5},{5,6},{6,7},{7,4},{8,9},{9,10},{10,1... | collective-permute-start | bytes 1474568 | tf_op jit(solution)/shard_map/ppermute | solution.py:165
  55.9 17.5 %collective-permute-start.14 = (bf16[4,960,128]{2,1,0:T(8,128)(2,1)}, bf16[4,960,128]{2,1,0:T(8,128)(2,1)S(1)}, u32[]{:S(2)}, u32[]{:S(2)}) collective-permute-start(bf16[4,960,128]{2,1,0:T(8,128)(2,1)} %get-tuple-element.10), channel_id=1, source_target_pairs={{0,4},{4,0},{8,12},{12,8},{16,20},{20,16},{24,28},{28,24},{1,5},{5... | collective-permute-start | bytes 2949128 | tf_op jit(solution)/shard_map/ppermute | solution.py:20
  56.3 2.6 %collective-permute-start.20 = (bf16[4,128,128]{2,1,0:T(8,128)(2,1)S(1)}, bf16[4,128,128]{2,1,0:T(8,128)(2,1)S(1)}, u32[]{:S(2)}, u32[]{:S(2)}) collective-permute-start(bf16[4,128,128]{2,1,0:T(8,128)(2,1)S(1)} %pad_maximum_fusion.1), channel_id=1, source_target_pairs={{0,4},{4,0},{8,12},{12,8},{16,20},{20,16},{24,28},{28,24},{1,5},{5... | collective-permute-start | bytes 393224 | tf_op jit(solution)/shard_map/ppermute | solution.py:20
  57.2 3.4 %collective-permute-start.23 = (bf16[4,128,128]{2,1,0:T(8,128)(2,1)S(1)}, bf16[4,128,128]{2,1,0:T(8,128)(2,1)S(1)}, u32[]{:S(2)}, u32[]{:S(2)}) collective-permute-start(bf16[4,128,128]{2,1,0:T(8,128)(2,1)S(1)} %pad_maximum_fusion.2), channel_id=1, source_target_pairs={{0,4},{4,0},{8,12},{12,8},{16,20},{20,16},{24,28},{28,24},{1,5},{5... | collective-permute-start | bytes 393224 | tf_op jit(solution)/shard_map/ppermute | solution.py:20
  57.3 17.2 %collective-permute-start.29 = (bf16[4,960,128]{2,1,0:T(8,128)(2,1)}, bf16[4,960,128]{2,1,0:T(8,128)(2,1)S(1)}, u32[]{:S(2)}, u32[]{:S(2)}) collective-permute-start(bf16[4,960,128]{2,1,0:T(8,128)(2,1)} %get-tuple-element.12), channel_id=1, source_target_pairs={{0,4},{4,0},{8,12},{12,8},{16,20},{20,16},{24,28},{28,24},{1,5},{5... | collective-permute-start | bytes 2949128 | tf_op jit(solution)/shard_map/ppermute | solution.py:20
  59.0 5.6 %collective-permute-start.21 = (bf16[4,128,128]{2,1,0:T(8,128)(2,1)S(1)}, bf16[4,128,128]{2,1,0:T(8,128)(2,1)S(1)}, u32[]{:S(2)}, u32[]{:S(2)}) collective-permute-start(bf16[4,128,128]{2,1,0:T(8,128)(2,1)S(1)} %add_convert_fusion.9), channel_id=1, source_target_pairs={{0,16},{4,20},{8,24},{12,28},{16,0},{20,4},{24,8},{28,12},{1,17},{... | collective-permute-start | bytes 393224 | tf_op jit(solution)/shard_map/ppermute | solution.py:20
  60.6 5.3 %collective-permute-start.24 = (bf16[4,128,128]{2,1,0:T(8,128)(2,1)S(1)}, bf16[4,128,128]{2,1,0:T(8,128)(2,1)S(1)}, u32[]{:S(2)}, u32[]{:S(2)}) collective-permute-start(bf16[4,128,128]{2,1,0:T(8,128)(2,1)S(1)} %add_convert_fusion.6), channel_id=1, source_target_pairs={{0,8},{4,12},{8,0},{12,4},{16,24},{20,28},{24,16},{28,20},{1,9},{5... | collective-permute-start | bytes 393224 | tf_op jit(solution)/shard_map/ppermute | solution.py:20
  62.2 14.7 %collective-permute-start.28 = (bf16[2,960,128]{2,1,0:T(8,128)(2,1)S(1)}, bf16[2,960,128]{2,1,0:T(8,128)(2,1)S(1)}, u32[]{:S(2)}, u32[]{:S(2)}) collective-permute-start(bf16[2,960,128]{2,1,0:T(8,128)(2,1)S(1)} %collective-permute-done.27), channel_id=1, source_target_pairs={{0,1},{1,2},{2,3},{3,0},{4,5},{5,6},{6,7},{7,4},{8,9},{9,10},{10,1... | collective-permute-start | bytes 1474568 | tf_op jit(solution)/shard_map/ppermute | solution.py:165
  64.6 5.0 %collective-permute-start.22 = (bf16[4,128,128]{2,1,0:T(8,128)(2,1)S(1)}, bf16[4,128,128]{2,1,0:T(8,128)(2,1)S(1)}, u32[]{:S(2)}, u32[]{:S(2)}) collective-permute-start(bf16[4,128,128]{2,1,0:T(8,128)(2,1)S(1)} %add_convert_fusion.8), channel_id=1, source_target_pairs={{0,8},{4,12},{8,0},{12,4},{16,24},{20,28},{24,16},{28,20},{1,9},{5... | collective-permute-start | bytes 393224 | tf_op jit(solution)/shard_map/ppermute | solution.py:20
  66.0 5.0 %collective-permute-start.25 = (bf16[4,128,128]{2,1,0:T(8,128)(2,1)S(1)}, bf16[4,128,128]{2,1,0:T(8,128)(2,1)S(1)}, u32[]{:S(2)}, u32[]{:S(2)}) collective-permute-start(bf16[4,128,128]{2,1,0:T(8,128)(2,1)S(1)} %add_convert_fusion.5), channel_id=1, source_target_pairs={{0,16},{4,20},{8,24},{12,28},{16,0},{20,4},{24,8},{28,12},{1,17},{... | collective-permute-start | bytes 393224 | tf_op jit(solution)/shard_map/ppermute | solution.py:20
  73.5 11.3 %collective-permute-start.15 = (bf16[2,960,128]{2,1,0:T(8,128)(2,1)S(1)}, bf16[2,960,128]{2,1,0:T(8,128)(2,1)S(1)}, u32[]{:S(2)}, u32[]{:S(2)}) collective-permute-start(bf16[2,960,128]{2,1,0:T(8,128)(2,1)S(1)} %add_convert_fusion.1), channel_id=1, source_target_pairs={{0,16},{4,20},{8,24},{12,28},{16,0},{20,4},{24,8},{28,12},{1,17},{... | collective-permute-start | bytes 1474568 | tf_op jit(solution)/shard_map/ppermute | solution.py:20
  74.6 11.8 %collective-permute-start.30 = (bf16[2,960,128]{2,1,0:T(8,128)(2,1)S(1)}, bf16[2,960,128]{2,1,0:T(8,128)(2,1)S(1)}, u32[]{:S(2)}, u32[]{:S(2)}) collective-permute-start(bf16[2,960,128]{2,1,0:T(8,128)(2,1)S(1)} %add_convert_fusion), channel_id=1, source_target_pairs={{0,8},{4,12},{8,0},{12,4},{16,24},{20,28},{24,16},{28,20},{1,9},{5... | collective-permute-start | bytes 1474568 | tf_op jit(solution)/shard_map/ppermute | solution.py:20
  85.0 6.3 %collective-permute-start.16 = (bf16[1,960,128]{2,1,0:T(8,128)(2,1)S(1)}, bf16[1,960,128]{2,1,0:T(8,128)(2,1)S(1)}, u32[]{:S(2)}, u32[]{:S(2)}) collective-permute-start(bf16[1,960,128]{2,1,0:T(8,128)(2,1)S(1)} %add_convert_fusion.3), channel_id=1, source_target_pairs={{0,8},{4,12},{8,0},{12,4},{16,24},{20,28},{24,16},{28,20},{1,9},{5... | collective-permute-start | bytes 737288 | tf_op jit(solution)/shard_map/ppermute | solution.py:20
  86.5 6.3 %collective-permute-start.31 = (bf16[1,960,128]{2,1,0:T(8,128)(2,1)S(1)}, bf16[1,960,128]{2,1,0:T(8,128)(2,1)S(1)}, u32[]{:S(2)}, u32[]{:S(2)}) collective-permute-start(bf16[1,960,128]{2,1,0:T(8,128)(2,1)S(1)} %add_convert_fusion.2), channel_id=1, source_target_pairs={{0,16},{4,20},{8,24},{12,28},{16,0},{20,4},{24,8},{28,12},{1,17},{... | collective-permute-start | bytes 737288 | tf_op jit(solution)/shard_map/ppermute | solution.py:20
  (2 other events, 29.5 us)

commit v2 on v1

v2 whole, which is shorter than its diff:
```python
import functools

import jax
import jax.numpy as jnp
from jax import lax
from jax.experimental import pallas as pl
from jax.experimental.pallas import tpu as pltpu
from jax.sharding import PartitionSpec as P

NB = 10
BLOCK = 768
PAIRS = NB * BLOCK
TRI_BLOCKS = NB * (NB + 1) // 2
F32 = jnp.float32
BF16 = jnp.bfloat16


def swap(value, axis_size, bit):
    pairs = [(i, i ^ (1 << bit)) for i in range(axis_size)]
    return lax.ppermute(value, "tri", pairs)


def after(value, *earlier):
    return lax.optimization_barrier((value, *earlier))[0]


def gather_tri(amplitudes, axis_size):
    if axis_size != 8:
        found = {0: amplitudes}
        for bit in range(axis_size.bit_length() - 1):
            for mask in list(found):
                found[mask | (1 << bit)] = swap(found[mask], axis_size, bit)
        return [(value, mask, None) for mask, value in found.items()]
    by_x = swap(amplitudes, axis_size, 1)
    by_y = swap(amplitudes, axis_size, 2)
    own_core = swap(amplitudes, axis_size, 0)
    far_real = swap(by_y[0], axis_size, 1)
    far_imag = swap(by_x[1], axis_size, 2)
    found = [
        (amplitudes, 0, None), (by_x, 2, None), (by_y, 4, None), (far_real, 6, 0), (far_imag, 6, 1),
        (own_core, 1, None),
    ]
    for value, mask, part in found[1:5]:
        found.append((swap(value, axis_size, 0), mask | 1, part))
    return found


def ladder_kernel(labels, groups, me_ref, code_ref, *refs):
    count = len(labels)
    piece_refs = refs[:count]
    ladder_ref = refs[count]
    out_refs = refs[count + 1:-3]
    amp, acc, sems = refs[-3:]
    columns = amp.shape[1] // 2
    rows = out_refs[0].shape[-2]
    step = pl.program_id(0)
    me = me_ref[0]

    def rows_of(mask):
        return pl.ds(pl.multiple_of((me ^ mask) * rows, rows), rows)

    @pl.when(step == 0)
    def _():
        copies = []
        for index, (mask, part) in enumerate(labels):
            for which in (0, 1) if part is None else (part,):
                source = piece_refs[index].at[which] if part is None else piece_refs[index]
                lanes = pl.ds(which * columns, columns)
                copy = pltpu.make_async_copy(source, amp.at[rows_of(mask), lanes], sems.at[len(copies)])
                copy.start()
                copies.append(copy)
        acc[...] = jnp.zeros_like(acc)
        for copy in copies:
            copy.wait()

    code = code_ref[step]
    row_block = jnp.int32(0)
    start = jnp.int32(0)
    for row in range(1, NB):
        first = row * NB - row * (row - 1) // 2
        past = code >= first
        row_block = jnp.where(past, row, row_block)
        start = jnp.where(past, first, start)
    column_block = jnp.minimum(row_block + code - start, NB - 1)
    weight = jnp.where(row_block == column_block, 0.5, 1.0) * jnp.where(code < TRI_BLOCKS, 1.0, 0.0)
    at_row = pl.ds(pl.multiple_of(row_block * BLOCK, BLOCK), BLOCK)
    at_column = pl.ds(pl.multiple_of(column_block * BLOCK, BLOCK), BLOCK)
    block = ladder_ref[0]
    to_row = lax.dot_general(block, amp[at_column, :], (((1,), (0,)), ((), ())), preferred_element_type=F32)
    acc[at_row, :] += weight * to_row
    to_column = lax.dot_general(block, amp[at_row, :], (((0,), (0,)), ((), ())), preferred_element_type=F32)
    acc[at_column, :] += weight * to_column

    @pl.when(step == pl.num_programs(0) - 1)
    def _():
        for target, places in zip(out_refs, groups, strict=True):
            for place, (mask, part) in enumerate(places):
                lanes = slice(part * columns, (part + 1) * columns)
                target[place] = acc[rows_of(mask), lanes].astype(BF16)


def ladder(me, codes, pieces, ladder_blocks, groups):
    slots = ladder_blocks.shape[0]
    rows, columns = pieces[0][0].shape[-2:]
    count = sum(len(places) for places in groups)
    return pl.pallas_call(
        functools.partial(ladder_kernel, [(mask, part) for _, mask, part in pieces], groups),
        grid_spec=pltpu.PrefetchScalarGridSpec(
            num_scalar_prefetch=2,
            grid=(slots,),
            in_specs=[pl.BlockSpec(memory_space=pl.ANY)] * len(pieces)
            + [pl.BlockSpec((1, BLOCK, BLOCK), lambda s, *_: (s, 0, 0))],
            out_specs=[pl.BlockSpec((len(places), rows, columns), lambda s, *_: (0, 0, 0)) for places in groups],
            scratch_shapes=[
                pltpu.VMEM((PAIRS, 2 * columns), BF16),
                pltpu.VMEM((PAIRS, 2 * columns), F32),
                pltpu.SemaphoreType.DMA((count,)),
            ],
        ),
        out_shape=[jax.ShapeDtypeStruct((len(places), rows, columns), BF16) for places in groups],
        compiler_params=pltpu.CompilerParams(
            dimension_semantics=("arbitrary",), vmem_limit_bytes=40 * 1024 * 1024
        ),
        cost_estimate=pl.CostEstimate(flops=1, bytes_accessed=1, transcendentals=0),
        name="ladder",
    )(me, codes, *[value for value, _, _ in pieces], ladder_blocks)


def add(*terms):
    total = terms[0].astype(F32)
    for term in terms[1:]:
        total = total + term.astype(F32)
    return total


def contract_kernel(me_ref, int_ref, real_ref, imag_ref, hold_ref, give_ref):
    vp_size, _, columns = real_ref.shape
    values = int_ref[...]
    for step in range(vp_size):
        target = lax.rem(me_ref[1] + step, vp_size)
        both = jnp.concatenate([real_ref[target], imag_ref[target]], axis=1)
        product = lax.dot_general(values, both, (((0,), (0,)), ((), ())), preferred_element_type=F32)
        real = product[:, :columns].astype(BF16)
        imag = product[:, columns:].astype(BF16)
        hold_ref[step] = jnp.where(me_ref[0] == 0, real, imag)
        give_ref[step] = jnp.where(me_ref[0] == 0, imag, real)


def contract(me, integrals, wide_real, wide_imag):
    vp_size, rows, columns = wide_real.shape
    vmem = pl.BlockSpec(memory_space=pltpu.VMEM)
    return pl.pallas_call(
        contract_kernel,
        in_specs=[pl.BlockSpec(memory_space=pltpu.SMEM)] + [vmem] * 3,
        out_specs=[vmem] * 2,
        out_shape=[jax.ShapeDtypeStruct((vp_size, columns, columns), BF16)] * 2,
        compiler_params=pltpu.CompilerParams(vmem_limit_bytes=24 * 1024 * 1024),
        cost_estimate=pl.CostEstimate(
            flops=4 * vp_size * rows * columns * columns,
            bytes_accessed=4 * wide_real.size + 2 * integrals.size,
            transcendentals=0,
        ),
        name="contract",
    )(me, integrals, wide_real, wide_imag)


def quadratic_kernel(me_ref, amp_ref, real_ref, imag_ref, mine_ref, other_ref, out_ref):
    vp_size, rows, columns = real_ref.shape
    core = me_ref[0]
    total = jnp.zeros((rows, 2 * columns), F32)
    for step in range(vp_size):
        source = lax.rem(me_ref[1] + vp_size - step, vp_size)
        both = jnp.concatenate([real_ref[source], imag_ref[source]], axis=1)
        real = jnp.where(core == 0, mine_ref[step], other_ref[step])
        imag = jnp.where(core == 0, other_ref[step], mine_ref[step])
        weights = jnp.concatenate(
            [jnp.concatenate([real, imag], axis=1), jnp.concatenate([-imag, real], axis=1)], axis=0
        )
        total += jnp.dot(both, weights, preferred_element_type=F32)
    out_ref[0] = amp_ref[0].astype(F32) + 0.25 * total[:, columns:]
    out_ref[1] = amp_ref[1].astype(F32) - 0.25 * total[:, :columns]


def quadratic(me, amplitudes, wide_real, wide_imag, mine, other):
    vmem = pl.BlockSpec(memory_space=pltpu.VMEM)
    return pl.pallas_call(
        quadratic_kernel,
        in_specs=[pl.BlockSpec(memory_space=pltpu.SMEM)] + [vmem] * 5,
        out_specs=vmem,
        out_shape=jax.ShapeDtypeStruct(amplitudes.shape, F32),
        compiler_params=pltpu.CompilerParams(vmem_limit_bytes=24 * 1024 * 1024),
        cost_estimate=pl.CostEstimate(
            flops=8 * wide_real.size * amplitudes.shape[2],
            bytes_accessed=4 * wide_real.size + 4 * amplitudes.size,
            transcendentals=0,
        ),
        name="quadratic",
    )(me, amplitudes, wide_real, wide_imag, mine, other)


def finish_kernel(places, base_ref, *refs):
    sums = [0.0, 0.0]
    for ref, (_, part, place) in zip(refs, places, strict=False):
        sums[part] = sums[part] + ref[place].astype(F32)
    refs[-1][0] = (base_ref[0] + 0.5 * sums[1]).astype(BF16)
    refs[-1][1] = (base_ref[1] - 0.5 * sums[0]).astype(BF16)


def finish(base, terms):
    vmem = pl.BlockSpec(memory_space=pltpu.VMEM)
    return pl.pallas_call(
        functools.partial(finish_kernel, [(None, part, place) for _, part, place in terms]),
        in_specs=[vmem] * (1 + len(terms)),
        out_specs=vmem,
        out_shape=jax.ShapeDtypeStruct(base.shape, BF16),
        compiler_params=pltpu.CompilerParams(vmem_limit_bytes=24 * 1024 * 1024),
        name="finish",
    )(base, *[value for value, _, _ in terms])


def scatter_plain(partial, tri_size):
    terms = [partial]
    for bit in reversed(range(tri_size.bit_length() - 1)):
        half = terms[0].shape[0] // 2
        outgoing = add(*[term[half:] for term in terms]).astype(BF16)
        terms = [term[:half] for term in terms] + [swap(outgoing, tri_size, bit)]
    return [(term[0], part, part) for term in terms for part in range(2)]


def shards(tri_size, vp_size, amplitudes, integrals, ladder_blocks, slot_block):
    bits = tri_size.bit_length() - 1
    tri_me = lax.axis_index("tri").astype(jnp.int32)
    me = jnp.stack([tri_me & 1, lax.axis_index("vp").astype(jnp.int32)])
    wide_real = lax.all_gather(amplitudes[0], "vp", axis=0, tiled=False)
    wide_imag = lax.all_gather(amplitudes[1], "vp", axis=0, tiled=False)
    pieces = gather_tri(amplitudes, tri_size)
    *values, wide_real = lax.optimization_barrier((*[value for value, _, _ in pieces], wide_real))
    pieces = [(value, mask, part) for value, (_, mask, part) in zip(values, pieces, strict=True)]

    if tri_size == 8:
        real_order, imag_order = (2, 6, 4), (4, 6, 2)
        groups = [[(mask | 1, 0) for mask in real_order], [(mask | 1, 1) for mask in imag_order], [(1, 0), (1, 1)]]
        groups += [[(mask, 0) for mask in real_order], [(mask, 1) for mask in imag_order], [(0, 0), (0, 1)]]
    else:
        groups = [[(mask, part) for mask in range(tri_size) for part in range(2)]]
    partials = ladder(tri_me[None], slot_block, pieces, ladder_blocks, groups)
    *partials, wide_real, wide_imag = lax.optimization_barrier((*partials, wide_real, wide_imag))
    hold, give = contract(me, integrals, wide_real, wide_imag)

    if tri_size == 8:
        real, imag, own = partials[3:]
        real_in, imag_in, own_in = (swap(value, tri_size, 0) for value in partials[:3])
        real_in, imag_in, hold, give = lax.optimization_barrier((real_in, imag_in, hold, give))
        by_x = add(real[:2], real_in[:2]).astype(BF16)
        by_y = add(imag[:2], imag_in[:2]).astype(BF16)
        by_x, by_y, hold, give = lax.optimization_barrier((by_x, by_y, hold, give))
        by_x, by_y = swap(by_x, tri_size, 1), swap(by_y, tri_size, 2)
        mine = add(hold, swap(give, tri_size, 0)).astype(BF16)
        mine = add(mine, swap(mine, tri_size, 1)).astype(BF16)
        received = swap(mine, tri_size, 2)
        then_y = add(real[2], real_in[2], by_x[1]).astype(BF16)
        then_x = add(imag[2], imag_in[2], by_y[1]).astype(BF16)
        then_y, then_x, received = lax.optimization_barrier((then_y, then_x, received))
        then_y, then_x = swap(then_y[None], tri_size, 2), swap(then_x[None], tri_size, 1)
        mine = add(mine, received).astype(BF16)
        terms = [(own, 0, 0), (own, 1, 1), (own_in, 0, 0), (own_in, 1, 1)]
        terms += [(by_x, 0, 0), (by_y, 1, 0), (then_y, 0, 0), (then_x, 1, 0)]
    else:
        terms = scatter_plain(partials[0].reshape(tri_size, 2, *amplitudes.shape[1:]), tri_size)
        mine = add(hold, swap(give, tri_size, 0)).astype(BF16)
        for bit in range(1, bits):
            mine = add(mine, swap(mine, tri_size, bit)).astype(BF16)
    shifted = [mine[0]]
    for step in range(1, vp_size):
        shifted.append(lax.ppermute(mine[step], "vp", [(i, (i + step) % vp_size) for i in range(vp_size)]))
    mine = jnp.stack(shifted)
    base = quadratic(me, amplitudes, wide_real, wide_imag, mine, swap(mine, tri_size, 0))
    return finish(base, terms)


def solution(mesh):
    in_specs = (P(None, "tri", "vp"), P("tri", "vp"), P("tri", None, None), P("tri"))
    out_specs = P(None, "tri", "vp")
    body = functools.partial(shards, mesh.shape["tri"], mesh.shape["vp"])
    return jax.shard_map(body, mesh=mesh, in_specs=in_specs, out_specs=out_specs, check_vma=False)
```

time: 94.4 us -> 119 us (1.26)
  blocking collectives: 0 us -> 43 us
  waiting for transfers between devices: 40.6 us -> 27.6 us
  matrix products: 11.6 us -> 0 us
  local copies, waits for them, and re-layouts: 1.75 us -> 9.83 us
  starting transfers between devices: 25.6 us -> 17.6 us
  Pallas kernels: 12.5 us -> 16 us
  other arithmetic: 1.59 us -> 4.27 us
    all_gather x0 -> x2, blocking collectives: none -> 43 us  [the longest x1 22 us: shards(): wide_real = lax.all_gather(amplitudes[0], 'vp', axis=0, tiled=False)]
    dot_general x24 -> x0, matrix products: 11.6 us -> none  [the longest x8 8.08 us: shards(): lax.dot_general(value, amplitudes[part], (((0,), (0,)), ((), ())), prefer...]
    unnamed x4 -> x22, local copies, waits for them, and re-layouts: 0.66 us -> 8.01 us
    ppermute x26 -> x20, waiting for transfers between devices: 30.3 us -> 23.6 us  [swap(): return lax.ppermute(value, 'tri', pairs)]
    ppermute x6 -> x3, waiting for transfers between devices: 10.3 us -> 4.08 us  [shards(): lax.ppermute(mine[step], 'vp', [(i, (i + step) % vp_size) for i in range(...]
    ppermute x26 -> x20, starting transfers between devices: 18.9 us -> 14.4 us  [swap(): return lax.ppermute(value, 'tri', pairs)]
    ppermute x6 -> x3, starting transfers between devices: 6.71 us -> 3.14 us  [shards(): lax.ppermute(mine[step], 'vp', [(i, (i + step) % vp_size) for i in range(...]
    pallas_call x1 -> x4, Pallas kernels: 12.5 us -> 16 us  [the longest x1 12.7 us: ladder(): pl.pallas_call(functools.partial(ladder_kernel, [(mask, part) for _, mask...]
  transfers between devices with their start and end apart: 32 -> 23, of which waited for: 16 -> 10; matrix products, arithmetic and copies ran while one was open for 13% -> 4% of each run, Pallas kernels for 13% -> 2%
where the time goes in v2:
time: 119 us
  blocking collectives  43 us (36%)
  waiting for transfers between devices  27.6 us (23%)
  starting transfers between devices  17.6 us (15%)
  Pallas kernels  16 us (13%)
  local copies, waits for them, and re-layouts  9.83 us (8%)
  other arithmetic  4.27 us (4%)
    ppermute x20, waiting for transfers between devices, swap(): return lax.ppermute(value, 'tri', pairs)  23.6 us
    all_gather x1, blocking collectives, shards(): wide_real = lax.all_gather(amplitudes[0], 'vp', axis=0, tiled=False)  22 us
    all_gather x1, blocking collectives, shards(): wide_imag = lax.all_gather(amplitudes[1], 'vp', axis=0, tiled=False)  21 us
    ppermute x20, starting transfers between devices, swap(): return lax.ppermute(value, 'tri', pairs)  14.4 us
    pallas_call x1, Pallas kernels, ladder(): pl.pallas_call(functools.partial(ladder_kernel, [(mask, part) for _, mask...  12.7 us
    unnamed x22, local copies, waits for them, and re-layouts  8.01 us
    ppermute x3, waiting for transfers between devices, shards(): lax.ppermute(mine[step], 'vp', [(i, (i + step) % vp_size) for i in range(...  4.08 us
    ppermute x3, starting transfers between devices, shards(): lax.ppermute(mine[step], 'vp', [(i, (i + step) % vp_size) for i in range(...  3.14 us
  transfers between devices with their start and end apart: 23, of which 10 were waited for; matrix products, arithmetic and copies ran while one was open for 4% of the time, Pallas kernels for 2%

profile of v2, /device:TPU:0, one launch (start us, length us, event | category | flops | bytes accessed | tf_op | source)
XLA Modules:
  0.0 118.5 jit_solution(232200243197176262)
XLA Ops:
  0.0 3.0 %collective-permute-start.1 = (bf16[2,960,128]{2,1,0:T(8,128)(2,1)}, bf16[2,960,128]{2,1,0:T(8,128)(2,1)S(1)}, u32[]{:S(2)}, u32[]{:S(2)}) collective-permute-start(bf16[2,960,128]{2,1,0:T(8,128)(2,1)} %amp_ref.1), channel_id=1, source_target_pairs={{0,16},{4,20},{8,24},{12,28},{16,0},{20,4},{24,8},{28,12},{1,17},{... | collective-permute-start | bytes 1474568 | tf_op jit(solution)/shard_map/ppermute | solution.py:20
  3.0 1.5 %collective-permute-start = (bf16[2,960,128]{2,1,0:T(8,128)(2,1)}, bf16[2,960,128]{2,1,0:T(8,128)(2,1)S(1)}, u32[]{:S(2)}, u32[]{:S(2)}) collective-permute-start(bf16[2,960,128]{2,1,0:T(8,128)(2,1)} %amp_ref.1), channel_id=1, source_target_pairs={{0,8},{4,12},{8,0},{12,4},{16,24},{20,28},{24,16},{28,20},{1,9},{5... | collective-permute-start | bytes 1474568 | tf_op jit(solution)/shard_map/ppermute | solution.py:20
  4.5 1.8 %fusion.2 = (bf16[1,960,128]{2,1,0:T(8,128)(2,1)}, bf16[1,960,128]{2,1,0:T(8,128)(2,1)S(1)}) fusion(bf16[2,960,128]{2,1,0:T(8,128)(2,1)} %amp_ref.1), kind=kLoop, calls=%fused_computation.16 | loop fusion | bytes 983040 | tf_op jit(solution)/shard_map/slice | solution.py:235
  6.2 8.2 %collective-permute-done.1.refs_2_ = bf16[2,960,128]{2,1,0:T(8,128)(2,1)S(1)} collective-permute-done((bf16[2,960,128]{2,1,0:T(8,128)(2,1)}, bf16[2,960,128]{2,1,0:T(8,128)(2,1)S(1)}, u32[]{:S(2)}, u32[]{:S(2)}) %collective-permute-start.1) | collective-permute-done | bytes 491552 | tf_op jit(solution)/shard_map/ppermute | solution.py:20
  14.4 1.8 %collective-permute-start.2 = (bf16[960,128]{1,0:T(8,128)(2,1)S(1)}, bf16[960,128]{1,0:T(8,128)(2,1)}, u32[]{:S(2)}, u32[]{:S(2)}) collective-permute-start(bf16[960,128]{1,0:T(8,128)(2,1)S(1)} %slice_bitcast_fusion.1), channel_id=1, source_target_pairs={{0,8},{4,12},{8,0},{12,4},{16,24},{20,28},{24,16},{28,20},{1,9},{5... | collective-permute-start | bytes 737288 | tf_op jit(solution)/shard_map/ppermute | solution.py:20
  16.2 1.6 %collective-permute-start.3 = (bf16[960,128]{1,0:T(8,128)(2,1)S(1)}, bf16[960,128]{1,0:T(8,128)(2,1)}, u32[]{:S(2)}, u32[]{:S(2)}) collective-permute-start(bf16[960,128]{1,0:T(8,128)(2,1)S(1)} %slice_bitcast_fusion), channel_id=1, source_target_pairs={{0,16},{4,20},{8,24},{12,28},{16,0},{20,4},{24,8},{28,12},{1,17},{... | collective-permute-start | bytes 737288 | tf_op jit(solution)/shard_map/ppermute | solution.py:20
  18.3 22.0 %all_gather.6.real_ref = bf16[4,960,128]{2,1,0:T(8,128)(2,1)S(1)} all-gather(bf16[1,960,128]{2,1,0:T(8,128)(2,1)S(1)} %get-tuple-element.82), channel_id=1, replica_groups=mesh['tri'=8,'vp'=4] {'vp'}, dimensions={0}, use_global_device_ids=true | all-gather | bytes 1228800 | tf_op jit(solution)/shard_map/all_gather | solution.py:234
  40.8 21.0 %all_gather.7.imag_ref = bf16[4,960,128]{2,1,0:T(8,128)(2,1)S(1)} all-gather(bf16[1,960,128]{2,1,0:T(8,128)(2,1)} %get-tuple-element.81), channel_id=1, replica_groups=mesh['tri'=8,'vp'=4] {'vp'}, dimensions={0}, use_global_device_ids=true | all-gather | bytes 1228800 | tf_op jit(solution)/shard_map/all_gather | solution.py:235
  62.7 1.0 copy-done
  63.7 1.0 copy-done.3
  64.7 1.0 copy-done.7
  66.4 12.7 %ladder.1 = (bf16[3,960,128]{2,1,0:T(8,128)(2,1)}, bf16[3,960,128]{2,1,0:T(8,128)(2,1)}, bf16[2,960,128]{2,1,0:T(8,128)(2,1)S(1)}, bf16[3,960,128]{2,1,0:T(8,128...) custom-call(s32[1]{0:T(128)} %bitcast.2.me_ref, s32[7]{0:T(128)S(1)} %copy-done.9, ...), custom_call_target="tpu_custom_call" | custom-call | flops 1 | bytes 1 | tf_op jit(solution)/shard_map/ladder/pallas_call | solution.py:106
  79.1 0.9 copy-done.4
  80.0 0.9 copy-done.5
  82.3 0.9 copy-done.8
  83.2 1.0 contract.1
  84.2 1.1 collective-permute-done.9
  85.3 1.7 %add_convert_fusion = (bf16[2,960,128]{2,1,0:T(8,128)(2,1)S(1)}, bf16[2,960,128]{2,1,0:T(8,128)(2,1)S(1)}) fusion(bf16[3,960,128]{2,1,0:T(8,128)(2,1)} %collective-permute-done.10, bf16[3,960,128]{2,1,0:T(8,128)(2,1)} %copy-done.5, bf16[3,960,128]{2,1,0:T(8,128)(2,1)} %collective-permute-done.9, bf16[3,960,128]{2,1,0:T(8,128)(2,1)} %copy-done.4), kind=kLoop, calls=%fused_computation | loop fusion | flops 1966080 | bytes 2949120 | tf_op jit(solution)/shard_map/convert_element_type | solution.py:255
  89.1 1.5 %collective-permute-start.13 = (bf16[2,960,128]{2,1,0:T(8,128)(2,1)S(1)}, bf16[2,960,128]{2,1,0:T(8,128)(2,1)S(1)}, u32[]{:S(2)}, u32[]{:S(2)}) collective-permute-start(bf16[2,960,128]{2,1,0:T(8,128)(2,1)S(1)} %get-tuple-element.74), channel_id=1, source_target_pairs={{0,8},{4,12},{8,0},{12,4},{16,24},{20,28},{24,16},{28,20},{1,9},{5... | collective-permute-start | bytes 1474568 | tf_op jit(solution)/shard_map/ppermute | solution.py:20
  90.6 4.3 %collective-permute-done.12 = bf16[4,128,128]{2,1,0:T(8,128)(2,1)S(1)} collective-permute-done((bf16[4,128,128]{2,1,0:T(8,128)(2,1)S(1)}, bf16[4,128,128]{2,1,0:T(8,128)(2,1)S(1)}, u32[]{:S(2)}, u32[]{:S(2)}) %collective-permute-start.12) | collective-permute-done | bytes 131104 | tf_op jit(solution)/shard_map/ppermute | solution.py:20
  94.9 0.9 collective-permute-start.15
  95.8 5.4 %collective-permute-done.14.refs_5_ = bf16[2,960,128]{2,1,0:T(8,128)(2,1)S(1)} collective-permute-done((bf16[2,960,128]{2,1,0:T(8,128)(2,1)S(1)}, bf16[2,960,128]{2,1,0:T(8,128)(2,1)S(1)}, u32[]{:S(2)}, u32[]{:S(2)}) %collective-permute-start.14) | collective-permute-done | bytes 491552 | tf_op jit(solution)/shard_map/ppermute | solution.py:20
  101.3 1.2 fusion.1
  102.4 2.2 %collective-permute-done.13.refs_4_ = bf16[2,960,128]{2,1,0:T(8,128)(2,1)S(1)} collective-permute-done((bf16[2,960,128]{2,1,0:T(8,128)(2,1)S(1)}, bf16[2,960,128]{2,1,0:T(8,128)(2,1)S(1)}, u32[]{:S(2)}, u32[]{:S(2)}) %collective-permute-start.13) | collective-permute-done | bytes 491552 | tf_op jit(solution)/shard_map/ppermute | solution.py:20
  104.6 1.2 fusion
  105.9 1.0 collective-permute-start.17
  106.8 1.9 %collective-permute-start.18 = (bf16[128,128]{1,0:T(8,128)(2,1)S(1)}, bf16[128,128]{1,0:T(8,128)(2,1)S(1)}, u32[]{:S(2)}, u32[]{:S(2)}) collective-permute-start(bf16[128,128]{1,0:T(8,128)(2,1)S(1)} %get-tuple-element.84), channel_id=1, source_target_pairs={{0,3},{1,0},{2,1},{3,2},{4,7},{5,4},{6,5},{7,6},{8,11},{9,8},{10,9... | collective-permute-start | bytes 98312 | tf_op jit(solution)/shard_map/ppermute | solution.py:275
  109.8 1.4 %collective-permute-done.17 = bf16[128,128]{1,0:T(8,128)(2,1)S(1)} collective-permute-done((bf16[128,128]{1,0:T(8,128)(2,1)S(1)}, bf16[128,128]{1,0:T(8,128)(2,1)S(1)}, u32[]{:S(2)}, u32[]{:S(2)}) %collective-permute-start.17) | collective-permute-done | bytes 32800 | tf_op jit(solution)/shard_map/ppermute | solution.py:275
  111.7 2.6 %collective-permute-done.16 = bf16[128,128]{1,0:T(8,128)(2,1)S(1)} collective-permute-done((bf16[128,128]{1,0:T(8,128)(2,1)S(1)}, bf16[128,128]{1,0:T(8,128)(2,1)S(1)}, u32[]{:S(2)}, u32[]{:S(2)}) %collective-permute-start.16) | collective-permute-done | bytes 32800 | tf_op jit(solution)/shard_map/ppermute | solution.py:275
  114.5 1.3 %collective-permute-done.19.other_ref = bf16[4,128,128]{2,1,0:T(8,128)(2,1)S(1)} collective-permute-done((bf16[4,128,128]{2,1,0:T(8,128)(2,1)S(1)}, bf16[4,128,128]{2,1,0:T(8,128)(2,1)S(1)}, u32[]{:S(2)}, u32[]{:S(2)}) %collective-permute-start.19) | collective-permute-done | bytes 131104 | tf_op jit(solution)/shard_map/ppermute | solution.py:20
  115.8 1.2 %quadratic.1.base_ref = f32[2,960,128]{2,1,0:T(8,128)S(1)} custom-call(s32[2]{0:T(128)S(1)} %pad_add_fusion.me_ref, bf16[2,960,128]{2,1,0:T(8,128)(2,1)S(1)} %copy-done.1, bf16[4,960,128]{2,1,0:T(8,128)(2,1)S(1)} %all_gather.6.real_ref, bf16[4,960,128]{2,1,0:T(8,128)(2,1)S(1)} %all_gather.7.imag_ref, bf16[4,128,128]{2,1,0:T(8,128)(2,1)S(1)} %pad_maximum_fusion.mine_ref, ...), custom_call_target="tpu_custom_call" | custom-call | flops 503316480 | bytes 2949120 | tf_op jit(solution)/shard_map/quadratic/pallas_call | solution.py:186
  117.4 1.1 finish.1
  (54 shorter events, 8.1 us)
Async XLA Ops:
  0.0 14.4 %collective-permute-start.1 = (bf16[2,960,128]{2,1,0:T(8,128)(2,1)}, bf16[2,960,128]{2,1,0:T(8,128)(2,1)S(1)}, u32[]{:S(2)}, u32[]{:S(2)}) collective-permute-start(bf16[2,960,128]{2,1,0:T(8,128)(2,1)} %amp_ref.1), channel_id=1, source_target_pairs={{0,16},{4,20},{8,24},{12,28},{16,0},{20,4},{24,8},{28,12},{1,17},{... | collective-permute-start | bytes 1474568 | tf_op jit(solution)/shard_map/ppermute | solution.py:20
  3.0 13.2 %collective-permute-start = (bf16[2,960,128]{2,1,0:T(8,128)(2,1)}, bf16[2,960,128]{2,1,0:T(8,128)(2,1)S(1)}, u32[]{:S(2)}, u32[]{:S(2)}) collective-permute-start(bf16[2,960,128]{2,1,0:T(8,128)(2,1)} %amp_ref.1), channel_id=1, source_target_pairs={{0,8},{4,12},{8,0},{12,4},{16,24},{20,28},{24,16},{28,20},{1,9},{5... | collective-permute-start | bytes 1474568 | tf_op jit(solution)/shard_map/ppermute | solution.py:20
  4.5 57.4 %collective-permute-start.4 = (bf16[2,960,128]{2,1,0:T(8,128)(2,1)}, bf16[2,960,128]{2,1,0:T(8,128)(2,1)S(1)}, u32[]{:S(2)}, u32[]{:S(2)}) collective-permute-start(bf16[2,960,128]{2,1,0:T(8,128)(2,1)} %amp_ref.1), channel_id=1, source_target_pairs={{0,4},{4,0},{8,12},{12,8},{16,20},{20,16},{24,28},{28,24},{1,5},{5... | collective-permute-start | bytes 1474568 | tf_op jit(solution)/shard_map/ppermute | solution.py:20
  14.4 25.9 %collective-permute-start.2 = (bf16[960,128]{1,0:T(8,128)(2,1)S(1)}, bf16[960,128]{1,0:T(8,128)(2,1)}, u32[]{:S(2)}, u32[]{:S(2)}) collective-permute-start(bf16[960,128]{1,0:T(8,128)(2,1)S(1)} %slice_bitcast_fusion.1), channel_id=1, source_target_pairs={{0,8},{4,12},{8,0},{12,4},{16,24},{20,28},{24,16},{28,20},{1,9},{5... | collective-permute-start | bytes 737288 | tf_op jit(solution)/shard_map/ppermute | solution.py:20
  16.2 46.5 %copy-start.2 = (bf16[2,960,128]{2,1,0:T(8,128)(2,1)}, bf16[2,960,128]{2,1,0:T(8,128)(2,1)S(1)}, u32[]{:S(2)}) copy-start(bf16[2,960,128]{2,1,0:T(8,128)(2,1)S(1)} %collective-permute-done.refs_1_) | copy-start | bytes 1474564
  16.2 24.1 %collective-permute-start.3 = (bf16[960,128]{1,0:T(8,128)(2,1)S(1)}, bf16[960,128]{1,0:T(8,128)(2,1)}, u32[]{:S(2)}, u32[]{:S(2)}) collective-permute-start(bf16[960,128]{1,0:T(8,128)(2,1)S(1)} %slice_bitcast_fusion), channel_id=1, source_target_pairs={{0,16},{4,20},{8,24},{12,28},{16,0},{20,4},{24,8},{28,12},{1,17},{... | collective-permute-start | bytes 737288 | tf_op jit(solution)/shard_map/ppermute | solution.py:20
  17.8 44.9 %collective-permute-start.5 = (bf16[2,960,128]{2,1,0:T(8,128)(2,1)S(1)}, bf16[2,960,128]{2,1,0:T(8,128)(2,1)}, u32[]{:S(2)}, u32[]{:S(2)}) collective-permute-start(bf16[2,960,128]{2,1,0:T(8,128)(2,1)S(1)} %collective-permute-done.refs_1_), channel_id=1, source_target_pairs={{0,4},{4,0},{8,12},{12,8},{16,20},{20,16},{24,28},{28,24},{1,5},{5... | collective-permute-start | bytes 1474568 | tf_op jit(solution)/shard_map/ppermute | solution.py:20
  17.8 44.9 %collective-permute-start.6 = (bf16[2,960,128]{2,1,0:T(8,128)(2,1)S(1)}, bf16[2,960,128]{2,1,0:T(8,128)(2,1)}, u32[]{:S(2)}, u32[]{:S(2)}) collective-permute-start(bf16[2,960,128]{2,1,0:T(8,128)(2,1)S(1)} %collective-permute-done.1.refs_2_), channel_id=1, source_target_pairs={{0,4},{4,0},{8,12},{12,8},{16,20},{20,16},{24,28},{28,24},{1,5},{5... | collective-permute-start | bytes 1474568 | tf_op jit(solution)/shard_map/ppermute | solution.py:20
  40.3 22.3 %collective-permute-start.7 = (bf16[960,128]{1,0:T(8,128)(2,1)}, bf16[960,128]{1,0:T(8,128)(2,1)S(1)}, u32[]{:S(2)}, u32[]{:S(2)}) collective-permute-start(bf16[960,128]{1,0:T(8,128)(2,1)} %collective-permute-done.2.refs_3_), channel_id=1, source_target_pairs={{0,4},{4,0},{8,12},{12,8},{16,20},{20,16},{24,28},{28,24},{1,5},{5... | collective-permute-start | bytes 737288 | tf_op jit(solution)/shard_map/ppermute | solution.py:20
  40.3 22.3 %collective-permute-start.8 = (bf16[960,128]{1,0:T(8,128)(2,1)}, bf16[960,128]{1,0:T(8,128)(2,1)S(1)}, u32[]{:S(2)}, u32[]{:S(2)}) collective-permute-start(bf16[960,128]{1,0:T(8,128)(2,1)} %collective-permute-done.3.refs_4_), channel_id=1, source_target_pairs={{0,4},{4,0},{8,12},{12,8},{16,20},{20,16},{24,28},{28,24},{1,5},{5... | collective-permute-start | bytes 737288 | tf_op jit(solution)/shard_map/ppermute | solution.py:20
  61.9 0.8 copy-start.6
  62.7 1.0 copy-start
  63.7 1.0 copy-start.3
  64.7 1.0 copy-start.7
  66.4 49.4 %copy-start.1 = (bf16[2,960,128]{2,1,0:T(8,128)(2,1)S(1)}, bf16[2,960,128]{2,1,0:T(8,128)(2,1)}, u32[]{:S(2)}) copy-start(bf16[2,960,128]{2,1,0:T(8,128)(2,1)} %amp_ref.1) | copy-start | bytes 1474564
  79.1 0.9 copy-start.4
  80.0 0.9 copy-start.5
  81.7 2.6 %collective-permute-start.10 = (bf16[3,960,128]{2,1,0:T(8,128)(2,1)}, bf16[3,960,128]{2,1,0:T(8,128)(2,1)}, u32[]{:S(2)}, u32[]{:S(2)}) collective-permute-start(bf16[3,960,128]{2,1,0:T(8,128)(2,1)} %get-tuple-element.64), channel_id=1, source_target_pairs={{0,4},{4,0},{8,12},{12,8},{16,20},{20,16},{24,28},{28,24},{1,5},{5... | collective-permute-start | bytes 2211848 | tf_op jit(solution)/shard_map/ppermute | solution.py:20
  81.7 3.6 %collective-permute-start.9 = (bf16[3,960,128]{2,1,0:T(8,128)(2,1)}, bf16[3,960,128]{2,1,0:T(8,128)(2,1)}, u32[]{:S(2)}, u32[]{:S(2)}) collective-permute-start(bf16[3,960,128]{2,1,0:T(8,128)(2,1)} %get-tuple-element.63), channel_id=1, source_target_pairs={{0,4},{4,0},{8,12},{12,8},{16,20},{20,16},{24,28},{28,24},{1,5},{5... | collective-permute-start | bytes 2211848 | tf_op jit(solution)/shard_map/ppermute | solution.py:20
  82.2 0.9 copy-start.8
  87.0 1.4 %collective-permute-start.11 = (bf16[4,128,128]{2,1,0:T(8,128)(2,1)S(1)}, bf16[4,128,128]{2,1,0:T(8,128)(2,1)S(1)}, u32[]{:S(2)}, u32[]{:S(2)}) collective-permute-start(bf16[4,128,128]{2,1,0:T(8,128)(2,1)S(1)} %get-tuple-element.73), channel_id=1, source_target_pairs={{0,4},{4,0},{8,12},{12,8},{16,20},{20,16},{24,28},{28,24},{1,5},{5... | collective-permute-start | bytes 393224 | tf_op jit(solution)/shard_map/ppermute | solution.py:20
  87.2 14.1 %collective-permute-start.14 = (bf16[2,960,128]{2,1,0:T(8,128)(2,1)S(1)}, bf16[2,960,128]{2,1,0:T(8,128)(2,1)S(1)}, u32[]{:S(2)}, u32[]{:S(2)}) collective-permute-start(bf16[2,960,128]{2,1,0:T(8,128)(2,1)S(1)} %get-tuple-element.75), channel_id=1, source_target_pairs={{0,16},{4,20},{8,24},{12,28},{16,0},{20,4},{24,8},{28,12},{1,17},{... | collective-permute-start | bytes 1474568 | tf_op jit(solution)/shard_map/ppermute | solution.py:20
  88.5 6.4 %collective-permute-start.12 = (bf16[4,128,128]{2,1,0:T(8,128)(2,1)S(1)}, bf16[4,128,128]{2,1,0:T(8,128)(2,1)S(1)}, u32[]{:S(2)}, u32[]{:S(2)}) collective-permute-start(bf16[4,128,128]{2,1,0:T(8,128)(2,1)S(1)} %add_convert_fusion.6), channel_id=1, source_target_pairs={{0,8},{4,12},{8,0},{12,4},{16,24},{20,28},{24,16},{28,20},{1,9},{5... | collective-permute-start | bytes 393224 | tf_op jit(solution)/shard_map/ppermute | solution.py:20
  89.1 15.5 %collective-permute-start.13 = (bf16[2,960,128]{2,1,0:T(8,128)(2,1)S(1)}, bf16[2,960,128]{2,1,0:T(8,128)(2,1)S(1)}, u32[]{:S(2)}, u32[]{:S(2)}) collective-permute-start(bf16[2,960,128]{2,1,0:T(8,128)(2,1)S(1)} %get-tuple-element.74), channel_id=1, source_target_pairs={{0,8},{4,12},{8,0},{12,4},{16,24},{20,28},{24,16},{28,20},{1,9},{5... | collective-permute-start | bytes 1474568 | tf_op jit(solution)/shard_map/ppermute | solution.py:20
  90.6 26.5 %collective-permute-start.20 = (bf16[2,960,128]{2,1,0:T(8,128)(2,1)}, bf16[2,960,128]{2,1,0:T(8,128)(2,1)S(1)}, u32[]{:S(2)}, u32[]{:S(2)}) collective-permute-start(bf16[2,960,128]{2,1,0:T(8,128)(2,1)} %copy-done.10), channel_id=1, source_target_pairs={{0,4},{4,0},{8,12},{12,8},{16,20},{20,16},{24,28},{28,24},{1,5},{5... | collective-permute-start | bytes 1474568 | tf_op jit(solution)/shard_map/ppermute | solution.py:20
  94.9 10.9 %collective-permute-start.15 = (bf16[4,128,128]{2,1,0:T(8,128)(2,1)S(1)}, bf16[4,128,128]{2,1,0:T(8,128)(2,1)S(1)}, u32[]{:S(2)}, u32[]{:S(2)}) collective-permute-start(bf16[4,128,128]{2,1,0:T(8,128)(2,1)S(1)} %add_convert_fusion.5), channel_id=1, source_target_pairs={{0,16},{4,20},{8,24},{12,28},{16,0},{20,4},{24,8},{28,12},{1,17},{... | collective-permute-start | bytes 393224 | tf_op jit(solution)/shard_map/ppermute | solution.py:20
  105.9 5.4 %collective-permute-start.17 = (bf16[128,128]{1,0:T(8,128)(2,1)S(1)}, bf16[128,128]{1,0:T(8,128)(2,1)S(1)}, u32[]{:S(2)}, u32[]{:S(2)}) collective-permute-start(bf16[128,128]{1,0:T(8,128)(2,1)S(1)} %get-tuple-element.85), channel_id=1, source_target_pairs={{0,2},{1,3},{2,0},{3,1},{4,6},{5,7},{6,4},{7,5},{8,10},{9,11},{10,... | collective-permute-start | bytes 98312 | tf_op jit(solution)/shard_map/ppermute | solution.py:275
  106.8 4.9 %collective-permute-start.18 = (bf16[128,128]{1,0:T(8,128)(2,1)S(1)}, bf16[128,128]{1,0:T(8,128)(2,1)S(1)}, u32[]{:S(2)}, u32[]{:S(2)}) collective-permute-start(bf16[128,128]{1,0:T(8,128)(2,1)S(1)} %get-tuple-element.84), channel_id=1, source_target_pairs={{0,3},{1,0},{2,1},{3,2},{4,7},{5,4},{6,5},{7,6},{8,11},{9,8},{10,9... | collective-permute-start | bytes 98312 | tf_op jit(solution)/shard_map/ppermute | solution.py:275
  108.7 5.7 %collective-permute-start.16 = (bf16[128,128]{1,0:T(8,128)(2,1)S(1)}, bf16[128,128]{1,0:T(8,128)(2,1)S(1)}, u32[]{:S(2)}, u32[]{:S(2)}) collective-permute-start(bf16[128,128]{1,0:T(8,128)(2,1)S(1)} %get-tuple-element.86), channel_id=1, source_target_pairs={{0,1},{1,2},{2,3},{3,0},{4,5},{5,6},{6,7},{7,4},{8,9},{9,10},{10,1... | collective-permute-start | bytes 98312 | tf_op jit(solution)/shard_map/ppermute | solution.py:275
  109.0 8.1 %collective-permute-start.21 = (bf16[1,960,128]{2,1,0:T(8,128)(2,1)S(1)}, bf16[1,960,128]{2,1,0:T(8,128)(2,1)S(1)}, u32[]{:S(2)}, u32[]{:S(2)}) collective-permute-start(bf16[1,960,128]{2,1,0:T(8,128)(2,1)S(1)} %bitcast.23), channel_id=1, source_target_pairs={{0,16},{4,20},{8,24},{12,28},{16,0},{20,4},{24,8},{28,12},{1,17},{... | collective-permute-start | bytes 737288 | tf_op jit(solution)/shard_map/ppermute | solution.py:20
  111.2 6.2 %collective-permute-start.22 = (bf16[1,960,128]{2,1,0:T(8,128)(2,1)S(1)}, bf16[1,960,128]{2,1,0:T(8,128)(2,1)S(1)}, u32[]{:S(2)}, u32[]{:S(2)}) collective-permute-start(bf16[1,960,128]{2,1,0:T(8,128)(2,1)S(1)} %bitcast.22), channel_id=1, source_target_pairs={{0,8},{4,12},{8,0},{12,4},{16,24},{20,28},{24,16},{28,20},{1,9},{5... | collective-permute-start | bytes 737288 | tf_op jit(solution)/shard_map/ppermute | solution.py:20
  114.4 1.4 %collective-permute-start.19 = (bf16[4,128,128]{2,1,0:T(8,128)(2,1)S(1)}, bf16[4,128,128]{2,1,0:T(8,128)(2,1)S(1)}, u32[]{:S(2)}, u32[]{:S(2)}) collective-permute-start(bf16[4,128,128]{2,1,0:T(8,128)(2,1)S(1)} %pad_maximum_fusion.mine_ref), channel_id=1, source_target_pairs={{0,4},{4,0},{8,12},{12,8},{16,20},{20,16},{24,28},{28,24},{1,5},{5... | collective-permute-start | bytes 393224 | tf_op jit(solution)/shard_map/ppermute | solution.py:20
  (2 other events, 1.4 us)

commit v3 on v2

--- a/solution.py
+++ b/solution.py
@@ -133,46 +133,48 @@
     return total
 
 
-def contract_kernel(me_ref, int_ref, real_ref, imag_ref, hold_ref, give_ref):
-    vp_size, _, columns = real_ref.shape
+def contract_kernel(core_ref, int_ref, *refs):
     values = int_ref[...]
-    for step in range(vp_size):
-        target = lax.rem(me_ref[1] + step, vp_size)
-        both = jnp.concatenate([real_ref[target], imag_ref[target]], axis=1)
+    columns = values.shape[1]
+    hold_ref, give_ref = refs[-2:]
+    for step, ref in enumerate(refs[:-2]):
+        both = jnp.concatenate([ref[0], ref[1]], axis=1)
         product = lax.dot_general(values, both, (((0,), (0,)), ((), ())), preferred_element_type=F32)
         real = product[:, :columns].astype(BF16)
         imag = product[:, columns:].astype(BF16)
-        hold_ref[step] = jnp.where(me_ref[0] == 0, real, imag)
-        give_ref[step] = jnp.where(me_ref[0] == 0, imag, real)
-
-
-def contract(me, integrals, wide_real, wide_imag):
-    vp_size, rows, columns = wide_real.shape
+        hold_ref[step] = jnp.where(core_ref[0] == 0, real, imag)
+        give_ref[step] = jnp.where(core_ref[0] == 0, imag, real)
+
+
+def contract(core, integrals, ring):
+    rows, columns = integrals.shape
     vmem = pl.BlockSpec(memory_space=pltpu.VMEM)
     return pl.pallas_call(
         contract_kernel,
-        in_specs=[pl.BlockSpec(memory_space=pltpu.SMEM)] + [vmem] * 3,
+        in_specs=[pl.BlockSpec(memory_space=pltpu.SMEM)] + [vmem] * (1 + len(ring)),
         out_specs=[vmem] * 2,
-        out_shape=[jax.ShapeDtypeStruct((vp_size, columns, columns), BF16)] * 2,
-        compiler_params=pltpu.CompilerParams(vmem_limit_bytes=24 * 1024 * 1024),
+        out_shape=[jax.ShapeDtypeStruct((len(ring), columns, columns), BF16)] * 2,
+        compiler_params=pltpu.CompilerParams(vmem_limit_bytes=20 * 1024 * 1024),
         cost_estimate=pl.CostEstimate(
-            flops=4 * vp_size * rows * columns * columns,
-            bytes_accessed=4 * wide_real.size + 2 * integrals.size,
+            flops=4 * len(ring) * rows * columns * columns,
+            bytes_accessed=(4 * len(ring) + 2) * rows * columns,
             transcendentals=0,
         ),
         name="contract",
-    )(me, integrals, wide_real, wide_imag)
-
-
-def quadratic_kernel(me_ref, amp_ref, real_ref, imag_ref, mine_ref, other_ref, out_ref):
-    vp_size, rows, columns = real_ref.shape
-    core = me_ref[0]
+    )(core, integrals, *ring)
+
+
+def quadratic_kernel(core_ref, mine_ref, other_ref, *refs):
+    amp_ref, out_ref = refs[0], refs[-1]
+    _, rows, columns = amp_ref.shape
+    vp_size = len(refs) - 1
+    core = core_ref[0]
     total = jnp.zeros((rows, 2 * columns), F32)
     for step in range(vp_size):
-        source = lax.rem(me_ref[1] + vp_size - step, vp_size)
-        both = jnp.concatenate([real_ref[source], imag_ref[source]], axis=1)
-        real = jnp.where(core == 0, mine_ref[step], other_ref[step])
-        imag = jnp.where(core == 0, other_ref[step], mine_ref[step])
+        both = jnp.concatenate([refs[step][0], refs[step][1]], axis=1)
+        source = (vp_size - step) % vp_size
+        real = jnp.where(core == 0, mine_ref[source], other_ref[source])
+        imag = jnp.where(core == 0, other_ref[source], mine_ref[source])
         weights = jnp.concatenate(
             [jnp.concatenate([real, imag], axis=1), jnp.concatenate([-imag, real], axis=1)], axis=0
         )
@@ -181,21 +183,22 @@
     out_ref[1] = amp_ref[1].astype(F32) - 0.25 * total[:, :columns]
 
 
-def quadratic(me, amplitudes, wide_real, wide_imag, mine, other):
+def quadratic(core, ring, mine, other):
     vmem = pl.BlockSpec(memory_space=pltpu.VMEM)
+    size = ring[0].size
     return pl.pallas_call(
         quadratic_kernel,
-        in_specs=[pl.BlockSpec(memory_space=pltpu.SMEM)] + [vmem] * 5,
+        in_specs=[pl.BlockSpec(memory_space=pltpu.SMEM)] + [vmem] * (2 + len(ring)),
         out_specs=vmem,
-        out_shape=jax.ShapeDtypeStruct(amplitudes.shape, F32),
-        compiler_params=pltpu.CompilerParams(vmem_limit_bytes=24 * 1024 * 1024),
+        out_shape=jax.ShapeDtypeStruct(ring[0].shape, F32),
+        compiler_params=pltpu.CompilerParams(vmem_limit_bytes=20 * 1024 * 1024),
         cost_estimate=pl.CostEstimate(
-            flops=8 * wide_real.size * amplitudes.shape[2],
-            bytes_accessed=4 * wide_real.size + 4 * amplitudes.size,
+            flops=4 * len(ring) * size * ring[0].shape[2],
+            bytes_accessed=(2 * len(ring) + 4) * size,
             transcendentals=0,
         ),
         name="quadratic",
-    )(me, amplitudes, wide_real, wide_imag, mine, other)
+    )(core, mine, other, *ring)
 
 
 def finish_kernel(places, base_ref, *refs):
@@ -229,13 +232,19 @@
 
 def shards(tri_size, vp_size, amplitudes, integrals, ladder_blocks, slot_block):
     bits = tri_size.bit_length() - 1
-    tri_me = lax.axis_index("tri").astype(jnp.int32)
-    me = jnp.stack([tri_me & 1, lax.axis_index("vp").astype(jnp.int32)])
-    wide_real = lax.all_gather(amplitudes[0], "vp", axis=0, tiled=False)
-    wide_imag = lax.all_gather(amplitudes[1], "vp", axis=0, tiled=False)
+    me = lax.axis_index("tri").astype(jnp.int32)[None]
+    core = me & 1
+
+    def turn(value, distance=1):
+        return lax.ppermute(value, "vp", [(i, (i + distance) % vp_size) for i in range(vp_size)])
+
+    ring = [amplitudes]
+    for _ in range(1, vp_size - 1):
+        ring.append(turn(ring[-1]))
     pieces = gather_tri(amplitudes, tri_size)
-    *values, wide_real = lax.optimization_barrier((*[value for value, _, _ in pieces], wide_real))
+    *values, ring[-1] = lax.optimization_barrier((*[value for value, _, _ in pieces], ring[-1]))
     pieces = [(value, mask, part) for value, (_, mask, part) in zip(values, pieces, strict=True)]
+    ring.append(turn(ring[-1]))
 
     if tri_size == 8:
         real_order, imag_order = (2, 6, 4), (4, 6, 2)
@@ -243,9 +252,9 @@
         groups += [[(mask, 0) for mask in real_order], [(mask, 1) for mask in imag_order], [(0, 0), (0, 1)]]
     else:
         groups = [[(mask, part) for mask in range(tri_size) for part in range(2)]]
-    partials = ladder(tri_me[None], slot_block, pieces, ladder_blocks, groups)
-    *partials, wide_real, wide_imag = lax.optimization_barrier((*partials, wide_real, wide_imag))
-    hold, give = contract(me, integrals, wide_real, wide_imag)
+    partials = ladder(me, slot_block, pieces, ladder_blocks, groups)
+    *partials, ring[-1] = lax.optimization_barrier((*partials, ring[-1]))
+    hold, give = contract(core, integrals, ring)
 
     if tri_size == 8:
         real, imag, own = partials[3:]
@@ -270,11 +279,8 @@
         mine = add(hold, swap(give, tri_size, 0)).astype(BF16)
         for bit in range(1, bits):
             mine = add(mine, swap(mine, tri_size, bit)).astype(BF16)
-    shifted = [mine[0]]
-    for step in range(1, vp_size):
-        shifted.append(lax.ppermute(mine[step], "vp", [(i, (i + step) % vp_size) for i in range(vp_size)]))
-    mine = jnp.stack(shifted)
-    base = quadratic(me, amplitudes, wide_real, wide_imag, mine, swap(mine, tri_size, 0))
+    mine = jnp.stack([mine[0]] + [turn(mine[step], vp_size - step) for step in range(1, vp_size)])
+    base = quadratic(core, ring, mine, swap(mine, tri_size, 0))
     return finish(base, terms)
 
 

time: 119 us -> 86.9 us (0.73)
  blocking collectives: 43 us -> 0 us
  waiting for transfers between devices: 27.6 us -> 42.1 us
  other arithmetic: 4.27 us -> 0.59 us
  Pallas kernels: 16 us -> 13.4 us
  starting transfers between devices: 17.6 us -> 20.2 us
    all_gather x2 -> x0, blocking collectives: 43 us -> none  [the longest x1 22 us: shards(): wide_real = lax.all_gather(amplitudes[0], 'vp', axis=0, tiled=False)]
    ppermute x3 -> x6, waiting for transfers between devices: 4.08 us -> 12.4 us  [turn(): lax.ppermute(value, 'vp', [(i, (i + distance) % vp_size) for i in range(v...]
    ppermute x20, waiting for transfers between devices: 23.6 us -> 29.6 us  [swap(): return lax.ppermute(value, 'tri', pairs)]
    ppermute x3 -> x6, starting transfers between devices: 3.14 us -> 6.44 us  [turn(): lax.ppermute(value, 'vp', [(i, (i + distance) % vp_size) for i in range(v...]
    unnamed x22 -> x26, local copies, waits for them, and re-layouts: 8.01 us -> 10 us
    slice x2 -> x1, local copies, waits for them, and re-layouts: 1.79 us -> 0.01 us  [shards(): mine[0]]
    pallas_call x1, Pallas kernels: 12.7 us -> 11.1 us  [ladder(): pl.pallas_call(functools.partial(ladder_kernel, [(mask, part) for _, mask...]
    convert_element_type x1, other arithmetic: 1.73 us -> 0.26 us  [shards(): by_y = add(imag[:2], imag_in[:2]).astype(BF16)]
  transfers between devices with their start and end apart: 23 -> 26, of which waited for: 10 -> 17; matrix products, arithmetic and copies ran while one was open for 4% -> 0% of each run, Pallas kernels for 2% -> 14%
where the time goes in v3:
time: 86.9 us; the launch traced here: 86.4 us
  waiting for transfers between devices  42.1 us (48%)
  starting transfers between devices  20.2 us (23%)
  Pallas kernels  13.4 us (15%)
  local copies, waits for them, and re-layouts  10.1 us (12%)
    ppermute x20, waiting for transfers between devices, swap(): return lax.ppermute(value, 'tri', pairs)  29.6 us
    ppermute x20, starting transfers between devices, swap(): return lax.ppermute(value, 'tri', pairs)  13.7 us
    ppermute x6, waiting for transfers between devices, turn(): lax.ppermute(value, 'vp', [(i, (i + distance) % vp_size) for i in range(v...  12.4 us
    pallas_call x1, Pallas kernels, ladder(): pl.pallas_call(functools.partial(ladder_kernel, [(mask, part) for _, mask...  11.1 us
    unnamed x26, local copies, waits for them, and re-layouts  10 us
    ppermute x6, starting transfers between devices, turn(): lax.ppermute(value, 'vp', [(i, (i + distance) % vp_size) for i in range(v...  6.44 us
  transfers between devices with their start and end apart: 26, of which 17 were waited for; matrix products, arithmetic and copies ran while one was open for 0% of the time, Pallas kernels for 14%

profile of v3, /device:TPU:0, one launch (start us, length us, event | category | flops | bytes accessed | tf_op | source)
XLA Modules:
  0.0 86.4 jit_solution(635723731669050198)
XLA Ops:
  0.0 3.0 %collective-permute-start.1 = (bf16[2,960,128]{2,1,0:T(8,128)(2,1)}, bf16[2,960,128]{2,1,0:T(8,128)(2,1)S(1)}, u32[]{:S(2)}, u32[]{:S(2)}) collective-permute-start(bf16[2,960,128]{2,1,0:T(8,128)(2,1)} %refs_0_.4), channel_id=1, source_target_pairs={{0,16},{4,20},{8,24},{12,28},{16,0},{20,4},{24,8},{28,12},{1,17},{... | collective-permute-start | bytes 1474568 | tf_op jit(solution)/shard_map/ppermute | solution.py:20
  3.0 1.5 %collective-permute-start = (bf16[2,960,128]{2,1,0:T(8,128)(2,1)}, bf16[2,960,128]{2,1,0:T(8,128)(2,1)S(1)}, u32[]{:S(2)}, u32[]{:S(2)}) collective-permute-start(bf16[2,960,128]{2,1,0:T(8,128)(2,1)} %refs_0_.4), channel_id=1, source_target_pairs={{0,8},{4,12},{8,0},{12,4},{16,24},{20,28},{24,16},{28,20},{1,9},{5... | collective-permute-start | bytes 1474568 | tf_op jit(solution)/shard_map/ppermute | solution.py:20
  4.5 1.6 %collective-permute-start.9 = (bf16[2,960,128]{2,1,0:T(8,128)(2,1)}, bf16[2,960,128]{2,1,0:T(8,128)(2,1)S(1)}, u32[]{:S(2)}, u32[]{:S(2)}) collective-permute-start(bf16[2,960,128]{2,1,0:T(8,128)(2,1)} %refs_0_.4), channel_id=1, source_target_pairs={{0,1},{1,2},{2,3},{3,0},{4,5},{5,6},{6,7},{7,4},{8,9},{9,10},{10,1... | collective-permute-start | bytes 1474568 | tf_op jit(solution)/shard_map/ppermute | solution.py:239
  6.0 8.4 %collective-permute-done.1.refs_2_ = bf16[2,960,128]{2,1,0:T(8,128)(2,1)S(1)} collective-permute-done((bf16[2,960,128]{2,1,0:T(8,128)(2,1)}, bf16[2,960,128]{2,1,0:T(8,128)(2,1)S(1)}, u32[]{:S(2)}, u32[]{:S(2)}) %collective-permute-start.1) | collective-permute-done | bytes 491552 | tf_op jit(solution)/shard_map/ppermute | solution.py:20
  14.4 1.8 %collective-permute-start.2 = (bf16[960,128]{1,0:T(8,128)(2,1)S(1)}, bf16[960,128]{1,0:T(8,128)(2,1)S(1)}, u32[]{:S(2)}, u32[]{:S(2)}) collective-permute-start(bf16[960,128]{1,0:T(8,128)(2,1)S(1)} %slice_bitcast_fusion.1), channel_id=1, source_target_pairs={{0,8},{4,12},{8,0},{12,4},{16,24},{20,28},{24,16},{28,20},{1,9},{5... | collective-permute-start | bytes 737288 | tf_op jit(solution)/shard_map/ppermute | solution.py:20
  16.2 1.6 %collective-permute-start.3 = (bf16[960,128]{1,0:T(8,128)(2,1)S(1)}, bf16[960,128]{1,0:T(8,128)(2,1)S(1)}, u32[]{:S(2)}, u32[]{:S(2)}) collective-permute-start(bf16[960,128]{1,0:T(8,128)(2,1)S(1)} %slice_bitcast_fusion), channel_id=1, source_target_pairs={{0,16},{4,20},{8,24},{12,28},{16,0},{20,4},{24,8},{28,12},{1,17},{... | collective-permute-start | bytes 737288 | tf_op jit(solution)/shard_map/ppermute | solution.py:20
  17.8 1.2 %collective-permute-done.9.refs_1_ = bf16[2,960,128]{2,1,0:T(8,128)(2,1)S(1)} collective-permute-done((bf16[2,960,128]{2,1,0:T(8,128)(2,1)}, bf16[2,960,128]{2,1,0:T(8,128)(2,1)S(1)}, u32[]{:S(2)}, u32[]{:S(2)}) %collective-permute-start.9) | collective-permute-done | bytes 491552 | tf_op jit(solution)/shard_map/ppermute | solution.py:239
  19.6 2.0 %collective-permute-done.2.refs_3_ = bf16[960,128]{1,0:T(8,128)(2,1)S(1)} collective-permute-done((bf16[960,128]{1,0:T(8,128)(2,1)S(1)}, bf16[960,128]{1,0:T(8,128)(2,1)S(1)}, u32[]{:S(2)}, u32[]{:S(2)}) %collective-permute-start.2) | collective-permute-done | bytes 245792 | tf_op jit(solution)/shard_map/ppermute | solution.py:20
  25.0 8.3 %collective-permute-done.10.refs_2_ = bf16[2,960,128]{2,1,0:T(8,128)(2,1)S(1)} collective-permute-done((bf16[2,960,128]{2,1,0:T(8,128)(2,1)S(1)}, bf16[2,960,128]{2,1,0:T(8,128)(2,1)S(1)}, u32[]{:S(2)}, u32[]{:S(2)}) %collective-permute-start.10) | collective-permute-done | bytes 491552 | tf_op jit(solution)/shard_map/ppermute | solution.py:239
  33.3 0.8 copy-done.1
  34.1 1.0 %copy-done = bf16[2,960,128]{2,1,0:T(8,128)(2,1)S(1)} copy-done((bf16[2,960,128]{2,1,0:T(8,128)(2,1)S(1)}, bf16[2,960,128]{2,1,0:T(8,128)(2,1)}, u32[]{:S(2)}) %copy-start) | copy-done | bytes 491544
  35.1 1.0 %copy-done.2 = bf16[2,960,128]{2,1,0:T(8,128)(2,1)S(1)} copy-done((bf16[2,960,128]{2,1,0:T(8,128)(2,1)S(1)}, bf16[2,960,128]{2,1,0:T(8,128)(2,1)}, u32[]{:S(2)}) %copy-start.2) | copy-done | bytes 491544
  36.2 0.9 %copy-done.5 = bf16[960,128]{1,0:T(8,128)(2,1)S(1)} copy-done((bf16[960,128]{1,0:T(8,128)(2,1)S(1)}, bf16[960,128]{1,0:T(8,128)(2,1)}, u32[]{:S(2)}) %copy-start.5) | copy-done | bytes 245784
  37.1 0.9 %copy-done.7 = bf16[960,128]{1,0:T(8,128)(2,1)S(1)} copy-done((bf16[960,128]{1,0:T(8,128)(2,1)S(1)}, bf16[960,128]{1,0:T(8,128)(2,1)}, u32[]{:S(2)}) %copy-start.7) | copy-done | bytes 245784
  38.1 0.9 %copy-done.9 = bf16[960,128]{1,0:T(8,128)(2,1)S(1)} copy-done((bf16[960,128]{1,0:T(8,128)(2,1)S(1)}, bf16[960,128]{1,0:T(8,128)(2,1)}, u32[]{:S(2)}) %copy-start.9) | copy-done | bytes 245784
  39.0 0.9 %copy-done.11 = bf16[960,128]{1,0:T(8,128)(2,1)S(1)} copy-done((bf16[960,128]{1,0:T(8,128)(2,1)S(1)}, bf16[960,128]{1,0:T(8,128)(2,1)}, u32[]{:S(2)}) %copy-start.11) | copy-done | bytes 245784
  40.6 11.1 %ladder.1 = (bf16[3,960,128]{2,1,0:T(8,128)(2,1)S(1)}, bf16[3,960,128]{2,1,0:T(8,128)(2,1)S(1)}, bf16[2,960,128]{2,1,0:T(8,128)(2,1)S(1)}, bf16[3,960,128]{2,1,0...) custom-call(s32[1]{0:T(128)} %bitcast.me_ref, s32[7]{0:T(128)S(1)} %copy-done.12, ...), custom_call_target="tpu_custom_call" | custom-call | flops 1 | bytes 1 | tf_op jit(solution)/shard_map/ladder/pallas_call | solution.py:106
  52.8 1.2 %collective-permute-done.12 = bf16[3,960,128]{2,1,0:T(8,128)(2,1)S(1)} collective-permute-done((bf16[3,960,128]{2,1,0:T(8,128)(2,1)S(1)}, bf16[3,960,128]{2,1,0:T(8,128)(2,1)S(1)}, u32[]{:S(2)}, u32[]{:S(2)}) %collective-permute-start.12) | collective-permute-done | bytes 737312 | tf_op jit(solution)/shard_map/ppermute | solution.py:20
  54.0 1.1 %collective-permute-done.13 = bf16[3,960,128]{2,1,0:T(8,128)(2,1)S(1)} collective-permute-done((bf16[3,960,128]{2,1,0:T(8,128)(2,1)S(1)}, bf16[3,960,128]{2,1,0:T(8,128)(2,1)S(1)}, u32[]{:S(2)}, u32[]{:S(2)}) %collective-permute-start.13) | collective-permute-done | bytes 737312 | tf_op jit(solution)/shard_map/ppermute | solution.py:20
  57.4 1.5 %collective-permute-start.16 = (bf16[2,960,128]{2,1,0:T(8,128)(2,1)S(1)}, bf16[2,960,128]{2,1,0:T(8,128)(2,1)S(1)}, u32[]{:S(2)}, u32[]{:S(2)}) collective-permute-start(bf16[2,960,128]{2,1,0:T(8,128)(2,1)S(1)} %get-tuple-element.72), channel_id=1, source_target_pairs={{0,8},{4,12},{8,0},{12,4},{16,24},{20,28},{24,16},{28,20},{1,9},{5... | collective-permute-start | bytes 1474568 | tf_op jit(solution)/shard_map/ppermute | solution.py:20
  58.9 4.3 %collective-permute-done.15 = bf16[4,128,128]{2,1,0:T(8,128)(2,1)S(1)} collective-permute-done((bf16[4,128,128]{2,1,0:T(8,128)(2,1)S(1)}, bf16[4,128,128]{2,1,0:T(8,128)(2,1)S(1)}, u32[]{:S(2)}, u32[]{:S(2)}) %collective-permute-start.15) | collective-permute-done | bytes 131104 | tf_op jit(solution)/shard_map/ppermute | solution.py:20
  63.3 0.9 %collective-permute-start.18 = (bf16[4,128,128]{2,1,0:T(8,128)(2,1)S(1)}, bf16[4,128,128]{2,1,0:T(8,128)(2,1)S(1)}, u32[]{:S(2)}, u32[]{:S(2)}) collective-permute-start(bf16[4,128,128]{2,1,0:T(8,128)(2,1)S(1)} %add_convert_fusion.5), channel_id=1, source_target_pairs={{0,16},{4,20},{8,24},{12,28},{16,0},{20,4},{24,8},{28,12},{1,17},{... | collective-permute-start | bytes 393224 | tf_op jit(solution)/shard_map/ppermute | solution.py:20
  64.2 5.4 %collective-permute-done.17.refs_5_ = bf16[2,960,128]{2,1,0:T(8,128)(2,1)S(1)} collective-permute-done((bf16[2,960,128]{2,1,0:T(8,128)(2,1)S(1)}, bf16[2,960,128]{2,1,0:T(8,128)(2,1)S(1)}, u32[]{:S(2)}, u32[]{:S(2)}) %collective-permute-start.17) | collective-permute-done | bytes 491552 | tf_op jit(solution)/shard_map/ppermute | solution.py:20
  69.7 3.2 %collective-permute-done.16.refs_4_ = bf16[2,960,128]{2,1,0:T(8,128)(2,1)S(1)} collective-permute-done((bf16[2,960,128]{2,1,0:T(8,128)(2,1)S(1)}, bf16[2,960,128]{2,1,0:T(8,128)(2,1)S(1)}, u32[]{:S(2)}, u32[]{:S(2)}) %collective-permute-start.16) | collective-permute-done | bytes 491552 | tf_op jit(solution)/shard_map/ppermute | solution.py:20
  73.1 1.3 %collective-permute-start.21 = (bf16[128,128]{1,0:T(8,128)(2,1)S(1)}, bf16[128,128]{1,0:T(8,128)(2,1)S(1)}, u32[]{:S(2)}, u32[]{:S(2)}) collective-permute-start(bf16[128,128]{1,0:T(8,128)(2,1)S(1)} %get-tuple-element.80), channel_id=1, source_target_pairs={{0,1},{1,2},{2,3},{3,0},{4,5},{5,6},{6,7},{7,4},{8,9},{9,10},{10,1... | collective-permute-start | bytes 98312 | tf_op jit(solution)/shard_map/ppermute | solution.py:239
  74.5 2.6 %collective-permute-start.19 = (bf16[128,128]{1,0:T(8,128)(2,1)S(1)}, bf16[128,128]{1,0:T(8,128)(2,1)S(1)}, u32[]{:S(2)}, u32[]{:S(2)}) collective-permute-start(bf16[128,128]{1,0:T(8,128)(2,1)S(1)} %get-tuple-element.82), channel_id=1, source_target_pairs={{0,3},{1,0},{2,1},{3,2},{4,7},{5,4},{6,5},{7,6},{8,11},{9,8},{10,9... | collective-permute-start | bytes 98312 | tf_op jit(solution)/shard_map/ppermute | solution.py:239
  77.6 0.8 collective-permute-start.24
  78.3 0.8 collective-permute-done.21
  79.7 2.2 %collective-permute-done.20 = bf16[128,128]{1,0:T(8,128)(2,1)S(1)} collective-permute-done((bf16[128,128]{1,0:T(8,128)(2,1)S(1)}, bf16[128,128]{1,0:T(8,128)(2,1)S(1)}, u32[]{:S(2)}, u32[]{:S(2)}) %collective-permute-start.20) | collective-permute-done | bytes 32800 | tf_op jit(solution)/shard_map/ppermute | solution.py:239
  82.0 1.3 %collective-permute-done.22.other_ref = bf16[4,128,128]{2,1,0:T(8,128)(2,1)S(1)} collective-permute-done((bf16[4,128,128]{2,1,0:T(8,128)(2,1)S(1)}, bf16[4,128,128]{2,1,0:T(8,128)(2,1)S(1)}, u32[]{:S(2)}, u32[]{:S(2)}) %collective-permute-start.22) | collective-permute-done | bytes 131104 | tf_op jit(solution)/shard_map/ppermute | solution.py:20
  84.2 1.2 %collective-permute-done.25.refs_7_ = bf16[1,960,128]{2,1,0:T(8,128)(2,1)S(1)} collective-permute-done((bf16[1,960,128]{2,1,0:T(8,128)(2,1)S(1)}, bf16[1,960,128]{2,1,0:T(8,128)(2,1)S(1)}, u32[]{:S(2)}, u32[]{:S(2)}) %collective-permute-start.25) | collective-permute-done | bytes 245792 | tf_op jit(solution)/shard_map/ppermute | solution.py:20
  85.4 1.1 %finish.1 = bf16[2,960,128]{2,1,0:T(8,128)(2,1)} custom-call(f32[2,960,128]{2,1,0:T(8,128)S(1)} %quadratic.1.base_ref, bf16[2,960,128]{2,1,0:T(8,128)(2,1)S(1)} %get-tuple-element.75.refs_0_.refs_1_, bf16[2,960,128]{2,1,0:T(8,128)(2,1)S(1)} %get-tuple-element.75.refs_0_.refs_1_, bf16[2,960,128]{2,1,0:T(8,128)(2,1)S(1)} %collective-permute-done.23.refs_2_.refs_3_, ...), custom_call_target="tpu_custom_call" | custom-call | tf_op jit(solution)/shard_map/finish/pallas_call | solution.py:214
  (60 shorter events, 10.4 us)
Async XLA Ops:
  0.0 14.4 %collective-permute-start.1 = (bf16[2,960,128]{2,1,0:T(8,128)(2,1)}, bf16[2,960,128]{2,1,0:T(8,128)(2,1)S(1)}, u32[]{:S(2)}, u32[]{:S(2)}) collective-permute-start(bf16[2,960,128]{2,1,0:T(8,128)(2,1)} %refs_0_.4), channel_id=1, source_target_pairs={{0,16},{4,20},{8,24},{12,28},{16,0},{20,4},{24,8},{28,12},{1,17},{... | collective-permute-start | bytes 1474568 | tf_op jit(solution)/shard_map/ppermute | solution.py:20
  3.0 13.2 %collective-permute-start = (bf16[2,960,128]{2,1,0:T(8,128)(2,1)}, bf16[2,960,128]{2,1,0:T(8,128)(2,1)S(1)}, u32[]{:S(2)}, u32[]{:S(2)}) collective-permute-start(bf16[2,960,128]{2,1,0:T(8,128)(2,1)} %refs_0_.4), channel_id=1, source_target_pairs={{0,8},{4,12},{8,0},{12,4},{16,24},{20,28},{24,16},{28,20},{1,9},{5... | collective-permute-start | bytes 1474568 | tf_op jit(solution)/shard_map/ppermute | solution.py:20
  4.5 14.5 %collective-permute-start.9 = (bf16[2,960,128]{2,1,0:T(8,128)(2,1)}, bf16[2,960,128]{2,1,0:T(8,128)(2,1)S(1)}, u32[]{:S(2)}, u32[]{:S(2)}) collective-permute-start(bf16[2,960,128]{2,1,0:T(8,128)(2,1)} %refs_0_.4), channel_id=1, source_target_pairs={{0,1},{1,2},{2,3},{3,0},{4,5},{5,6},{6,7},{7,4},{8,9},{9,10},{10,1... | collective-permute-start | bytes 1474568 | tf_op jit(solution)/shard_map/ppermute | solution.py:239
  6.0 13.4 %collective-permute-start.4 = (bf16[2,960,128]{2,1,0:T(8,128)(2,1)}, bf16[2,960,128]{2,1,0:T(8,128)(2,1)S(1)}, u32[]{:S(2)}, u32[]{:S(2)}) collective-permute-start(bf16[2,960,128]{2,1,0:T(8,128)(2,1)} %refs_0_.4), channel_id=1, source_target_pairs={{0,4},{4,0},{8,12},{12,8},{16,20},{20,16},{24,28},{28,24},{1,5},{5... | collective-permute-start | bytes 1474568 | tf_op jit(solution)/shard_map/ppermute | solution.py:20
  14.4 7.2 %collective-permute-start.2 = (bf16[960,128]{1,0:T(8,128)(2,1)S(1)}, bf16[960,128]{1,0:T(8,128)(2,1)S(1)}, u32[]{:S(2)}, u32[]{:S(2)}) collective-permute-start(bf16[960,128]{1,0:T(8,128)(2,1)S(1)} %slice_bitcast_fusion.1), channel_id=1, source_target_pairs={{0,8},{4,12},{8,0},{12,4},{16,24},{20,28},{24,16},{28,20},{1,9},{5... | collective-permute-start | bytes 737288 | tf_op jit(solution)/shard_map/ppermute | solution.py:20
  16.2 6.6 %collective-permute-start.3 = (bf16[960,128]{1,0:T(8,128)(2,1)S(1)}, bf16[960,128]{1,0:T(8,128)(2,1)S(1)}, u32[]{:S(2)}, u32[]{:S(2)}) collective-permute-start(bf16[960,128]{1,0:T(8,128)(2,1)S(1)} %slice_bitcast_fusion), channel_id=1, source_target_pairs={{0,16},{4,20},{8,24},{12,28},{16,0},{20,4},{24,8},{28,12},{1,17},{... | collective-permute-start | bytes 737288 | tf_op jit(solution)/shard_map/ppermute | solution.py:20
  17.8 15.5 %collective-permute-start.5 = (bf16[2,960,128]{2,1,0:T(8,128)(2,1)S(1)}, bf16[2,960,128]{2,1,0:T(8,128)(2,1)S(1)}, u32[]{:S(2)}, u32[]{:S(2)}) collective-permute-start(bf16[2,960,128]{2,1,0:T(8,128)(2,1)S(1)} %collective-permute-done.refs_1_), channel_id=1, source_target_pairs={{0,4},{4,0},{8,12},{12,8},{16,20},{20,16},{24,28},{28,24},{1,5},{5... | collective-permute-start | bytes 1474568 | tf_op jit(solution)/shard_map/ppermute | solution.py:20
  19.0 14.3 %collective-permute-start.10 = (bf16[2,960,128]{2,1,0:T(8,128)(2,1)S(1)}, bf16[2,960,128]{2,1,0:T(8,128)(2,1)S(1)}, u32[]{:S(2)}, u32[]{:S(2)}) collective-permute-start(bf16[2,960,128]{2,1,0:T(8,128)(2,1)S(1)} %collective-permute-done.9.refs_1_), channel_id=1, source_target_pairs={{0,1},{1,2},{2,3},{3,0},{4,5},{5,6},{6,7},{7,4},{8,9},{9,10},{10,1... | collective-permute-start | bytes 1474568 | tf_op jit(solution)/shard_map/ppermute | solution.py:239
  19.4 13.9 %collective-permute-start.6 = (bf16[2,960,128]{2,1,0:T(8,128)(2,1)S(1)}, bf16[2,960,128]{2,1,0:T(8,128)(2,1)S(1)}, u32[]{:S(2)}, u32[]{:S(2)}) collective-permute-start(bf16[2,960,128]{2,1,0:T(8,128)(2,1)S(1)} %collective-permute-done.1.refs_2_), channel_id=1, source_target_pairs={{0,4},{4,0},{8,12},{12,8},{16,20},{20,16},{24,28},{28,24},{1,5},{5... | collective-permute-start | bytes 1474568 | tf_op jit(solution)/shard_map/ppermute | solution.py:20
  21.6 1.9 %collective-permute-start.7 = (bf16[960,128]{1,0:T(8,128)(2,1)S(1)}, bf16[960,128]{1,0:T(8,128)(2,1)S(1)}, u32[]{:S(2)}, u32[]{:S(2)}) collective-permute-start(bf16[960,128]{1,0:T(8,128)(2,1)S(1)} %collective-permute-done.2.refs_3_), channel_id=1, source_target_pairs={{0,4},{4,0},{8,12},{12,8},{16,20},{20,16},{24,28},{28,24},{1,5},{5... | collective-permute-start | bytes 737288 | tf_op jit(solution)/shard_map/ppermute | solution.py:20
  22.8 1.5 %collective-permute-start.8 = (bf16[960,128]{1,0:T(8,128)(2,1)S(1)}, bf16[960,128]{1,0:T(8,128)(2,1)S(1)}, u32[]{:S(2)}, u32[]{:S(2)}) collective-permute-start(bf16[960,128]{1,0:T(8,128)(2,1)S(1)} %collective-permute-done.3.refs_4_), channel_id=1, source_target_pairs={{0,4},{4,0},{8,12},{12,8},{16,20},{20,16},{24,28},{28,24},{1,5},{5... | collective-permute-start | bytes 737288 | tf_op jit(solution)/shard_map/ppermute | solution.py:20
  34.1 17.7 %collective-permute-start.11 = (bf16[2,960,128]{2,1,0:T(8,128)(2,1)S(1)}, bf16[2,960,128]{2,1,0:T(8,128)(2,1)S(1)}, u32[]{:S(2)}, u32[]{:S(2)}) collective-permute-start(bf16[2,960,128]{2,1,0:T(8,128)(2,1)S(1)} %collective-permute-done.10.refs_2_), channel_id=1, source_target_pairs={{0,1},{1,2},{2,3},{3,0},{4,5},{5,6},{6,7},{7,4},{8,9},{9,10},{10,1... | collective-permute-start | bytes 1474568 | tf_op jit(solution)/shard_map/ppermute | solution.py:239
  34.1 1.0 %copy-start = (bf16[2,960,128]{2,1,0:T(8,128)(2,1)S(1)}, bf16[2,960,128]{2,1,0:T(8,128)(2,1)}, u32[]{:S(2)}) copy-start(bf16[2,960,128]{2,1,0:T(8,128)(2,1)} %refs_0_.4) | copy-start | bytes 1474564
  35.1 1.0 %copy-start.2 = (bf16[2,960,128]{2,1,0:T(8,128)(2,1)S(1)}, bf16[2,960,128]{2,1,0:T(8,128)(2,1)}, u32[]{:S(2)}) copy-start(bf16[2,960,128]{2,1,0:T(8,128)(2,1)} %copy-done.1) | copy-start | bytes 1474564
  36.2 0.9 %copy-start.5 = (bf16[960,128]{1,0:T(8,128)(2,1)S(1)}, bf16[960,128]{1,0:T(8,128)(2,1)}, u32[]{:S(2)}) copy-start(bf16[960,128]{1,0:T(8,128)(2,1)} %copy-done.4) | copy-start | bytes 737284
  37.1 0.9 %copy-start.7 = (bf16[960,128]{1,0:T(8,128)(2,1)S(1)}, bf16[960,128]{1,0:T(8,128)(2,1)}, u32[]{:S(2)}) copy-start(bf16[960,128]{1,0:T(8,128)(2,1)} %copy-done.6) | copy-start | bytes 737284
  38.0 0.9 %copy-start.9 = (bf16[960,128]{1,0:T(8,128)(2,1)S(1)}, bf16[960,128]{1,0:T(8,128)(2,1)}, u32[]{:S(2)}) copy-start(bf16[960,128]{1,0:T(8,128)(2,1)} %copy-done.8) | copy-start | bytes 737284
  40.6 11.7 %copy-start.3 = (bf16[960,128]{1,0:T(8,128)(2,1)S(1)}, bf16[960,128]{1,0:T(8,128)(2,1)}, u32[]{:S(2)}) copy-start(bf16[960,128]{1,0:T(8,128)(2,1)} %int_ref.1) | copy-start | bytes 737284
  51.8 2.3 %collective-permute-start.12 = (bf16[3,960,128]{2,1,0:T(8,128)(2,1)S(1)}, bf16[3,960,128]{2,1,0:T(8,128)(2,1)S(1)}, u32[]{:S(2)}, u32[]{:S(2)}) collective-permute-start(bf16[3,960,128]{2,1,0:T(8,128)(2,1)S(1)} %get-tuple-element.60), channel_id=1, source_target_pairs={{0,4},{4,0},{8,12},{12,8},{16,20},{20,16},{24,28},{28,24},{1,5},{5... | collective-permute-start | bytes 2211848 | tf_op jit(solution)/shard_map/ppermute | solution.py:20
  51.8 3.3 %collective-permute-start.13 = (bf16[3,960,128]{2,1,0:T(8,128)(2,1)S(1)}, bf16[3,960,128]{2,1,0:T(8,128)(2,1)S(1)}, u32[]{:S(2)}, u32[]{:S(2)}) collective-permute-start(bf16[3,960,128]{2,1,0:T(8,128)(2,1)S(1)} %get-tuple-element.61), channel_id=1, source_target_pairs={{0,4},{4,0},{8,12},{12,8},{16,20},{20,16},{24,28},{28,24},{1,5},{5... | collective-permute-start | bytes 2211848 | tf_op jit(solution)/shard_map/ppermute | solution.py:20
  55.4 1.4 %collective-permute-start.14 = (bf16[4,128,128]{2,1,0:T(8,128)(2,1)S(1)}, bf16[4,128,128]{2,1,0:T(8,128)(2,1)S(1)}, u32[]{:S(2)}, u32[]{:S(2)}) collective-permute-start(bf16[4,128,128]{2,1,0:T(8,128)(2,1)S(1)} %get-tuple-element.71), channel_id=1, source_target_pairs={{0,4},{4,0},{8,12},{12,8},{16,20},{20,16},{24,28},{28,24},{1,5},{5... | collective-permute-start | bytes 393224 | tf_op jit(solution)/shard_map/ppermute | solution.py:20
  55.6 14.1 %collective-permute-start.17 = (bf16[2,960,128]{2,1,0:T(8,128)(2,1)S(1)}, bf16[2,960,128]{2,1,0:T(8,128)(2,1)S(1)}, u32[]{:S(2)}, u32[]{:S(2)}) collective-permute-start(bf16[2,960,128]{2,1,0:T(8,128)(2,1)S(1)} %get-tuple-element.73), channel_id=1, source_target_pairs={{0,16},{4,20},{8,24},{12,28},{16,0},{20,4},{24,8},{28,12},{1,17},{... | collective-permute-start | bytes 1474568 | tf_op jit(solution)/shard_map/ppermute | solution.py:20
  56.8 6.4 %collective-permute-start.15 = (bf16[4,128,128]{2,1,0:T(8,128)(2,1)S(1)}, bf16[4,128,128]{2,1,0:T(8,128)(2,1)S(1)}, u32[]{:S(2)}, u32[]{:S(2)}) collective-permute-start(bf16[4,128,128]{2,1,0:T(8,128)(2,1)S(1)} %add_convert_fusion.6), channel_id=1, source_target_pairs={{0,8},{4,12},{8,0},{12,4},{16,24},{20,28},{24,16},{28,20},{1,9},{5... | collective-permute-start | bytes 393224 | tf_op jit(solution)/shard_map/ppermute | solution.py:20
  57.4 15.5 %collective-permute-start.16 = (bf16[2,960,128]{2,1,0:T(8,128)(2,1)S(1)}, bf16[2,960,128]{2,1,0:T(8,128)(2,1)S(1)}, u32[]{:S(2)}, u32[]{:S(2)}) collective-permute-start(bf16[2,960,128]{2,1,0:T(8,128)(2,1)S(1)} %get-tuple-element.72), channel_id=1, source_target_pairs={{0,8},{4,12},{8,0},{12,4},{16,24},{20,28},{24,16},{28,20},{1,9},{5... | collective-permute-start | bytes 1474568 | tf_op jit(solution)/shard_map/ppermute | solution.py:20
  58.9 25.1 %collective-permute-start.23 = (bf16[2,960,128]{2,1,0:T(8,128)(2,1)S(1)}, bf16[2,960,128]{2,1,0:T(8,128)(2,1)S(1)}, u32[]{:S(2)}, u32[]{:S(2)}) collective-permute-start(bf16[2,960,128]{2,1,0:T(8,128)(2,1)S(1)} %get-tuple-element.76), channel_id=1, source_target_pairs={{0,4},{4,0},{8,12},{12,8},{16,20},{20,16},{24,28},{28,24},{1,5},{5... | collective-permute-start | bytes 1474568 | tf_op jit(solution)/shard_map/ppermute | solution.py:20
  63.3 9.8 %collective-permute-start.18 = (bf16[4,128,128]{2,1,0:T(8,128)(2,1)S(1)}, bf16[4,128,128]{2,1,0:T(8,128)(2,1)S(1)}, u32[]{:S(2)}, u32[]{:S(2)}) collective-permute-start(bf16[4,128,128]{2,1,0:T(8,128)(2,1)S(1)} %add_convert_fusion.5), channel_id=1, source_target_pairs={{0,16},{4,20},{8,24},{12,28},{16,0},{20,4},{24,8},{28,12},{1,17},{... | collective-permute-start | bytes 393224 | tf_op jit(solution)/shard_map/ppermute | solution.py:20
  73.1 6.0 %collective-permute-start.21 = (bf16[128,128]{1,0:T(8,128)(2,1)S(1)}, bf16[128,128]{1,0:T(8,128)(2,1)S(1)}, u32[]{:S(2)}, u32[]{:S(2)}) collective-permute-start(bf16[128,128]{1,0:T(8,128)(2,1)S(1)} %get-tuple-element.80), channel_id=1, source_target_pairs={{0,1},{1,2},{2,3},{3,0},{4,5},{5,6},{6,7},{7,4},{8,9},{9,10},{10,1... | collective-permute-start | bytes 98312 | tf_op jit(solution)/shard_map/ppermute | solution.py:239
  74.5 5.2 %collective-permute-start.19 = (bf16[128,128]{1,0:T(8,128)(2,1)S(1)}, bf16[128,128]{1,0:T(8,128)(2,1)S(1)}, u32[]{:S(2)}, u32[]{:S(2)}) collective-permute-start(bf16[128,128]{1,0:T(8,128)(2,1)S(1)} %get-tuple-element.82), channel_id=1, source_target_pairs={{0,3},{1,0},{2,1},{3,2},{4,7},{5,4},{6,5},{7,6},{8,11},{9,8},{10,9... | collective-permute-start | bytes 98312 | tf_op jit(solution)/shard_map/ppermute | solution.py:239
  77.1 4.8 %collective-permute-start.20 = (bf16[128,128]{1,0:T(8,128)(2,1)S(1)}, bf16[128,128]{1,0:T(8,128)(2,1)S(1)}, u32[]{:S(2)}, u32[]{:S(2)}) collective-permute-start(bf16[128,128]{1,0:T(8,128)(2,1)S(1)} %get-tuple-element.81), channel_id=1, source_target_pairs={{0,2},{1,3},{2,0},{3,1},{4,6},{5,7},{6,4},{7,5},{8,10},{9,11},{10,... | collective-permute-start | bytes 98312 | tf_op jit(solution)/shard_map/ppermute | solution.py:239
  77.6 6.6 %collective-permute-start.24 = (bf16[1,960,128]{2,1,0:T(8,128)(2,1)S(1)}, bf16[1,960,128]{2,1,0:T(8,128)(2,1)S(1)}, u32[]{:S(2)}, u32[]{:S(2)}) collective-permute-start(bf16[1,960,128]{2,1,0:T(8,128)(2,1)S(1)} %bitcast.21), channel_id=1, source_target_pairs={{0,16},{4,20},{8,24},{12,28},{16,0},{20,4},{24,8},{28,12},{1,17},{... | collective-permute-start | bytes 737288 | tf_op jit(solution)/shard_map/ppermute | solution.py:20
  79.2 6.2 %collective-permute-start.25 = (bf16[1,960,128]{2,1,0:T(8,128)(2,1)S(1)}, bf16[1,960,128]{2,1,0:T(8,128)(2,1)S(1)}, u32[]{:S(2)}, u32[]{:S(2)}) collective-permute-start(bf16[1,960,128]{2,1,0:T(8,128)(2,1)S(1)} %bitcast.20), channel_id=1, source_target_pairs={{0,8},{4,12},{8,0},{12,4},{16,24},{20,28},{24,16},{28,20},{1,9},{5... | collective-permute-start | bytes 737288 | tf_op jit(solution)/shard_map/ppermute | solution.py:20
  81.9 1.4 %collective-permute-start.22 = (bf16[4,128,128]{2,1,0:T(8,128)(2,1)S(1)}, bf16[4,128,128]{2,1,0:T(8,128)(2,1)S(1)}, u32[]{:S(2)}, u32[]{:S(2)}) collective-permute-start(bf16[4,128,128]{2,1,0:T(8,128)(2,1)S(1)} %pad_maximum_fusion.mine_ref), channel_id=1, source_target_pairs={{0,4},{4,0},{8,12},{12,8},{16,20},{20,16},{24,28},{28,24},{1,5},{5... | collective-permute-start | bytes 393224 | tf_op jit(solution)/shard_map/ppermute | solution.py:20
  (7 other events, 5.1 us)

commit v4 on v2

--- a/solution.py
+++ b/solution.py
@@ -133,12 +133,12 @@
     return total
 
 
-def contract_kernel(me_ref, int_ref, real_ref, imag_ref, hold_ref, give_ref):
-    vp_size, _, columns = real_ref.shape
+def contract_kernel(me_ref, int_ref, wide_ref, hold_ref, give_ref):
+    vp_size, _, _, columns = wide_ref.shape
     values = int_ref[...]
     for step in range(vp_size):
         target = lax.rem(me_ref[1] + step, vp_size)
-        both = jnp.concatenate([real_ref[target], imag_ref[target]], axis=1)
+        both = jnp.concatenate([wide_ref[target, 0], wide_ref[target, 1]], axis=1)
         product = lax.dot_general(values, both, (((0,), (0,)), ((), ())), preferred_element_type=F32)
         real = product[:, :columns].astype(BF16)
         imag = product[:, columns:].astype(BF16)
@@ -146,31 +146,31 @@
         give_ref[step] = jnp.where(me_ref[0] == 0, imag, real)
 
 
-def contract(me, integrals, wide_real, wide_imag):
-    vp_size, rows, columns = wide_real.shape
+def contract(me, integrals, wide):
+    vp_size, _, rows, columns = wide.shape
     vmem = pl.BlockSpec(memory_space=pltpu.VMEM)
     return pl.pallas_call(
         contract_kernel,
-        in_specs=[pl.BlockSpec(memory_space=pltpu.SMEM)] + [vmem] * 3,
+        in_specs=[pl.BlockSpec(memory_space=pltpu.SMEM)] + [vmem] * 2,
         out_specs=[vmem] * 2,
         out_shape=[jax.ShapeDtypeStruct((vp_size, columns, columns), BF16)] * 2,
-        compiler_params=pltpu.CompilerParams(vmem_limit_bytes=24 * 1024 * 1024),
+        compiler_params=pltpu.CompilerParams(vmem_limit_bytes=20 * 1024 * 1024),
         cost_estimate=pl.CostEstimate(
-            flops=4 * vp_size * rows * columns * columns,
-            bytes_accessed=4 * wide_real.size + 2 * integrals.size,
+            flops=2 * wide.size * columns,
+            bytes_accessed=2 * (wide.size + integrals.size),
             transcendentals=0,
         ),
         name="contract",
-    )(me, integrals, wide_real, wide_imag)
-
-
-def quadratic_kernel(me_ref, amp_ref, real_ref, imag_ref, mine_ref, other_ref, out_ref):
-    vp_size, rows, columns = real_ref.shape
+    )(me, integrals, wide)
+
+
+def quadratic_kernel(me_ref, amp_ref, wide_ref, mine_ref, other_ref, out_ref):
+    vp_size, _, rows, columns = wide_ref.shape
     core = me_ref[0]
     total = jnp.zeros((rows, 2 * columns), F32)
     for step in range(vp_size):
         source = lax.rem(me_ref[1] + vp_size - step, vp_size)
-        both = jnp.concatenate([real_ref[source], imag_ref[source]], axis=1)
+        both = jnp.concatenate([wide_ref[source, 0], wide_ref[source, 1]], axis=1)
         real = jnp.where(core == 0, mine_ref[step], other_ref[step])
         imag = jnp.where(core == 0, other_ref[step], mine_ref[step])
         weights = jnp.concatenate(
@@ -181,21 +181,21 @@
     out_ref[1] = amp_ref[1].astype(F32) - 0.25 * total[:, :columns]
 
 
-def quadratic(me, amplitudes, wide_real, wide_imag, mine, other):
+def quadratic(me, amplitudes, wide, mine, other):
     vmem = pl.BlockSpec(memory_space=pltpu.VMEM)
     return pl.pallas_call(
         quadratic_kernel,
-        in_specs=[pl.BlockSpec(memory_space=pltpu.SMEM)] + [vmem] * 5,
+        in_specs=[pl.BlockSpec(memory_space=pltpu.SMEM)] + [vmem] * 4,
         out_specs=vmem,
         out_shape=jax.ShapeDtypeStruct(amplitudes.shape, F32),
-        compiler_params=pltpu.CompilerParams(vmem_limit_bytes=24 * 1024 * 1024),
+        compiler_params=pltpu.CompilerParams(vmem_limit_bytes=20 * 1024 * 1024),
         cost_estimate=pl.CostEstimate(
-            flops=8 * wide_real.size * amplitudes.shape[2],
-            bytes_accessed=4 * wide_real.size + 4 * amplitudes.size,
+            flops=4 * wide.size * amplitudes.shape[2],
+            bytes_accessed=2 * wide.size + 4 * amplitudes.size,
             transcendentals=0,
         ),
         name="quadratic",
-    )(me, amplitudes, wide_real, wide_imag, mine, other)
+    )(me, amplitudes, wide, mine, other)
 
 
 def finish_kernel(places, base_ref, *refs):
@@ -213,7 +213,7 @@
         in_specs=[vmem] * (1 + len(terms)),
         out_specs=vmem,
         out_shape=jax.ShapeDtypeStruct(base.shape, BF16),
-        compiler_params=pltpu.CompilerParams(vmem_limit_bytes=24 * 1024 * 1024),
+        compiler_params=pltpu.CompilerParams(vmem_limit_bytes=20 * 1024 * 1024),
         name="finish",
     )(base, *[value for value, _, _ in terms])
 
@@ -229,13 +229,10 @@
 
 def shards(tri_size, vp_size, amplitudes, integrals, ladder_blocks, slot_block):
     bits = tri_size.bit_length() - 1
-    tri_me = lax.axis_index("tri").astype(jnp.int32)
-    me = jnp.stack([tri_me & 1, lax.axis_index("vp").astype(jnp.int32)])
-    wide_real = lax.all_gather(amplitudes[0], "vp", axis=0, tiled=False)
-    wide_imag = lax.all_gather(amplitudes[1], "vp", axis=0, tiled=False)
+    me = lax.axis_index("tri").astype(jnp.int32)[None]
+    where = jnp.stack([me[0] & 1, lax.axis_index("vp").astype(jnp.int32)])
+    wide = lax.all_gather(amplitudes, "vp", axis=0, tiled=False)
     pieces = gather_tri(amplitudes, tri_size)
-    *values, wide_real = lax.optimization_barrier((*[value for value, _, _ in pieces], wide_real))
-    pieces = [(value, mask, part) for value, (_, mask, part) in zip(values, pieces, strict=True)]
 
     if tri_size == 8:
         real_order, imag_order = (2, 6, 4), (4, 6, 2)
@@ -243,9 +240,15 @@
         groups += [[(mask, 0) for mask in real_order], [(mask, 1) for mask in imag_order], [(0, 0), (0, 1)]]
     else:
         groups = [[(mask, part) for mask in range(tri_size) for part in range(2)]]
-    partials = ladder(tri_me[None], slot_block, pieces, ladder_blocks, groups)
-    *partials, wide_real, wide_imag = lax.optimization_barrier((*partials, wide_real, wide_imag))
-    hold, give = contract(me, integrals, wide_real, wide_imag)
+    partials = ladder(me, slot_block, pieces, ladder_blocks, groups)
+    *partials, wide = lax.optimization_barrier((*partials, wide))
+    hold, give = contract(where, integrals, wide)
+
+    def shift(value):
+        moved = [value[0]]
+        for step in range(1, vp_size):
+            moved.append(lax.ppermute(value[step], "vp", [(i, (i + step) % vp_size) for i in range(vp_size)]))
+        return jnp.stack(moved)
 
     if tri_size == 8:
         real, imag, own = partials[3:]
@@ -255,26 +258,22 @@
         by_y = add(imag[:2], imag_in[:2]).astype(BF16)
         by_x, by_y, hold, give = lax.optimization_barrier((by_x, by_y, hold, give))
         by_x, by_y = swap(by_x, tri_size, 1), swap(by_y, tri_size, 2)
-        mine = add(hold, swap(give, tri_size, 0)).astype(BF16)
-        mine = add(mine, swap(mine, tri_size, 1)).astype(BF16)
-        received = swap(mine, tri_size, 2)
+        mine = shift(add(hold, swap(give, tri_size, 0)).astype(BF16))
+        received = swap(mine, tri_size, 1)
         then_y = add(real[2], real_in[2], by_x[1]).astype(BF16)
         then_x = add(imag[2], imag_in[2], by_y[1]).astype(BF16)
         then_y, then_x, received = lax.optimization_barrier((then_y, then_x, received))
         then_y, then_x = swap(then_y[None], tri_size, 2), swap(then_x[None], tri_size, 1)
         mine = add(mine, received).astype(BF16)
+        mine = add(mine, swap(mine, tri_size, 2)).astype(BF16)
         terms = [(own, 0, 0), (own, 1, 1), (own_in, 0, 0), (own_in, 1, 1)]
         terms += [(by_x, 0, 0), (by_y, 1, 0), (then_y, 0, 0), (then_x, 1, 0)]
     else:
         terms = scatter_plain(partials[0].reshape(tri_size, 2, *amplitudes.shape[1:]), tri_size)
-        mine = add(hold, swap(give, tri_size, 0)).astype(BF16)
+        mine = shift(add(hold, swap(give, tri_size, 0)).astype(BF16))
         for bit in range(1, bits):
             mine = add(mine, swap(mine, tri_size, bit)).astype(BF16)
-    shifted = [mine[0]]
-    for step in range(1, vp_size):
-        shifted.append(lax.ppermute(mine[step], "vp", [(i, (i + step) % vp_size) for i in range(vp_size)]))
-    mine = jnp.stack(shifted)
-    base = quadratic(me, amplitudes, wide_real, wide_imag, mine, swap(mine, tri_size, 0))
+    base = quadratic(where, amplitudes, wide, mine, swap(mine, tri_size, 0))
     return finish(base, terms)
 
 

time: 119 us -> 99.3 us (0.83)
  blocking collectives: 43 us -> 0 us
  between operations: 0.17 us -> 13.5 us
  local copies, waits for them, and re-layouts: 9.83 us -> 18.8 us
  starting transfers between devices: 17.6 us -> 21.3 us
  Pallas kernels: 16 us -> 14.5 us
    all_gather x2 -> x0, blocking collectives: 43 us -> none  [the longest x1 22 us: shards(): wide_real = lax.all_gather(amplitudes[0], 'vp', axis=0, tiled=False)]
    unnamed x22 -> x48, local copies, waits for them, and re-layouts: 8.01 us -> 18.7 us
    ppermute x20, waiting for transfers between devices: 23.6 us -> 21.4 us  [swap(): return lax.ppermute(value, 'tri', pairs)]
    ppermute x20, starting transfers between devices: 14.4 us -> 16.6 us  [swap(): return lax.ppermute(value, 'tri', pairs)]
    slice x2 -> x1, local copies, waits for them, and re-layouts: 1.79 us -> 0.01 us  [shift(): moved = [value[0]]]
    ppermute x3, starting transfers between devices: 3.14 us -> 4.67 us  [shift(): lax.ppermute(value[step], 'vp', [(i, (i + step) % vp_size) for i in range...]
    pallas_call x1, Pallas kernels: 12.7 us -> 11.2 us  [ladder(): pl.pallas_call(functools.partial(ladder_kernel, [(mask, part) for _, mask...]
  transfers between devices with their start and end apart: 23 -> 24, of which waited for: 10 -> 11; matrix products, arithmetic and copies ran while one was open for 4% -> 2% of each run, Pallas kernels for 2% -> 14%
where the time goes in v4:
time: 99.3 us; the launch traced here: 98.6 us
  waiting for transfers between devices  26.8 us (27%)
  starting transfers between devices  21.3 us (21%)
  local copies, waits for them, and re-layouts  18.8 us (19%)
  Pallas kernels  14.5 us (15%)
  between operations  13.5 us (14%)
  other arithmetic  3.75 us (4%)
    ppermute x20, waiting for transfers between devices, swap(): return lax.ppermute(value, 'tri', pairs)  21.4 us
    unnamed x48, local copies, waits for them, and re-layouts  18.7 us
    ppermute x20, starting transfers between devices, swap(): return lax.ppermute(value, 'tri', pairs)  16.6 us
    pallas_call x1, Pallas kernels, ladder(): pl.pallas_call(functools.partial(ladder_kernel, [(mask, part) for _, mask...  11.2 us
    ppermute x3, waiting for transfers between devices, shift(): lax.ppermute(value[step], 'vp', [(i, (i + step) % vp_size) for i in range...  4.68 us
    ppermute x3, starting transfers between devices, shift(): lax.ppermute(value[step], 'vp', [(i, (i + step) % vp_size) for i in range...  4.67 us
  transfers between devices with their start and end apart: 24, of which 11 were waited for; matrix products, arithmetic and copies ran while one was open for 2% of the time, Pallas kernels for 14%

profile of v4, /device:TPU:0, one launch (start us, length us, event | category | flops | bytes accessed | tf_op | source)
XLA Modules:
  0.0 98.6 jit_solution(12548831229747707565)
XLA Ops:
  7.3 3.0 %collective-permute-start.1 = (bf16[2,960,128]{2,1,0:T(8,128)(2,1)}, bf16[2,960,128]{2,1,0:T(8,128)(2,1)S(1)}, u32[]{:S(2)}, u32[]{:S(2)}) collective-permute-start(bf16[2,960,128]{2,1,0:T(8,128)(2,1)} %amp_ref.1), channel_id=1, source_target_pairs={{0,16},{4,20},{8,24},{12,28},{16,0},{20,4},{24,8},{28,12},{1,17},{... | collective-permute-start | bytes 1474568 | tf_op jit(solution)/shard_map/ppermute | solution.py:20
  10.3 1.5 %collective-permute-start = (bf16[2,960,128]{2,1,0:T(8,128)(2,1)}, bf16[2,960,128]{2,1,0:T(8,128)(2,1)S(1)}, u32[]{:S(2)}, u32[]{:S(2)}) collective-permute-start(bf16[2,960,128]{2,1,0:T(8,128)(2,1)} %amp_ref.1), channel_id=1, source_target_pairs={{0,8},{4,12},{8,0},{12,4},{16,24},{20,28},{24,16},{28,20},{1,9},{5... | collective-permute-start | bytes 1474568 | tf_op jit(solution)/shard_map/ppermute | solution.py:20
  11.8 9.9 %collective-permute-done.1.refs_2_ = bf16[2,960,128]{2,1,0:T(8,128)(2,1)S(1)} collective-permute-done((bf16[2,960,128]{2,1,0:T(8,128)(2,1)}, bf16[2,960,128]{2,1,0:T(8,128)(2,1)S(1)}, u32[]{:S(2)}, u32[]{:S(2)}) %collective-permute-start.1) | collective-permute-done | bytes 491552 | tf_op jit(solution)/shard_map/ppermute | solution.py:20
  21.7 1.8 %collective-permute-start.2 = (bf16[960,128]{1,0:T(8,128)(2,1)S(1)}, bf16[960,128]{1,0:T(8,128)(2,1)S(1)}, u32[]{:S(2)}, u32[]{:S(2)}) collective-permute-start(bf16[960,128]{1,0:T(8,128)(2,1)S(1)} %slice_bitcast_fusion.1), channel_id=1, source_target_pairs={{0,8},{4,12},{8,0},{12,4},{16,24},{20,28},{24,16},{28,20},{1,9},{5... | collective-permute-start | bytes 737288 | tf_op jit(solution)/shard_map/ppermute | solution.py:20
  23.5 1.6 %collective-permute-start.3 = (bf16[960,128]{1,0:T(8,128)(2,1)S(1)}, bf16[960,128]{1,0:T(8,128)(2,1)S(1)}, u32[]{:S(2)}, u32[]{:S(2)}) collective-permute-start(bf16[960,128]{1,0:T(8,128)(2,1)S(1)} %slice_bitcast_fusion), channel_id=1, source_target_pairs={{0,16},{4,20},{8,24},{12,28},{16,0},{20,4},{24,8},{28,12},{1,17},{... | collective-permute-start | bytes 737288 | tf_op jit(solution)/shard_map/ppermute | solution.py:20
  25.6 3.3 %collective-permute-done.2.refs_3_ = bf16[960,128]{1,0:T(8,128)(2,1)S(1)} collective-permute-done((bf16[960,128]{1,0:T(8,128)(2,1)S(1)}, bf16[960,128]{1,0:T(8,128)(2,1)S(1)}, u32[]{:S(2)}, u32[]{:S(2)}) %collective-permute-start.2) | collective-permute-done | bytes 245792 | tf_op jit(solution)/shard_map/ppermute | solution.py:20
  34.6 1.0 %copy-done.2 = bf16[2,960,128]{2,1,0:T(8,128)(2,1)S(1)} copy-done((bf16[2,960,128]{2,1,0:T(8,128)(2,1)S(1)}, bf16[2,960,128]{2,1,0:T(8,128)(2,1)}, u32[]{:S(2)}) %copy-start.2) | copy-done | bytes 491544
  35.7 1.0 %copy-done.5 = bf16[2,960,128]{2,1,0:T(8,128)(2,1)S(1)} copy-done((bf16[2,960,128]{2,1,0:T(8,128)(2,1)S(1)}, bf16[2,960,128]{2,1,0:T(8,128)(2,1)}, u32[]{:S(2)}) %copy-start.5) | copy-done | bytes 491544
  36.7 1.0 %copy-done.7 = bf16[2,960,128]{2,1,0:T(8,128)(2,1)S(1)} copy-done((bf16[2,960,128]{2,1,0:T(8,128)(2,1)S(1)}, bf16[2,960,128]{2,1,0:T(8,128)(2,1)}, u32[]{:S(2)}) %copy-start.7) | copy-done | bytes 491544
  37.7 1.0 %copy-done.9 = bf16[2,960,128]{2,1,0:T(8,128)(2,1)S(1)} copy-done((bf16[2,960,128]{2,1,0:T(8,128)(2,1)S(1)}, bf16[2,960,128]{2,1,0:T(8,128)(2,1)}, u32[]{:S(2)}) %copy-start.9) | copy-done | bytes 491544
  39.7 0.9 copy-done.14
  40.7 0.9 copy-done.16
  43.2 11.2 %ladder.1 = (bf16[3,960,128]{2,1,0:T(8,128)(2,1)S(1)}, bf16[3,960,128]{2,1,0:T(8,128)(2,1)S(1)}, bf16[2,960,128]{2,1,0:T(8,128)(2,1)S(1)}, bf16[3,960,128]{2,1,0...) custom-call(s32[1]{0:T(128)} %bitcast.2.me_ref, s32[7]{0:T(128)S(1)} %copy-done.19, ...), custom_call_target="tpu_custom_call" | custom-call | flops 1 | bytes 1 | tf_op jit(solution)/shard_map/ladder/pallas_call | solution.py:106
  57.5 1.5 %copy-done = bf16[8,960,128]{2,1,0:T(8,128)(2,1)S(1)} copy-done((bf16[8,960,128]{2,1,0:T(8,128)(2,1)S(1)}, bf16[8,960,128]{2,1,0:T(8,128)(2,1)}, u32[]{:S(2)}) %copy-start) | copy-done | bytes 1966104
  60.0 1.0 %contract.1 = (bf16[4,128,128]{2,1,0:T(8,128)(2,1)S(1)}, bf16[4,128,128]{2,1,0:T(8,128)(2,1)S(1)}) custom-call(s32[2]{0:T(128)S(1)} %pad_add_fusion.me_ref, bf16[960,128]{1,0:T(8,128)(2,1)S(1)} %copy-done.10, bf16[4,2,960,128]{3,2,1,0:T(8,128)(2,1)S(1)} %bitcast.23), custom_call_target="tpu_custom_call" | custom-call | flops 251658240 | bytes 2211840 | tf_op jit(solution)/shard_map/contract/pallas_call | solution.py:152
  61.0 1.4 %add_convert_fusion = (bf16[2,960,128]{2,1,0:T(8,128)(2,1)S(1)}, bf16[2,960,128]{2,1,0:T(8,128)(2,1)S(1)}) fusion(bf16[3,960,128]{2,1,0:T(8,128)(2,1)} %collective-permute-done.10, bf16[3,960,128]{2,1,0:T(8,128)(2,1)S(1)} %get-tuple-element.44, bf16[3,960,128]{2,1,0:T(8,128)(2,1)} %collective-permute-done.9, bf16[3,960,128]{2,1,0:T(8,128)(2,1)S(1)} %get-tuple-element.38), kind=kLoop, calls=%fused_computation | loop fusion | flops 1966080 | bytes 2949120 | tf_op jit(solution)/shard_map/convert_element_type | solution.py:258
  63.0 1.5 %collective-permute-start.16 = (bf16[2,960,128]{2,1,0:T(8,128)(2,1)S(1)}, bf16[2,960,128]{2,1,0:T(8,128)(2,1)S(1)}, u32[]{:S(2)}, u32[]{:S(2)}) collective-permute-start(bf16[2,960,128]{2,1,0:T(8,128)(2,1)S(1)} %get-tuple-element.51), channel_id=1, source_target_pairs={{0,16},{4,20},{8,24},{12,28},{16,0},{20,4},{24,8},{28,12},{1,17},{... | collective-permute-start | bytes 1474568 | tf_op jit(solution)/shard_map/ppermute | solution.py:20
  64.6 1.0 collective-permute-start.15
  65.6 3.6 %collective-permute-start.14 = (bf16[128,128]{1,0:T(8,128)(2,1)S(1)}, bf16[128,128]{1,0:T(8,128)(2,1)S(1)}, u32[]{:S(2)}, u32[]{:S(2)}) collective-permute-start(bf16[128,128]{1,0:T(8,128)(2,1)S(1)} %get-tuple-element.58), channel_id=1, source_target_pairs={{0,3},{1,0},{2,1},{3,2},{4,7},{5,4},{6,5},{7,6},{8,11},{9,8},{10,9... | collective-permute-start | bytes 98312 | tf_op jit(solution)/shard_map/ppermute | solution.py:250
  69.2 1.0 %collective-permute-start.13 = (bf16[128,128]{1,0:T(8,128)(2,1)S(1)}, bf16[128,128]{1,0:T(8,128)(2,1)S(1)}, u32[]{:S(2)}, u32[]{:S(2)}) collective-permute-start(bf16[128,128]{1,0:T(8,128)(2,1)S(1)} %get-tuple-element.59), channel_id=1, source_target_pairs={{0,2},{1,3},{2,0},{3,1},{4,6},{5,7},{6,4},{7,5},{8,10},{9,11},{10,... | collective-permute-start | bytes 98312 | tf_op jit(solution)/shard_map/ppermute | solution.py:250
  70.8 4.1 %collective-permute-done.12 = bf16[128,128]{1,0:T(8,128)(2,1)S(1)} collective-permute-done((bf16[128,128]{1,0:T(8,128)(2,1)S(1)}, bf16[128,128]{1,0:T(8,128)(2,1)S(1)}, u32[]{:S(2)}, u32[]{:S(2)}) %collective-permute-start.12) | collective-permute-done | bytes 32800 | tf_op jit(solution)/shard_map/ppermute | solution.py:250
  75.0 1.2 %collective-permute-start.17 = (bf16[4,128,128]{2,1,0:T(8,128)(2,1)S(1)}, bf16[4,128,128]{2,1,0:T(8,128)(2,1)S(1)}, u32[]{:S(2)}, u32[]{:S(2)}) collective-permute-start(bf16[4,128,128]{2,1,0:T(8,128)(2,1)S(1)} %pad_maximum_fusion), channel_id=1, source_target_pairs={{0,8},{4,12},{8,0},{12,4},{16,24},{20,28},{24,16},{28,20},{1,9},{5... | collective-permute-start | bytes 393224 | tf_op jit(solution)/shard_map/ppermute | solution.py:20
  76.2 1.0 %fusion.1 = bf16[960,128]{1,0:T(8,128)(2,1)S(1)} fusion(bf16[2,960,128]{2,1,0:T(8,128)(2,1)S(1)} %collective-permute-done.16.refs_5_, bf16[3,960,128]{2,1,0:T(8,128)(2,1)} %collective-permute-done.10, bf16[3,960,128]{2,1,0:T(8,128)(2,1)S(1)} %get-tuple-element.44), kind=kLoop, calls=%fused_computation.8 | loop fusion | flops 737280 | bytes 983040 | tf_op jit(solution)/shard_map/convert_element_type | solution.py:264
  77.3 1.4 %collective-permute-done.15.refs_4_ = bf16[2,960,128]{2,1,0:T(8,128)(2,1)S(1)} collective-permute-done((bf16[2,960,128]{2,1,0:T(8,128)(2,1)S(1)}, bf16[2,960,128]{2,1,0:T(8,128)(2,1)S(1)}, u32[]{:S(2)}, u32[]{:S(2)}) %collective-permute-start.15) | collective-permute-done | bytes 491552 | tf_op jit(solution)/shard_map/ppermute | solution.py:20
  78.7 1.0 %fusion = bf16[960,128]{1,0:T(8,128)(2,1)S(1)} fusion(bf16[2,960,128]{2,1,0:T(8,128)(2,1)S(1)} %collective-permute-done.15.refs_4_, bf16[3,960,128]{2,1,0:T(8,128)(2,1)} %collective-permute-done.9, bf16[3,960,128]{2,1,0:T(8,128)(2,1)S(1)} %get-tuple-element.38), kind=kLoop, calls=%fused_computation.7 | loop fusion | flops 737280 | bytes 983040 | tf_op jit(solution)/shard_map/convert_element_type | solution.py:263
  80.9 1.5 %collective-permute-start.21 = (bf16[1,960,128]{2,1,0:T(8,128)(2,1)S(1)}, bf16[1,960,128]{2,1,0:T(8,128)(2,1)S(1)}, u32[]{:S(2)}, u32[]{:S(2)}) collective-permute-start(bf16[1,960,128]{2,1,0:T(8,128)(2,1)S(1)} %bitcast.35), channel_id=1, source_target_pairs={{0,16},{4,20},{8,24},{12,28},{16,0},{20,4},{24,8},{28,12},{1,17},{... | collective-permute-start | bytes 737288 | tf_op jit(solution)/shard_map/ppermute | solution.py:20
  82.4 1.3 %collective-permute-start.22 = (bf16[1,960,128]{2,1,0:T(8,128)(2,1)S(1)}, bf16[1,960,128]{2,1,0:T(8,128)(2,1)S(1)}, u32[]{:S(2)}, u32[]{:S(2)}) collective-permute-start(bf16[1,960,128]{2,1,0:T(8,128)(2,1)S(1)} %bitcast.34), channel_id=1, source_target_pairs={{0,8},{4,12},{8,0},{12,4},{16,24},{20,28},{24,16},{28,20},{1,9},{5... | collective-permute-start | bytes 737288 | tf_op jit(solution)/shard_map/ppermute | solution.py:20
  83.8 3.0 %collective-permute-done.18 = bf16[4,128,128]{2,1,0:T(8,128)(2,1)S(1)} collective-permute-done((bf16[4,128,128]{2,1,0:T(8,128)(2,1)S(1)}, bf16[4,128,128]{2,1,0:T(8,128)(2,1)S(1)}, u32[]{:S(2)}, u32[]{:S(2)}) %collective-permute-start.18) | collective-permute-done | bytes 131104 | tf_op jit(solution)/shard_map/ppermute | solution.py:20
  86.9 1.3 %collective-permute-done.19.other_ref = bf16[4,128,128]{2,1,0:T(8,128)(2,1)S(1)} collective-permute-done((bf16[4,128,128]{2,1,0:T(8,128)(2,1)S(1)}, bf16[4,128,128]{2,1,0:T(8,128)(2,1)S(1)}, u32[]{:S(2)}, u32[]{:S(2)}) %collective-permute-start.19) | collective-permute-done | bytes 131104 | tf_op jit(solution)/shard_map/ppermute | solution.py:20
  88.2 1.2 %quadratic.1.base_ref = f32[2,960,128]{2,1,0:T(8,128)S(1)} custom-call(s32[2]{0:T(128)S(1)} %pad_add_fusion.me_ref, bf16[2,960,128]{2,1,0:T(8,128)(2,1)S(1)} %copy-done.3, bf16[4,2,960,128]{3,2,1,0:T(8,128)(2,1)S(1)} %bitcast.24, bf16[4,128,128]{2,1,0:T(8,128)(2,1)S(1)} %add_convert_fusion.4.mine_ref, bf16[4,128,128]{2,1,0:T(8,128)(2,1)S(1)} %collective-permute-done.19.other_ref), custom_call_target="tpu_custom_call" | custom-call | flops 503316480 | bytes 2949120 | tf_op jit(solution)/shard_map/quadratic/pallas_call | solution.py:186
  89.4 1.2 %collective-permute-done.21.refs_6_ = bf16[1,960,128]{2,1,0:T(8,128)(2,1)S(1)} collective-permute-done((bf16[1,960,128]{2,1,0:T(8,128)(2,1)S(1)}, bf16[1,960,128]{2,1,0:T(8,128)(2,1)S(1)}, u32[]{:S(2)}, u32[]{:S(2)}) %collective-permute-start.21) | collective-permute-done | bytes 245792 | tf_op jit(solution)/shard_map/ppermute | solution.py:20
  90.6 1.1 %finish.1 = bf16[2,960,128]{2,1,0:T(8,128)(2,1)} custom-call(f32[2,960,128]{2,1,0:T(8,128)S(1)} %quadratic.1.base_ref, bf16[2,960,128]{2,1,0:T(8,128)(2,1)S(1)} %get-tuple-element.53.refs_0_.refs_1_, bf16[2,960,128]{2,1,0:T(8,128)(2,1)S(1)} %get-tuple-element.53.refs_0_.refs_1_, bf16[2,960,128]{2,1,0:T(8,128)(2,1)S(1)} %collective-permute-done.20.refs_2_.refs_3_, ...), custom_call_target="tpu_custom_call" | custom-call | tf_op jit(solution)/shard_map/finish/pallas_call | solution.py:211
  (80 shorter events, 16.2 us)
Async XLA Ops:
  6.5 50.4 %all-gather.3.cloned.1.call-start = ((), (), s32[]{:S(2)}) async-start(), calls=%async_computation | async-start | bytes 2457600 | tf_op jit(solution)/shard_map/all_gather | solution.py:234
  7.3 14.5 %collective-permute-start.1 = (bf16[2,960,128]{2,1,0:T(8,128)(2,1)}, bf16[2,960,128]{2,1,0:T(8,128)(2,1)S(1)}, u32[]{:S(2)}, u32[]{:S(2)}) collective-permute-start(bf16[2,960,128]{2,1,0:T(8,128)(2,1)} %amp_ref.1), channel_id=1, source_target_pairs={{0,16},{4,20},{8,24},{12,28},{16,0},{20,4},{24,8},{28,12},{1,17},{... | collective-permute-start | bytes 1474568 | tf_op jit(solution)/shard_map/ppermute | solution.py:20
  10.3 13.2 %collective-permute-start = (bf16[2,960,128]{2,1,0:T(8,128)(2,1)}, bf16[2,960,128]{2,1,0:T(8,128)(2,1)S(1)}, u32[]{:S(2)}, u32[]{:S(2)}) collective-permute-start(bf16[2,960,128]{2,1,0:T(8,128)(2,1)} %amp_ref.1), channel_id=1, source_target_pairs={{0,8},{4,12},{8,0},{12,4},{16,24},{20,28},{24,16},{28,20},{1,9},{5... | collective-permute-start | bytes 1474568 | tf_op jit(solution)/shard_map/ppermute | solution.py:20
  11.8 19.1 %collective-permute-start.4 = (bf16[2,960,128]{2,1,0:T(8,128)(2,1)}, bf16[2,960,128]{2,1,0:T(8,128)(2,1)S(1)}, u32[]{:S(2)}, u32[]{:S(2)}) collective-permute-start(bf16[2,960,128]{2,1,0:T(8,128)(2,1)} %amp_ref.1), channel_id=1, source_target_pairs={{0,4},{4,0},{8,12},{12,8},{16,20},{20,16},{24,28},{28,24},{1,5},{5... | collective-permute-start | bytes 1474568 | tf_op jit(solution)/shard_map/ppermute | solution.py:20
  21.7 7.2 %collective-permute-start.2 = (bf16[960,128]{1,0:T(8,128)(2,1)S(1)}, bf16[960,128]{1,0:T(8,128)(2,1)S(1)}, u32[]{:S(2)}, u32[]{:S(2)}) collective-permute-start(bf16[960,128]{1,0:T(8,128)(2,1)S(1)} %slice_bitcast_fusion.1), channel_id=1, source_target_pairs={{0,8},{4,12},{8,0},{12,4},{16,24},{20,28},{24,16},{28,20},{1,9},{5... | collective-permute-start | bytes 737288 | tf_op jit(solution)/shard_map/ppermute | solution.py:20
  23.5 6.6 %collective-permute-start.3 = (bf16[960,128]{1,0:T(8,128)(2,1)S(1)}, bf16[960,128]{1,0:T(8,128)(2,1)S(1)}, u32[]{:S(2)}, u32[]{:S(2)}) collective-permute-start(bf16[960,128]{1,0:T(8,128)(2,1)S(1)} %slice_bitcast_fusion), channel_id=1, source_target_pairs={{0,16},{4,20},{8,24},{12,28},{16,0},{20,4},{24,8},{28,12},{1,17},{... | collective-permute-start | bytes 737288 | tf_op jit(solution)/shard_map/ppermute | solution.py:20
  25.1 7.9 %collective-permute-start.5 = (bf16[2,960,128]{2,1,0:T(8,128)(2,1)S(1)}, bf16[2,960,128]{2,1,0:T(8,128)(2,1)S(1)}, u32[]{:S(2)}, u32[]{:S(2)}) collective-permute-start(bf16[2,960,128]{2,1,0:T(8,128)(2,1)S(1)} %collective-permute-done.refs_1_), channel_id=1, source_target_pairs={{0,4},{4,0},{8,12},{12,8},{16,20},{20,16},{24,28},{28,24},{1,5},{5... | collective-permute-start | bytes 1474568 | tf_op jit(solution)/shard_map/ppermute | solution.py:20
  25.1 8.7 %collective-permute-start.6 = (bf16[2,960,128]{2,1,0:T(8,128)(2,1)S(1)}, bf16[2,960,128]{2,1,0:T(8,128)(2,1)S(1)}, u32[]{:S(2)}, u32[]{:S(2)}) collective-permute-start(bf16[2,960,128]{2,1,0:T(8,128)(2,1)S(1)} %collective-permute-done.1.refs_2_), channel_id=1, source_target_pairs={{0,4},{4,0},{8,12},{12,8},{16,20},{20,16},{24,28},{28,24},{1,5},{5... | collective-permute-start | bytes 1474568 | tf_op jit(solution)/shard_map/ppermute | solution.py:20
  28.9 2.7 %collective-permute-start.7 = (bf16[960,128]{1,0:T(8,128)(2,1)S(1)}, bf16[960,128]{1,0:T(8,128)(2,1)S(1)}, u32[]{:S(2)}, u32[]{:S(2)}) collective-permute-start(bf16[960,128]{1,0:T(8,128)(2,1)S(1)} %collective-permute-done.2.refs_3_), channel_id=1, source_target_pairs={{0,4},{4,0},{8,12},{12,8},{16,20},{20,16},{24,28},{28,24},{1,5},{5... | collective-permute-start | bytes 737288 | tf_op jit(solution)/shard_map/ppermute | solution.py:20
  30.2 2.2 %collective-permute-start.8 = (bf16[960,128]{1,0:T(8,128)(2,1)S(1)}, bf16[960,128]{1,0:T(8,128)(2,1)S(1)}, u32[]{:S(2)}, u32[]{:S(2)}) collective-permute-start(bf16[960,128]{1,0:T(8,128)(2,1)S(1)} %collective-permute-done.3.refs_4_), channel_id=1, source_target_pairs={{0,4},{4,0},{8,12},{12,8},{16,20},{20,16},{24,28},{28,24},{1,5},{5... | collective-permute-start | bytes 737288 | tf_op jit(solution)/shard_map/ppermute | solution.py:20
  34.6 1.0 %copy-start.2 = (bf16[2,960,128]{2,1,0:T(8,128)(2,1)S(1)}, bf16[2,960,128]{2,1,0:T(8,128)(2,1)}, u32[]{:S(2)}) copy-start(bf16[2,960,128]{2,1,0:T(8,128)(2,1)} %amp_ref.1) | copy-start | bytes 1474564
  35.7 1.0 %copy-start.5 = (bf16[2,960,128]{2,1,0:T(8,128)(2,1)S(1)}, bf16[2,960,128]{2,1,0:T(8,128)(2,1)}, u32[]{:S(2)}) copy-start(bf16[2,960,128]{2,1,0:T(8,128)(2,1)} %copy-done.4) | copy-start | bytes 1474564
  36.7 1.0 %copy-start.7 = (bf16[2,960,128]{2,1,0:T(8,128)(2,1)S(1)}, bf16[2,960,128]{2,1,0:T(8,128)(2,1)}, u32[]{:S(2)}) copy-start(bf16[2,960,128]{2,1,0:T(8,128)(2,1)} %copy-done.6) | copy-start | bytes 1474564
  37.7 1.0 %copy-start.9 = (bf16[2,960,128]{2,1,0:T(8,128)(2,1)S(1)}, bf16[2,960,128]{2,1,0:T(8,128)(2,1)}, u32[]{:S(2)}) copy-start(bf16[2,960,128]{2,1,0:T(8,128)(2,1)} %copy-done.8) | copy-start | bytes 1474564
  43.2 45.0 %copy-start.3 = (bf16[2,960,128]{2,1,0:T(8,128)(2,1)S(1)}, bf16[2,960,128]{2,1,0:T(8,128)(2,1)}, u32[]{:S(2)}) copy-start(bf16[2,960,128]{2,1,0:T(8,128)(2,1)} %amp_ref.1) | copy-start | bytes 1474564
  56.9 4.1 %collective-permute-start.10 = (bf16[3,960,128]{2,1,0:T(8,128)(2,1)}, bf16[3,960,128]{2,1,0:T(8,128)(2,1)}, u32[]{:S(2)}, u32[]{:S(2)}) collective-permute-start(bf16[3,960,128]{2,1,0:T(8,128)(2,1)} %copy-done.21), channel_id=1, source_target_pairs={{0,4},{4,0},{8,12},{12,8},{16,20},{20,16},{24,28},{28,24},{1,5},{5... | collective-permute-start | bytes 2211848 | tf_op jit(solution)/shard_map/ppermute | solution.py:20
  57.4 3.6 %collective-permute-start.9 = (bf16[3,960,128]{2,1,0:T(8,128)(2,1)}, bf16[3,960,128]{2,1,0:T(8,128)(2,1)}, u32[]{:S(2)}, u32[]{:S(2)}) collective-permute-start(bf16[3,960,128]{2,1,0:T(8,128)(2,1)} %copy-done.20), channel_id=1, source_target_pairs={{0,4},{4,0},{8,12},{12,8},{16,20},{20,16},{24,28},{28,24},{1,5},{5... | collective-permute-start | bytes 2211848 | tf_op jit(solution)/shard_map/ppermute | solution.py:20
  57.5 1.5 %copy-start = (bf16[8,960,128]{2,1,0:T(8,128)(2,1)S(1)}, bf16[8,960,128]{2,1,0:T(8,128)(2,1)}, u32[]{:S(2)}) copy-start(bf16[8,960,128]{2,1,0:T(8,128)(2,1)} %all-gather.3.cloned.1.call-done) | copy-start | bytes 5898244
  60.0 20.9 %copy-start.23 = (bf16[2,960,128]{2,1,0:T(8,128)(2,1)S(1)}, bf16[2,960,128]{2,1,0:T(8,128)(2,1)}, u32[]{:S(2)}) copy-start(bf16[2,960,128]{2,1,0:T(8,128)(2,1)} %copy-done.22) | copy-start | bytes 1474564
  60.0 28.2 %copy-start.1 = (bf16[8,960,128]{2,1,0:T(8,128)(2,1)S(1)}, bf16[8,960,128]{2,1,0:T(8,128)(2,1)}, u32[]{:S(2)}) copy-start(bf16[8,960,128]{2,1,0:T(8,128)(2,1)} %all-gather.3.cloned.1.call-done) | copy-start | bytes 5898244
  62.5 3.0 %collective-permute-start.11 = (bf16[4,128,128]{2,1,0:T(8,128)(2,1)S(1)}, bf16[4,128,128]{2,1,0:T(8,128)(2,1)S(1)}, u32[]{:S(2)}, u32[]{:S(2)}) collective-permute-start(bf16[4,128,128]{2,1,0:T(8,128)(2,1)S(1)} %get-tuple-element.49), channel_id=1, source_target_pairs={{0,4},{4,0},{8,12},{12,8},{16,20},{20,16},{24,28},{28,24},{1,5},{5... | collective-permute-start | bytes 393224 | tf_op jit(solution)/shard_map/ppermute | solution.py:20
  63.0 13.2 %collective-permute-start.16 = (bf16[2,960,128]{2,1,0:T(8,128)(2,1)S(1)}, bf16[2,960,128]{2,1,0:T(8,128)(2,1)S(1)}, u32[]{:S(2)}, u32[]{:S(2)}) collective-permute-start(bf16[2,960,128]{2,1,0:T(8,128)(2,1)S(1)} %get-tuple-element.51), channel_id=1, source_target_pairs={{0,16},{4,20},{8,24},{12,28},{16,0},{20,4},{24,8},{28,12},{1,17},{... | collective-permute-start | bytes 1474568 | tf_op jit(solution)/shard_map/ppermute | solution.py:20
  64.6 14.1 %collective-permute-start.15 = (bf16[2,960,128]{2,1,0:T(8,128)(2,1)S(1)}, bf16[2,960,128]{2,1,0:T(8,128)(2,1)S(1)}, u32[]{:S(2)}, u32[]{:S(2)}) collective-permute-start(bf16[2,960,128]{2,1,0:T(8,128)(2,1)S(1)} %get-tuple-element.50), channel_id=1, source_target_pairs={{0,8},{4,12},{8,0},{12,4},{16,24},{20,28},{24,16},{28,20},{1,9},{5... | collective-permute-start | bytes 1474568 | tf_op jit(solution)/shard_map/ppermute | solution.py:20
  65.6 5.2 %collective-permute-start.14 = (bf16[128,128]{1,0:T(8,128)(2,1)S(1)}, bf16[128,128]{1,0:T(8,128)(2,1)S(1)}, u32[]{:S(2)}, u32[]{:S(2)}) collective-permute-start(bf16[128,128]{1,0:T(8,128)(2,1)S(1)} %get-tuple-element.58), channel_id=1, source_target_pairs={{0,3},{1,0},{2,1},{3,2},{4,7},{5,4},{6,5},{7,6},{8,11},{9,8},{10,9... | collective-permute-start | bytes 98312 | tf_op jit(solution)/shard_map/ppermute | solution.py:250
  69.2 5.7 %collective-permute-start.12 = (bf16[128,128]{1,0:T(8,128)(2,1)S(1)}, bf16[128,128]{1,0:T(8,128)(2,1)S(1)}, u32[]{:S(2)}, u32[]{:S(2)}) collective-permute-start(bf16[128,128]{1,0:T(8,128)(2,1)S(1)} %get-tuple-element.60), channel_id=1, source_target_pairs={{0,1},{1,2},{2,3},{3,0},{4,5},{5,6},{6,7},{7,4},{8,9},{9,10},{10,1... | collective-permute-start | bytes 98312 | tf_op jit(solution)/shard_map/ppermute | solution.py:250
  69.2 5.7 %collective-permute-start.13 = (bf16[128,128]{1,0:T(8,128)(2,1)S(1)}, bf16[128,128]{1,0:T(8,128)(2,1)S(1)}, u32[]{:S(2)}, u32[]{:S(2)}) collective-permute-start(bf16[128,128]{1,0:T(8,128)(2,1)S(1)} %get-tuple-element.59), channel_id=1, source_target_pairs={{0,2},{1,3},{2,0},{3,1},{4,6},{5,7},{6,4},{7,5},{8,10},{9,11},{10,... | collective-permute-start | bytes 98312 | tf_op jit(solution)/shard_map/ppermute | solution.py:250
  75.0 5.3 %collective-permute-start.17 = (bf16[4,128,128]{2,1,0:T(8,128)(2,1)S(1)}, bf16[4,128,128]{2,1,0:T(8,128)(2,1)S(1)}, u32[]{:S(2)}, u32[]{:S(2)}) collective-permute-start(bf16[4,128,128]{2,1,0:T(8,128)(2,1)S(1)} %pad_maximum_fusion), channel_id=1, source_target_pairs={{0,8},{4,12},{8,0},{12,4},{16,24},{20,28},{24,16},{28,20},{1,9},{5... | collective-permute-start | bytes 393224 | tf_op jit(solution)/shard_map/ppermute | solution.py:20
  80.3 6.4 %collective-permute-start.18 = (bf16[4,128,128]{2,1,0:T(8,128)(2,1)S(1)}, bf16[4,128,128]{2,1,0:T(8,128)(2,1)S(1)}, u32[]{:S(2)}, u32[]{:S(2)}) collective-permute-start(bf16[4,128,128]{2,1,0:T(8,128)(2,1)S(1)} %add_convert_fusion.5), channel_id=1, source_target_pairs={{0,16},{4,20},{8,24},{12,28},{16,0},{20,4},{24,8},{28,12},{1,17},{... | collective-permute-start | bytes 393224 | tf_op jit(solution)/shard_map/ppermute | solution.py:20
  80.9 8.5 %collective-permute-start.20 = (bf16[2,960,128]{2,1,0:T(8,128)(2,1)S(1)}, bf16[2,960,128]{2,1,0:T(8,128)(2,1)S(1)}, u32[]{:S(2)}, u32[]{:S(2)}) collective-permute-start(bf16[2,960,128]{2,1,0:T(8,128)(2,1)S(1)} %copy-done.23), channel_id=1, source_target_pairs={{0,4},{4,0},{8,12},{12,8},{16,20},{20,16},{24,28},{28,24},{1,5},{5... | collective-permute-start | bytes 1474568 | tf_op jit(solution)/shard_map/ppermute | solution.py:20
  80.9 9.7 %collective-permute-start.21 = (bf16[1,960,128]{2,1,0:T(8,128)(2,1)S(1)}, bf16[1,960,128]{2,1,0:T(8,128)(2,1)S(1)}, u32[]{:S(2)}, u32[]{:S(2)}) collective-permute-start(bf16[1,960,128]{2,1,0:T(8,128)(2,1)S(1)} %bitcast.35), channel_id=1, source_target_pairs={{0,16},{4,20},{8,24},{12,28},{16,0},{20,4},{24,8},{28,12},{1,17},{... | collective-permute-start | bytes 737288 | tf_op jit(solution)/shard_map/ppermute | solution.py:20
  82.4 8.2 %collective-permute-start.22 = (bf16[1,960,128]{2,1,0:T(8,128)(2,1)S(1)}, bf16[1,960,128]{2,1,0:T(8,128)(2,1)S(1)}, u32[]{:S(2)}, u32[]{:S(2)}) collective-permute-start(bf16[1,960,128]{2,1,0:T(8,128)(2,1)S(1)} %bitcast.34), channel_id=1, source_target_pairs={{0,8},{4,12},{8,0},{12,4},{16,24},{20,28},{24,16},{28,20},{1,9},{5... | collective-permute-start | bytes 737288 | tf_op jit(solution)/shard_map/ppermute | solution.py:20
  86.8 1.4 %collective-permute-start.19 = (bf16[4,128,128]{2,1,0:T(8,128)(2,1)S(1)}, bf16[4,128,128]{2,1,0:T(8,128)(2,1)S(1)}, u32[]{:S(2)}, u32[]{:S(2)}) collective-permute-start(bf16[4,128,128]{2,1,0:T(8,128)(2,1)S(1)} %add_convert_fusion.4.mine_ref), channel_id=1, source_target_pairs={{0,4},{4,0},{8,12},{12,8},{16,20},{20,16},{24,28},{28,24},{1,5},{5... | collective-permute-start | bytes 393224 | tf_op jit(solution)/shard_map/ppermute | solution.py:20
  (16 other events, 13.1 us)
Sparse Core Ops, SparseCore 0:
  8.9 46.2 all-gather.2

commit v5 on v3

--- a/solution.py
+++ b/solution.py
@@ -121,7 +121,11 @@
         compiler_params=pltpu.CompilerParams(
             dimension_semantics=("arbitrary",), vmem_limit_bytes=40 * 1024 * 1024
         ),
-        cost_estimate=pl.CostEstimate(flops=1, bytes_accessed=1, transcendentals=0),
+        cost_estimate=pl.CostEstimate(
+            flops=slots * 8 * BLOCK * BLOCK * columns,
+            bytes_accessed=slots * BLOCK * BLOCK * 2 + 8 * PAIRS * columns,
+            transcendentals=0,
+        ),
         name="ladder",
     )(me, codes, *[value for value, _, _ in pieces], ladder_blocks)
 
@@ -133,35 +137,36 @@
     return total
 
 
-def contract_kernel(core_ref, int_ref, *refs):
-    values = int_ref[...]
-    columns = values.shape[1]
+def contract_kernel(core_ref, int_ref, last_ref, *refs):
+    columns = int_ref.shape[1]
     hold_ref, give_ref = refs[-2:]
-    for step, ref in enumerate(refs[:-2]):
+    for step in range(len(refs) - 1):
+        values, ref = (int_ref, refs[step]) if step < len(refs) - 2 else (last_ref, refs[0])
         both = jnp.concatenate([ref[0], ref[1]], axis=1)
-        product = lax.dot_general(values, both, (((0,), (0,)), ((), ())), preferred_element_type=F32)
+        product = lax.dot_general(values[...], both, (((0,), (0,)), ((), ())), preferred_element_type=F32)
         real = product[:, :columns].astype(BF16)
         imag = product[:, columns:].astype(BF16)
         hold_ref[step] = jnp.where(core_ref[0] == 0, real, imag)
         give_ref[step] = jnp.where(core_ref[0] == 0, imag, real)
 
 
-def contract(core, integrals, ring):
+def contract(core, integrals, back_integrals, ring):
     rows, columns = integrals.shape
     vmem = pl.BlockSpec(memory_space=pltpu.VMEM)
+    count = len(ring) + 1
     return pl.pallas_call(
         contract_kernel,
-        in_specs=[pl.BlockSpec(memory_space=pltpu.SMEM)] + [vmem] * (1 + len(ring)),
+        in_specs=[pl.BlockSpec(memory_space=pltpu.SMEM)] + [vmem] * (2 + len(ring)),
         out_specs=[vmem] * 2,
-        out_shape=[jax.ShapeDtypeStruct((len(ring), columns, columns), BF16)] * 2,
+        out_shape=[jax.ShapeDtypeStruct((count, columns, columns), BF16)] * 2,
         compiler_params=pltpu.CompilerParams(vmem_limit_bytes=20 * 1024 * 1024),
         cost_estimate=pl.CostEstimate(
-            flops=4 * len(ring) * rows * columns * columns,
-            bytes_accessed=(4 * len(ring) + 2) * rows * columns,
+            flops=4 * count * rows * columns * columns,
+            bytes_accessed=4 * count * rows * columns,
             transcendentals=0,
         ),
         name="contract",
-    )(core, integrals, *ring)
+    )(core, integrals, back_integrals, *ring)
 
 
 def quadratic_kernel(core_ref, mine_ref, other_ref, *refs):
@@ -216,7 +221,7 @@
         in_specs=[vmem] * (1 + len(terms)),
         out_specs=vmem,
         out_shape=jax.ShapeDtypeStruct(base.shape, BF16),
-        compiler_params=pltpu.CompilerParams(vmem_limit_bytes=24 * 1024 * 1024),
+        compiler_params=pltpu.CompilerParams(vmem_limit_bytes=20 * 1024 * 1024),
         name="finish",
     )(base, *[value for value, _, _ in terms])
 
@@ -234,17 +239,17 @@
     bits = tri_size.bit_length() - 1
     me = lax.axis_index("tri").astype(jnp.int32)[None]
     core = me & 1
+    order = list(range(0, vp_size, 2)) + list(range(1, vp_size, 2))[::-1]
 
     def turn(value, distance=1):
-        return lax.ppermute(value, "vp", [(i, (i + distance) % vp_size) for i in range(vp_size)])
+        return lax.ppermute(value, "vp", [(order[i], order[(i + distance) % vp_size]) for i in range(vp_size)])
 
     ring = [amplitudes]
-    for _ in range(1, vp_size - 1):
+    for _ in range(2, vp_size):
         ring.append(turn(ring[-1]))
+    back_integrals = turn(integrals)
     pieces = gather_tri(amplitudes, tri_size)
-    *values, ring[-1] = lax.optimization_barrier((*[value for value, _, _ in pieces], ring[-1]))
-    pieces = [(value, mask, part) for value, (_, mask, part) in zip(values, pieces, strict=True)]
-    ring.append(turn(ring[-1]))
+    me = after(me, ring[1], back_integrals)
 
     if tri_size == 8:
         real_order, imag_order = (2, 6, 4), (4, 6, 2)
@@ -254,7 +259,12 @@
         groups = [[(mask, part) for mask in range(tri_size) for part in range(2)]]
     partials = ladder(me, slot_block, pieces, ladder_blocks, groups)
     *partials, ring[-1] = lax.optimization_barrier((*partials, ring[-1]))
-    hold, give = contract(core, integrals, ring)
+    hold, give = contract(core, integrals, back_integrals, ring)
+    last = turn(ring[-1])
+
+    def shift(value):
+        moved = [turn(value[step], vp_size - step) for step in range(1, vp_size - 1)]
+        return jnp.stack([value[0], *moved, value[vp_size - 1]])
 
     if tri_size == 8:
         real, imag, own = partials[3:]
@@ -264,23 +274,22 @@
         by_y = add(imag[:2], imag_in[:2]).astype(BF16)
         by_x, by_y, hold, give = lax.optimization_barrier((by_x, by_y, hold, give))
         by_x, by_y = swap(by_x, tri_size, 1), swap(by_y, tri_size, 2)
-        mine = add(hold, swap(give, tri_size, 0)).astype(BF16)
-        mine = add(mine, swap(mine, tri_size, 1)).astype(BF16)
-        received = swap(mine, tri_size, 2)
+        mine = shift(add(hold, swap(give, tri_size, 0)).astype(BF16))
+        received = swap(mine, tri_size, 1)
         then_y = add(real[2], real_in[2], by_x[1]).astype(BF16)
         then_x = add(imag[2], imag_in[2], by_y[1]).astype(BF16)
-        then_y, then_x, received = lax.optimization_barrier((then_y, then_x, received))
+        then_y, then_x, received, last = lax.optimization_barrier((then_y, then_x, received, last))
         then_y, then_x = swap(then_y[None], tri_size, 2), swap(then_x[None], tri_size, 1)
         mine = add(mine, received).astype(BF16)
+        mine = add(mine, swap(mine, tri_size, 2)).astype(BF16)
         terms = [(own, 0, 0), (own, 1, 1), (own_in, 0, 0), (own_in, 1, 1)]
         terms += [(by_x, 0, 0), (by_y, 1, 0), (then_y, 0, 0), (then_x, 1, 0)]
     else:
         terms = scatter_plain(partials[0].reshape(tri_size, 2, *amplitudes.shape[1:]), tri_size)
-        mine = add(hold, swap(give, tri_size, 0)).astype(BF16)
+        mine = shift(add(hold, swap(give, tri_size, 0)).astype(BF16))
         for bit in range(1, bits):
             mine = add(mine, swap(mine, tri_size, bit)).astype(BF16)
-    mine = jnp.stack([mine[0]] + [turn(mine[step], vp_size - step) for step in range(1, vp_size)])
-    base = quadratic(core, ring, mine, swap(mine, tri_size, 0))
+    base = quadratic(core, [*ring, last], mine, swap(mine, tri_size, 0))
     return finish(base, terms)
 
 

time: 86.9 us -> 77.2 us (0.89)
  the two profiles are of different devices: /device:TPU:0 before, /device:TPU:8 now
where the time goes in v5:
time: 77.2 us; the launch traced here: 76.9 us
  waiting for transfers between devices  39.1 us (51%)
  starting transfers between devices  21.3 us (28%)
  Pallas kernels  14 us (18%)
  local copies, waits for them, and re-layouts  1.73 us (2%)
    ppermute x20, waiting for transfers between devices, swap(): return lax.ppermute(value, 'tri', pairs)  21.7 us
    ppermute x6, waiting for transfers between devices, turn(): lax.ppermute(value, 'vp', [(order[i], order[(i + distance) % vp_size]) fo...  17.5 us
    ppermute x20, starting transfers between devices, swap(): return lax.ppermute(value, 'tri', pairs)  13.7 us
    pallas_call x1, Pallas kernels, ladder(): pl.pallas_call(functools.partial(ladder_kernel, [(mask, part) for _, mask...  11.6 us
    ppermute x6, starting transfers between devices, turn(): lax.ppermute(value, 'vp', [(order[i], order[(i + distance) % vp_size]) fo...  7.58 us
    unnamed x6, local copies, waits for them, and re-layouts  1.69 us
  transfers between devices with their start and end apart: 26, of which 12 were waited for; matrix products, arithmetic and copies ran while one was open for 0% of the time, Pallas kernels for 17%

profile of v5, /device:TPU:8, one launch (start us, length us, event | category | flops | bytes accessed | tf_op | source)
XLA Modules:
  0.0 76.9 jit_solution(15288774746872439900)
XLA Ops:
  0.0 1.5 %collective-permute-start.2 = (bf16[2,960,128]{2,1,0:T(8,128)(2,1)}, bf16[2,960,128]{2,1,0:T(8,128)(2,1)S(1)}, u32[]{:S(2)}, u32[]{:S(2)}) collective-permute-start(bf16[2,960,128]{2,1,0:T(8,128)(2,1)} %refs_0_.5), channel_id=1, source_target_pairs={{0,8},{4,12},{8,0},{12,4},{16,24},{20,28},{24,16},{28,20},{1,9},{5... | collective-permute-start | bytes 1474568 | tf_op jit(solution)/shard_map/ppermute | solution.py:20
  1.5 1.5 %collective-permute-start.3 = (bf16[2,960,128]{2,1,0:T(8,128)(2,1)}, bf16[2,960,128]{2,1,0:T(8,128)(2,1)S(1)}, u32[]{:S(2)}, u32[]{:S(2)}) collective-permute-start(bf16[2,960,128]{2,1,0:T(8,128)(2,1)} %refs_0_.5), channel_id=1, source_target_pairs={{0,16},{4,20},{8,24},{12,28},{16,0},{20,4},{24,8},{28,12},{1,17},{... | collective-permute-start | bytes 1474568 | tf_op jit(solution)/shard_map/ppermute | solution.py:20
  3.0 0.4 collective-permute-start
  3.5 2.6 %collective-permute-start.1 = (bf16[960,128]{1,0:T(8,128)(2,1)}, bf16[960,128]{1,0:T(8,128)(2,1)S(1)}, u32[]{:S(2)}, u32[]{:S(2)}) collective-permute-start(bf16[960,128]{1,0:T(8,128)(2,1)} %int_ref.1), channel_id=1, source_target_pairs={{0,2},{2,3},{3,1},{1,0},{4,6},{6,7},{7,5},{5,4},{8,10},{10,11},{11... | collective-permute-start | bytes 737288 | tf_op jit(solution)/shard_map/ppermute | solution.py:245
  6.1 7.1 %collective-permute-done.2.refs_1_ = bf16[2,960,128]{2,1,0:T(8,128)(2,1)S(1)} collective-permute-done((bf16[2,960,128]{2,1,0:T(8,128)(2,1)}, bf16[2,960,128]{2,1,0:T(8,128)(2,1)S(1)}, u32[]{:S(2)}, u32[]{:S(2)}) %collective-permute-start.2) | collective-permute-done | bytes 491552 | tf_op jit(solution)/shard_map/ppermute | solution.py:20
  13.2 1.6 %collective-permute-start.5 = (bf16[960,128]{1,0:T(8,128)(2,1)S(1)}, bf16[960,128]{1,0:T(8,128)(2,1)}, u32[]{:S(2)}, u32[]{:S(2)}) collective-permute-start(bf16[960,128]{1,0:T(8,128)(2,1)S(1)} %slice_bitcast_fusion), channel_id=1, source_target_pairs={{0,16},{4,20},{8,24},{12,28},{16,0},{20,4},{24,8},{28,12},{1,17},{... | collective-permute-start | bytes 737288 | tf_op jit(solution)/shard_map/ppermute | solution.py:20
  14.8 1.6 %collective-permute-start.4 = (bf16[960,128]{1,0:T(8,128)(2,1)S(1)}, bf16[960,128]{1,0:T(8,128)(2,1)}, u32[]{:S(2)}, u32[]{:S(2)}) collective-permute-start(bf16[960,128]{1,0:T(8,128)(2,1)S(1)} %slice_bitcast_fusion.1), channel_id=1, source_target_pairs={{0,8},{4,12},{8,0},{12,4},{16,24},{20,28},{24,16},{28,20},{1,9},{5... | collective-permute-start | bytes 737288 | tf_op jit(solution)/shard_map/ppermute | solution.py:20
  16.4 5.4 %collective-permute-done.1.last_ref = bf16[960,128]{1,0:T(8,128)(2,1)S(1)} collective-permute-done((bf16[960,128]{1,0:T(8,128)(2,1)}, bf16[960,128]{1,0:T(8,128)(2,1)S(1)}, u32[]{:S(2)}, u32[]{:S(2)}) %collective-permute-start.1) | collective-permute-done | bytes 245792 | tf_op jit(solution)/shard_map/ppermute | solution.py:245
  21.8 0.5 collective-permute-start.8
  22.4 0.4 collective-permute-start.9
  22.8 2.2 %collective-permute-done.10.refs_9_ = bf16[960,128]{1,0:T(8,128)(2,1)} collective-permute-done((bf16[960,128]{1,0:T(8,128)(2,1)}, bf16[960,128]{1,0:T(8,128)(2,1)}, u32[]{:S(2)}, u32[]{:S(2)}) %collective-permute-start.10) | collective-permute-done | bytes 245792 | tf_op jit(solution)/shard_map/ppermute | solution.py:20
  25.4 1.0 %copy-done = bf16[2,960,128]{2,1,0:T(8,128)(2,1)S(1)} copy-done((bf16[2,960,128]{2,1,0:T(8,128)(2,1)S(1)}, bf16[2,960,128]{2,1,0:T(8,128)(2,1)}, u32[]{:S(2)}) %copy-start) | copy-done | bytes 491544
  26.5 0.7 copy-done.2
  27.1 11.6 %ladder.1 = (bf16[3,960,128]{2,1,0:T(8,128)(2,1)S(1)}, bf16[3,960,128]{2,1,0:T(8,128)(2,1)S(1)}, bf16[2,960,128]{2,1,0:T(8,128)(2,1)S(1)}, bf16[3,960,128]{2,1,0...) custom-call(s32[1]{0:T(128)} %bitcast.me_ref, s32[7]{0:T(128)S(1)} %copy-done.2, ...), custom_call_target="tpu_custom_call" | custom-call | flops 4227858432 | bytes 16121856 | tf_op jit(solution)/shard_map/ladder/pallas_call | solution.py:106
  39.3 0.6 contract.1
  39.9 1.1 %collective-permute-done.12 = bf16[3,960,128]{2,1,0:T(8,128)(2,1)S(1)} collective-permute-done((bf16[3,960,128]{2,1,0:T(8,128)(2,1)S(1)}, bf16[3,960,128]{2,1,0:T(8,128)(2,1)S(1)}, u32[]{:S(2)}, u32[]{:S(2)}) %collective-permute-start.12) | collective-permute-done | bytes 737312 | tf_op jit(solution)/shard_map/ppermute | solution.py:20
  41.0 1.1 %collective-permute-done.13 = bf16[3,960,128]{2,1,0:T(8,128)(2,1)S(1)} collective-permute-done((bf16[3,960,128]{2,1,0:T(8,128)(2,1)S(1)}, bf16[3,960,128]{2,1,0:T(8,128)(2,1)S(1)}, u32[]{:S(2)}, u32[]{:S(2)}) %collective-permute-start.13) | collective-permute-done | bytes 737312 | tf_op jit(solution)/shard_map/ppermute | solution.py:20
  42.6 0.5 collective-permute-start.18
  43.1 0.5 collective-permute-start.17
  43.8 1.7 %collective-permute-start.15 = (bf16[128,128]{1,0:T(8,128)(2,1)S(1)}, bf16[128,128]{1,0:T(8,128)(2,1)S(1)}, u32[]{:S(2)}, u32[]{:S(2)}) collective-permute-start(bf16[128,128]{1,0:T(8,128)(2,1)S(1)} %get-tuple-element.64), channel_id=1, source_target_pairs={{0,1},{2,0},{3,2},{1,3},{4,5},{6,4},{7,6},{5,7},{8,9},{10,8},{11,1... | collective-permute-start | bytes 98312 | tf_op jit(solution)/shard_map/ppermute | solution.py:245
  45.8 2.6 %collective-permute-start.20 = (bf16[2,960,128]{2,1,0:T(8,128)(2,1)S(1)}, bf16[2,960,128]{2,1,0:T(8,128)(2,1)S(1)}, u32[]{:S(2)}, u32[]{:S(2)}) collective-permute-start(bf16[2,960,128]{2,1,0:T(8,128)(2,1)S(1)} %collective-permute-done.11.refs_2_), channel_id=1, source_target_pairs={{0,2},{2,3},{3,1},{1,0},{4,6},{6,7},{7,5},{5,4},{8,10},{10,11},{11... | collective-permute-start | bytes 1474568 | tf_op jit(solution)/shard_map/ppermute | solution.py:245
  48.4 12.0 %collective-permute-done.16 = bf16[128,128]{1,0:T(8,128)(2,1)S(1)} collective-permute-done((bf16[128,128]{1,0:T(8,128)(2,1)S(1)}, bf16[128,128]{1,0:T(8,128)(2,1)S(1)}, u32[]{:S(2)}, u32[]{:S(2)}) %collective-permute-start.16) | collective-permute-done | bytes 32800 | tf_op jit(solution)/shard_map/ppermute | solution.py:245
  60.4 1.3 %collective-permute-start.19 = (bf16[4,128,128]{2,1,0:T(8,128)(2,1)S(1)}, bf16[4,128,128]{2,1,0:T(8,128)(2,1)S(1)}, u32[]{:S(2)}, u32[]{:S(2)}) collective-permute-start(bf16[4,128,128]{2,1,0:T(8,128)(2,1)S(1)} %pad_maximum_fusion), channel_id=1, source_target_pairs={{0,8},{4,12},{8,0},{12,4},{16,24},{20,28},{24,16},{28,20},{1,9},{5... | collective-permute-start | bytes 393224 | tf_op jit(solution)/shard_map/ppermute | solution.py:20
  61.9 3.5 %collective-permute-done.19 = bf16[4,128,128]{2,1,0:T(8,128)(2,1)S(1)} collective-permute-done((bf16[4,128,128]{2,1,0:T(8,128)(2,1)S(1)}, bf16[4,128,128]{2,1,0:T(8,128)(2,1)S(1)}, u32[]{:S(2)}, u32[]{:S(2)}) %collective-permute-start.19) | collective-permute-done | bytes 131104 | tf_op jit(solution)/shard_map/ppermute | solution.py:20
  65.5 1.3 %collective-permute-start.21 = (bf16[4,128,128]{2,1,0:T(8,128)(2,1)S(1)}, bf16[4,128,128]{2,1,0:T(8,128)(2,1)S(1)}, u32[]{:S(2)}, u32[]{:S(2)}) collective-permute-start(bf16[4,128,128]{2,1,0:T(8,128)(2,1)S(1)} %add_convert_fusion.5), channel_id=1, source_target_pairs={{0,16},{4,20},{8,24},{12,28},{16,0},{20,4},{24,8},{28,12},{1,17},{... | collective-permute-start | bytes 393224 | tf_op jit(solution)/shard_map/ppermute | solution.py:20
  66.8 0.7 collective-permute-start.24
  67.6 1.2 %collective-permute-start.25 = (bf16[1,960,128]{2,1,0:T(8,128)(2,1)S(1)}, bf16[1,960,128]{2,1,0:T(8,128)(2,1)S(1)}, u32[]{:S(2)}, u32[]{:S(2)}) collective-permute-start(bf16[1,960,128]{2,1,0:T(8,128)(2,1)S(1)} %bitcast.23), channel_id=1, source_target_pairs={{0,8},{4,12},{8,0},{12,4},{16,24},{20,28},{24,16},{28,20},{1,9},{5... | collective-permute-start | bytes 737288 | tf_op jit(solution)/shard_map/ppermute | solution.py:20
  68.8 2.3 %collective-permute-done.21 = bf16[4,128,128]{2,1,0:T(8,128)(2,1)S(1)} collective-permute-done((bf16[4,128,128]{2,1,0:T(8,128)(2,1)S(1)}, bf16[4,128,128]{2,1,0:T(8,128)(2,1)S(1)}, u32[]{:S(2)}, u32[]{:S(2)}) %collective-permute-start.21) | collective-permute-done | bytes 131104 | tf_op jit(solution)/shard_map/ppermute | solution.py:20
  71.3 1.3 %collective-permute-done.22.other_ref = bf16[4,128,128]{2,1,0:T(8,128)(2,1)S(1)} collective-permute-done((bf16[4,128,128]{2,1,0:T(8,128)(2,1)S(1)}, bf16[4,128,128]{2,1,0:T(8,128)(2,1)S(1)}, u32[]{:S(2)}, u32[]{:S(2)}) %collective-permute-start.22) | collective-permute-done | bytes 131104 | tf_op jit(solution)/shard_map/ppermute | solution.py:20
  72.6 0.7 quadratic.1.base_ref
  73.3 2.5 %collective-permute-done.24.refs_6_ = bf16[1,960,128]{2,1,0:T(8,128)(2,1)S(1)} collective-permute-done((bf16[1,960,128]{2,1,0:T(8,128)(2,1)S(1)}, bf16[1,960,128]{2,1,0:T(8,128)(2,1)S(1)}, u32[]{:S(2)}, u32[]{:S(2)}) %collective-permute-start.24) | collective-permute-done | bytes 245792 | tf_op jit(solution)/shard_map/ppermute | solution.py:20
  75.8 1.1 %finish.1 = bf16[2,960,128]{2,1,0:T(8,128)(2,1)} custom-call(f32[2,960,128]{2,1,0:T(8,128)S(1)} %quadratic.1.base_ref, bf16[2,960,128]{2,1,0:T(8,128)(2,1)S(1)} %get-tuple-element.57.refs_0_.refs_1_, bf16[2,960,128]{2,1,0:T(8,128)(2,1)S(1)} %get-tuple-element.57.refs_0_.refs_1_, bf16[2,960,128]{2,1,0:T(8,128)(2,1)S(1)} %collective-permute-done.23.refs_2_.refs_3_, ...), custom_call_target="tpu_custom_call" | custom-call | tf_op jit(solution)/shard_map/finish/pallas_call | solution.py:219
  (40 shorter events, 2.4 us)
Async XLA Ops:
  0.0 39.3 %copy-start.1 = (bf16[960,128]{1,0:T(8,128)(2,1)S(1)}, bf16[960,128]{1,0:T(8,128)(2,1)}, u32[]{:S(2)}) copy-start(bf16[960,128]{1,0:T(8,128)(2,1)} %int_ref.1) | copy-start | bytes 737284
  0.0 13.2 %collective-permute-start.2 = (bf16[2,960,128]{2,1,0:T(8,128)(2,1)}, bf16[2,960,128]{2,1,0:T(8,128)(2,1)S(1)}, u32[]{:S(2)}, u32[]{:S(2)}) collective-permute-start(bf16[2,960,128]{2,1,0:T(8,128)(2,1)} %refs_0_.5), channel_id=1, source_target_pairs={{0,8},{4,12},{8,0},{12,4},{16,24},{20,28},{24,16},{28,20},{1,9},{5... | collective-permute-start | bytes 1474568 | tf_op jit(solution)/shard_map/ppermute | solution.py:20
  1.5 13.3 %collective-permute-start.3 = (bf16[2,960,128]{2,1,0:T(8,128)(2,1)}, bf16[2,960,128]{2,1,0:T(8,128)(2,1)S(1)}, u32[]{:S(2)}, u32[]{:S(2)}) collective-permute-start(bf16[2,960,128]{2,1,0:T(8,128)(2,1)} %refs_0_.5), channel_id=1, source_target_pairs={{0,16},{4,20},{8,24},{12,28},{16,0},{20,4},{24,8},{28,12},{1,17},{... | collective-permute-start | bytes 1474568 | tf_op jit(solution)/shard_map/ppermute | solution.py:20
  3.0 18.8 %collective-permute-start = (bf16[2,960,128]{2,1,0:T(8,128)(2,1)}, bf16[2,960,128]{2,1,0:T(8,128)(2,1)S(1)}, u32[]{:S(2)}, u32[]{:S(2)}) collective-permute-start(bf16[2,960,128]{2,1,0:T(8,128)(2,1)} %refs_0_.5), channel_id=1, source_target_pairs={{0,2},{2,3},{3,1},{1,0},{4,6},{6,7},{7,5},{5,4},{8,10},{10,11},{11... | collective-permute-start | bytes 1474568 | tf_op jit(solution)/shard_map/ppermute | solution.py:245
  3.5 19.4 %collective-permute-start.6 = (bf16[2,960,128]{2,1,0:T(8,128)(2,1)}, bf16[2,960,128]{2,1,0:T(8,128)(2,1)S(1)}, u32[]{:S(2)}, u32[]{:S(2)}) collective-permute-start(bf16[2,960,128]{2,1,0:T(8,128)(2,1)} %refs_0_.5), channel_id=1, source_target_pairs={{0,4},{4,0},{8,12},{12,8},{16,20},{20,16},{24,28},{28,24},{1,5},{5... | collective-permute-start | bytes 1474568 | tf_op jit(solution)/shard_map/ppermute | solution.py:20
  3.5 18.3 %collective-permute-start.1 = (bf16[960,128]{1,0:T(8,128)(2,1)}, bf16[960,128]{1,0:T(8,128)(2,1)S(1)}, u32[]{:S(2)}, u32[]{:S(2)}) collective-permute-start(bf16[960,128]{1,0:T(8,128)(2,1)} %int_ref.1), channel_id=1, source_target_pairs={{0,2},{2,3},{3,1},{1,0},{4,6},{6,7},{7,5},{5,4},{8,10},{10,11},{11... | collective-permute-start | bytes 737288 | tf_op jit(solution)/shard_map/ppermute | solution.py:245
  13.2 9.1 %collective-permute-start.5 = (bf16[960,128]{1,0:T(8,128)(2,1)S(1)}, bf16[960,128]{1,0:T(8,128)(2,1)}, u32[]{:S(2)}, u32[]{:S(2)}) collective-permute-start(bf16[960,128]{1,0:T(8,128)(2,1)S(1)} %slice_bitcast_fusion), channel_id=1, source_target_pairs={{0,16},{4,20},{8,24},{12,28},{16,0},{20,4},{24,8},{28,12},{1,17},{... | collective-permute-start | bytes 737288 | tf_op jit(solution)/shard_map/ppermute | solution.py:20
  14.8 7.6 %collective-permute-start.4 = (bf16[960,128]{1,0:T(8,128)(2,1)S(1)}, bf16[960,128]{1,0:T(8,128)(2,1)}, u32[]{:S(2)}, u32[]{:S(2)}) collective-permute-start(bf16[960,128]{1,0:T(8,128)(2,1)S(1)} %slice_bitcast_fusion.1), channel_id=1, source_target_pairs={{0,8},{4,12},{8,0},{12,4},{16,24},{20,28},{24,16},{28,20},{1,9},{5... | collective-permute-start | bytes 737288 | tf_op jit(solution)/shard_map/ppermute | solution.py:20
  21.8 3.6 %collective-permute-start.7 = (bf16[2,960,128]{2,1,0:T(8,128)(2,1)S(1)}, bf16[2,960,128]{2,1,0:T(8,128)(2,1)S(1)}, u32[]{:S(2)}, u32[]{:S(2)}) collective-permute-start(bf16[2,960,128]{2,1,0:T(8,128)(2,1)S(1)} %collective-permute-done.2.refs_1_), channel_id=1, source_target_pairs={{0,4},{4,0},{8,12},{12,8},{16,20},{20,16},{24,28},{28,24},{1,5},{5... | collective-permute-start | bytes 1474568 | tf_op jit(solution)/shard_map/ppermute | solution.py:20
  21.8 3.6 %collective-permute-start.8 = (bf16[2,960,128]{2,1,0:T(8,128)(2,1)S(1)}, bf16[2,960,128]{2,1,0:T(8,128)(2,1)}, u32[]{:S(2)}, u32[]{:S(2)}) collective-permute-start(bf16[2,960,128]{2,1,0:T(8,128)(2,1)S(1)} %collective-permute-done.3.refs_2_), channel_id=1, source_target_pairs={{0,4},{4,0},{8,12},{12,8},{16,20},{20,16},{24,28},{28,24},{1,5},{5... | collective-permute-start | bytes 1474568 | tf_op jit(solution)/shard_map/ppermute | solution.py:20
  22.3 2.7 %collective-permute-start.10 = (bf16[960,128]{1,0:T(8,128)(2,1)}, bf16[960,128]{1,0:T(8,128)(2,1)}, u32[]{:S(2)}, u32[]{:S(2)}) collective-permute-start(bf16[960,128]{1,0:T(8,128)(2,1)} %collective-permute-done.5.refs_4_), channel_id=1, source_target_pairs={{0,4},{4,0},{8,12},{12,8},{16,20},{20,16},{24,28},{28,24},{1,5},{5... | collective-permute-start | bytes 737288 | tf_op jit(solution)/shard_map/ppermute | solution.py:20
  22.4 3.0 %collective-permute-start.9 = (bf16[960,128]{1,0:T(8,128)(2,1)}, bf16[960,128]{1,0:T(8,128)(2,1)}, u32[]{:S(2)}, u32[]{:S(2)}) collective-permute-start(bf16[960,128]{1,0:T(8,128)(2,1)} %collective-permute-done.4.refs_3_), channel_id=1, source_target_pairs={{0,4},{4,0},{8,12},{12,8},{16,20},{20,16},{24,28},{28,24},{1,5},{5... | collective-permute-start | bytes 737288 | tf_op jit(solution)/shard_map/ppermute | solution.py:20
  22.8 15.9 %collective-permute-start.11 = (bf16[2,960,128]{2,1,0:T(8,128)(2,1)S(1)}, bf16[2,960,128]{2,1,0:T(8,128)(2,1)S(1)}, u32[]{:S(2)}, u32[]{:S(2)}) collective-permute-start(bf16[2,960,128]{2,1,0:T(8,128)(2,1)S(1)} %collective-permute-done.refs_1_), channel_id=1, source_target_pairs={{0,2},{2,3},{3,1},{1,0},{4,6},{6,7},{7,5},{5,4},{8,10},{10,11},{11... | collective-permute-start | bytes 1474568 | tf_op jit(solution)/shard_map/ppermute | solution.py:245
  25.4 1.0 %copy-start = (bf16[2,960,128]{2,1,0:T(8,128)(2,1)S(1)}, bf16[2,960,128]{2,1,0:T(8,128)(2,1)}, u32[]{:S(2)}) copy-start(bf16[2,960,128]{2,1,0:T(8,128)(2,1)} %refs_0_.5) | copy-start | bytes 1474564
  26.5 0.7 copy-start.2
  38.7 2.3 %collective-permute-start.12 = (bf16[3,960,128]{2,1,0:T(8,128)(2,1)S(1)}, bf16[3,960,128]{2,1,0:T(8,128)(2,1)S(1)}, u32[]{:S(2)}, u32[]{:S(2)}) collective-permute-start(bf16[3,960,128]{2,1,0:T(8,128)(2,1)S(1)} %get-tuple-element.41), channel_id=1, source_target_pairs={{0,4},{4,0},{8,12},{12,8},{16,20},{20,16},{24,28},{28,24},{1,5},{5... | collective-permute-start | bytes 2211848 | tf_op jit(solution)/shard_map/ppermute | solution.py:20
  39.0 3.1 %collective-permute-start.13 = (bf16[3,960,128]{2,1,0:T(8,128)(2,1)S(1)}, bf16[3,960,128]{2,1,0:T(8,128)(2,1)S(1)}, u32[]{:S(2)}, u32[]{:S(2)}) collective-permute-start(bf16[3,960,128]{2,1,0:T(8,128)(2,1)S(1)} %get-tuple-element.42), channel_id=1, source_target_pairs={{0,4},{4,0},{8,12},{12,8},{16,20},{20,16},{24,28},{28,24},{1,5},{5... | collective-permute-start | bytes 2211848 | tf_op jit(solution)/shard_map/ppermute | solution.py:20
  42.4 1.4 %collective-permute-start.14 = (bf16[4,128,128]{2,1,0:T(8,128)(2,1)S(1)}, bf16[4,128,128]{2,1,0:T(8,128)(2,1)S(1)}, u32[]{:S(2)}, u32[]{:S(2)}) collective-permute-start(bf16[4,128,128]{2,1,0:T(8,128)(2,1)S(1)} %get-tuple-element.52), channel_id=1, source_target_pairs={{0,4},{4,0},{8,12},{12,8},{16,20},{20,16},{24,28},{28,24},{1,5},{5... | collective-permute-start | bytes 393224 | tf_op jit(solution)/shard_map/ppermute | solution.py:20
  42.6 19.1 %collective-permute-start.18 = (bf16[2,960,128]{2,1,0:T(8,128)(2,1)S(1)}, bf16[2,960,128]{2,1,0:T(8,128)(2,1)S(1)}, u32[]{:S(2)}, u32[]{:S(2)}) collective-permute-start(bf16[2,960,128]{2,1,0:T(8,128)(2,1)S(1)} %get-tuple-element.54), channel_id=1, source_target_pairs={{0,16},{4,20},{8,24},{12,28},{16,0},{20,4},{24,8},{28,12},{1,17},{... | collective-permute-start | bytes 1474568 | tf_op jit(solution)/shard_map/ppermute | solution.py:20
  43.1 18.7 %collective-permute-start.17 = (bf16[2,960,128]{2,1,0:T(8,128)(2,1)S(1)}, bf16[2,960,128]{2,1,0:T(8,128)(2,1)S(1)}, u32[]{:S(2)}, u32[]{:S(2)}) collective-permute-start(bf16[2,960,128]{2,1,0:T(8,128)(2,1)S(1)} %get-tuple-element.53), channel_id=1, source_target_pairs={{0,8},{4,12},{8,0},{12,4},{16,24},{20,28},{24,16},{28,20},{1,9},{5... | collective-permute-start | bytes 1474568 | tf_op jit(solution)/shard_map/ppermute | solution.py:20
  43.8 4.5 %collective-permute-start.15 = (bf16[128,128]{1,0:T(8,128)(2,1)S(1)}, bf16[128,128]{1,0:T(8,128)(2,1)S(1)}, u32[]{:S(2)}, u32[]{:S(2)}) collective-permute-start(bf16[128,128]{1,0:T(8,128)(2,1)S(1)} %get-tuple-element.64), channel_id=1, source_target_pairs={{0,1},{2,0},{3,2},{1,3},{4,5},{6,4},{7,6},{5,7},{8,9},{10,8},{11,1... | collective-permute-start | bytes 98312 | tf_op jit(solution)/shard_map/ppermute | solution.py:245
  45.6 14.8 %collective-permute-start.16 = (bf16[128,128]{1,0:T(8,128)(2,1)S(1)}, bf16[128,128]{1,0:T(8,128)(2,1)S(1)}, u32[]{:S(2)}, u32[]{:S(2)}) collective-permute-start(bf16[128,128]{1,0:T(8,128)(2,1)S(1)} %get-tuple-element.63), channel_id=1, source_target_pairs={{0,3},{2,1},{3,0},{1,2},{4,7},{6,5},{7,4},{5,6},{8,11},{10,9},{11,... | collective-permute-start | bytes 98312 | tf_op jit(solution)/shard_map/ppermute | solution.py:245
  45.8 16.1 %collective-permute-start.20 = (bf16[2,960,128]{2,1,0:T(8,128)(2,1)S(1)}, bf16[2,960,128]{2,1,0:T(8,128)(2,1)S(1)}, u32[]{:S(2)}, u32[]{:S(2)}) collective-permute-start(bf16[2,960,128]{2,1,0:T(8,128)(2,1)S(1)} %collective-permute-done.11.refs_2_), channel_id=1, source_target_pairs={{0,2},{2,3},{3,1},{1,0},{4,6},{6,7},{7,5},{5,4},{8,10},{10,11},{11... | collective-permute-start | bytes 1474568 | tf_op jit(solution)/shard_map/ppermute | solution.py:245
  60.4 5.0 %collective-permute-start.19 = (bf16[4,128,128]{2,1,0:T(8,128)(2,1)S(1)}, bf16[4,128,128]{2,1,0:T(8,128)(2,1)S(1)}, u32[]{:S(2)}, u32[]{:S(2)}) collective-permute-start(bf16[4,128,128]{2,1,0:T(8,128)(2,1)S(1)} %pad_maximum_fusion), channel_id=1, source_target_pairs={{0,8},{4,12},{8,0},{12,4},{16,24},{20,28},{24,16},{28,20},{1,9},{5... | collective-permute-start | bytes 393224 | tf_op jit(solution)/shard_map/ppermute | solution.py:20
  65.5 5.6 %collective-permute-start.21 = (bf16[4,128,128]{2,1,0:T(8,128)(2,1)S(1)}, bf16[4,128,128]{2,1,0:T(8,128)(2,1)S(1)}, u32[]{:S(2)}, u32[]{:S(2)}) collective-permute-start(bf16[4,128,128]{2,1,0:T(8,128)(2,1)S(1)} %add_convert_fusion.5), channel_id=1, source_target_pairs={{0,16},{4,20},{8,24},{12,28},{16,0},{20,4},{24,8},{28,12},{1,17},{... | collective-permute-start | bytes 393224 | tf_op jit(solution)/shard_map/ppermute | solution.py:20
  66.8 6.5 %collective-permute-start.23 = (bf16[2,960,128]{2,1,0:T(8,128)(2,1)S(1)}, bf16[2,960,128]{2,1,0:T(8,128)(2,1)S(1)}, u32[]{:S(2)}, u32[]{:S(2)}) collective-permute-start(bf16[2,960,128]{2,1,0:T(8,128)(2,1)S(1)} %get-tuple-element.58), channel_id=1, source_target_pairs={{0,4},{4,0},{8,12},{12,8},{16,20},{20,16},{24,28},{28,24},{1,5},{5... | collective-permute-start | bytes 1474568 | tf_op jit(solution)/shard_map/ppermute | solution.py:20
  66.8 9.0 %collective-permute-start.24 = (bf16[1,960,128]{2,1,0:T(8,128)(2,1)S(1)}, bf16[1,960,128]{2,1,0:T(8,128)(2,1)S(1)}, u32[]{:S(2)}, u32[]{:S(2)}) collective-permute-start(bf16[1,960,128]{2,1,0:T(8,128)(2,1)S(1)} %bitcast.24), channel_id=1, source_target_pairs={{0,16},{4,20},{8,24},{12,28},{16,0},{20,4},{24,8},{28,12},{1,17},{... | collective-permute-start | bytes 737288 | tf_op jit(solution)/shard_map/ppermute | solution.py:20
  67.6 8.2 %collective-permute-start.25 = (bf16[1,960,128]{2,1,0:T(8,128)(2,1)S(1)}, bf16[1,960,128]{2,1,0:T(8,128)(2,1)S(1)}, u32[]{:S(2)}, u32[]{:S(2)}) collective-permute-start(bf16[1,960,128]{2,1,0:T(8,128)(2,1)S(1)} %bitcast.23), channel_id=1, source_target_pairs={{0,8},{4,12},{8,0},{12,4},{16,24},{20,28},{24,16},{28,20},{1,9},{5... | collective-permute-start | bytes 737288 | tf_op jit(solution)/shard_map/ppermute | solution.py:20
  71.2 1.4 %collective-permute-start.22 = (bf16[4,128,128]{2,1,0:T(8,128)(2,1)S(1)}, bf16[4,128,128]{2,1,0:T(8,128)(2,1)S(1)}, u32[]{:S(2)}, u32[]{:S(2)}) collective-permute-start(bf16[4,128,128]{2,1,0:T(8,128)(2,1)S(1)} %add_convert_fusion.4.mine_ref), channel_id=1, source_target_pairs={{0,4},{4,0},{8,12},{12,8},{16,20},{20,16},{24,28},{28,24},{1,5},{5... | collective-permute-start | bytes 393224 | tf_op jit(solution)/shard_map/ppermute | solution.py:20

commit v6 on v5

--- a/solution.py
+++ b/solution.py
@@ -24,32 +24,80 @@
     return lax.optimization_barrier((value, *earlier))[0]
 
 
-def gather_tri(amplitudes, axis_size):
+def gather_tri(amplitudes, codes, ladder_blocks, axis_size):
     if axis_size != 8:
-        found = {0: amplitudes}
+        turned, own, table = prepare(codes, ladder_blocks, amplitudes)
+        found = {0: own}
         for bit in range(axis_size.bit_length() - 1):
             for mask in list(found):
                 found[mask | (1 << bit)] = swap(found[mask], axis_size, bit)
-        return [(value, mask, None) for mask, value in found.items()]
+        return turned, own, table, [(value, mask, None) for mask, value in found.items()]
     by_x = swap(amplitudes, axis_size, 1)
     by_y = swap(amplitudes, axis_size, 2)
     own_core = swap(amplitudes, axis_size, 0)
+    turned, own, table = prepare(codes, ladder_blocks, amplitudes)
+    by_x, by_y, table = lax.optimization_barrier((by_x, by_y, table))
     far_real = swap(by_y[0], axis_size, 1)
     far_imag = swap(by_x[1], axis_size, 2)
     found = [
-        (amplitudes, 0, None), (by_x, 2, None), (by_y, 4, None), (far_real, 6, 0), (far_imag, 6, 1),
+        (own, 0, None), (by_x, 2, None), (by_y, 4, None), (far_real, 6, 0), (far_imag, 6, 1),
         (own_core, 1, None),
     ]
     for value, mask, part in found[1:5]:
         found.append((swap(value, axis_size, 0), mask | 1, part))
-    return found
-
-
-def ladder_kernel(labels, groups, me_ref, code_ref, *refs):
+    return turned, own, table, found
+
+
+def prepare_kernel(code_ref, ladder_ref, amp_ref, turned_ref, own_ref, table_ref):
+    step = pl.program_id(0)
+    turned_ref[0] = ladder_ref[0].T
+
+    @pl.when(step == 0)
+    def _():
+        own_ref[...] = amp_ref[...]
+
+    code = code_ref[step]
+    row_block = jnp.int32(0)
+    start = jnp.int32(0)
+    for row in range(1, NB):
+        first = row * NB - row * (row - 1) // 2
+        past = code >= first
+        row_block = jnp.where(past, row, row_block)
+        start = jnp.where(past, first, start)
+    column_block = jnp.minimum(row_block + code - start, NB - 1)
+    table_ref[0, step] = row_block
+    table_ref[1, step] = column_block
+    table_ref[2, step] = jnp.where(code < TRI_BLOCKS, jnp.where(row_block == column_block, 1, 2), 0)
+
+
+def prepare(codes, ladder_blocks, amplitudes):
+    slots = ladder_blocks.shape[0]
+    block = pl.BlockSpec((1, BLOCK, BLOCK), lambda s: (s, 0, 0))
+    whole = pl.BlockSpec(amplitudes.shape, lambda s: (0, 0, 0))
+    smem = pl.BlockSpec(memory_space=pltpu.SMEM)
+    return pl.pallas_call(
+        prepare_kernel,
+        grid=(slots,),
+        in_specs=[smem, block, whole],
+        out_specs=[block, whole, smem],
+        out_shape=[
+            jax.ShapeDtypeStruct(ladder_blocks.shape, BF16),
+            jax.ShapeDtypeStruct(amplitudes.shape, BF16),
+            jax.ShapeDtypeStruct((3, slots), jnp.int32),
+        ],
+        compiler_params=pltpu.CompilerParams(
+            dimension_semantics=("arbitrary",), vmem_limit_bytes=52 * 1024 * 1024
+        ),
+        cost_estimate=pl.CostEstimate(flops=0, bytes_accessed=4 * ladder_blocks.size, transcendentals=0),
+        name="prepare",
+    )(codes, ladder_blocks, amplitudes)
+
+
+def ladder_kernel(labels, groups, me_ref, table_ref, *refs):
     count = len(labels)
     piece_refs = refs[:count]
-    ladder_ref = refs[count]
-    out_refs = refs[count + 1:-3]
+    ladder_ref, turned_ref = refs[count:count + 2]
+    out_refs = refs[count + 2:-3]
     amp, acc, sems = refs[-3:]
     columns = amp.shape[1] // 2
     rows = out_refs[0].shape[-2]
@@ -73,23 +121,11 @@
         for copy in copies:
             copy.wait()
 
-    code = code_ref[step]
-    row_block = jnp.int32(0)
-    start = jnp.int32(0)
-    for row in range(1, NB):
-        first = row * NB - row * (row - 1) // 2
-        past = code >= first
-        row_block = jnp.where(past, row, row_block)
-        start = jnp.where(past, first, start)
-    column_block = jnp.minimum(row_block + code - start, NB - 1)
-    weight = jnp.where(row_block == column_block, 0.5, 1.0) * jnp.where(code < TRI_BLOCKS, 1.0, 0.0)
-    at_row = pl.ds(pl.multiple_of(row_block * BLOCK, BLOCK), BLOCK)
-    at_column = pl.ds(pl.multiple_of(column_block * BLOCK, BLOCK), BLOCK)
-    block = ladder_ref[0]
-    to_row = lax.dot_general(block, amp[at_column, :], (((1,), (0,)), ((), ())), preferred_element_type=F32)
-    acc[at_row, :] += weight * to_row
-    to_column = lax.dot_general(block, amp[at_row, :], (((0,), (0,)), ((), ())), preferred_element_type=F32)
-    acc[at_column, :] += weight * to_column
+    weight = 0.5 * table_ref[2, step].astype(F32)
+    at_row = pl.ds(pl.multiple_of(table_ref[0, step] * BLOCK, BLOCK), BLOCK)
+    at_column = pl.ds(pl.multiple_of(table_ref[1, step] * BLOCK, BLOCK), BLOCK)
+    acc[at_row, :] += weight * jnp.dot(ladder_ref[0], amp[at_column, :], preferred_element_type=F32)
+    acc[at_column, :] += weight * jnp.dot(turned_ref[0], amp[at_row, :], preferred_element_type=F32)
 
     @pl.when(step == pl.num_programs(0) - 1)
     def _():
@@ -99,17 +135,17 @@
                 target[place] = acc[rows_of(mask), lanes].astype(BF16)
 
 
-def ladder(me, codes, pieces, ladder_blocks, groups):
+def ladder(me, table, pieces, ladder_blocks, turned, groups):
     slots = ladder_blocks.shape[0]
     rows, columns = pieces[0][0].shape[-2:]
     count = sum(len(places) for places in groups)
+    block = pl.BlockSpec((1, BLOCK, BLOCK), lambda s, *_: (s, 0, 0))
     return pl.pallas_call(
         functools.partial(ladder_kernel, [(mask, part) for _, mask, part in pieces], groups),
         grid_spec=pltpu.PrefetchScalarGridSpec(
             num_scalar_prefetch=2,
             grid=(slots,),
-            in_specs=[pl.BlockSpec(memory_space=pl.ANY)] * len(pieces)
-            + [pl.BlockSpec((1, BLOCK, BLOCK), lambda s, *_: (s, 0, 0))],
+            in_specs=[pl.BlockSpec(memory_space=pl.ANY)] * len(pieces) + [block, block],
             out_specs=[pl.BlockSpec((len(places), rows, columns), lambda s, *_: (0, 0, 0)) for places in groups],
             scratch_shapes=[
                 pltpu.VMEM((PAIRS, 2 * columns), BF16),
@@ -127,7 +163,7 @@
             transcendentals=0,
         ),
         name="ladder",
-    )(me, codes, *[value for value, _, _ in pieces], ladder_blocks)
+    )(me, table, *[value for value, _, _ in pieces], ladder_blocks, turned)
 
 
 def add(*terms):
@@ -248,7 +284,7 @@
     for _ in range(2, vp_size):
         ring.append(turn(ring[-1]))
     back_integrals = turn(integrals)
-    pieces = gather_tri(amplitudes, tri_size)
+    turned, ring[0], table, pieces = gather_tri(amplitudes, slot_block, ladder_blocks, tri_size)
     me = after(me, ring[1], back_integrals)
 
     if tri_size == 8:
@@ -257,7 +293,7 @@
         groups += [[(mask, 0) for mask in real_order], [(mask, 1) for mask in imag_order], [(0, 0), (0, 1)]]
     else:
         groups = [[(mask, part) for mask in range(tri_size) for part in range(2)]]
-    partials = ladder(me, slot_block, pieces, ladder_blocks, groups)
+    partials = ladder(me, table, pieces, ladder_blocks, turned, groups)
     *partials, ring[-1] = lax.optimization_barrier((*partials, ring[-1]))
     hold, give = contract(core, integrals, back_integrals, ring)
     last = turn(ring[-1])
@@ -269,18 +305,18 @@
     if tri_size == 8:
         real, imag, own = partials[3:]
         real_in, imag_in, own_in = (swap(value, tri_size, 0) for value in partials[:3])
-        real_in, imag_in, hold, give = lax.optimization_barrier((real_in, imag_in, hold, give))
+        mine = add(hold, swap(give, tri_size, 0)).astype(BF16)
+        real_in, imag_in, mine = lax.optimization_barrier((real_in, imag_in, mine))
         by_x = add(real[:2], real_in[:2]).astype(BF16)
         by_y = add(imag[:2], imag_in[:2]).astype(BF16)
-        by_x, by_y, hold, give = lax.optimization_barrier((by_x, by_y, hold, give))
+        by_x, by_y, mine = lax.optimization_barrier((by_x, by_y, mine))
         by_x, by_y = swap(by_x, tri_size, 1), swap(by_y, tri_size, 2)
-        mine = shift(add(hold, swap(give, tri_size, 0)).astype(BF16))
-        received = swap(mine, tri_size, 1)
+        mine = add(mine, swap(mine, tri_size, 1)).astype(BF16)
+        mine = shift(mine)
         then_y = add(real[2], real_in[2], by_x[1]).astype(BF16)
         then_x = add(imag[2], imag_in[2], by_y[1]).astype(BF16)
-        then_y, then_x, received, last = lax.optimization_barrier((then_y, then_x, received, last))
+        then_y, then_x, mine, last = lax.optimization_barrier((then_y, then_x, mine, last))
         then_y, then_x = swap(then_y[None], tri_size, 2), swap(then_x[None], tri_size, 1)
-        mine = add(mine, received).astype(BF16)
         mine = add(mine, swap(mine, tri_size, 2)).astype(BF16)
         terms = [(own, 0, 0), (own, 1, 1), (own_in, 0, 0), (own_in, 1, 1)]
         terms += [(by_x, 0, 0), (by_y, 1, 0), (then_y, 0, 0), (then_x, 1, 0)]

time: 77.2 us -> 82.5 us (1.069)
  the two profiles are of different devices: /device:TPU:8 before, /device:TPU:0 now
where the time goes in v6:
time: 82.5 us; the launch traced here: 82 us
  waiting for transfers between devices  32.3 us (39%)
  Pallas kernels  25.7 us (31%)
  starting transfers between devices  20.7 us (25%)
  local copies, waits for them, and re-layouts  2.43 us (3%)
    ppermute x20, waiting for transfers between devices, swap(): return lax.ppermute(value, 'tri', pairs)  19.1 us
    ppermute x6, waiting for transfers between devices, turn(): lax.ppermute(value, 'vp', [(order[i], order[(i + distance) % vp_size]) fo...  13.2 us
    pallas_call x1, Pallas kernels, ladder(): pl.pallas_call(functools.partial(ladder_kernel, [(mask, part) for _, mask...  13 us
    ppermute x20, starting transfers between devices, swap(): return lax.ppermute(value, 'tri', pairs)  13 us
    pallas_call x1, Pallas kernels, prepare(): pl.pallas_call(prepare_kernel, grid=(slots,), in_specs=[smem, block, whol...  10.3 us
    ppermute x6, starting transfers between devices, turn(): lax.ppermute(value, 'vp', [(order[i], order[(i + distance) % vp_size]) fo...  7.75 us
    unnamed x10, local copies, waits for them, and re-layouts  2.39 us
  transfers between devices with their start and end apart: 26, of which 11 were waited for; matrix products, arithmetic and copies ran while one was open for 0% of the time, Pallas kernels for 30%

profile of v6, /device:TPU:0, one launch (start us, length us, event | category | flops | bytes accessed | tf_op | source)
XLA Modules:
  0.0 82.0 jit_solution(10063166688951520826)
XLA Ops:
  0.0 2.9 %collective-permute-start.2 = (bf16[2,960,128]{2,1,0:T(8,128)(2,1)}, bf16[2,960,128]{2,1,0:T(8,128)(2,1)S(1)}, u32[]{:S(2)}, u32[]{:S(2)}) collective-permute-start(bf16[2,960,128]{2,1,0:T(8,128)(2,1)} %amp_ref.1), channel_id=1, source_target_pairs={{0,8},{4,12},{8,0},{12,4},{16,24},{20,28},{24,16},{28,20},{1,9},{5... | collective-permute-start | bytes 1474568 | tf_op jit(solution)/shard_map/ppermute | solution.py:20
  2.9 1.5 %collective-permute-start.3 = (bf16[2,960,128]{2,1,0:T(8,128)(2,1)}, bf16[2,960,128]{2,1,0:T(8,128)(2,1)S(1)}, u32[]{:S(2)}, u32[]{:S(2)}) collective-permute-start(bf16[2,960,128]{2,1,0:T(8,128)(2,1)} %amp_ref.1), channel_id=1, source_target_pairs={{0,16},{4,20},{8,24},{12,28},{16,0},{20,4},{24,8},{28,12},{1,17},{... | collective-permute-start | bytes 1474568 | tf_op jit(solution)/shard_map/ppermute | solution.py:20
  4.5 2.6 %collective-permute-start = (bf16[2,960,128]{2,1,0:T(8,128)(2,1)}, bf16[2,960,128]{2,1,0:T(8,128)(2,1)S(1)}, u32[]{:S(2)}, u32[]{:S(2)}) collective-permute-start(bf16[2,960,128]{2,1,0:T(8,128)(2,1)} %amp_ref.1), channel_id=1, source_target_pairs={{0,2},{2,3},{3,1},{1,0},{4,6},{6,7},{7,5},{5,4},{8,10},{10,11},{11... | collective-permute-start | bytes 1474568 | tf_op jit(solution)/shard_map/ppermute | solution.py:281
  7.1 1.6 %collective-permute-start.1 = (bf16[960,128]{1,0:T(8,128)(2,1)}, bf16[960,128]{1,0:T(8,128)(2,1)S(1)}, u32[]{:S(2)}, u32[]{:S(2)}) collective-permute-start(bf16[960,128]{1,0:T(8,128)(2,1)} %int_ref.1), channel_id=1, source_target_pairs={{0,2},{2,3},{3,1},{1,0},{4,6},{6,7},{7,5},{5,4},{8,10},{10,11},{11... | collective-permute-start | bytes 737288 | tf_op jit(solution)/shard_map/ppermute | solution.py:281
  8.6 1.0 %copy-done = bf16[2,960,128]{2,1,0:T(8,128)(2,1)S(1)} copy-done((bf16[2,960,128]{2,1,0:T(8,128)(2,1)S(1)}, bf16[2,960,128]{2,1,0:T(8,128)(2,1)}, u32[]{:S(2)}) %copy-start) | copy-done | bytes 491544
  9.7 0.7 copy-done.4
  10.3 10.3 %prepare.1 = (bf16[7,768,768]{2,1,0:T(8,128)(2,1)}, bf16[2,960,128]{2,1,0:T(8,128)(2,1)S(1)}, s32[3,7]{1,0:T(4,128)S(1)}) custom-call(s32[7]{0:T(128)S(1)} %copy-done.4, bf16[7,768,768]{2,1,0:T(8,128)(2,1)} %refs_10_.1, bf16[2,960,128]{2,1,0:T(8,128)(2,1)S(1)} %copy-done), custom_call_target="tpu_custom_call" | custom-call | bytes 16515072 | tf_op jit(solution)/shard_map/prepare/pallas_call | solution.py:78
  20.6 0.6 collective-permute-start.5
  21.2 0.6 collective-permute-start.4
  21.8 0.7 collective-permute-done.1.last_ref
  22.6 0.7 copy-done.2
  23.3 0.5 collective-permute-start.8
  23.8 5.1 %collective-permute-done.5.refs_4_ = bf16[960,128]{1,0:T(8,128)(2,1)} collective-permute-done((bf16[960,128]{1,0:T(8,128)(2,1)S(1)}, bf16[960,128]{1,0:T(8,128)(2,1)}, u32[]{:S(2)}, u32[]{:S(2)}) %collective-permute-start.5) | collective-permute-done | bytes 245792 | tf_op jit(solution)/shard_map/ppermute | solution.py:20
  29.8 1.0 %collective-permute-done.10.refs_9_ = bf16[960,128]{1,0:T(8,128)(2,1)} collective-permute-done((bf16[960,128]{1,0:T(8,128)(2,1)}, bf16[960,128]{1,0:T(8,128)(2,1)}, u32[]{:S(2)}, u32[]{:S(2)}) %collective-permute-start.10) | collective-permute-done | bytes 245792 | tf_op jit(solution)/shard_map/ppermute | solution.py:20
  31.1 13.0 %ladder.1 = (bf16[3,960,128]{2,1,0:T(8,128)(2,1)S(1)}, bf16[3,960,128]{2,1,0:T(8,128)(2,1)S(1)}, bf16[2,960,128]{2,1,0:T(8,128)(2,1)S(1)}, bf16[3,960,128]{2,1,0...) custom-call(s32[1]{0:T(128)} %bitcast.me_ref, ...), custom_call_target="tpu_custom_call" | custom-call | flops 4227858432 | bytes 16121856 | tf_op jit(solution)/shard_map/ladder/pallas_call | solution.py:143
  44.8 0.6 contract.1
  45.6 2.1 %collective-permute-done.14 = bf16[4,128,128]{2,1,0:T(8,128)(2,1)S(1)} collective-permute-done((bf16[4,128,128]{2,1,0:T(8,128)(2,1)S(1)}, bf16[4,128,128]{2,1,0:T(8,128)(2,1)S(1)}, u32[]{:S(2)}, u32[]{:S(2)}) %collective-permute-start.14) | collective-permute-done | bytes 131104 | tf_op jit(solution)/shard_map/ppermute | solution.py:20
  48.1 0.6 collective-permute-start.17
  48.7 1.5 %collective-permute-start.16 = (bf16[2,960,128]{2,1,0:T(8,128)(2,1)S(1)}, bf16[2,960,128]{2,1,0:T(8,128)(2,1)S(1)}, u32[]{:S(2)}, u32[]{:S(2)}) collective-permute-start(bf16[2,960,128]{2,1,0:T(8,128)(2,1)S(1)} %get-tuple-element.61), channel_id=1, source_target_pairs={{0,16},{4,20},{8,24},{12,28},{16,0},{20,4},{24,8},{28,12},{1,17},{... | collective-permute-start | bytes 1474568 | tf_op jit(solution)/shard_map/ppermute | solution.py:20
  50.2 1.5 %collective-permute-start.15 = (bf16[2,960,128]{2,1,0:T(8,128)(2,1)S(1)}, bf16[2,960,128]{2,1,0:T(8,128)(2,1)S(1)}, u32[]{:S(2)}, u32[]{:S(2)}) collective-permute-start(bf16[2,960,128]{2,1,0:T(8,128)(2,1)S(1)} %get-tuple-element.60), channel_id=1, source_target_pairs={{0,8},{4,12},{8,0},{12,4},{16,24},{20,28},{24,16},{28,20},{1,9},{5... | collective-permute-start | bytes 1474568 | tf_op jit(solution)/shard_map/ppermute | solution.py:20
  51.6 2.8 %collective-permute-done.17 = bf16[4,128,128]{2,1,0:T(8,128)(2,1)S(1)} collective-permute-done((bf16[4,128,128]{2,1,0:T(8,128)(2,1)S(1)}, bf16[4,128,128]{2,1,0:T(8,128)(2,1)S(1)}, u32[]{:S(2)}, u32[]{:S(2)}) %collective-permute-start.17) | collective-permute-done | bytes 131104 | tf_op jit(solution)/shard_map/ppermute | solution.py:20
  54.5 0.5 collective-permute-start.18
  55.0 1.4 %collective-permute-start.19 = (bf16[128,128]{1,0:T(8,128)(2,1)S(1)}, bf16[128,128]{1,0:T(8,128)(2,1)S(1)}, u32[]{:S(2)}, u32[]{:S(2)}) collective-permute-start(bf16[128,128]{1,0:T(8,128)(2,1)S(1)} %get-tuple-element.71), channel_id=1, source_target_pairs={{0,3},{2,1},{3,0},{1,2},{4,7},{6,5},{7,4},{5,6},{8,11},{10,9},{11,... | collective-permute-start | bytes 98312 | tf_op jit(solution)/shard_map/ppermute | solution.py:281
  56.4 1.4 %collective-permute-start.20 = (bf16[2,960,128]{2,1,0:T(8,128)(2,1)S(1)}, bf16[2,960,128]{2,1,0:T(8,128)(2,1)S(1)}, u32[]{:S(2)}, u32[]{:S(2)}) collective-permute-start(bf16[2,960,128]{2,1,0:T(8,128)(2,1)S(1)} %collective-permute-done.11.refs_2_), channel_id=1, source_target_pairs={{0,2},{2,3},{3,1},{1,0},{4,6},{6,7},{7,5},{5,4},{8,10},{10,11},{11... | collective-permute-start | bytes 1474568 | tf_op jit(solution)/shard_map/ppermute | solution.py:281
  57.8 12.5 %collective-permute-done.18 = bf16[128,128]{1,0:T(8,128)(2,1)S(1)} collective-permute-done((bf16[128,128]{1,0:T(8,128)(2,1)S(1)}, bf16[128,128]{1,0:T(8,128)(2,1)S(1)}, u32[]{:S(2)}, u32[]{:S(2)}) %collective-permute-start.18) | collective-permute-done | bytes 32800 | tf_op jit(solution)/shard_map/ppermute | solution.py:281
  70.5 1.5 %collective-permute-start.21 = (bf16[4,128,128]{2,1,0:T(8,128)(2,1)S(1)}, bf16[4,128,128]{2,1,0:T(8,128)(2,1)S(1)}, u32[]{:S(2)}, u32[]{:S(2)}) collective-permute-start(bf16[4,128,128]{2,1,0:T(8,128)(2,1)S(1)} %pad_maximum_fusion), channel_id=1, source_target_pairs={{0,16},{4,20},{8,24},{12,28},{16,0},{20,4},{24,8},{28,12},{1,17},{... | collective-permute-start | bytes 393224 | tf_op jit(solution)/shard_map/ppermute | solution.py:20
  72.0 0.6 collective-permute-start.24
  72.7 3.3 %collective-permute-done.21 = bf16[4,128,128]{2,1,0:T(8,128)(2,1)S(1)} collective-permute-done((bf16[4,128,128]{2,1,0:T(8,128)(2,1)S(1)}, bf16[4,128,128]{2,1,0:T(8,128)(2,1)S(1)}, u32[]{:S(2)}, u32[]{:S(2)}) %collective-permute-start.21) | collective-permute-done | bytes 131104 | tf_op jit(solution)/shard_map/ppermute | solution.py:20
  76.2 1.3 %collective-permute-done.22.other_ref = bf16[4,128,128]{2,1,0:T(8,128)(2,1)S(1)} collective-permute-done((bf16[4,128,128]{2,1,0:T(8,128)(2,1)S(1)}, bf16[4,128,128]{2,1,0:T(8,128)(2,1)S(1)}, u32[]{:S(2)}, u32[]{:S(2)}) %collective-permute-start.22) | collective-permute-done | bytes 131104 | tf_op jit(solution)/shard_map/ppermute | solution.py:20
  77.5 0.7 quadratic.1.base_ref
  78.2 2.6 %collective-permute-done.24.refs_6_ = bf16[1,960,128]{2,1,0:T(8,128)(2,1)S(1)} collective-permute-done((bf16[1,960,128]{2,1,0:T(8,128)(2,1)S(1)}, bf16[1,960,128]{2,1,0:T(8,128)(2,1)S(1)}, u32[]{:S(2)}, u32[]{:S(2)}) %collective-permute-start.24) | collective-permute-done | bytes 245792 | tf_op jit(solution)/shard_map/ppermute | solution.py:20
  80.8 1.1 %finish.1 = bf16[2,960,128]{2,1,0:T(8,128)(2,1)} custom-call(f32[2,960,128]{2,1,0:T(8,128)S(1)} %quadratic.1.base_ref, bf16[2,960,128]{2,1,0:T(8,128)(2,1)S(1)} %get-tuple-element.65.refs_0_.refs_1_, bf16[2,960,128]{2,1,0:T(8,128)(2,1)S(1)} %get-tuple-element.65.refs_0_.refs_1_, bf16[2,960,128]{2,1,0:T(8,128)(2,1)S(1)} %collective-permute-done.23.refs_2_.refs_3_, ...), custom_call_target="tpu_custom_call" | custom-call | tf_op jit(solution)/shard_map/finish/pallas_call | solution.py:255
  (45 shorter events, 2.9 us)
Async XLA Ops:
  0.0 20.6 %collective-permute-start.2 = (bf16[2,960,128]{2,1,0:T(8,128)(2,1)}, bf16[2,960,128]{2,1,0:T(8,128)(2,1)S(1)}, u32[]{:S(2)}, u32[]{:S(2)}) collective-permute-start(bf16[2,960,128]{2,1,0:T(8,128)(2,1)} %amp_ref.1), channel_id=1, source_target_pairs={{0,8},{4,12},{8,0},{12,4},{16,24},{20,28},{24,16},{28,20},{1,9},{5... | collective-permute-start | bytes 1474568 | tf_op jit(solution)/shard_map/ppermute | solution.py:20
  2.9 17.7 %collective-permute-start.3 = (bf16[2,960,128]{2,1,0:T(8,128)(2,1)}, bf16[2,960,128]{2,1,0:T(8,128)(2,1)S(1)}, u32[]{:S(2)}, u32[]{:S(2)}) collective-permute-start(bf16[2,960,128]{2,1,0:T(8,128)(2,1)} %amp_ref.1), channel_id=1, source_target_pairs={{0,16},{4,20},{8,24},{12,28},{16,0},{20,4},{24,8},{28,12},{1,17},{... | collective-permute-start | bytes 1474568 | tf_op jit(solution)/shard_map/ppermute | solution.py:20
  4.5 18.8 %collective-permute-start = (bf16[2,960,128]{2,1,0:T(8,128)(2,1)}, bf16[2,960,128]{2,1,0:T(8,128)(2,1)S(1)}, u32[]{:S(2)}, u32[]{:S(2)}) collective-permute-start(bf16[2,960,128]{2,1,0:T(8,128)(2,1)} %amp_ref.1), channel_id=1, source_target_pairs={{0,2},{2,3},{3,1},{1,0},{4,6},{6,7},{7,5},{5,4},{8,10},{10,11},{11... | collective-permute-start | bytes 1474568 | tf_op jit(solution)/shard_map/ppermute | solution.py:281
  7.0 22.4 %collective-permute-start.6 = (bf16[2,960,128]{2,1,0:T(8,128)(2,1)}, bf16[2,960,128]{2,1,0:T(8,128)(2,1)S(1)}, u32[]{:S(2)}, u32[]{:S(2)}) collective-permute-start(bf16[2,960,128]{2,1,0:T(8,128)(2,1)} %amp_ref.1), channel_id=1, source_target_pairs={{0,4},{4,0},{8,12},{12,8},{16,20},{20,16},{24,28},{28,24},{1,5},{5... | collective-permute-start | bytes 1474568 | tf_op jit(solution)/shard_map/ppermute | solution.py:20
  7.1 15.5 %collective-permute-start.1 = (bf16[960,128]{1,0:T(8,128)(2,1)}, bf16[960,128]{1,0:T(8,128)(2,1)S(1)}, u32[]{:S(2)}, u32[]{:S(2)}) collective-permute-start(bf16[960,128]{1,0:T(8,128)(2,1)} %int_ref.1), channel_id=1, source_target_pairs={{0,2},{2,3},{3,1},{1,0},{4,6},{6,7},{7,5},{5,4},{8,10},{10,11},{11... | collective-permute-start | bytes 737288 | tf_op jit(solution)/shard_map/ppermute | solution.py:281
  8.6 1.0 %copy-start = (bf16[2,960,128]{2,1,0:T(8,128)(2,1)S(1)}, bf16[2,960,128]{2,1,0:T(8,128)(2,1)}, u32[]{:S(2)}) copy-start(bf16[2,960,128]{2,1,0:T(8,128)(2,1)} %amp_ref.1) | copy-start | bytes 1474564
  9.7 0.7 copy-start.4
  20.6 8.3 %collective-permute-start.5 = (bf16[960,128]{1,0:T(8,128)(2,1)S(1)}, bf16[960,128]{1,0:T(8,128)(2,1)}, u32[]{:S(2)}, u32[]{:S(2)}) collective-permute-start(bf16[960,128]{1,0:T(8,128)(2,1)S(1)} %slice_bitcast_fusion), channel_id=1, source_target_pairs={{0,16},{4,20},{8,24},{12,28},{16,0},{20,4},{24,8},{28,12},{1,17},{... | collective-permute-start | bytes 737288 | tf_op jit(solution)/shard_map/ppermute | solution.py:20
  21.2 8.0 %collective-permute-start.4 = (bf16[960,128]{1,0:T(8,128)(2,1)S(1)}, bf16[960,128]{1,0:T(8,128)(2,1)}, u32[]{:S(2)}, u32[]{:S(2)}) collective-permute-start(bf16[960,128]{1,0:T(8,128)(2,1)S(1)} %slice_bitcast_fusion.1), channel_id=1, source_target_pairs={{0,8},{4,12},{8,0},{12,4},{16,24},{20,28},{24,16},{28,20},{1,9},{5... | collective-permute-start | bytes 737288 | tf_op jit(solution)/shard_map/ppermute | solution.py:20
  22.6 0.7 copy-start.2
  23.2 7.9 %collective-permute-start.7 = (bf16[2,960,128]{2,1,0:T(8,128)(2,1)S(1)}, bf16[2,960,128]{2,1,0:T(8,128)(2,1)S(1)}, u32[]{:S(2)}, u32[]{:S(2)}) collective-permute-start(bf16[2,960,128]{2,1,0:T(8,128)(2,1)S(1)} %collective-permute-done.2.refs_1_), channel_id=1, source_target_pairs={{0,4},{4,0},{8,12},{12,8},{16,20},{20,16},{24,28},{28,24},{1,5},{5... | collective-permute-start | bytes 1474568 | tf_op jit(solution)/shard_map/ppermute | solution.py:20
  23.3 7.9 %collective-permute-start.8 = (bf16[2,960,128]{2,1,0:T(8,128)(2,1)S(1)}, bf16[2,960,128]{2,1,0:T(8,128)(2,1)}, u32[]{:S(2)}, u32[]{:S(2)}) collective-permute-start(bf16[2,960,128]{2,1,0:T(8,128)(2,1)S(1)} %collective-permute-done.3.refs_2_), channel_id=1, source_target_pairs={{0,4},{4,0},{8,12},{12,8},{16,20},{20,16},{24,28},{28,24},{1,5},{5... | collective-permute-start | bytes 1474568 | tf_op jit(solution)/shard_map/ppermute | solution.py:20
  28.9 1.9 %collective-permute-start.10 = (bf16[960,128]{1,0:T(8,128)(2,1)}, bf16[960,128]{1,0:T(8,128)(2,1)}, u32[]{:S(2)}, u32[]{:S(2)}) collective-permute-start(bf16[960,128]{1,0:T(8,128)(2,1)} %collective-permute-done.5.refs_4_), channel_id=1, source_target_pairs={{0,4},{4,0},{8,12},{12,8},{16,20},{20,16},{24,28},{28,24},{1,5},{5... | collective-permute-start | bytes 737288 | tf_op jit(solution)/shard_map/ppermute | solution.py:20
  29.2 1.9 %collective-permute-start.9 = (bf16[960,128]{1,0:T(8,128)(2,1)}, bf16[960,128]{1,0:T(8,128)(2,1)}, u32[]{:S(2)}, u32[]{:S(2)}) collective-permute-start(bf16[960,128]{1,0:T(8,128)(2,1)} %collective-permute-done.4.refs_3_), channel_id=1, source_target_pairs={{0,4},{4,0},{8,12},{12,8},{16,20},{20,16},{24,28},{28,24},{1,5},{5... | collective-permute-start | bytes 737288 | tf_op jit(solution)/shard_map/ppermute | solution.py:20
  29.4 14.8 %collective-permute-start.11 = (bf16[2,960,128]{2,1,0:T(8,128)(2,1)S(1)}, bf16[2,960,128]{2,1,0:T(8,128)(2,1)S(1)}, u32[]{:S(2)}, u32[]{:S(2)}) collective-permute-start(bf16[2,960,128]{2,1,0:T(8,128)(2,1)S(1)} %collective-permute-done.refs_1_), channel_id=1, source_target_pairs={{0,2},{2,3},{3,1},{1,0},{4,6},{6,7},{7,5},{5,4},{8,10},{10,11},{11... | collective-permute-start | bytes 1474568 | tf_op jit(solution)/shard_map/ppermute | solution.py:281
  31.1 13.7 %copy-start.1 = (bf16[960,128]{1,0:T(8,128)(2,1)S(1)}, bf16[960,128]{1,0:T(8,128)(2,1)}, u32[]{:S(2)}) copy-start(bf16[960,128]{1,0:T(8,128)(2,1)} %int_ref.1) | copy-start | bytes 737284
  31.1 13.7 %copy-start.3 = (bf16[960,128]{1,0:T(8,128)(2,1)S(1)}, bf16[960,128]{1,0:T(8,128)(2,1)}, u32[]{:S(2)}) copy-start(bf16[960,128]{1,0:T(8,128)(2,1)} %copy-done.2) | copy-start | bytes 737284
  44.2 3.6 %collective-permute-start.12 = (bf16[3,960,128]{2,1,0:T(8,128)(2,1)S(1)}, bf16[3,960,128]{2,1,0:T(8,128)(2,1)S(1)}, u32[]{:S(2)}, u32[]{:S(2)}) collective-permute-start(bf16[3,960,128]{2,1,0:T(8,128)(2,1)S(1)} %get-tuple-element.51), channel_id=1, source_target_pairs={{0,4},{4,0},{8,12},{12,8},{16,20},{20,16},{24,28},{28,24},{1,5},{5... | collective-permute-start | bytes 2211848 | tf_op jit(solution)/shard_map/ppermute | solution.py:20
  44.4 3.3 %collective-permute-start.13 = (bf16[3,960,128]{2,1,0:T(8,128)(2,1)S(1)}, bf16[3,960,128]{2,1,0:T(8,128)(2,1)S(1)}, u32[]{:S(2)}, u32[]{:S(2)}) collective-permute-start(bf16[3,960,128]{2,1,0:T(8,128)(2,1)S(1)} %get-tuple-element.52), channel_id=1, source_target_pairs={{0,4},{4,0},{8,12},{12,8},{16,20},{20,16},{24,28},{28,24},{1,5},{5... | collective-permute-start | bytes 2211848 | tf_op jit(solution)/shard_map/ppermute | solution.py:20
  45.4 2.4 %collective-permute-start.14 = (bf16[4,128,128]{2,1,0:T(8,128)(2,1)S(1)}, bf16[4,128,128]{2,1,0:T(8,128)(2,1)S(1)}, u32[]{:S(2)}, u32[]{:S(2)}) collective-permute-start(bf16[4,128,128]{2,1,0:T(8,128)(2,1)S(1)} %get-tuple-element.55), channel_id=1, source_target_pairs={{0,4},{4,0},{8,12},{12,8},{16,20},{20,16},{24,28},{28,24},{1,5},{5... | collective-permute-start | bytes 393224 | tf_op jit(solution)/shard_map/ppermute | solution.py:20
  48.1 6.4 %collective-permute-start.17 = (bf16[4,128,128]{2,1,0:T(8,128)(2,1)S(1)}, bf16[4,128,128]{2,1,0:T(8,128)(2,1)S(1)}, u32[]{:S(2)}, u32[]{:S(2)}) collective-permute-start(bf16[4,128,128]{2,1,0:T(8,128)(2,1)S(1)} %add_convert_fusion.6), channel_id=1, source_target_pairs={{0,8},{4,12},{8,0},{12,4},{16,24},{20,28},{24,16},{28,20},{1,9},{5... | collective-permute-start | bytes 393224 | tf_op jit(solution)/shard_map/ppermute | solution.py:20
  48.7 21.6 %collective-permute-start.16 = (bf16[2,960,128]{2,1,0:T(8,128)(2,1)S(1)}, bf16[2,960,128]{2,1,0:T(8,128)(2,1)S(1)}, u32[]{:S(2)}, u32[]{:S(2)}) collective-permute-start(bf16[2,960,128]{2,1,0:T(8,128)(2,1)S(1)} %get-tuple-element.61), channel_id=1, source_target_pairs={{0,16},{4,20},{8,24},{12,28},{16,0},{20,4},{24,8},{28,12},{1,17},{... | collective-permute-start | bytes 1474568 | tf_op jit(solution)/shard_map/ppermute | solution.py:20
  50.2 20.3 %collective-permute-start.15 = (bf16[2,960,128]{2,1,0:T(8,128)(2,1)S(1)}, bf16[2,960,128]{2,1,0:T(8,128)(2,1)S(1)}, u32[]{:S(2)}, u32[]{:S(2)}) collective-permute-start(bf16[2,960,128]{2,1,0:T(8,128)(2,1)S(1)} %get-tuple-element.60), channel_id=1, source_target_pairs={{0,8},{4,12},{8,0},{12,4},{16,24},{20,28},{24,16},{28,20},{1,9},{5... | collective-permute-start | bytes 1474568 | tf_op jit(solution)/shard_map/ppermute | solution.py:20
  54.5 15.7 %collective-permute-start.18 = (bf16[128,128]{1,0:T(8,128)(2,1)S(1)}, bf16[128,128]{1,0:T(8,128)(2,1)S(1)}, u32[]{:S(2)}, u32[]{:S(2)}) collective-permute-start(bf16[128,128]{1,0:T(8,128)(2,1)S(1)} %get-tuple-element.72), channel_id=1, source_target_pairs={{0,1},{2,0},{3,2},{1,3},{4,5},{6,4},{7,6},{5,7},{8,9},{10,8},{11,1... | collective-permute-start | bytes 98312 | tf_op jit(solution)/shard_map/ppermute | solution.py:281
  55.0 15.2 %collective-permute-start.19 = (bf16[128,128]{1,0:T(8,128)(2,1)S(1)}, bf16[128,128]{1,0:T(8,128)(2,1)S(1)}, u32[]{:S(2)}, u32[]{:S(2)}) collective-permute-start(bf16[128,128]{1,0:T(8,128)(2,1)S(1)} %get-tuple-element.71), channel_id=1, source_target_pairs={{0,3},{2,1},{3,0},{1,2},{4,7},{6,5},{7,4},{5,6},{8,11},{10,9},{11,... | collective-permute-start | bytes 98312 | tf_op jit(solution)/shard_map/ppermute | solution.py:281
  56.4 14.1 %collective-permute-start.20 = (bf16[2,960,128]{2,1,0:T(8,128)(2,1)S(1)}, bf16[2,960,128]{2,1,0:T(8,128)(2,1)S(1)}, u32[]{:S(2)}, u32[]{:S(2)}) collective-permute-start(bf16[2,960,128]{2,1,0:T(8,128)(2,1)S(1)} %collective-permute-done.11.refs_2_), channel_id=1, source_target_pairs={{0,2},{2,3},{3,1},{1,0},{4,6},{6,7},{7,5},{5,4},{8,10},{10,11},{11... | collective-permute-start | bytes 1474568 | tf_op jit(solution)/shard_map/ppermute | solution.py:281
  70.5 5.5 %collective-permute-start.21 = (bf16[4,128,128]{2,1,0:T(8,128)(2,1)S(1)}, bf16[4,128,128]{2,1,0:T(8,128)(2,1)S(1)}, u32[]{:S(2)}, u32[]{:S(2)}) collective-permute-start(bf16[4,128,128]{2,1,0:T(8,128)(2,1)S(1)} %pad_maximum_fusion), channel_id=1, source_target_pairs={{0,16},{4,20},{8,24},{12,28},{16,0},{20,4},{24,8},{28,12},{1,17},{... | collective-permute-start | bytes 393224 | tf_op jit(solution)/shard_map/ppermute | solution.py:20
  72.0 6.2 %collective-permute-start.23 = (bf16[2,960,128]{2,1,0:T(8,128)(2,1)S(1)}, bf16[2,960,128]{2,1,0:T(8,128)(2,1)S(1)}, u32[]{:S(2)}, u32[]{:S(2)}) collective-permute-start(bf16[2,960,128]{2,1,0:T(8,128)(2,1)S(1)} %get-tuple-element.66), channel_id=1, source_target_pairs={{0,4},{4,0},{8,12},{12,8},{16,20},{20,16},{24,28},{28,24},{1,5},{5... | collective-permute-start | bytes 1474568 | tf_op jit(solution)/shard_map/ppermute | solution.py:20
  72.0 8.8 %collective-permute-start.24 = (bf16[1,960,128]{2,1,0:T(8,128)(2,1)S(1)}, bf16[1,960,128]{2,1,0:T(8,128)(2,1)S(1)}, u32[]{:S(2)}, u32[]{:S(2)}) collective-permute-start(bf16[1,960,128]{2,1,0:T(8,128)(2,1)S(1)} %bitcast.18), channel_id=1, source_target_pairs={{0,16},{4,20},{8,24},{12,28},{16,0},{20,4},{24,8},{28,12},{1,17},{... | collective-permute-start | bytes 737288 | tf_op jit(solution)/shard_map/ppermute | solution.py:20
  72.6 8.2 %collective-permute-start.25 = (bf16[1,960,128]{2,1,0:T(8,128)(2,1)S(1)}, bf16[1,960,128]{2,1,0:T(8,128)(2,1)S(1)}, u32[]{:S(2)}, u32[]{:S(2)}) collective-permute-start(bf16[1,960,128]{2,1,0:T(8,128)(2,1)S(1)} %bitcast.17), channel_id=1, source_target_pairs={{0,8},{4,12},{8,0},{12,4},{16,24},{20,28},{24,16},{28,20},{1,9},{5... | collective-permute-start | bytes 737288 | tf_op jit(solution)/shard_map/ppermute | solution.py:20
  76.1 1.4 %collective-permute-start.22 = (bf16[4,128,128]{2,1,0:T(8,128)(2,1)S(1)}, bf16[4,128,128]{2,1,0:T(8,128)(2,1)S(1)}, u32[]{:S(2)}, u32[]{:S(2)}) collective-permute-start(bf16[4,128,128]{2,1,0:T(8,128)(2,1)S(1)} %add_convert_fusion.4.mine_ref), channel_id=1, source_target_pairs={{0,4},{4,0},{8,12},{12,8},{16,20},{20,16},{24,28},{28,24},{1,5},{5... | collective-permute-start | bytes 393224 | tf_op jit(solution)/shard_map/ppermute | solution.py:20

commit v7 on v5

--- a/solution.py
+++ b/solution.py
@@ -24,28 +24,49 @@
     return lax.optimization_barrier((value, *earlier))[0]
 
 
-def gather_tri(amplitudes, axis_size):
+def stage_kernel(source_ref, target_ref, sem):
+    copy = pltpu.make_async_copy(source_ref, target_ref, sem)
+    copy.start()
+    copy.wait()
+
+
+def stage(value):
+    return pl.pallas_call(
+        stage_kernel,
+        in_specs=[pl.BlockSpec(memory_space=pl.ANY)],
+        out_specs=pl.BlockSpec(memory_space=pltpu.VMEM),
+        out_shape=jax.ShapeDtypeStruct(value.shape, value.dtype),
+        scratch_shapes=[pltpu.SemaphoreType.DMA],
+        compiler_params=pltpu.CompilerParams(vmem_limit_bytes=16 * 1024 * 1024),
+        cost_estimate=pl.CostEstimate(flops=0, bytes_accessed=4 * value.size, transcendentals=0),
+        name="stage",
+    )(value)
+
+
+def gather_tri(amplitudes, small, axis_size):
     if axis_size != 8:
         found = {0: amplitudes}
         for bit in range(axis_size.bit_length() - 1):
             for mask in list(found):
                 found[mask | (1 << bit)] = swap(found[mask], axis_size, bit)
-        return [(value, mask, None) for mask, value in found.items()]
+        return [(value, mask, None) for mask, value in found.items()], small
     by_x = swap(amplitudes, axis_size, 1)
     by_y = swap(amplitudes, axis_size, 2)
     own_core = swap(amplitudes, axis_size, 0)
+    own = stage(amplitudes)
+    by_x, by_y, small, _ = lax.optimization_barrier((by_x, by_y, small, own))
     far_real = swap(by_y[0], axis_size, 1)
     far_imag = swap(by_x[1], axis_size, 2)
     found = [
-        (amplitudes, 0, None), (by_x, 2, None), (by_y, 4, None), (far_real, 6, 0), (far_imag, 6, 1),
+        (own, 0, None), (by_x, 2, None), (by_y, 4, None), (far_real, 6, 0), (far_imag, 6, 1),
         (own_core, 1, None),
     ]
     for value, mask, part in found[1:5]:
         found.append((swap(value, axis_size, 0), mask | 1, part))
-    return found
-
-
-def ladder_kernel(labels, groups, me_ref, code_ref, *refs):
+    return found, small
+
+
+def ladder_kernel(labels, groups, small_ref, *refs):
     count = len(labels)
     piece_refs = refs[:count]
     ladder_ref = refs[count]
@@ -54,7 +75,7 @@
     columns = amp.shape[1] // 2
     rows = out_refs[0].shape[-2]
     step = pl.program_id(0)
-    me = me_ref[0]
+    me = small_ref[0]
 
     def rows_of(mask):
         return pl.ds(pl.multiple_of((me ^ mask) * rows, rows), rows)
@@ -73,7 +94,7 @@
         for copy in copies:
             copy.wait()
 
-    code = code_ref[step]
+    code = small_ref[1 + step]
     row_block = jnp.int32(0)
     start = jnp.int32(0)
     for row in range(1, NB):
@@ -85,11 +106,11 @@
     weight = jnp.where(row_block == column_block, 0.5, 1.0) * jnp.where(code < TRI_BLOCKS, 1.0, 0.0)
     at_row = pl.ds(pl.multiple_of(row_block * BLOCK, BLOCK), BLOCK)
     at_column = pl.ds(pl.multiple_of(column_block * BLOCK, BLOCK), BLOCK)
+    weight = weight.astype(BF16)
     block = ladder_ref[0]
-    to_row = lax.dot_general(block, amp[at_column, :], (((1,), (0,)), ((), ())), preferred_element_type=F32)
-    acc[at_row, :] += weight * to_row
-    to_column = lax.dot_general(block, amp[at_row, :], (((0,), (0,)), ((), ())), preferred_element_type=F32)
-    acc[at_column, :] += weight * to_column
+    column_amp, row_amp = weight * amp[at_column, :], weight * amp[at_row, :]
+    acc[at_row, :] += lax.dot_general(block, column_amp, (((1,), (0,)), ((), ())), preferred_element_type=F32)
+    acc[at_column, :] += lax.dot_general(block, row_amp, (((0,), (0,)), ((), ())), preferred_element_type=F32)
 
     @pl.when(step == pl.num_programs(0) - 1)
     def _():
@@ -99,14 +120,14 @@
                 target[place] = acc[rows_of(mask), lanes].astype(BF16)
 
 
-def ladder(me, codes, pieces, ladder_blocks, groups):
+def ladder(small, pieces, ladder_blocks, groups):
     slots = ladder_blocks.shape[0]
     rows, columns = pieces[0][0].shape[-2:]
     count = sum(len(places) for places in groups)
     return pl.pallas_call(
         functools.partial(ladder_kernel, [(mask, part) for _, mask, part in pieces], groups),
         grid_spec=pltpu.PrefetchScalarGridSpec(
-            num_scalar_prefetch=2,
+            num_scalar_prefetch=1,
             grid=(slots,),
             in_specs=[pl.BlockSpec(memory_space=pl.ANY)] * len(pieces)
             + [pl.BlockSpec((1, BLOCK, BLOCK), lambda s, *_: (s, 0, 0))],
@@ -127,7 +148,7 @@
             transcendentals=0,
         ),
         name="ladder",
-    )(me, codes, *[value for value, _, _ in pieces], ladder_blocks)
+    )(small, *[value for value, _, _ in pieces], ladder_blocks)
 
 
 def add(*terms):
@@ -248,8 +269,9 @@
     for _ in range(2, vp_size):
         ring.append(turn(ring[-1]))
     back_integrals = turn(integrals)
-    pieces = gather_tri(amplitudes, tri_size)
-    me = after(me, ring[1], back_integrals)
+    pieces, small = gather_tri(amplitudes, jnp.concatenate([me, slot_block]), tri_size)
+    small = after(small, ring[1], back_integrals)
+    ring[0] = pieces[0][0]
 
     if tri_size == 8:
         real_order, imag_order = (2, 6, 4), (4, 6, 2)
@@ -257,10 +279,9 @@
         groups += [[(mask, 0) for mask in real_order], [(mask, 1) for mask in imag_order], [(0, 0), (0, 1)]]
     else:
         groups = [[(mask, part) for mask in range(tri_size) for part in range(2)]]
-    partials = ladder(me, slot_block, pieces, ladder_blocks, groups)
+    partials = ladder(small, pieces, ladder_blocks, groups)
     *partials, ring[-1] = lax.optimization_barrier((*partials, ring[-1]))
     hold, give = contract(core, integrals, back_integrals, ring)
-    last = turn(ring[-1])
 
     def shift(value):
         moved = [turn(value[step], vp_size - step) for step in range(1, vp_size - 1)]
@@ -275,16 +296,19 @@
         by_x, by_y, hold, give = lax.optimization_barrier((by_x, by_y, hold, give))
         by_x, by_y = swap(by_x, tri_size, 1), swap(by_y, tri_size, 2)
         mine = shift(add(hold, swap(give, tri_size, 0)).astype(BF16))
+        last = turn(after(ring[-1], mine))
         received = swap(mine, tri_size, 1)
         then_y = add(real[2], real_in[2], by_x[1]).astype(BF16)
         then_x = add(imag[2], imag_in[2], by_y[1]).astype(BF16)
-        then_y, then_x, received, last = lax.optimization_barrier((then_y, then_x, received, last))
+        then_y, then_x, received = lax.optimization_barrier((then_y, then_x, received))
         then_y, then_x = swap(then_y[None], tri_size, 2), swap(then_x[None], tri_size, 1)
         mine = add(mine, received).astype(BF16)
-        mine = add(mine, swap(mine, tri_size, 2)).astype(BF16)
+        received, last = lax.optimization_barrier((swap(mine, tri_size, 2), last))
+        mine = add(mine, received).astype(BF16)
         terms = [(own, 0, 0), (own, 1, 1), (own_in, 0, 0), (own_in, 1, 1)]
         terms += [(by_x, 0, 0), (by_y, 1, 0), (then_y, 0, 0), (then_x, 1, 0)]
     else:
+        last = turn(ring[-1])
         terms = scatter_plain(partials[0].reshape(tri_size, 2, *amplitudes.shape[1:]), tri_size)
         mine = shift(add(hold, swap(give, tri_size, 0)).astype(BF16))
         for bit in range(1, bits):

time: 77.2 us -> 71.1 us (0.921)
  the two profiles are of different devices: /device:TPU:8 before, /device:TPU:0 now
where the time goes in v7:
time: 71.1 us; the launch traced here: 70.8 us
  waiting for transfers between devices  29.9 us (42%)
  starting transfers between devices  24.5 us (34%)
  Pallas kernels  13.8 us (19%)
  other arithmetic  1.34 us (2%)
  local copies, waits for them, and re-layouts  1.08 us (2%)
    ppermute x20, waiting for transfers between devices, swap(): return lax.ppermute(value, 'tri', pairs)  20.4 us
    ppermute x20, starting transfers between devices, swap(): return lax.ppermute(value, 'tri', pairs)  13.5 us
    pallas_call x1, Pallas kernels, ladder(): pl.pallas_call(functools.partial(ladder_kernel, [(mask, part) for _, mask...  11.1 us
    ppermute x6, starting transfers between devices, turn(): lax.ppermute(value, 'vp', [(order[i], order[(i + distance) % vp_size]) fo...  11.1 us
    ppermute x6, waiting for transfers between devices, turn(): lax.ppermute(value, 'vp', [(order[i], order[(i + distance) % vp_size]) fo...  9.52 us
  transfers between devices with their start and end apart: 26, of which 14 were waited for; matrix products, arithmetic and copies ran while one was open for 2% of the time, Pallas kernels for 18%

profile of v7, /device:TPU:0, one launch (start us, length us, event | category | flops | bytes accessed | tf_op | source)
XLA Modules:
  0.0 70.8 jit_solution(10286514302769553889)
XLA Ops:
  0.0 3.0 %collective-permute-start.1 = (bf16[2,960,128]{2,1,0:T(8,128)(2,1)}, bf16[2,960,128]{2,1,0:T(8,128)(2,1)S(1)}, u32[]{:S(2)}, u32[]{:S(2)}) collective-permute-start(bf16[2,960,128]{2,1,0:T(8,128)(2,1)} %source_ref.1), channel_id=1, source_target_pairs={{0,16},{4,20},{8,24},{12,28},{16,0},{20,4},{24,8},{28,12},{1,17},{... | collective-permute-start | bytes 1474568 | tf_op jit(solution)/shard_map/ppermute | solution.py:20
  3.0 1.5 %collective-permute-start = (bf16[2,960,128]{2,1,0:T(8,128)(2,1)}, bf16[2,960,128]{2,1,0:T(8,128)(2,1)S(1)}, u32[]{:S(2)}, u32[]{:S(2)}) collective-permute-start(bf16[2,960,128]{2,1,0:T(8,128)(2,1)} %source_ref.1), channel_id=1, source_target_pairs={{0,8},{4,12},{8,0},{12,4},{16,24},{20,28},{24,16},{28,20},{1,9},{5... | collective-permute-start | bytes 1474568 | tf_op jit(solution)/shard_map/ppermute | solution.py:20
  4.5 2.6 %collective-permute-start.2 = (bf16[2,960,128]{2,1,0:T(8,128)(2,1)}, bf16[2,960,128]{2,1,0:T(8,128)(2,1)S(1)}, u32[]{:S(2)}, u32[]{:S(2)}) collective-permute-start(bf16[2,960,128]{2,1,0:T(8,128)(2,1)} %source_ref.1), channel_id=1, source_target_pairs={{0,2},{2,3},{3,1},{1,0},{4,6},{6,7},{7,5},{5,4},{8,10},{10,11},{11... | collective-permute-start | bytes 1474568 | tf_op jit(solution)/shard_map/ppermute | solution.py:266
  7.1 1.6 %collective-permute-start.3 = (bf16[960,128]{1,0:T(8,128)(2,1)}, bf16[960,128]{1,0:T(8,128)(2,1)S(1)}, u32[]{:S(2)}, u32[]{:S(2)}) collective-permute-start(bf16[960,128]{1,0:T(8,128)(2,1)} %int_ref.1), channel_id=1, source_target_pairs={{0,2},{2,3},{3,1},{1,0},{4,6},{6,7},{7,5},{5,4},{8,10},{10,11},{11... | collective-permute-start | bytes 737288 | tf_op jit(solution)/shard_map/ppermute | solution.py:266
  8.6 0.7 %pad_add_fusion.small_ref = s32[8]{0:T(128)S(1)} fusion(s32[7]{0:T(128)} %param.7, s32[1]{0:T(128)} %bitcast), kind=kLoop, calls=%fused_computation.14 | loop fusion | flops 8 | bytes 64 | tf_op jit(solution)/shard_map/concatenate | solution.py:272
  9.4 1.0 %copy-done = bf16[2,960,128]{2,1,0:T(8,128)(2,1)S(1)} copy-done((bf16[2,960,128]{2,1,0:T(8,128)(2,1)S(1)}, bf16[2,960,128]{2,1,0:T(8,128)(2,1)}, u32[]{:S(2)}) %copy-start) | copy-done | bytes 491544
  10.7 3.7 %collective-permute-done.1.refs_2_ = bf16[2,960,128]{2,1,0:T(8,128)(2,1)S(1)} collective-permute-done((bf16[2,960,128]{2,1,0:T(8,128)(2,1)}, bf16[2,960,128]{2,1,0:T(8,128)(2,1)S(1)}, u32[]{:S(2)}, u32[]{:S(2)}) %collective-permute-start.1) | collective-permute-done | bytes 491552 | tf_op jit(solution)/shard_map/ppermute | solution.py:20
  14.4 1.5 %collective-permute-done.refs_1_ = bf16[2,960,128]{2,1,0:T(8,128)(2,1)S(1)} collective-permute-done((bf16[2,960,128]{2,1,0:T(8,128)(2,1)}, bf16[2,960,128]{2,1,0:T(8,128)(2,1)S(1)}, u32[]{:S(2)}, u32[]{:S(2)}) %collective-permute-start) | collective-permute-done | bytes 491552 | tf_op jit(solution)/shard_map/ppermute | solution.py:20
  15.9 1.6 %collective-permute-start.4 = (bf16[960,128]{1,0:T(8,128)(2,1)S(1)}, bf16[960,128]{1,0:T(8,128)(2,1)S(1)}, u32[]{:S(2)}, u32[]{:S(2)}) collective-permute-start(bf16[960,128]{1,0:T(8,128)(2,1)S(1)} %slice_bitcast_fusion.1), channel_id=1, source_target_pairs={{0,8},{4,12},{8,0},{12,4},{16,24},{20,28},{24,16},{28,20},{1,9},{5... | collective-permute-start | bytes 737288 | tf_op jit(solution)/shard_map/ppermute | solution.py:20
  18.0 5.8 %collective-permute-done.3.last_ref = bf16[960,128]{1,0:T(8,128)(2,1)S(1)} collective-permute-done((bf16[960,128]{1,0:T(8,128)(2,1)}, bf16[960,128]{1,0:T(8,128)(2,1)S(1)}, u32[]{:S(2)}, u32[]{:S(2)}) %collective-permute-start.3) | collective-permute-done | bytes 245792 | tf_op jit(solution)/shard_map/ppermute | solution.py:266
  24.8 3.3 %collective-permute-start.11 = (bf16[2,960,128]{2,1,0:T(8,128)(2,1)S(1)}, bf16[2,960,128]{2,1,0:T(8,128)(2,1)S(1)}, u32[]{:S(2)}, u32[]{:S(2)}) collective-permute-start(bf16[2,960,128]{2,1,0:T(8,128)(2,1)S(1)} %collective-permute-done.2.refs_1_), channel_id=1, source_target_pairs={{0,2},{2,3},{3,1},{1,0},{4,6},{6,7},{7,5},{5,4},{8,10},{10,11},{11... | collective-permute-start | bytes 1474568 | tf_op jit(solution)/shard_map/ppermute | solution.py:266
  28.1 11.1 %ladder.1 = (bf16[3,960,128]{2,1,0:T(8,128)(2,1)S(1)}, bf16[3,960,128]{2,1,0:T(8,128)(2,1)S(1)}, bf16[2,960,128]{2,1,0:T(8,128)(2,1)S(1)}, bf16[3,960,128]{2,1,0...) custom-call(s32[8]{0:T(128)S(1)} %pad_add_fusion.small_ref, ...), custom_call_target="tpu_custom_call" | custom-call | flops 4227858432 | bytes 16121856 | tf_op jit(solution)/shard_map/ladder/pallas_call | solution.py:127
  39.8 0.6 contract.1
  40.4 1.1 %collective-permute-done.12 = bf16[3,960,128]{2,1,0:T(8,128)(2,1)S(1)} collective-permute-done((bf16[3,960,128]{2,1,0:T(8,128)(2,1)S(1)}, bf16[3,960,128]{2,1,0:T(8,128)(2,1)S(1)}, u32[]{:S(2)}, u32[]{:S(2)}) %collective-permute-start.12) | collective-permute-done | bytes 737312 | tf_op jit(solution)/shard_map/ppermute | solution.py:20
  41.5 1.1 %collective-permute-done.13 = bf16[3,960,128]{2,1,0:T(8,128)(2,1)S(1)} collective-permute-done((bf16[3,960,128]{2,1,0:T(8,128)(2,1)S(1)}, bf16[3,960,128]{2,1,0:T(8,128)(2,1)S(1)}, u32[]{:S(2)}, u32[]{:S(2)}) %collective-permute-start.13) | collective-permute-done | bytes 737312 | tf_op jit(solution)/shard_map/ppermute | solution.py:20
  43.1 0.5 collective-permute-start.17
  44.3 2.4 %collective-permute-start.16 = (bf16[128,128]{1,0:T(8,128)(2,1)S(1)}, bf16[128,128]{1,0:T(8,128)(2,1)S(1)}, u32[]{:S(2)}, u32[]{:S(2)}) collective-permute-start(bf16[128,128]{1,0:T(8,128)(2,1)S(1)} %get-tuple-element.73), channel_id=1, source_target_pairs={{0,3},{2,1},{3,0},{1,2},{4,7},{6,5},{7,4},{5,6},{8,11},{10,9},{11,... | collective-permute-start | bytes 98312 | tf_op jit(solution)/shard_map/ppermute | solution.py:266
  46.7 1.1 %collective-permute-start.15 = (bf16[128,128]{1,0:T(8,128)(2,1)S(1)}, bf16[128,128]{1,0:T(8,128)(2,1)S(1)}, u32[]{:S(2)}, u32[]{:S(2)}) collective-permute-start(bf16[128,128]{1,0:T(8,128)(2,1)S(1)} %get-tuple-element.74), channel_id=1, source_target_pairs={{0,1},{2,0},{3,2},{1,3},{4,5},{6,4},{7,6},{5,7},{8,9},{10,8},{11,1... | collective-permute-start | bytes 98312 | tf_op jit(solution)/shard_map/ppermute | solution.py:266
  47.8 2.6 %collective-permute-done.16 = bf16[128,128]{1,0:T(8,128)(2,1)S(1)} collective-permute-done((bf16[128,128]{1,0:T(8,128)(2,1)S(1)}, bf16[128,128]{1,0:T(8,128)(2,1)S(1)}, u32[]{:S(2)}, u32[]{:S(2)}) %collective-permute-start.16) | collective-permute-done | bytes 32800 | tf_op jit(solution)/shard_map/ppermute | solution.py:266
  50.4 1.1 %collective-permute-done.15 = bf16[128,128]{1,0:T(8,128)(2,1)S(1)} collective-permute-done((bf16[128,128]{1,0:T(8,128)(2,1)S(1)}, bf16[128,128]{1,0:T(8,128)(2,1)S(1)}, u32[]{:S(2)}, u32[]{:S(2)}) %collective-permute-start.15) | collective-permute-done | bytes 32800 | tf_op jit(solution)/shard_map/ppermute | solution.py:266
  51.5 1.4 %collective-permute-start.19 = (bf16[4,128,128]{2,1,0:T(8,128)(2,1)S(1)}, bf16[4,128,128]{2,1,0:T(8,128)(2,1)S(1)}, u32[]{:S(2)}, u32[]{:S(2)}) collective-permute-start(bf16[4,128,128]{2,1,0:T(8,128)(2,1)S(1)} %pad_maximum_fusion), channel_id=1, source_target_pairs={{0,8},{4,12},{8,0},{12,4},{16,24},{20,28},{24,16},{28,20},{1,9},{5... | collective-permute-start | bytes 393224 | tf_op jit(solution)/shard_map/ppermute | solution.py:20
  53.1 4.0 %collective-permute-done.17.refs_4_ = bf16[2,960,128]{2,1,0:T(8,128)(2,1)S(1)} collective-permute-done((bf16[2,960,128]{2,1,0:T(8,128)(2,1)S(1)}, bf16[2,960,128]{2,1,0:T(8,128)(2,1)S(1)}, u32[]{:S(2)}, u32[]{:S(2)}) %collective-permute-start.17) | collective-permute-done | bytes 491552 | tf_op jit(solution)/shard_map/ppermute | solution.py:20
  57.3 2.0 %collective-permute-done.19 = bf16[4,128,128]{2,1,0:T(8,128)(2,1)S(1)} collective-permute-done((bf16[4,128,128]{2,1,0:T(8,128)(2,1)S(1)}, bf16[4,128,128]{2,1,0:T(8,128)(2,1)S(1)}, u32[]{:S(2)}, u32[]{:S(2)}) %collective-permute-start.19) | collective-permute-done | bytes 131104 | tf_op jit(solution)/shard_map/ppermute | solution.py:20
  59.4 0.6 collective-permute-start.20
  60.0 0.5 collective-permute-start.25
  60.5 1.5 %collective-permute-start.24 = (bf16[1,960,128]{2,1,0:T(8,128)(2,1)S(1)}, bf16[1,960,128]{2,1,0:T(8,128)(2,1)S(1)}, u32[]{:S(2)}, u32[]{:S(2)}) collective-permute-start(bf16[1,960,128]{2,1,0:T(8,128)(2,1)S(1)} %bitcast.23), channel_id=1, source_target_pairs={{0,16},{4,20},{8,24},{12,28},{16,0},{20,4},{24,8},{28,12},{1,17},{... | collective-permute-start | bytes 737288 | tf_op jit(solution)/shard_map/ppermute | solution.py:20
  62.0 3.5 %collective-permute-done.20 = bf16[4,128,128]{2,1,0:T(8,128)(2,1)S(1)} collective-permute-done((bf16[4,128,128]{2,1,0:T(8,128)(2,1)S(1)}, bf16[4,128,128]{2,1,0:T(8,128)(2,1)S(1)}, u32[]{:S(2)}, u32[]{:S(2)}) %collective-permute-start.20) | collective-permute-done | bytes 131104 | tf_op jit(solution)/shard_map/ppermute | solution.py:20
  65.7 1.3 %collective-permute-done.22.other_ref = bf16[4,128,128]{2,1,0:T(8,128)(2,1)S(1)} collective-permute-done((bf16[4,128,128]{2,1,0:T(8,128)(2,1)S(1)}, bf16[4,128,128]{2,1,0:T(8,128)(2,1)S(1)}, u32[]{:S(2)}, u32[]{:S(2)}) %collective-permute-start.22) | collective-permute-done | bytes 131104 | tf_op jit(solution)/shard_map/ppermute | solution.py:20
  67.0 0.7 quadratic.1.base_ref
  67.7 0.6 collective-permute-done.25.refs_7_
  68.3 1.4 %collective-permute-done.24.refs_6_ = bf16[1,960,128]{2,1,0:T(8,128)(2,1)S(1)} collective-permute-done((bf16[1,960,128]{2,1,0:T(8,128)(2,1)S(1)}, bf16[1,960,128]{2,1,0:T(8,128)(2,1)S(1)}, u32[]{:S(2)}, u32[]{:S(2)}) %collective-permute-start.24) | collective-permute-done | bytes 245792 | tf_op jit(solution)/shard_map/ppermute | solution.py:20
  69.7 1.1 %finish.1 = bf16[2,960,128]{2,1,0:T(8,128)(2,1)} custom-call(f32[2,960,128]{2,1,0:T(8,128)S(1)} %quadratic.1.base_ref, bf16[2,960,128]{2,1,0:T(8,128)(2,1)S(1)} %get-tuple-element.67.refs_0_.refs_1_, bf16[2,960,128]{2,1,0:T(8,128)(2,1)S(1)} %get-tuple-element.67.refs_0_.refs_1_, bf16[2,960,128]{2,1,0:T(8,128)(2,1)S(1)} %collective-permute-done.23.refs_2_.refs_3_, ...), custom_call_target="tpu_custom_call" | custom-call | tf_op jit(solution)/shard_map/finish/pallas_call | solution.py:240
  (40 shorter events, 4.2 us)
Async XLA Ops:
  0.0 14.4 %collective-permute-start.1 = (bf16[2,960,128]{2,1,0:T(8,128)(2,1)}, bf16[2,960,128]{2,1,0:T(8,128)(2,1)S(1)}, u32[]{:S(2)}, u32[]{:S(2)}) collective-permute-start(bf16[2,960,128]{2,1,0:T(8,128)(2,1)} %source_ref.1), channel_id=1, source_target_pairs={{0,16},{4,20},{8,24},{12,28},{16,0},{20,4},{24,8},{28,12},{1,17},{... | collective-permute-start | bytes 1474568 | tf_op jit(solution)/shard_map/ppermute | solution.py:20
  3.0 12.9 %collective-permute-start = (bf16[2,960,128]{2,1,0:T(8,128)(2,1)}, bf16[2,960,128]{2,1,0:T(8,128)(2,1)S(1)}, u32[]{:S(2)}, u32[]{:S(2)}) collective-permute-start(bf16[2,960,128]{2,1,0:T(8,128)(2,1)} %source_ref.1), channel_id=1, source_target_pairs={{0,8},{4,12},{8,0},{12,4},{16,24},{20,28},{24,16},{28,20},{1,9},{5... | collective-permute-start | bytes 1474568 | tf_op jit(solution)/shard_map/ppermute | solution.py:20
  4.5 19.3 %collective-permute-start.6 = (bf16[2,960,128]{2,1,0:T(8,128)(2,1)}, bf16[2,960,128]{2,1,0:T(8,128)(2,1)S(1)}, u32[]{:S(2)}, u32[]{:S(2)}) collective-permute-start(bf16[2,960,128]{2,1,0:T(8,128)(2,1)} %source_ref.1), channel_id=1, source_target_pairs={{0,4},{4,0},{8,12},{12,8},{16,20},{20,16},{24,28},{28,24},{1,5},{5... | collective-permute-start | bytes 1474568 | tf_op jit(solution)/shard_map/ppermute | solution.py:20
  4.5 20.4 %collective-permute-start.2 = (bf16[2,960,128]{2,1,0:T(8,128)(2,1)}, bf16[2,960,128]{2,1,0:T(8,128)(2,1)S(1)}, u32[]{:S(2)}, u32[]{:S(2)}) collective-permute-start(bf16[2,960,128]{2,1,0:T(8,128)(2,1)} %source_ref.1), channel_id=1, source_target_pairs={{0,2},{2,3},{3,1},{1,0},{4,6},{6,7},{7,5},{5,4},{8,10},{10,11},{11... | collective-permute-start | bytes 1474568 | tf_op jit(solution)/shard_map/ppermute | solution.py:266
  7.1 16.7 %collective-permute-start.3 = (bf16[960,128]{1,0:T(8,128)(2,1)}, bf16[960,128]{1,0:T(8,128)(2,1)S(1)}, u32[]{:S(2)}, u32[]{:S(2)}) collective-permute-start(bf16[960,128]{1,0:T(8,128)(2,1)} %int_ref.1), channel_id=1, source_target_pairs={{0,2},{2,3},{3,1},{1,0},{4,6},{6,7},{7,5},{5,4},{8,10},{10,11},{11... | collective-permute-start | bytes 737288 | tf_op jit(solution)/shard_map/ppermute | solution.py:266
  9.4 1.0 %copy-start = (bf16[2,960,128]{2,1,0:T(8,128)(2,1)S(1)}, bf16[2,960,128]{2,1,0:T(8,128)(2,1)}, u32[]{:S(2)}) copy-start(bf16[2,960,128]{2,1,0:T(8,128)(2,1)} %source_ref.1) | copy-start | bytes 1474564
  10.7 29.1 %copy-start.1 = (bf16[960,128]{1,0:T(8,128)(2,1)S(1)}, bf16[960,128]{1,0:T(8,128)(2,1)}, u32[]{:S(2)}) copy-start(bf16[960,128]{1,0:T(8,128)(2,1)} %int_ref.1) | copy-start | bytes 737284
  15.9 8.4 %collective-permute-start.4 = (bf16[960,128]{1,0:T(8,128)(2,1)S(1)}, bf16[960,128]{1,0:T(8,128)(2,1)S(1)}, u32[]{:S(2)}, u32[]{:S(2)}) collective-permute-start(bf16[960,128]{1,0:T(8,128)(2,1)S(1)} %slice_bitcast_fusion.1), channel_id=1, source_target_pairs={{0,8},{4,12},{8,0},{12,4},{16,24},{20,28},{24,16},{28,20},{1,9},{5... | collective-permute-start | bytes 737288 | tf_op jit(solution)/shard_map/ppermute | solution.py:20
  17.5 6.9 %collective-permute-start.5 = (bf16[960,128]{1,0:T(8,128)(2,1)S(1)}, bf16[960,128]{1,0:T(8,128)(2,1)S(1)}, u32[]{:S(2)}, u32[]{:S(2)}) collective-permute-start(bf16[960,128]{1,0:T(8,128)(2,1)S(1)} %slice_bitcast_fusion), channel_id=1, source_target_pairs={{0,16},{4,20},{8,24},{12,28},{16,0},{20,4},{24,8},{28,12},{1,17},{... | collective-permute-start | bytes 737288 | tf_op jit(solution)/shard_map/ppermute | solution.py:20
  23.8 4.3 %collective-permute-start.7 = (bf16[2,960,128]{2,1,0:T(8,128)(2,1)S(1)}, bf16[2,960,128]{2,1,0:T(8,128)(2,1)S(1)}, u32[]{:S(2)}, u32[]{:S(2)}) collective-permute-start(bf16[2,960,128]{2,1,0:T(8,128)(2,1)S(1)} %collective-permute-done.refs_1_), channel_id=1, source_target_pairs={{0,4},{4,0},{8,12},{12,8},{16,20},{20,16},{24,28},{28,24},{1,5},{5... | collective-permute-start | bytes 1474568 | tf_op jit(solution)/shard_map/ppermute | solution.py:20
  23.8 4.3 %collective-permute-start.8 = (bf16[2,960,128]{2,1,0:T(8,128)(2,1)S(1)}, bf16[2,960,128]{2,1,0:T(8,128)(2,1)S(1)}, u32[]{:S(2)}, u32[]{:S(2)}) collective-permute-start(bf16[2,960,128]{2,1,0:T(8,128)(2,1)S(1)} %collective-permute-done.1.refs_2_), channel_id=1, source_target_pairs={{0,4},{4,0},{8,12},{12,8},{16,20},{20,16},{24,28},{28,24},{1,5},{5... | collective-permute-start | bytes 1474568 | tf_op jit(solution)/shard_map/ppermute | solution.py:20
  24.3 3.8 %collective-permute-start.9 = (bf16[960,128]{1,0:T(8,128)(2,1)S(1)}, bf16[960,128]{1,0:T(8,128)(2,1)S(1)}, u32[]{:S(2)}, u32[]{:S(2)}) collective-permute-start(bf16[960,128]{1,0:T(8,128)(2,1)S(1)} %collective-permute-done.4.refs_3_), channel_id=1, source_target_pairs={{0,4},{4,0},{8,12},{12,8},{16,20},{20,16},{24,28},{28,24},{1,5},{5... | collective-permute-start | bytes 737288 | tf_op jit(solution)/shard_map/ppermute | solution.py:20
  24.4 3.7 %collective-permute-start.10 = (bf16[960,128]{1,0:T(8,128)(2,1)S(1)}, bf16[960,128]{1,0:T(8,128)(2,1)S(1)}, u32[]{:S(2)}, u32[]{:S(2)}) collective-permute-start(bf16[960,128]{1,0:T(8,128)(2,1)S(1)} %collective-permute-done.5.refs_4_), channel_id=1, source_target_pairs={{0,4},{4,0},{8,12},{12,8},{16,20},{20,16},{24,28},{28,24},{1,5},{5... | collective-permute-start | bytes 737288 | tf_op jit(solution)/shard_map/ppermute | solution.py:20
  24.8 14.4 %collective-permute-start.11 = (bf16[2,960,128]{2,1,0:T(8,128)(2,1)S(1)}, bf16[2,960,128]{2,1,0:T(8,128)(2,1)S(1)}, u32[]{:S(2)}, u32[]{:S(2)}) collective-permute-start(bf16[2,960,128]{2,1,0:T(8,128)(2,1)S(1)} %collective-permute-done.2.refs_1_), channel_id=1, source_target_pairs={{0,2},{2,3},{3,1},{1,0},{4,6},{6,7},{7,5},{5,4},{8,10},{10,11},{11... | collective-permute-start | bytes 1474568 | tf_op jit(solution)/shard_map/ppermute | solution.py:266
  39.3 2.3 %collective-permute-start.12 = (bf16[3,960,128]{2,1,0:T(8,128)(2,1)S(1)}, bf16[3,960,128]{2,1,0:T(8,128)(2,1)S(1)}, u32[]{:S(2)}, u32[]{:S(2)}) collective-permute-start(bf16[3,960,128]{2,1,0:T(8,128)(2,1)S(1)} %get-tuple-element.49), channel_id=1, source_target_pairs={{0,4},{4,0},{8,12},{12,8},{16,20},{20,16},{24,28},{28,24},{1,5},{5... | collective-permute-start | bytes 2211848 | tf_op jit(solution)/shard_map/ppermute | solution.py:20
  39.3 3.3 %collective-permute-start.13 = (bf16[3,960,128]{2,1,0:T(8,128)(2,1)S(1)}, bf16[3,960,128]{2,1,0:T(8,128)(2,1)S(1)}, u32[]{:S(2)}, u32[]{:S(2)}) collective-permute-start(bf16[3,960,128]{2,1,0:T(8,128)(2,1)S(1)} %get-tuple-element.50), channel_id=1, source_target_pairs={{0,4},{4,0},{8,12},{12,8},{16,20},{20,16},{24,28},{28,24},{1,5},{5... | collective-permute-start | bytes 2211848 | tf_op jit(solution)/shard_map/ppermute | solution.py:20
  42.8 1.4 %collective-permute-start.14 = (bf16[4,128,128]{2,1,0:T(8,128)(2,1)S(1)}, bf16[4,128,128]{2,1,0:T(8,128)(2,1)S(1)}, u32[]{:S(2)}, u32[]{:S(2)}) collective-permute-start(bf16[4,128,128]{2,1,0:T(8,128)(2,1)S(1)} %get-tuple-element.60), channel_id=1, source_target_pairs={{0,4},{4,0},{8,12},{12,8},{16,20},{20,16},{24,28},{28,24},{1,5},{5... | collective-permute-start | bytes 393224 | tf_op jit(solution)/shard_map/ppermute | solution.py:20
  43.1 14.1 %collective-permute-start.17 = (bf16[2,960,128]{2,1,0:T(8,128)(2,1)S(1)}, bf16[2,960,128]{2,1,0:T(8,128)(2,1)S(1)}, u32[]{:S(2)}, u32[]{:S(2)}) collective-permute-start(bf16[2,960,128]{2,1,0:T(8,128)(2,1)S(1)} %get-tuple-element.61), channel_id=1, source_target_pairs={{0,8},{4,12},{8,0},{12,4},{16,24},{20,28},{24,16},{28,20},{1,9},{5... | collective-permute-start | bytes 1474568 | tf_op jit(solution)/shard_map/ppermute | solution.py:20
  43.6 13.6 %collective-permute-start.18 = (bf16[2,960,128]{2,1,0:T(8,128)(2,1)S(1)}, bf16[2,960,128]{2,1,0:T(8,128)(2,1)S(1)}, u32[]{:S(2)}, u32[]{:S(2)}) collective-permute-start(bf16[2,960,128]{2,1,0:T(8,128)(2,1)S(1)} %get-tuple-element.62), channel_id=1, source_target_pairs={{0,16},{4,20},{8,24},{12,28},{16,0},{20,4},{24,8},{28,12},{1,17},{... | collective-permute-start | bytes 1474568 | tf_op jit(solution)/shard_map/ppermute | solution.py:20
  44.3 6.1 %collective-permute-start.16 = (bf16[128,128]{1,0:T(8,128)(2,1)S(1)}, bf16[128,128]{1,0:T(8,128)(2,1)S(1)}, u32[]{:S(2)}, u32[]{:S(2)}) collective-permute-start(bf16[128,128]{1,0:T(8,128)(2,1)S(1)} %get-tuple-element.73), channel_id=1, source_target_pairs={{0,3},{2,1},{3,0},{1,2},{4,7},{6,5},{7,4},{5,6},{8,11},{10,9},{11,... | collective-permute-start | bytes 98312 | tf_op jit(solution)/shard_map/ppermute | solution.py:266
  46.7 4.8 %collective-permute-start.15 = (bf16[128,128]{1,0:T(8,128)(2,1)S(1)}, bf16[128,128]{1,0:T(8,128)(2,1)S(1)}, u32[]{:S(2)}, u32[]{:S(2)}) collective-permute-start(bf16[128,128]{1,0:T(8,128)(2,1)S(1)} %get-tuple-element.74), channel_id=1, source_target_pairs={{0,1},{2,0},{3,2},{1,3},{4,5},{6,4},{7,6},{5,7},{8,9},{10,8},{11,1... | collective-permute-start | bytes 98312 | tf_op jit(solution)/shard_map/ppermute | solution.py:266
  51.5 7.8 %collective-permute-start.19 = (bf16[4,128,128]{2,1,0:T(8,128)(2,1)S(1)}, bf16[4,128,128]{2,1,0:T(8,128)(2,1)S(1)}, u32[]{:S(2)}, u32[]{:S(2)}) collective-permute-start(bf16[4,128,128]{2,1,0:T(8,128)(2,1)S(1)} %pad_maximum_fusion), channel_id=1, source_target_pairs={{0,8},{4,12},{8,0},{12,4},{16,24},{20,28},{24,16},{28,20},{1,9},{5... | collective-permute-start | bytes 393224 | tf_op jit(solution)/shard_map/ppermute | solution.py:20
  53.0 12.6 %collective-permute-start.21 = (bf16[2,960,128]{2,1,0:T(8,128)(2,1)S(1)}, bf16[2,960,128]{2,1,0:T(8,128)(2,1)S(1)}, u32[]{:S(2)}, u32[]{:S(2)}) collective-permute-start(bf16[2,960,128]{2,1,0:T(8,128)(2,1)S(1)} %collective-permute-done.11.refs_2_), channel_id=1, source_target_pairs={{0,2},{2,3},{3,1},{1,0},{4,6},{6,7},{7,5},{5,4},{8,10},{10,11},{11... | collective-permute-start | bytes 1474568 | tf_op jit(solution)/shard_map/ppermute | solution.py:266
  59.4 6.1 %collective-permute-start.20 = (bf16[4,128,128]{2,1,0:T(8,128)(2,1)S(1)}, bf16[4,128,128]{2,1,0:T(8,128)(2,1)S(1)}, u32[]{:S(2)}, u32[]{:S(2)}) collective-permute-start(bf16[4,128,128]{2,1,0:T(8,128)(2,1)S(1)} %add_convert_fusion.5), channel_id=1, source_target_pairs={{0,16},{4,20},{8,24},{12,28},{16,0},{20,4},{24,8},{28,12},{1,17},{... | collective-permute-start | bytes 393224 | tf_op jit(solution)/shard_map/ppermute | solution.py:20
  60.0 7.7 %collective-permute-start.23 = (bf16[2,960,128]{2,1,0:T(8,128)(2,1)S(1)}, bf16[2,960,128]{2,1,0:T(8,128)(2,1)S(1)}, u32[]{:S(2)}, u32[]{:S(2)}) collective-permute-start(bf16[2,960,128]{2,1,0:T(8,128)(2,1)S(1)} %get-tuple-element.68), channel_id=1, source_target_pairs={{0,4},{4,0},{8,12},{12,8},{16,20},{20,16},{24,28},{28,24},{1,5},{5... | collective-permute-start | bytes 1474568 | tf_op jit(solution)/shard_map/ppermute | solution.py:20
  60.0 8.4 %collective-permute-start.25 = (bf16[1,960,128]{2,1,0:T(8,128)(2,1)S(1)}, bf16[1,960,128]{2,1,0:T(8,128)(2,1)S(1)}, u32[]{:S(2)}, u32[]{:S(2)}) collective-permute-start(bf16[1,960,128]{2,1,0:T(8,128)(2,1)S(1)} %bitcast.24), channel_id=1, source_target_pairs={{0,8},{4,12},{8,0},{12,4},{16,24},{20,28},{24,16},{28,20},{1,9},{5... | collective-permute-start | bytes 737288 | tf_op jit(solution)/shard_map/ppermute | solution.py:20
  60.5 9.2 %collective-permute-start.24 = (bf16[1,960,128]{2,1,0:T(8,128)(2,1)S(1)}, bf16[1,960,128]{2,1,0:T(8,128)(2,1)S(1)}, u32[]{:S(2)}, u32[]{:S(2)}) collective-permute-start(bf16[1,960,128]{2,1,0:T(8,128)(2,1)S(1)} %bitcast.23), channel_id=1, source_target_pairs={{0,16},{4,20},{8,24},{12,28},{16,0},{20,4},{24,8},{28,12},{1,17},{... | collective-permute-start | bytes 737288 | tf_op jit(solution)/shard_map/ppermute | solution.py:20
  65.6 1.4 %collective-permute-start.22 = (bf16[4,128,128]{2,1,0:T(8,128)(2,1)S(1)}, bf16[4,128,128]{2,1,0:T(8,128)(2,1)S(1)}, u32[]{:S(2)}, u32[]{:S(2)}) collective-permute-start(bf16[4,128,128]{2,1,0:T(8,128)(2,1)S(1)} %add_convert_fusion.4.mine_ref), channel_id=1, source_target_pairs={{0,4},{4,0},{8,12},{12,8},{16,20},{20,16},{24,28},{28,24},{1,5},{5... | collective-permute-start | bytes 393224 | tf_op jit(solution)/shard_map/ppermute | solution.py:20

commit v8 on v7

--- a/solution.py
+++ b/solution.py
@@ -109,8 +109,15 @@
     weight = weight.astype(BF16)
     block = ladder_ref[0]
     column_amp, row_amp = weight * amp[at_column, :], weight * amp[at_row, :]
-    acc[at_row, :] += lax.dot_general(block, column_amp, (((1,), (0,)), ((), ())), preferred_element_type=F32)
-    acc[at_column, :] += lax.dot_general(block, row_amp, (((0,), (0,)), ((), ())), preferred_element_type=F32)
+    chunk = BLOCK // 3
+    for first in range(0, BLOCK, chunk):
+        span = slice(first, first + chunk)
+        here = pl.ds(pl.multiple_of(row_block * BLOCK + first, chunk), chunk)
+        acc[here, :] += jnp.dot(block[span], column_amp, preferred_element_type=F32)
+        here = pl.ds(pl.multiple_of(column_block * BLOCK + first, chunk), chunk)
+        acc[here, :] += lax.dot_general(
+            block[:, span], row_amp, (((0,), (0,)), ((), ())), preferred_element_type=F32
+        )
 
     @pl.when(step == pl.num_programs(0) - 1)
     def _():
@@ -291,22 +298,27 @@
         real, imag, own = partials[3:]
         real_in, imag_in, own_in = (swap(value, tri_size, 0) for value in partials[:3])
         real_in, imag_in, hold, give = lax.optimization_barrier((real_in, imag_in, hold, give))
-        by_x = add(real[:2], real_in[:2]).astype(BF16)
-        by_y = add(imag[:2], imag_in[:2]).astype(BF16)
-        by_x, by_y, hold, give = lax.optimization_barrier((by_x, by_y, hold, give))
-        by_x, by_y = swap(by_x, tri_size, 1), swap(by_y, tri_size, 2)
+        far_x, far_y, near_x, near_y = (
+            add(kept[i], came[i]).astype(BF16)[None]
+            for i, kept, came in ((1, real, real_in), (1, imag, imag_in), (0, real, real_in), (0, imag, imag_in))
+        )
+        far_x, far_y, near_x, near_y, hold, give = lax.optimization_barrier(
+            (far_x, far_y, near_x, near_y, hold, give)
+        )
+        far_x, far_y = swap(far_x, tri_size, 1), swap(far_y, tri_size, 2)
+        near_x, near_y = swap(near_x, tri_size, 1), swap(near_y, tri_size, 2)
         mine = shift(add(hold, swap(give, tri_size, 0)).astype(BF16))
+        mine, far_x, far_y = lax.optimization_barrier((mine, far_x, far_y))
         last = turn(after(ring[-1], mine))
-        received = swap(mine, tri_size, 1)
-        then_y = add(real[2], real_in[2], by_x[1]).astype(BF16)
-        then_x = add(imag[2], imag_in[2], by_y[1]).astype(BF16)
-        then_y, then_x, received = lax.optimization_barrier((then_y, then_x, received))
-        then_y, then_x = swap(then_y[None], tri_size, 2), swap(then_x[None], tri_size, 1)
-        mine = add(mine, received).astype(BF16)
-        received, last = lax.optimization_barrier((swap(mine, tri_size, 2), last))
+        then_y = swap(add(real[2], real_in[2], far_x[0]).astype(BF16)[None], tri_size, 2)
+        then_x = swap(add(imag[2], imag_in[2], far_y[0]).astype(BF16)[None], tri_size, 1)
+        mine = add(mine, swap(mine, tri_size, 1)).astype(BF16)
+        received, last, then_y, then_x, near_x, near_y = lax.optimization_barrier(
+            (swap(mine, tri_size, 2), last, then_y, then_x, near_x, near_y)
+        )
         mine = add(mine, received).astype(BF16)
         terms = [(own, 0, 0), (own, 1, 1), (own_in, 0, 0), (own_in, 1, 1)]
-        terms += [(by_x, 0, 0), (by_y, 1, 0), (then_y, 0, 0), (then_x, 1, 0)]
+        terms += [(near_x, 0, 0), (near_y, 1, 0), (then_y, 0, 0), (then_x, 1, 0)]
     else:
         last = turn(ring[-1])
         terms = scatter_plain(partials[0].reshape(tri_size, 2, *amplitudes.shape[1:]), tri_size)

time: 71.1 us -> 70.3 us (0.989)
  waiting for transfers between devices: 29.9 us -> 23.9 us
  starting transfers between devices: 24.5 us -> 29.8 us
    ppermute x6, starting transfers between devices: 11.1 us -> 14.6 us  [turn(): lax.ppermute(value, 'vp', [(order[i], order[(i + distance) % vp_size]) fo...]
    ppermute x20 -> x22, waiting for transfers between devices: 20.4 us -> 16.8 us  [swap(): return lax.ppermute(value, 'tri', pairs)]
    ppermute x6, waiting for transfers between devices: 9.52 us -> 7.07 us  [turn(): lax.ppermute(value, 'vp', [(order[i], order[(i + distance) % vp_size]) fo...]
    ppermute x20 -> x22, starting transfers between devices: 13.5 us -> 15.2 us  [swap(): return lax.ppermute(value, 'tri', pairs)]
  transfers between devices with their start and end apart: 26 -> 28, of which waited for: 14 -> 12; matrix products, arithmetic and copies ran while one was open for 2% -> 2% of each run, Pallas kernels for 18% -> 18%
where the time goes in v8:
time: 70.3 us; the launch traced here: 70 us
  starting transfers between devices  29.8 us (42%)
  waiting for transfers between devices  23.9 us (34%)
  Pallas kernels  13.7 us (19%)
  other arithmetic  1.32 us (2%)
  local copies, waits for them, and re-layouts  1.08 us (2%)
    ppermute x22, waiting for transfers between devices, swap(): return lax.ppermute(value, 'tri', pairs)  16.8 us
    ppermute x22, starting transfers between devices, swap(): return lax.ppermute(value, 'tri', pairs)  15.2 us
    ppermute x6, starting transfers between devices, turn(): lax.ppermute(value, 'vp', [(order[i], order[(i + distance) % vp_size]) fo...  14.6 us
    pallas_call x1, Pallas kernels, ladder(): pl.pallas_call(functools.partial(ladder_kernel, [(mask, part) for _, mask...  11 us
    ppermute x6, waiting for transfers between devices, turn(): lax.ppermute(value, 'vp', [(order[i], order[(i + distance) % vp_size]) fo...  7.07 us
  transfers between devices with their start and end apart: 28, of which 12 were waited for; matrix products, arithmetic and copies ran while one was open for 2% of the time, Pallas kernels for 18%

profile of v8, /device:TPU:0, one launch (start us, length us, event | category | flops | bytes accessed | tf_op | source)
XLA Modules:
  0.0 70.0 jit_solution(16355165724712559665)
XLA Ops:
  0.0 3.0 %collective-permute-start.1 = (bf16[2,960,128]{2,1,0:T(8,128)(2,1)}, bf16[2,960,128]{2,1,0:T(8,128)(2,1)S(1)}, u32[]{:S(2)}, u32[]{:S(2)}) collective-permute-start(bf16[2,960,128]{2,1,0:T(8,128)(2,1)} %source_ref.1), channel_id=1, source_target_pairs={{0,16},{4,20},{8,24},{12,28},{16,0},{20,4},{24,8},{28,12},{1,17},{... | collective-permute-start | bytes 1474568 | tf_op jit(solution)/shard_map/ppermute | solution.py:20
  3.0 1.5 %collective-permute-start = (bf16[2,960,128]{2,1,0:T(8,128)(2,1)}, bf16[2,960,128]{2,1,0:T(8,128)(2,1)S(1)}, u32[]{:S(2)}, u32[]{:S(2)}) collective-permute-start(bf16[2,960,128]{2,1,0:T(8,128)(2,1)} %source_ref.1), channel_id=1, source_target_pairs={{0,8},{4,12},{8,0},{12,4},{16,24},{20,28},{24,16},{28,20},{1,9},{5... | collective-permute-start | bytes 1474568 | tf_op jit(solution)/shard_map/ppermute | solution.py:20
  4.5 2.6 %collective-permute-start.2 = (bf16[2,960,128]{2,1,0:T(8,128)(2,1)}, bf16[2,960,128]{2,1,0:T(8,128)(2,1)S(1)}, u32[]{:S(2)}, u32[]{:S(2)}) collective-permute-start(bf16[2,960,128]{2,1,0:T(8,128)(2,1)} %source_ref.1), channel_id=1, source_target_pairs={{0,2},{2,3},{3,1},{1,0},{4,6},{6,7},{7,5},{5,4},{8,10},{10,11},{11... | collective-permute-start | bytes 1474568 | tf_op jit(solution)/shard_map/ppermute | solution.py:273
  7.1 1.6 %collective-permute-start.3 = (bf16[960,128]{1,0:T(8,128)(2,1)}, bf16[960,128]{1,0:T(8,128)(2,1)S(1)}, u32[]{:S(2)}, u32[]{:S(2)}) collective-permute-start(bf16[960,128]{1,0:T(8,128)(2,1)} %int_ref.1), channel_id=1, source_target_pairs={{0,2},{2,3},{3,1},{1,0},{4,6},{6,7},{7,5},{5,4},{8,10},{10,11},{11... | collective-permute-start | bytes 737288 | tf_op jit(solution)/shard_map/ppermute | solution.py:273
  8.6 0.7 %pad_add_fusion.small_ref = s32[8]{0:T(128)S(1)} fusion(s32[7]{0:T(128)} %param.7, s32[1]{0:T(128)} %bitcast), kind=kLoop, calls=%fused_computation.14 | loop fusion | flops 8 | bytes 64 | tf_op jit(solution)/shard_map/concatenate | solution.py:279
  9.4 1.0 %copy-done = bf16[2,960,128]{2,1,0:T(8,128)(2,1)S(1)} copy-done((bf16[2,960,128]{2,1,0:T(8,128)(2,1)S(1)}, bf16[2,960,128]{2,1,0:T(8,128)(2,1)}, u32[]{:S(2)}) %copy-start) | copy-done | bytes 491544
  10.7 3.7 %collective-permute-done.1.refs_2_ = bf16[2,960,128]{2,1,0:T(8,128)(2,1)S(1)} collective-permute-done((bf16[2,960,128]{2,1,0:T(8,128)(2,1)}, bf16[2,960,128]{2,1,0:T(8,128)(2,1)S(1)}, u32[]{:S(2)}, u32[]{:S(2)}) %collective-permute-start.1) | collective-permute-done | bytes 491552 | tf_op jit(solution)/shard_map/ppermute | solution.py:20
  14.4 1.5 %collective-permute-done.refs_1_ = bf16[2,960,128]{2,1,0:T(8,128)(2,1)S(1)} collective-permute-done((bf16[2,960,128]{2,1,0:T(8,128)(2,1)}, bf16[2,960,128]{2,1,0:T(8,128)(2,1)S(1)}, u32[]{:S(2)}, u32[]{:S(2)}) %collective-permute-start) | collective-permute-done | bytes 491552 | tf_op jit(solution)/shard_map/ppermute | solution.py:20
  15.9 1.6 %collective-permute-start.4 = (bf16[960,128]{1,0:T(8,128)(2,1)S(1)}, bf16[960,128]{1,0:T(8,128)(2,1)S(1)}, u32[]{:S(2)}, u32[]{:S(2)}) collective-permute-start(bf16[960,128]{1,0:T(8,128)(2,1)S(1)} %slice_bitcast_fusion.1), channel_id=1, source_target_pairs={{0,8},{4,12},{8,0},{12,4},{16,24},{20,28},{24,16},{28,20},{1,9},{5... | collective-permute-start | bytes 737288 | tf_op jit(solution)/shard_map/ppermute | solution.py:20
  18.0 5.8 %collective-permute-done.3.last_ref = bf16[960,128]{1,0:T(8,128)(2,1)S(1)} collective-permute-done((bf16[960,128]{1,0:T(8,128)(2,1)}, bf16[960,128]{1,0:T(8,128)(2,1)S(1)}, u32[]{:S(2)}, u32[]{:S(2)}) %collective-permute-start.3) | collective-permute-done | bytes 245792 | tf_op jit(solution)/shard_map/ppermute | solution.py:273
  23.8 0.5 collective-permute-start.8
  24.8 3.3 %collective-permute-start.11 = (bf16[2,960,128]{2,1,0:T(8,128)(2,1)S(1)}, bf16[2,960,128]{2,1,0:T(8,128)(2,1)S(1)}, u32[]{:S(2)}, u32[]{:S(2)}) collective-permute-start(bf16[2,960,128]{2,1,0:T(8,128)(2,1)S(1)} %collective-permute-done.2.refs_1_), channel_id=1, source_target_pairs={{0,2},{2,3},{3,1},{1,0},{4,6},{6,7},{7,5},{5,4},{8,10},{10,11},{11... | collective-permute-start | bytes 1474568 | tf_op jit(solution)/shard_map/ppermute | solution.py:273
  28.1 11.0 %ladder.1 = (bf16[3,960,128]{2,1,0:T(8,128)(2,1)S(1)}, bf16[3,960,128]{2,1,0:T(8,128)(2,1)S(1)}, bf16[2,960,128]{2,1,0:T(8,128)(2,1)S(1)}, bf16[3,960,128]{2,1,0...) custom-call(s32[8]{0:T(128)S(1)} %pad_add_fusion.small_ref, ...), custom_call_target="tpu_custom_call" | custom-call | flops 4227858432 | bytes 16121856 | tf_op jit(solution)/shard_map/ladder/pallas_call | solution.py:134
  39.8 0.6 contract.1
  40.3 1.1 %collective-permute-done.12 = bf16[3,960,128]{2,1,0:T(8,128)(2,1)S(1)} collective-permute-done((bf16[3,960,128]{2,1,0:T(8,128)(2,1)S(1)}, bf16[3,960,128]{2,1,0:T(8,128)(2,1)S(1)}, u32[]{:S(2)}, u32[]{:S(2)}) %collective-permute-start.12) | collective-permute-done | bytes 737312 | tf_op jit(solution)/shard_map/ppermute | solution.py:20
  41.5 1.1 %collective-permute-done.13 = bf16[3,960,128]{2,1,0:T(8,128)(2,1)S(1)} collective-permute-done((bf16[3,960,128]{2,1,0:T(8,128)(2,1)S(1)}, bf16[3,960,128]{2,1,0:T(8,128)(2,1)S(1)}, u32[]{:S(2)}, u32[]{:S(2)}) %collective-permute-start.13) | collective-permute-done | bytes 737312 | tf_op jit(solution)/shard_map/ppermute | solution.py:20
  43.0 0.5 collective-permute-start.17
  44.3 2.4 %collective-permute-start.16 = (bf16[128,128]{1,0:T(8,128)(2,1)S(1)}, bf16[128,128]{1,0:T(8,128)(2,1)S(1)}, u32[]{:S(2)}, u32[]{:S(2)}) collective-permute-start(bf16[128,128]{1,0:T(8,128)(2,1)S(1)} %get-tuple-element.89), channel_id=1, source_target_pairs={{0,3},{2,1},{3,0},{1,2},{4,7},{6,5},{7,4},{5,6},{8,11},{10,9},{11,... | collective-permute-start | bytes 98312 | tf_op jit(solution)/shard_map/ppermute | solution.py:273
  46.6 1.2 %collective-permute-start.15 = (bf16[128,128]{1,0:T(8,128)(2,1)S(1)}, bf16[128,128]{1,0:T(8,128)(2,1)S(1)}, u32[]{:S(2)}, u32[]{:S(2)}) collective-permute-start(bf16[128,128]{1,0:T(8,128)(2,1)S(1)} %get-tuple-element.90), channel_id=1, source_target_pairs={{0,1},{2,0},{3,2},{1,3},{4,5},{6,4},{7,6},{5,7},{8,9},{10,8},{11,1... | collective-permute-start | bytes 98312 | tf_op jit(solution)/shard_map/ppermute | solution.py:273
  47.8 1.3 %collective-permute-start.24 = (bf16[1,960,128]{2,1,0:T(8,128)(2,1)S(1)}, bf16[1,960,128]{2,1,0:T(8,128)(2,1)S(1)}, u32[]{:S(2)}, u32[]{:S(2)}) collective-permute-start(bf16[1,960,128]{2,1,0:T(8,128)(2,1)S(1)} %get-tuple-element.73), channel_id=1, source_target_pairs={{0,8},{4,12},{8,0},{12,4},{16,24},{20,28},{24,16},{28,20},{1,9},{5... | collective-permute-start | bytes 737288 | tf_op jit(solution)/shard_map/ppermute | solution.py:20
  49.2 1.2 %collective-permute-done.16 = bf16[128,128]{1,0:T(8,128)(2,1)S(1)} collective-permute-done((bf16[128,128]{1,0:T(8,128)(2,1)S(1)}, bf16[128,128]{1,0:T(8,128)(2,1)S(1)}, u32[]{:S(2)}, u32[]{:S(2)}) %collective-permute-start.16) | collective-permute-done | bytes 32800 | tf_op jit(solution)/shard_map/ppermute | solution.py:273
  50.4 1.1 %collective-permute-start.25 = (bf16[1,960,128]{2,1,0:T(8,128)(2,1)S(1)}, bf16[1,960,128]{2,1,0:T(8,128)(2,1)S(1)}, u32[]{:S(2)}, u32[]{:S(2)}) collective-permute-start(bf16[1,960,128]{2,1,0:T(8,128)(2,1)S(1)} %get-tuple-element.74), channel_id=1, source_target_pairs={{0,16},{4,20},{8,24},{12,28},{16,0},{20,4},{24,8},{28,12},{1,17},{... | collective-permute-start | bytes 737288 | tf_op jit(solution)/shard_map/ppermute | solution.py:20
  51.8 1.5 %collective-permute-start.19 = (bf16[4,128,128]{2,1,0:T(8,128)(2,1)S(1)}, bf16[4,128,128]{2,1,0:T(8,128)(2,1)S(1)}, u32[]{:S(2)}, u32[]{:S(2)}) collective-permute-start(bf16[4,128,128]{2,1,0:T(8,128)(2,1)S(1)} %pad_maximum_fusion), channel_id=1, source_target_pairs={{0,8},{4,12},{8,0},{12,4},{16,24},{20,28},{24,16},{28,20},{1,9},{5... | collective-permute-start | bytes 393224 | tf_op jit(solution)/shard_map/ppermute | solution.py:20
  53.3 3.6 %collective-permute-start.21 = (bf16[2,960,128]{2,1,0:T(8,128)(2,1)S(1)}, bf16[2,960,128]{2,1,0:T(8,128)(2,1)S(1)}, u32[]{:S(2)}, u32[]{:S(2)}) collective-permute-start(bf16[2,960,128]{2,1,0:T(8,128)(2,1)S(1)} %collective-permute-done.11.refs_2_), channel_id=1, source_target_pairs={{0,2},{2,3},{3,1},{1,0},{4,6},{6,7},{7,5},{5,4},{8,10},{10,11},{11... | collective-permute-start | bytes 1474568 | tf_op jit(solution)/shard_map/ppermute | solution.py:273
  57.5 1.8 %collective-permute-done.19 = bf16[4,128,128]{2,1,0:T(8,128)(2,1)S(1)} collective-permute-done((bf16[4,128,128]{2,1,0:T(8,128)(2,1)S(1)}, bf16[4,128,128]{2,1,0:T(8,128)(2,1)S(1)}, u32[]{:S(2)}, u32[]{:S(2)}) %collective-permute-start.19) | collective-permute-done | bytes 131104 | tf_op jit(solution)/shard_map/ppermute | solution.py:20
  59.3 0.5 collective-permute-start.23
  59.9 0.8 %collective-permute-start.20 = (bf16[4,128,128]{2,1,0:T(8,128)(2,1)S(1)}, bf16[4,128,128]{2,1,0:T(8,128)(2,1)S(1)}, u32[]{:S(2)}, u32[]{:S(2)}) collective-permute-start(bf16[4,128,128]{2,1,0:T(8,128)(2,1)S(1)} %add_convert_fusion.7), channel_id=1, source_target_pairs={{0,16},{4,20},{8,24},{12,28},{16,0},{20,4},{24,8},{28,12},{1,17},{... | collective-permute-start | bytes 393224 | tf_op jit(solution)/shard_map/ppermute | solution.py:20
  60.7 4.0 %collective-permute-done.22.refs_6_ = bf16[1,960,128]{2,1,0:T(8,128)(2,1)S(1)} collective-permute-done((bf16[1,960,128]{2,1,0:T(8,128)(2,1)S(1)}, bf16[1,960,128]{2,1,0:T(8,128)(2,1)S(1)}, u32[]{:S(2)}, u32[]{:S(2)}) %collective-permute-start.22) | collective-permute-done | bytes 245792 | tf_op jit(solution)/shard_map/ppermute | solution.py:20
  64.7 2.0 %collective-permute-done.23.refs_7_ = bf16[1,960,128]{2,1,0:T(8,128)(2,1)S(1)} collective-permute-done((bf16[1,960,128]{2,1,0:T(8,128)(2,1)S(1)}, bf16[1,960,128]{2,1,0:T(8,128)(2,1)S(1)}, u32[]{:S(2)}, u32[]{:S(2)}) %collective-permute-start.23) | collective-permute-done | bytes 245792 | tf_op jit(solution)/shard_map/ppermute | solution.py:20
  66.8 1.3 %collective-permute-done.26.other_ref = bf16[4,128,128]{2,1,0:T(8,128)(2,1)S(1)} collective-permute-done((bf16[4,128,128]{2,1,0:T(8,128)(2,1)S(1)}, bf16[4,128,128]{2,1,0:T(8,128)(2,1)S(1)}, u32[]{:S(2)}, u32[]{:S(2)}) %collective-permute-start.26) | collective-permute-done | bytes 131104 | tf_op jit(solution)/shard_map/ppermute | solution.py:20
  68.2 0.7 quadratic.1.base_ref
  68.9 1.1 %finish.1 = bf16[2,960,128]{2,1,0:T(8,128)(2,1)} custom-call(f32[2,960,128]{2,1,0:T(8,128)S(1)} %quadratic.1.base_ref, bf16[2,960,128]{2,1,0:T(8,128)(2,1)S(1)} %get-tuple-element.77.refs_0_.refs_1_, bf16[2,960,128]{2,1,0:T(8,128)(2,1)S(1)} %get-tuple-element.77.refs_0_.refs_1_, bf16[2,960,128]{2,1,0:T(8,128)(2,1)S(1)} %collective-permute-done.27.refs_2_.refs_3_, ...), custom_call_target="tpu_custom_call" | custom-call | tf_op jit(solution)/shard_map/finish/pallas_call | solution.py:247
  (44 shorter events, 4.2 us)
Async XLA Ops:
  0.0 14.4 %collective-permute-start.1 = (bf16[2,960,128]{2,1,0:T(8,128)(2,1)}, bf16[2,960,128]{2,1,0:T(8,128)(2,1)S(1)}, u32[]{:S(2)}, u32[]{:S(2)}) collective-permute-start(bf16[2,960,128]{2,1,0:T(8,128)(2,1)} %source_ref.1), channel_id=1, source_target_pairs={{0,16},{4,20},{8,24},{12,28},{16,0},{20,4},{24,8},{28,12},{1,17},{... | collective-permute-start | bytes 1474568 | tf_op jit(solution)/shard_map/ppermute | solution.py:20
  3.0 12.9 %collective-permute-start = (bf16[2,960,128]{2,1,0:T(8,128)(2,1)}, bf16[2,960,128]{2,1,0:T(8,128)(2,1)S(1)}, u32[]{:S(2)}, u32[]{:S(2)}) collective-permute-start(bf16[2,960,128]{2,1,0:T(8,128)(2,1)} %source_ref.1), channel_id=1, source_target_pairs={{0,8},{4,12},{8,0},{12,4},{16,24},{20,28},{24,16},{28,20},{1,9},{5... | collective-permute-start | bytes 1474568 | tf_op jit(solution)/shard_map/ppermute | solution.py:20
  4.5 19.3 %collective-permute-start.6 = (bf16[2,960,128]{2,1,0:T(8,128)(2,1)}, bf16[2,960,128]{2,1,0:T(8,128)(2,1)S(1)}, u32[]{:S(2)}, u32[]{:S(2)}) collective-permute-start(bf16[2,960,128]{2,1,0:T(8,128)(2,1)} %source_ref.1), channel_id=1, source_target_pairs={{0,4},{4,0},{8,12},{12,8},{16,20},{20,16},{24,28},{28,24},{1,5},{5... | collective-permute-start | bytes 1474568 | tf_op jit(solution)/shard_map/ppermute | solution.py:20
  4.5 20.4 %collective-permute-start.2 = (bf16[2,960,128]{2,1,0:T(8,128)(2,1)}, bf16[2,960,128]{2,1,0:T(8,128)(2,1)S(1)}, u32[]{:S(2)}, u32[]{:S(2)}) collective-permute-start(bf16[2,960,128]{2,1,0:T(8,128)(2,1)} %source_ref.1), channel_id=1, source_target_pairs={{0,2},{2,3},{3,1},{1,0},{4,6},{6,7},{7,5},{5,4},{8,10},{10,11},{11... | collective-permute-start | bytes 1474568 | tf_op jit(solution)/shard_map/ppermute | solution.py:273
  7.1 16.7 %collective-permute-start.3 = (bf16[960,128]{1,0:T(8,128)(2,1)}, bf16[960,128]{1,0:T(8,128)(2,1)S(1)}, u32[]{:S(2)}, u32[]{:S(2)}) collective-permute-start(bf16[960,128]{1,0:T(8,128)(2,1)} %int_ref.1), channel_id=1, source_target_pairs={{0,2},{2,3},{3,1},{1,0},{4,6},{6,7},{7,5},{5,4},{8,10},{10,11},{11... | collective-permute-start | bytes 737288 | tf_op jit(solution)/shard_map/ppermute | solution.py:273
  9.4 1.0 %copy-start = (bf16[2,960,128]{2,1,0:T(8,128)(2,1)S(1)}, bf16[2,960,128]{2,1,0:T(8,128)(2,1)}, u32[]{:S(2)}) copy-start(bf16[2,960,128]{2,1,0:T(8,128)(2,1)} %source_ref.1) | copy-start | bytes 1474564
  10.7 29.0 %copy-start.1 = (bf16[960,128]{1,0:T(8,128)(2,1)S(1)}, bf16[960,128]{1,0:T(8,128)(2,1)}, u32[]{:S(2)}) copy-start(bf16[960,128]{1,0:T(8,128)(2,1)} %int_ref.1) | copy-start | bytes 737284
  15.9 8.4 %collective-permute-start.4 = (bf16[960,128]{1,0:T(8,128)(2,1)S(1)}, bf16[960,128]{1,0:T(8,128)(2,1)S(1)}, u32[]{:S(2)}, u32[]{:S(2)}) collective-permute-start(bf16[960,128]{1,0:T(8,128)(2,1)S(1)} %slice_bitcast_fusion.1), channel_id=1, source_target_pairs={{0,8},{4,12},{8,0},{12,4},{16,24},{20,28},{24,16},{28,20},{1,9},{5... | collective-permute-start | bytes 737288 | tf_op jit(solution)/shard_map/ppermute | solution.py:20
  17.5 6.9 %collective-permute-start.5 = (bf16[960,128]{1,0:T(8,128)(2,1)S(1)}, bf16[960,128]{1,0:T(8,128)(2,1)S(1)}, u32[]{:S(2)}, u32[]{:S(2)}) collective-permute-start(bf16[960,128]{1,0:T(8,128)(2,1)S(1)} %slice_bitcast_fusion), channel_id=1, source_target_pairs={{0,16},{4,20},{8,24},{12,28},{16,0},{20,4},{24,8},{28,12},{1,17},{... | collective-permute-start | bytes 737288 | tf_op jit(solution)/shard_map/ppermute | solution.py:20
  23.8 4.3 %collective-permute-start.7 = (bf16[2,960,128]{2,1,0:T(8,128)(2,1)S(1)}, bf16[2,960,128]{2,1,0:T(8,128)(2,1)S(1)}, u32[]{:S(2)}, u32[]{:S(2)}) collective-permute-start(bf16[2,960,128]{2,1,0:T(8,128)(2,1)S(1)} %collective-permute-done.refs_1_), channel_id=1, source_target_pairs={{0,4},{4,0},{8,12},{12,8},{16,20},{20,16},{24,28},{28,24},{1,5},{5... | collective-permute-start | bytes 1474568 | tf_op jit(solution)/shard_map/ppermute | solution.py:20
  23.8 4.3 %collective-permute-start.8 = (bf16[2,960,128]{2,1,0:T(8,128)(2,1)S(1)}, bf16[2,960,128]{2,1,0:T(8,128)(2,1)S(1)}, u32[]{:S(2)}, u32[]{:S(2)}) collective-permute-start(bf16[2,960,128]{2,1,0:T(8,128)(2,1)S(1)} %collective-permute-done.1.refs_2_), channel_id=1, source_target_pairs={{0,4},{4,0},{8,12},{12,8},{16,20},{20,16},{24,28},{28,24},{1,5},{5... | collective-permute-start | bytes 1474568 | tf_op jit(solution)/shard_map/ppermute | solution.py:20
  24.3 3.8 %collective-permute-start.9 = (bf16[960,128]{1,0:T(8,128)(2,1)S(1)}, bf16[960,128]{1,0:T(8,128)(2,1)S(1)}, u32[]{:S(2)}, u32[]{:S(2)}) collective-permute-start(bf16[960,128]{1,0:T(8,128)(2,1)S(1)} %collective-permute-done.4.refs_3_), channel_id=1, source_target_pairs={{0,4},{4,0},{8,12},{12,8},{16,20},{20,16},{24,28},{28,24},{1,5},{5... | collective-permute-start | bytes 737288 | tf_op jit(solution)/shard_map/ppermute | solution.py:20
  24.4 3.7 %collective-permute-start.10 = (bf16[960,128]{1,0:T(8,128)(2,1)S(1)}, bf16[960,128]{1,0:T(8,128)(2,1)S(1)}, u32[]{:S(2)}, u32[]{:S(2)}) collective-permute-start(bf16[960,128]{1,0:T(8,128)(2,1)S(1)} %collective-permute-done.5.refs_4_), channel_id=1, source_target_pairs={{0,4},{4,0},{8,12},{12,8},{16,20},{20,16},{24,28},{28,24},{1,5},{5... | collective-permute-start | bytes 737288 | tf_op jit(solution)/shard_map/ppermute | solution.py:20
  24.8 14.3 %collective-permute-start.11 = (bf16[2,960,128]{2,1,0:T(8,128)(2,1)S(1)}, bf16[2,960,128]{2,1,0:T(8,128)(2,1)S(1)}, u32[]{:S(2)}, u32[]{:S(2)}) collective-permute-start(bf16[2,960,128]{2,1,0:T(8,128)(2,1)S(1)} %collective-permute-done.2.refs_1_), channel_id=1, source_target_pairs={{0,2},{2,3},{3,1},{1,0},{4,6},{6,7},{7,5},{5,4},{8,10},{10,11},{11... | collective-permute-start | bytes 1474568 | tf_op jit(solution)/shard_map/ppermute | solution.py:273
  39.2 2.3 %collective-permute-start.12 = (bf16[3,960,128]{2,1,0:T(8,128)(2,1)S(1)}, bf16[3,960,128]{2,1,0:T(8,128)(2,1)S(1)}, u32[]{:S(2)}, u32[]{:S(2)}) collective-permute-start(bf16[3,960,128]{2,1,0:T(8,128)(2,1)S(1)} %get-tuple-element.55), channel_id=1, source_target_pairs={{0,4},{4,0},{8,12},{12,8},{16,20},{20,16},{24,28},{28,24},{1,5},{5... | collective-permute-start | bytes 2211848 | tf_op jit(solution)/shard_map/ppermute | solution.py:20
  39.3 3.3 %collective-permute-start.13 = (bf16[3,960,128]{2,1,0:T(8,128)(2,1)S(1)}, bf16[3,960,128]{2,1,0:T(8,128)(2,1)S(1)}, u32[]{:S(2)}, u32[]{:S(2)}) collective-permute-start(bf16[3,960,128]{2,1,0:T(8,128)(2,1)S(1)} %get-tuple-element.56), channel_id=1, source_target_pairs={{0,4},{4,0},{8,12},{12,8},{16,20},{20,16},{24,28},{28,24},{1,5},{5... | collective-permute-start | bytes 2211848 | tf_op jit(solution)/shard_map/ppermute | solution.py:20
  42.8 1.4 %collective-permute-start.14 = (bf16[4,128,128]{2,1,0:T(8,128)(2,1)S(1)}, bf16[4,128,128]{2,1,0:T(8,128)(2,1)S(1)}, u32[]{:S(2)}, u32[]{:S(2)}) collective-permute-start(bf16[4,128,128]{2,1,0:T(8,128)(2,1)S(1)} %get-tuple-element.66), channel_id=1, source_target_pairs={{0,4},{4,0},{8,12},{12,8},{16,20},{20,16},{24,28},{28,24},{1,5},{5... | collective-permute-start | bytes 393224 | tf_op jit(solution)/shard_map/ppermute | solution.py:20
  43.0 8.8 %collective-permute-start.17 = (bf16[1,960,128]{2,1,0:T(8,128)(2,1)S(1)}, bf16[1,960,128]{2,1,0:T(8,128)(2,1)S(1)}, u32[]{:S(2)}, u32[]{:S(2)}) collective-permute-start(bf16[1,960,128]{2,1,0:T(8,128)(2,1)S(1)} %get-tuple-element.67), channel_id=1, source_target_pairs={{0,8},{4,12},{8,0},{12,4},{16,24},{20,28},{24,16},{28,20},{1,9},{5... | collective-permute-start | bytes 737288 | tf_op jit(solution)/shard_map/ppermute | solution.py:20
  43.5 8.2 %collective-permute-start.18 = (bf16[1,960,128]{2,1,0:T(8,128)(2,1)S(1)}, bf16[1,960,128]{2,1,0:T(8,128)(2,1)S(1)}, u32[]{:S(2)}, u32[]{:S(2)}) collective-permute-start(bf16[1,960,128]{2,1,0:T(8,128)(2,1)S(1)} %get-tuple-element.68), channel_id=1, source_target_pairs={{0,16},{4,20},{8,24},{12,28},{16,0},{20,4},{24,8},{28,12},{1,17},{... | collective-permute-start | bytes 737288 | tf_op jit(solution)/shard_map/ppermute | solution.py:20
  44.3 6.2 %collective-permute-start.16 = (bf16[128,128]{1,0:T(8,128)(2,1)S(1)}, bf16[128,128]{1,0:T(8,128)(2,1)S(1)}, u32[]{:S(2)}, u32[]{:S(2)}) collective-permute-start(bf16[128,128]{1,0:T(8,128)(2,1)S(1)} %get-tuple-element.89), channel_id=1, source_target_pairs={{0,3},{2,1},{3,0},{1,2},{4,7},{6,5},{7,4},{5,6},{8,11},{10,9},{11,... | collective-permute-start | bytes 98312 | tf_op jit(solution)/shard_map/ppermute | solution.py:273
  46.6 4.9 %collective-permute-start.15 = (bf16[128,128]{1,0:T(8,128)(2,1)S(1)}, bf16[128,128]{1,0:T(8,128)(2,1)S(1)}, u32[]{:S(2)}, u32[]{:S(2)}) collective-permute-start(bf16[128,128]{1,0:T(8,128)(2,1)S(1)} %get-tuple-element.90), channel_id=1, source_target_pairs={{0,1},{2,0},{3,2},{1,3},{4,5},{6,4},{7,6},{5,7},{8,9},{10,8},{11,1... | collective-permute-start | bytes 98312 | tf_op jit(solution)/shard_map/ppermute | solution.py:273
  47.8 12.0 %collective-permute-start.24 = (bf16[1,960,128]{2,1,0:T(8,128)(2,1)S(1)}, bf16[1,960,128]{2,1,0:T(8,128)(2,1)S(1)}, u32[]{:S(2)}, u32[]{:S(2)}) collective-permute-start(bf16[1,960,128]{2,1,0:T(8,128)(2,1)S(1)} %get-tuple-element.73), channel_id=1, source_target_pairs={{0,8},{4,12},{8,0},{12,4},{16,24},{20,28},{24,16},{28,20},{1,9},{5... | collective-permute-start | bytes 737288 | tf_op jit(solution)/shard_map/ppermute | solution.py:20
  50.4 10.3 %collective-permute-start.25 = (bf16[1,960,128]{2,1,0:T(8,128)(2,1)S(1)}, bf16[1,960,128]{2,1,0:T(8,128)(2,1)S(1)}, u32[]{:S(2)}, u32[]{:S(2)}) collective-permute-start(bf16[1,960,128]{2,1,0:T(8,128)(2,1)S(1)} %get-tuple-element.74), channel_id=1, source_target_pairs={{0,16},{4,20},{8,24},{12,28},{16,0},{20,4},{24,8},{28,12},{1,17},{... | collective-permute-start | bytes 737288 | tf_op jit(solution)/shard_map/ppermute | solution.py:20
  51.8 7.5 %collective-permute-start.19 = (bf16[4,128,128]{2,1,0:T(8,128)(2,1)S(1)}, bf16[4,128,128]{2,1,0:T(8,128)(2,1)S(1)}, u32[]{:S(2)}, u32[]{:S(2)}) collective-permute-start(bf16[4,128,128]{2,1,0:T(8,128)(2,1)S(1)} %pad_maximum_fusion), channel_id=1, source_target_pairs={{0,8},{4,12},{8,0},{12,4},{16,24},{20,28},{24,16},{28,20},{1,9},{5... | collective-permute-start | bytes 393224 | tf_op jit(solution)/shard_map/ppermute | solution.py:20
  53.3 13.4 %collective-permute-start.21 = (bf16[2,960,128]{2,1,0:T(8,128)(2,1)S(1)}, bf16[2,960,128]{2,1,0:T(8,128)(2,1)S(1)}, u32[]{:S(2)}, u32[]{:S(2)}) collective-permute-start(bf16[2,960,128]{2,1,0:T(8,128)(2,1)S(1)} %collective-permute-done.11.refs_2_), channel_id=1, source_target_pairs={{0,2},{2,3},{3,1},{1,0},{4,6},{6,7},{7,5},{5,4},{8,10},{10,11},{11... | collective-permute-start | bytes 1474568 | tf_op jit(solution)/shard_map/ppermute | solution.py:273
  57.0 7.7 %collective-permute-start.22 = (bf16[1,960,128]{2,1,0:T(8,128)(2,1)S(1)}, bf16[1,960,128]{2,1,0:T(8,128)(2,1)S(1)}, u32[]{:S(2)}, u32[]{:S(2)}) collective-permute-start(bf16[1,960,128]{2,1,0:T(8,128)(2,1)S(1)} %add_convert_fusion.1), channel_id=1, source_target_pairs={{0,16},{4,20},{8,24},{12,28},{16,0},{20,4},{24,8},{28,12},{1,17},{... | collective-permute-start | bytes 737288 | tf_op jit(solution)/shard_map/ppermute | solution.py:20
  59.3 7.4 %collective-permute-start.23 = (bf16[1,960,128]{2,1,0:T(8,128)(2,1)S(1)}, bf16[1,960,128]{2,1,0:T(8,128)(2,1)S(1)}, u32[]{:S(2)}, u32[]{:S(2)}) collective-permute-start(bf16[1,960,128]{2,1,0:T(8,128)(2,1)S(1)} %add_convert_fusion), channel_id=1, source_target_pairs={{0,8},{4,12},{8,0},{12,4},{16,24},{20,28},{24,16},{28,20},{1,9},{5... | collective-permute-start | bytes 737288 | tf_op jit(solution)/shard_map/ppermute | solution.py:20
  59.9 6.8 %collective-permute-start.20 = (bf16[4,128,128]{2,1,0:T(8,128)(2,1)S(1)}, bf16[4,128,128]{2,1,0:T(8,128)(2,1)S(1)}, u32[]{:S(2)}, u32[]{:S(2)}) collective-permute-start(bf16[4,128,128]{2,1,0:T(8,128)(2,1)S(1)} %add_convert_fusion.7), channel_id=1, source_target_pairs={{0,16},{4,20},{8,24},{12,28},{16,0},{20,4},{24,8},{28,12},{1,17},{... | collective-permute-start | bytes 393224 | tf_op jit(solution)/shard_map/ppermute | solution.py:20
  60.7 8.1 %collective-permute-start.27 = (bf16[2,960,128]{2,1,0:T(8,128)(2,1)S(1)}, bf16[2,960,128]{2,1,0:T(8,128)(2,1)S(1)}, u32[]{:S(2)}, u32[]{:S(2)}) collective-permute-start(bf16[2,960,128]{2,1,0:T(8,128)(2,1)S(1)} %get-tuple-element.78), channel_id=1, source_target_pairs={{0,4},{4,0},{8,12},{12,8},{16,20},{20,16},{24,28},{28,24},{1,5},{5... | collective-permute-start | bytes 1474568 | tf_op jit(solution)/shard_map/ppermute | solution.py:20
  66.8 1.4 %collective-permute-start.26 = (bf16[4,128,128]{2,1,0:T(8,128)(2,1)S(1)}, bf16[4,128,128]{2,1,0:T(8,128)(2,1)S(1)}, u32[]{:S(2)}, u32[]{:S(2)}) collective-permute-start(bf16[4,128,128]{2,1,0:T(8,128)(2,1)S(1)} %add_convert_fusion.6.mine_ref), channel_id=1, source_target_pairs={{0,4},{4,0},{8,12},{12,8},{16,20},{20,16},{24,28},{28,24},{1,5},{5... | collective-permute-start | bytes 393224 | tf_op jit(solution)/shard_map/ppermute | solution.py:20

commit v9 on v8

--- a/solution.py
+++ b/solution.py
@@ -70,8 +70,8 @@
     count = len(labels)
     piece_refs = refs[:count]
     ladder_ref = refs[count]
-    out_refs = refs[count + 1:-3]
-    amp, acc, sems = refs[-3:]
+    out_refs = refs[count + 1:-2]
+    amp, acc = refs[-2:]
     columns = amp.shape[1] // 2
     rows = out_refs[0].shape[-2]
     step = pl.program_id(0)
@@ -82,17 +82,11 @@
 
     @pl.when(step == 0)
     def _():
-        copies = []
-        for index, (mask, part) in enumerate(labels):
+        for ref, (mask, part) in zip(piece_refs, labels, strict=True):
             for which in (0, 1) if part is None else (part,):
-                source = piece_refs[index].at[which] if part is None else piece_refs[index]
-                lanes = pl.ds(which * columns, columns)
-                copy = pltpu.make_async_copy(source, amp.at[rows_of(mask), lanes], sems.at[len(copies)])
-                copy.start()
-                copies.append(copy)
+                value = ref[which] if part is None else ref[...]
+                amp[rows_of(mask), which * columns:(which + 1) * columns] = value
         acc[...] = jnp.zeros_like(acc)
-        for copy in copies:
-            copy.wait()
 
     code = small_ref[1 + step]
     row_block = jnp.int32(0)
@@ -130,19 +124,17 @@
 def ladder(small, pieces, ladder_blocks, groups):
     slots = ladder_blocks.shape[0]
     rows, columns = pieces[0][0].shape[-2:]
-    count = sum(len(places) for places in groups)
     return pl.pallas_call(
         functools.partial(ladder_kernel, [(mask, part) for _, mask, part in pieces], groups),
         grid_spec=pltpu.PrefetchScalarGridSpec(
             num_scalar_prefetch=1,
             grid=(slots,),
-            in_specs=[pl.BlockSpec(memory_space=pl.ANY)] * len(pieces)
+            in_specs=[pl.BlockSpec(memory_space=pltpu.VMEM)] * len(pieces)
             + [pl.BlockSpec((1, BLOCK, BLOCK), lambda s, *_: (s, 0, 0))],
             out_specs=[pl.BlockSpec((len(places), rows, columns), lambda s, *_: (0, 0, 0)) for places in groups],
             scratch_shapes=[
                 pltpu.VMEM((PAIRS, 2 * columns), BF16),
                 pltpu.VMEM((PAIRS, 2 * columns), F32),
-                pltpu.SemaphoreType.DMA((count,)),
             ],
         ),
         out_shape=[jax.ShapeDtypeStruct((len(places), rows, columns), BF16) for places in groups],

time: 70.3 us -> 70.1 us (level)
  no operation moved by 1% of the time
where the time goes in v9:
time: 70.1 us; the launch traced here: 69.8 us
  starting transfers between devices  30.3 us (43%)
  waiting for transfers between devices  23.4 us (33%)
  Pallas kernels  13.5 us (19%)
  other arithmetic  1.32 us (2%)
  local copies, waits for them, and re-layouts  1.08 us (2%)
    ppermute x22, waiting for transfers between devices, swap(): return lax.ppermute(value, 'tri', pairs)  16.7 us
    ppermute x22, starting transfers between devices, swap(): return lax.ppermute(value, 'tri', pairs)  15.3 us
    ppermute x6, starting transfers between devices, turn(): lax.ppermute(value, 'vp', [(order[i], order[(i + distance) % vp_size]) fo...  15 us
    pallas_call x1, Pallas kernels, ladder(): pl.pallas_call(functools.partial(ladder_kernel, [(mask, part) for _, mask...  10.8 us
    ppermute x6, waiting for transfers between devices, turn(): lax.ppermute(value, 'vp', [(order[i], order[(i + distance) % vp_size]) fo...  6.72 us
  transfers between devices with their start and end apart: 28, of which 12 were waited for; matrix products, arithmetic and copies ran while one was open for 2% of the time, Pallas kernels for 18%

profile of v9, /device:TPU:0, one launch (start us, length us, event | category | flops | bytes accessed | tf_op | source)
XLA Modules:
  0.0 69.8 jit_solution(17748132159691147571)
XLA Ops:
  0.0 3.0 %collective-permute-start.1 = (bf16[2,960,128]{2,1,0:T(8,128)(2,1)}, bf16[2,960,128]{2,1,0:T(8,128)(2,1)S(1)}, u32[]{:S(2)}, u32[]{:S(2)}) collective-permute-start(bf16[2,960,128]{2,1,0:T(8,128)(2,1)} %source_ref.1), channel_id=1, source_target_pairs={{0,16},{4,20},{8,24},{12,28},{16,0},{20,4},{24,8},{28,12},{1,17},{... | collective-permute-start | bytes 1474568 | tf_op jit(solution)/shard_map/ppermute | solution.py:20
  3.0 1.5 %collective-permute-start = (bf16[2,960,128]{2,1,0:T(8,128)(2,1)}, bf16[2,960,128]{2,1,0:T(8,128)(2,1)S(1)}, u32[]{:S(2)}, u32[]{:S(2)}) collective-permute-start(bf16[2,960,128]{2,1,0:T(8,128)(2,1)} %source_ref.1), channel_id=1, source_target_pairs={{0,8},{4,12},{8,0},{12,4},{16,24},{20,28},{24,16},{28,20},{1,9},{5... | collective-permute-start | bytes 1474568 | tf_op jit(solution)/shard_map/ppermute | solution.py:20
  4.5 2.6 %collective-permute-start.2 = (bf16[2,960,128]{2,1,0:T(8,128)(2,1)}, bf16[2,960,128]{2,1,0:T(8,128)(2,1)S(1)}, u32[]{:S(2)}, u32[]{:S(2)}) collective-permute-start(bf16[2,960,128]{2,1,0:T(8,128)(2,1)} %source_ref.1), channel_id=1, source_target_pairs={{0,2},{2,3},{3,1},{1,0},{4,6},{6,7},{7,5},{5,4},{8,10},{10,11},{11... | collective-permute-start | bytes 1474568 | tf_op jit(solution)/shard_map/ppermute | solution.py:265
  7.1 1.6 %collective-permute-start.3 = (bf16[960,128]{1,0:T(8,128)(2,1)}, bf16[960,128]{1,0:T(8,128)(2,1)S(1)}, u32[]{:S(2)}, u32[]{:S(2)}) collective-permute-start(bf16[960,128]{1,0:T(8,128)(2,1)} %int_ref.1), channel_id=1, source_target_pairs={{0,2},{2,3},{3,1},{1,0},{4,6},{6,7},{7,5},{5,4},{8,10},{10,11},{11... | collective-permute-start | bytes 737288 | tf_op jit(solution)/shard_map/ppermute | solution.py:265
  8.6 0.7 %pad_add_fusion.small_ref = s32[8]{0:T(128)S(1)} fusion(s32[7]{0:T(128)} %param.7, s32[1]{0:T(128)} %bitcast), kind=kLoop, calls=%fused_computation.14 | loop fusion | flops 8 | bytes 64 | tf_op jit(solution)/shard_map/concatenate | solution.py:271
  9.4 1.0 %copy-done = bf16[2,960,128]{2,1,0:T(8,128)(2,1)S(1)} copy-done((bf16[2,960,128]{2,1,0:T(8,128)(2,1)S(1)}, bf16[2,960,128]{2,1,0:T(8,128)(2,1)}, u32[]{:S(2)}) %copy-start) | copy-done | bytes 491544
  10.7 3.7 %collective-permute-done.1.refs_2_ = bf16[2,960,128]{2,1,0:T(8,128)(2,1)S(1)} collective-permute-done((bf16[2,960,128]{2,1,0:T(8,128)(2,1)}, bf16[2,960,128]{2,1,0:T(8,128)(2,1)S(1)}, u32[]{:S(2)}, u32[]{:S(2)}) %collective-permute-start.1) | collective-permute-done | bytes 491552 | tf_op jit(solution)/shard_map/ppermute | solution.py:20
  14.4 1.5 %collective-permute-done.refs_1_ = bf16[2,960,128]{2,1,0:T(8,128)(2,1)S(1)} collective-permute-done((bf16[2,960,128]{2,1,0:T(8,128)(2,1)}, bf16[2,960,128]{2,1,0:T(8,128)(2,1)S(1)}, u32[]{:S(2)}, u32[]{:S(2)}) %collective-permute-start) | collective-permute-done | bytes 491552 | tf_op jit(solution)/shard_map/ppermute | solution.py:20
  15.9 1.6 %collective-permute-start.4 = (bf16[960,128]{1,0:T(8,128)(2,1)S(1)}, bf16[960,128]{1,0:T(8,128)(2,1)S(1)}, u32[]{:S(2)}, u32[]{:S(2)}) collective-permute-start(bf16[960,128]{1,0:T(8,128)(2,1)S(1)} %slice_bitcast_fusion.1), channel_id=1, source_target_pairs={{0,8},{4,12},{8,0},{12,4},{16,24},{20,28},{24,16},{28,20},{1,9},{5... | collective-permute-start | bytes 737288 | tf_op jit(solution)/shard_map/ppermute | solution.py:20
  18.0 5.8 %collective-permute-done.3.last_ref = bf16[960,128]{1,0:T(8,128)(2,1)S(1)} collective-permute-done((bf16[960,128]{1,0:T(8,128)(2,1)}, bf16[960,128]{1,0:T(8,128)(2,1)S(1)}, u32[]{:S(2)}, u32[]{:S(2)}) %collective-permute-start.3) | collective-permute-done | bytes 245792 | tf_op jit(solution)/shard_map/ppermute | solution.py:265
  24.8 3.3 %collective-permute-start.11 = (bf16[2,960,128]{2,1,0:T(8,128)(2,1)S(1)}, bf16[2,960,128]{2,1,0:T(8,128)(2,1)S(1)}, u32[]{:S(2)}, u32[]{:S(2)}) collective-permute-start(bf16[2,960,128]{2,1,0:T(8,128)(2,1)S(1)} %collective-permute-done.2.refs_1_), channel_id=1, source_target_pairs={{0,2},{2,3},{3,1},{1,0},{4,6},{6,7},{7,5},{5,4},{8,10},{10,11},{11... | collective-permute-start | bytes 1474568 | tf_op jit(solution)/shard_map/ppermute | solution.py:265
  28.1 10.8 %ladder.1 = (bf16[3,960,128]{2,1,0:T(8,128)(2,1)S(1)}, bf16[3,960,128]{2,1,0:T(8,128)(2,1)S(1)}, bf16[2,960,128]{2,1,0:T(8,128)(2,1)S(1)}, bf16[3,960,128]{2,1,0...) custom-call(s32[8]{0:T(128)S(1)} %pad_add_fusion.small_ref, ...), custom_call_target="tpu_custom_call" | custom-call | flops 4227858432 | bytes 16121856 | tf_op jit(solution)/shard_map/ladder/pallas_call | solution.py:127
  39.6 0.6 contract.1
  40.1 1.1 %collective-permute-done.12 = bf16[3,960,128]{2,1,0:T(8,128)(2,1)S(1)} collective-permute-done((bf16[3,960,128]{2,1,0:T(8,128)(2,1)S(1)}, bf16[3,960,128]{2,1,0:T(8,128)(2,1)S(1)}, u32[]{:S(2)}, u32[]{:S(2)}) %collective-permute-start.12) | collective-permute-done | bytes 737312 | tf_op jit(solution)/shard_map/ppermute | solution.py:20
  41.3 1.1 %collective-permute-done.13 = bf16[3,960,128]{2,1,0:T(8,128)(2,1)S(1)} collective-permute-done((bf16[3,960,128]{2,1,0:T(8,128)(2,1)S(1)}, bf16[3,960,128]{2,1,0:T(8,128)(2,1)S(1)}, u32[]{:S(2)}, u32[]{:S(2)}) %collective-permute-start.13) | collective-permute-done | bytes 737312 | tf_op jit(solution)/shard_map/ppermute | solution.py:20
  42.8 0.5 collective-permute-start.17
  43.3 0.5 collective-permute-start.18
  44.1 2.4 %collective-permute-start.16 = (bf16[128,128]{1,0:T(8,128)(2,1)S(1)}, bf16[128,128]{1,0:T(8,128)(2,1)S(1)}, u32[]{:S(2)}, u32[]{:S(2)}) collective-permute-start(bf16[128,128]{1,0:T(8,128)(2,1)S(1)} %get-tuple-element.89), channel_id=1, source_target_pairs={{0,3},{2,1},{3,0},{1,2},{4,7},{6,5},{7,4},{5,6},{8,11},{10,9},{11,... | collective-permute-start | bytes 98312 | tf_op jit(solution)/shard_map/ppermute | solution.py:265
  46.5 1.3 %collective-permute-start.15 = (bf16[128,128]{1,0:T(8,128)(2,1)S(1)}, bf16[128,128]{1,0:T(8,128)(2,1)S(1)}, u32[]{:S(2)}, u32[]{:S(2)}) collective-permute-start(bf16[128,128]{1,0:T(8,128)(2,1)S(1)} %get-tuple-element.90), channel_id=1, source_target_pairs={{0,1},{2,0},{3,2},{1,3},{4,5},{6,4},{7,6},{5,7},{8,9},{10,8},{11,1... | collective-permute-start | bytes 98312 | tf_op jit(solution)/shard_map/ppermute | solution.py:265
  47.8 1.3 %collective-permute-start.24 = (bf16[1,960,128]{2,1,0:T(8,128)(2,1)S(1)}, bf16[1,960,128]{2,1,0:T(8,128)(2,1)S(1)}, u32[]{:S(2)}, u32[]{:S(2)}) collective-permute-start(bf16[1,960,128]{2,1,0:T(8,128)(2,1)S(1)} %get-tuple-element.73), channel_id=1, source_target_pairs={{0,8},{4,12},{8,0},{12,4},{16,24},{20,28},{24,16},{28,20},{1,9},{5... | collective-permute-start | bytes 737288 | tf_op jit(solution)/shard_map/ppermute | solution.py:20
  49.2 0.9 %collective-permute-done.16 = bf16[128,128]{1,0:T(8,128)(2,1)S(1)} collective-permute-done((bf16[128,128]{1,0:T(8,128)(2,1)S(1)}, bf16[128,128]{1,0:T(8,128)(2,1)S(1)}, u32[]{:S(2)}, u32[]{:S(2)}) %collective-permute-start.16) | collective-permute-done | bytes 32800 | tf_op jit(solution)/shard_map/ppermute | solution.py:265
  50.1 1.4 %collective-permute-start.25 = (bf16[1,960,128]{2,1,0:T(8,128)(2,1)S(1)}, bf16[1,960,128]{2,1,0:T(8,128)(2,1)S(1)}, u32[]{:S(2)}, u32[]{:S(2)}) collective-permute-start(bf16[1,960,128]{2,1,0:T(8,128)(2,1)S(1)} %get-tuple-element.74), channel_id=1, source_target_pairs={{0,16},{4,20},{8,24},{12,28},{16,0},{20,4},{24,8},{28,12},{1,17},{... | collective-permute-start | bytes 737288 | tf_op jit(solution)/shard_map/ppermute | solution.py:20
  51.6 1.5 %collective-permute-start.19 = (bf16[4,128,128]{2,1,0:T(8,128)(2,1)S(1)}, bf16[4,128,128]{2,1,0:T(8,128)(2,1)S(1)}, u32[]{:S(2)}, u32[]{:S(2)}) collective-permute-start(bf16[4,128,128]{2,1,0:T(8,128)(2,1)S(1)} %pad_maximum_fusion), channel_id=1, source_target_pairs={{0,8},{4,12},{8,0},{12,4},{16,24},{20,28},{24,16},{28,20},{1,9},{5... | collective-permute-start | bytes 393224 | tf_op jit(solution)/shard_map/ppermute | solution.py:20
  53.1 3.8 %collective-permute-start.21 = (bf16[2,960,128]{2,1,0:T(8,128)(2,1)S(1)}, bf16[2,960,128]{2,1,0:T(8,128)(2,1)S(1)}, u32[]{:S(2)}, u32[]{:S(2)}) collective-permute-start(bf16[2,960,128]{2,1,0:T(8,128)(2,1)S(1)} %collective-permute-done.11.refs_2_), channel_id=1, source_target_pairs={{0,2},{2,3},{3,1},{1,0},{4,6},{6,7},{7,5},{5,4},{8,10},{10,11},{11... | collective-permute-start | bytes 1474568 | tf_op jit(solution)/shard_map/ppermute | solution.py:265
  57.2 1.9 %collective-permute-done.19 = bf16[4,128,128]{2,1,0:T(8,128)(2,1)S(1)} collective-permute-done((bf16[4,128,128]{2,1,0:T(8,128)(2,1)S(1)}, bf16[4,128,128]{2,1,0:T(8,128)(2,1)S(1)}, u32[]{:S(2)}, u32[]{:S(2)}) %collective-permute-start.19) | collective-permute-done | bytes 131104 | tf_op jit(solution)/shard_map/ppermute | solution.py:20
  59.1 0.5 collective-permute-start.23
  59.7 1.0 %collective-permute-start.20 = (bf16[4,128,128]{2,1,0:T(8,128)(2,1)S(1)}, bf16[4,128,128]{2,1,0:T(8,128)(2,1)S(1)}, u32[]{:S(2)}, u32[]{:S(2)}) collective-permute-start(bf16[4,128,128]{2,1,0:T(8,128)(2,1)S(1)} %add_convert_fusion.7), channel_id=1, source_target_pairs={{0,16},{4,20},{8,24},{12,28},{16,0},{20,4},{24,8},{28,12},{1,17},{... | collective-permute-start | bytes 393224 | tf_op jit(solution)/shard_map/ppermute | solution.py:20
  60.7 4.0 %collective-permute-done.22.refs_6_ = bf16[1,960,128]{2,1,0:T(8,128)(2,1)S(1)} collective-permute-done((bf16[1,960,128]{2,1,0:T(8,128)(2,1)S(1)}, bf16[1,960,128]{2,1,0:T(8,128)(2,1)S(1)}, u32[]{:S(2)}, u32[]{:S(2)}) %collective-permute-start.22) | collective-permute-done | bytes 245792 | tf_op jit(solution)/shard_map/ppermute | solution.py:20
  64.7 1.8 %collective-permute-done.23.refs_7_ = bf16[1,960,128]{2,1,0:T(8,128)(2,1)S(1)} collective-permute-done((bf16[1,960,128]{2,1,0:T(8,128)(2,1)S(1)}, bf16[1,960,128]{2,1,0:T(8,128)(2,1)S(1)}, u32[]{:S(2)}, u32[]{:S(2)}) %collective-permute-start.23) | collective-permute-done | bytes 245792 | tf_op jit(solution)/shard_map/ppermute | solution.py:20
  66.6 1.3 %collective-permute-done.26.other_ref = bf16[4,128,128]{2,1,0:T(8,128)(2,1)S(1)} collective-permute-done((bf16[4,128,128]{2,1,0:T(8,128)(2,1)S(1)}, bf16[4,128,128]{2,1,0:T(8,128)(2,1)S(1)}, u32[]{:S(2)}, u32[]{:S(2)}) %collective-permute-start.26) | collective-permute-done | bytes 131104 | tf_op jit(solution)/shard_map/ppermute | solution.py:20
  68.0 0.7 quadratic.1.base_ref
  68.7 1.1 %finish.1 = bf16[2,960,128]{2,1,0:T(8,128)(2,1)} custom-call(f32[2,960,128]{2,1,0:T(8,128)S(1)} %quadratic.1.base_ref, bf16[2,960,128]{2,1,0:T(8,128)(2,1)S(1)} %get-tuple-element.77.refs_0_.refs_1_, bf16[2,960,128]{2,1,0:T(8,128)(2,1)S(1)} %get-tuple-element.77.refs_0_.refs_1_, bf16[2,960,128]{2,1,0:T(8,128)(2,1)S(1)} %collective-permute-done.27.refs_2_.refs_3_, ...), custom_call_target="tpu_custom_call" | custom-call | tf_op jit(solution)/shard_map/finish/pallas_call | solution.py:239
  (44 shorter events, 3.8 us)
Async XLA Ops:
  0.0 14.4 %collective-permute-start.1 = (bf16[2,960,128]{2,1,0:T(8,128)(2,1)}, bf16[2,960,128]{2,1,0:T(8,128)(2,1)S(1)}, u32[]{:S(2)}, u32[]{:S(2)}) collective-permute-start(bf16[2,960,128]{2,1,0:T(8,128)(2,1)} %source_ref.1), channel_id=1, source_target_pairs={{0,16},{4,20},{8,24},{12,28},{16,0},{20,4},{24,8},{28,12},{1,17},{... | collective-permute-start | bytes 1474568 | tf_op jit(solution)/shard_map/ppermute | solution.py:20
  3.0 12.9 %collective-permute-start = (bf16[2,960,128]{2,1,0:T(8,128)(2,1)}, bf16[2,960,128]{2,1,0:T(8,128)(2,1)S(1)}, u32[]{:S(2)}, u32[]{:S(2)}) collective-permute-start(bf16[2,960,128]{2,1,0:T(8,128)(2,1)} %source_ref.1), channel_id=1, source_target_pairs={{0,8},{4,12},{8,0},{12,4},{16,24},{20,28},{24,16},{28,20},{1,9},{5... | collective-permute-start | bytes 1474568 | tf_op jit(solution)/shard_map/ppermute | solution.py:20
  4.5 19.3 %collective-permute-start.6 = (bf16[2,960,128]{2,1,0:T(8,128)(2,1)}, bf16[2,960,128]{2,1,0:T(8,128)(2,1)S(1)}, u32[]{:S(2)}, u32[]{:S(2)}) collective-permute-start(bf16[2,960,128]{2,1,0:T(8,128)(2,1)} %source_ref.1), channel_id=1, source_target_pairs={{0,4},{4,0},{8,12},{12,8},{16,20},{20,16},{24,28},{28,24},{1,5},{5... | collective-permute-start | bytes 1474568 | tf_op jit(solution)/shard_map/ppermute | solution.py:20
  4.5 20.4 %collective-permute-start.2 = (bf16[2,960,128]{2,1,0:T(8,128)(2,1)}, bf16[2,960,128]{2,1,0:T(8,128)(2,1)S(1)}, u32[]{:S(2)}, u32[]{:S(2)}) collective-permute-start(bf16[2,960,128]{2,1,0:T(8,128)(2,1)} %source_ref.1), channel_id=1, source_target_pairs={{0,2},{2,3},{3,1},{1,0},{4,6},{6,7},{7,5},{5,4},{8,10},{10,11},{11... | collective-permute-start | bytes 1474568 | tf_op jit(solution)/shard_map/ppermute | solution.py:265
  7.1 16.7 %collective-permute-start.3 = (bf16[960,128]{1,0:T(8,128)(2,1)}, bf16[960,128]{1,0:T(8,128)(2,1)S(1)}, u32[]{:S(2)}, u32[]{:S(2)}) collective-permute-start(bf16[960,128]{1,0:T(8,128)(2,1)} %int_ref.1), channel_id=1, source_target_pairs={{0,2},{2,3},{3,1},{1,0},{4,6},{6,7},{7,5},{5,4},{8,10},{10,11},{11... | collective-permute-start | bytes 737288 | tf_op jit(solution)/shard_map/ppermute | solution.py:265
  9.4 1.0 %copy-start = (bf16[2,960,128]{2,1,0:T(8,128)(2,1)S(1)}, bf16[2,960,128]{2,1,0:T(8,128)(2,1)}, u32[]{:S(2)}) copy-start(bf16[2,960,128]{2,1,0:T(8,128)(2,1)} %source_ref.1) | copy-start | bytes 1474564
  10.7 28.9 %copy-start.1 = (bf16[960,128]{1,0:T(8,128)(2,1)S(1)}, bf16[960,128]{1,0:T(8,128)(2,1)}, u32[]{:S(2)}) copy-start(bf16[960,128]{1,0:T(8,128)(2,1)} %int_ref.1) | copy-start | bytes 737284
  15.9 8.4 %collective-permute-start.4 = (bf16[960,128]{1,0:T(8,128)(2,1)S(1)}, bf16[960,128]{1,0:T(8,128)(2,1)S(1)}, u32[]{:S(2)}, u32[]{:S(2)}) collective-permute-start(bf16[960,128]{1,0:T(8,128)(2,1)S(1)} %slice_bitcast_fusion.1), channel_id=1, source_target_pairs={{0,8},{4,12},{8,0},{12,4},{16,24},{20,28},{24,16},{28,20},{1,9},{5... | collective-permute-start | bytes 737288 | tf_op jit(solution)/shard_map/ppermute | solution.py:20
  17.5 6.9 %collective-permute-start.5 = (bf16[960,128]{1,0:T(8,128)(2,1)S(1)}, bf16[960,128]{1,0:T(8,128)(2,1)S(1)}, u32[]{:S(2)}, u32[]{:S(2)}) collective-permute-start(bf16[960,128]{1,0:T(8,128)(2,1)S(1)} %slice_bitcast_fusion), channel_id=1, source_target_pairs={{0,16},{4,20},{8,24},{12,28},{16,0},{20,4},{24,8},{28,12},{1,17},{... | collective-permute-start | bytes 737288 | tf_op jit(solution)/shard_map/ppermute | solution.py:20
  23.8 4.3 %collective-permute-start.7 = (bf16[2,960,128]{2,1,0:T(8,128)(2,1)S(1)}, bf16[2,960,128]{2,1,0:T(8,128)(2,1)S(1)}, u32[]{:S(2)}, u32[]{:S(2)}) collective-permute-start(bf16[2,960,128]{2,1,0:T(8,128)(2,1)S(1)} %collective-permute-done.refs_1_), channel_id=1, source_target_pairs={{0,4},{4,0},{8,12},{12,8},{16,20},{20,16},{24,28},{28,24},{1,5},{5... | collective-permute-start | bytes 1474568 | tf_op jit(solution)/shard_map/ppermute | solution.py:20
  23.8 4.3 %collective-permute-start.8 = (bf16[2,960,128]{2,1,0:T(8,128)(2,1)S(1)}, bf16[2,960,128]{2,1,0:T(8,128)(2,1)S(1)}, u32[]{:S(2)}, u32[]{:S(2)}) collective-permute-start(bf16[2,960,128]{2,1,0:T(8,128)(2,1)S(1)} %collective-permute-done.1.refs_2_), channel_id=1, source_target_pairs={{0,4},{4,0},{8,12},{12,8},{16,20},{20,16},{24,28},{28,24},{1,5},{5... | collective-permute-start | bytes 1474568 | tf_op jit(solution)/shard_map/ppermute | solution.py:20
  24.3 3.8 %collective-permute-start.9 = (bf16[960,128]{1,0:T(8,128)(2,1)S(1)}, bf16[960,128]{1,0:T(8,128)(2,1)S(1)}, u32[]{:S(2)}, u32[]{:S(2)}) collective-permute-start(bf16[960,128]{1,0:T(8,128)(2,1)S(1)} %collective-permute-done.4.refs_3_), channel_id=1, source_target_pairs={{0,4},{4,0},{8,12},{12,8},{16,20},{20,16},{24,28},{28,24},{1,5},{5... | collective-permute-start | bytes 737288 | tf_op jit(solution)/shard_map/ppermute | solution.py:20
  24.4 3.7 %collective-permute-start.10 = (bf16[960,128]{1,0:T(8,128)(2,1)S(1)}, bf16[960,128]{1,0:T(8,128)(2,1)S(1)}, u32[]{:S(2)}, u32[]{:S(2)}) collective-permute-start(bf16[960,128]{1,0:T(8,128)(2,1)S(1)} %collective-permute-done.5.refs_4_), channel_id=1, source_target_pairs={{0,4},{4,0},{8,12},{12,8},{16,20},{20,16},{24,28},{28,24},{1,5},{5... | collective-permute-start | bytes 737288 | tf_op jit(solution)/shard_map/ppermute | solution.py:20
  24.8 14.2 %collective-permute-start.11 = (bf16[2,960,128]{2,1,0:T(8,128)(2,1)S(1)}, bf16[2,960,128]{2,1,0:T(8,128)(2,1)S(1)}, u32[]{:S(2)}, u32[]{:S(2)}) collective-permute-start(bf16[2,960,128]{2,1,0:T(8,128)(2,1)S(1)} %collective-permute-done.2.refs_1_), channel_id=1, source_target_pairs={{0,2},{2,3},{3,1},{1,0},{4,6},{6,7},{7,5},{5,4},{8,10},{10,11},{11... | collective-permute-start | bytes 1474568 | tf_op jit(solution)/shard_map/ppermute | solution.py:265
  39.0 2.3 %collective-permute-start.12 = (bf16[3,960,128]{2,1,0:T(8,128)(2,1)S(1)}, bf16[3,960,128]{2,1,0:T(8,128)(2,1)S(1)}, u32[]{:S(2)}, u32[]{:S(2)}) collective-permute-start(bf16[3,960,128]{2,1,0:T(8,128)(2,1)S(1)} %get-tuple-element.55), channel_id=1, source_target_pairs={{0,4},{4,0},{8,12},{12,8},{16,20},{20,16},{24,28},{28,24},{1,5},{5... | collective-permute-start | bytes 2211848 | tf_op jit(solution)/shard_map/ppermute | solution.py:20
  39.1 3.3 %collective-permute-start.13 = (bf16[3,960,128]{2,1,0:T(8,128)(2,1)S(1)}, bf16[3,960,128]{2,1,0:T(8,128)(2,1)S(1)}, u32[]{:S(2)}, u32[]{:S(2)}) collective-permute-start(bf16[3,960,128]{2,1,0:T(8,128)(2,1)S(1)} %get-tuple-element.56), channel_id=1, source_target_pairs={{0,4},{4,0},{8,12},{12,8},{16,20},{20,16},{24,28},{28,24},{1,5},{5... | collective-permute-start | bytes 2211848 | tf_op jit(solution)/shard_map/ppermute | solution.py:20
  42.6 1.4 %collective-permute-start.14 = (bf16[4,128,128]{2,1,0:T(8,128)(2,1)S(1)}, bf16[4,128,128]{2,1,0:T(8,128)(2,1)S(1)}, u32[]{:S(2)}, u32[]{:S(2)}) collective-permute-start(bf16[4,128,128]{2,1,0:T(8,128)(2,1)S(1)} %get-tuple-element.66), channel_id=1, source_target_pairs={{0,4},{4,0},{8,12},{12,8},{16,20},{20,16},{24,28},{28,24},{1,5},{5... | collective-permute-start | bytes 393224 | tf_op jit(solution)/shard_map/ppermute | solution.py:20
  42.8 8.8 %collective-permute-start.17 = (bf16[1,960,128]{2,1,0:T(8,128)(2,1)S(1)}, bf16[1,960,128]{2,1,0:T(8,128)(2,1)S(1)}, u32[]{:S(2)}, u32[]{:S(2)}) collective-permute-start(bf16[1,960,128]{2,1,0:T(8,128)(2,1)S(1)} %get-tuple-element.67), channel_id=1, source_target_pairs={{0,8},{4,12},{8,0},{12,4},{16,24},{20,28},{24,16},{28,20},{1,9},{5... | collective-permute-start | bytes 737288 | tf_op jit(solution)/shard_map/ppermute | solution.py:20
  43.3 8.2 %collective-permute-start.18 = (bf16[1,960,128]{2,1,0:T(8,128)(2,1)S(1)}, bf16[1,960,128]{2,1,0:T(8,128)(2,1)S(1)}, u32[]{:S(2)}, u32[]{:S(2)}) collective-permute-start(bf16[1,960,128]{2,1,0:T(8,128)(2,1)S(1)} %get-tuple-element.68), channel_id=1, source_target_pairs={{0,16},{4,20},{8,24},{12,28},{16,0},{20,4},{24,8},{28,12},{1,17},{... | collective-permute-start | bytes 737288 | tf_op jit(solution)/shard_map/ppermute | solution.py:20
  44.1 6.0 %collective-permute-start.16 = (bf16[128,128]{1,0:T(8,128)(2,1)S(1)}, bf16[128,128]{1,0:T(8,128)(2,1)S(1)}, u32[]{:S(2)}, u32[]{:S(2)}) collective-permute-start(bf16[128,128]{1,0:T(8,128)(2,1)S(1)} %get-tuple-element.89), channel_id=1, source_target_pairs={{0,3},{2,1},{3,0},{1,2},{4,7},{6,5},{7,4},{5,6},{8,11},{10,9},{11,... | collective-permute-start | bytes 98312 | tf_op jit(solution)/shard_map/ppermute | solution.py:265
  46.5 5.0 %collective-permute-start.15 = (bf16[128,128]{1,0:T(8,128)(2,1)S(1)}, bf16[128,128]{1,0:T(8,128)(2,1)S(1)}, u32[]{:S(2)}, u32[]{:S(2)}) collective-permute-start(bf16[128,128]{1,0:T(8,128)(2,1)S(1)} %get-tuple-element.90), channel_id=1, source_target_pairs={{0,1},{2,0},{3,2},{1,3},{4,5},{6,4},{7,6},{5,7},{8,9},{10,8},{11,1... | collective-permute-start | bytes 98312 | tf_op jit(solution)/shard_map/ppermute | solution.py:265
  47.8 11.8 %collective-permute-start.24 = (bf16[1,960,128]{2,1,0:T(8,128)(2,1)S(1)}, bf16[1,960,128]{2,1,0:T(8,128)(2,1)S(1)}, u32[]{:S(2)}, u32[]{:S(2)}) collective-permute-start(bf16[1,960,128]{2,1,0:T(8,128)(2,1)S(1)} %get-tuple-element.73), channel_id=1, source_target_pairs={{0,8},{4,12},{8,0},{12,4},{16,24},{20,28},{24,16},{28,20},{1,9},{5... | collective-permute-start | bytes 737288 | tf_op jit(solution)/shard_map/ppermute | solution.py:20
  50.1 10.7 %collective-permute-start.25 = (bf16[1,960,128]{2,1,0:T(8,128)(2,1)S(1)}, bf16[1,960,128]{2,1,0:T(8,128)(2,1)S(1)}, u32[]{:S(2)}, u32[]{:S(2)}) collective-permute-start(bf16[1,960,128]{2,1,0:T(8,128)(2,1)S(1)} %get-tuple-element.74), channel_id=1, source_target_pairs={{0,16},{4,20},{8,24},{12,28},{16,0},{20,4},{24,8},{28,12},{1,17},{... | collective-permute-start | bytes 737288 | tf_op jit(solution)/shard_map/ppermute | solution.py:20
  51.6 7.5 %collective-permute-start.19 = (bf16[4,128,128]{2,1,0:T(8,128)(2,1)S(1)}, bf16[4,128,128]{2,1,0:T(8,128)(2,1)S(1)}, u32[]{:S(2)}, u32[]{:S(2)}) collective-permute-start(bf16[4,128,128]{2,1,0:T(8,128)(2,1)S(1)} %pad_maximum_fusion), channel_id=1, source_target_pairs={{0,8},{4,12},{8,0},{12,4},{16,24},{20,28},{24,16},{28,20},{1,9},{5... | collective-permute-start | bytes 393224 | tf_op jit(solution)/shard_map/ppermute | solution.py:20
  53.1 13.4 %collective-permute-start.21 = (bf16[2,960,128]{2,1,0:T(8,128)(2,1)S(1)}, bf16[2,960,128]{2,1,0:T(8,128)(2,1)S(1)}, u32[]{:S(2)}, u32[]{:S(2)}) collective-permute-start(bf16[2,960,128]{2,1,0:T(8,128)(2,1)S(1)} %collective-permute-done.11.refs_2_), channel_id=1, source_target_pairs={{0,2},{2,3},{3,1},{1,0},{4,6},{6,7},{7,5},{5,4},{8,10},{10,11},{11... | collective-permute-start | bytes 1474568 | tf_op jit(solution)/shard_map/ppermute | solution.py:265
  57.0 7.7 %collective-permute-start.22 = (bf16[1,960,128]{2,1,0:T(8,128)(2,1)S(1)}, bf16[1,960,128]{2,1,0:T(8,128)(2,1)S(1)}, u32[]{:S(2)}, u32[]{:S(2)}) collective-permute-start(bf16[1,960,128]{2,1,0:T(8,128)(2,1)S(1)} %add_convert_fusion.1), channel_id=1, source_target_pairs={{0,16},{4,20},{8,24},{12,28},{16,0},{20,4},{24,8},{28,12},{1,17},{... | collective-permute-start | bytes 737288 | tf_op jit(solution)/shard_map/ppermute | solution.py:20
  59.1 7.4 %collective-permute-start.23 = (bf16[1,960,128]{2,1,0:T(8,128)(2,1)S(1)}, bf16[1,960,128]{2,1,0:T(8,128)(2,1)S(1)}, u32[]{:S(2)}, u32[]{:S(2)}) collective-permute-start(bf16[1,960,128]{2,1,0:T(8,128)(2,1)S(1)} %add_convert_fusion), channel_id=1, source_target_pairs={{0,8},{4,12},{8,0},{12,4},{16,24},{20,28},{24,16},{28,20},{1,9},{5... | collective-permute-start | bytes 737288 | tf_op jit(solution)/shard_map/ppermute | solution.py:20
  59.7 6.8 %collective-permute-start.20 = (bf16[4,128,128]{2,1,0:T(8,128)(2,1)S(1)}, bf16[4,128,128]{2,1,0:T(8,128)(2,1)S(1)}, u32[]{:S(2)}, u32[]{:S(2)}) collective-permute-start(bf16[4,128,128]{2,1,0:T(8,128)(2,1)S(1)} %add_convert_fusion.7), channel_id=1, source_target_pairs={{0,16},{4,20},{8,24},{12,28},{16,0},{20,4},{24,8},{28,12},{1,17},{... | collective-permute-start | bytes 393224 | tf_op jit(solution)/shard_map/ppermute | solution.py:20
  60.7 8.0 %collective-permute-start.27 = (bf16[2,960,128]{2,1,0:T(8,128)(2,1)S(1)}, bf16[2,960,128]{2,1,0:T(8,128)(2,1)S(1)}, u32[]{:S(2)}, u32[]{:S(2)}) collective-permute-start(bf16[2,960,128]{2,1,0:T(8,128)(2,1)S(1)} %get-tuple-element.78), channel_id=1, source_target_pairs={{0,4},{4,0},{8,12},{12,8},{16,20},{20,16},{24,28},{28,24},{1,5},{5... | collective-permute-start | bytes 1474568 | tf_op jit(solution)/shard_map/ppermute | solution.py:20
  66.6 1.4 %collective-permute-start.26 = (bf16[4,128,128]{2,1,0:T(8,128)(2,1)S(1)}, bf16[4,128,128]{2,1,0:T(8,128)(2,1)S(1)}, u32[]{:S(2)}, u32[]{:S(2)}) collective-permute-start(bf16[4,128,128]{2,1,0:T(8,128)(2,1)S(1)} %add_convert_fusion.6.mine_ref), channel_id=1, source_target_pairs={{0,4},{4,0},{8,12},{12,8},{16,20},{20,16},{24,28},{28,24},{1,5},{5... | collective-permute-start | bytes 393224 | tf_op jit(solution)/shard_map/ppermute | solution.py:20

commit v10 on v9

--- a/solution.py
+++ b/solution.py
@@ -70,8 +70,8 @@
     count = len(labels)
     piece_refs = refs[:count]
     ladder_ref = refs[count]
-    out_refs = refs[count + 1:-2]
-    amp, acc = refs[-2:]
+    out_refs = refs[count + 1:-4]
+    amp, acc, blocks, sems = refs[-4:]
     columns = amp.shape[1] // 2
     rows = out_refs[0].shape[-2]
     step = pl.program_id(0)
@@ -80,8 +80,17 @@
     def rows_of(mask):
         return pl.ds(pl.multiple_of((me ^ mask) * rows, rows), rows)
 
+    halves = BLOCK // 2
+
+    def fetch(slot, side):
+        span = pl.ds(side * halves, halves)
+        return pltpu.make_async_copy(ladder_ref.at[slot, span], blocks.at[slot, span], sems.at[slot, side])
+
     @pl.when(step == 0)
     def _():
+        for slot in range(blocks.shape[0]):
+            for side in range(2):
+                fetch(slot, side).start()
         for ref, (mask, part) in zip(piece_refs, labels, strict=True):
             for which in (0, 1) if part is None else (part,):
                 value = ref[which] if part is None else ref[...]
@@ -101,7 +110,9 @@
     at_row = pl.ds(pl.multiple_of(row_block * BLOCK, BLOCK), BLOCK)
     at_column = pl.ds(pl.multiple_of(column_block * BLOCK, BLOCK), BLOCK)
     weight = weight.astype(BF16)
-    block = ladder_ref[0]
+    for side in range(2):
+        fetch(step, side).wait()
+    block = blocks[step]
     column_amp, row_amp = weight * amp[at_column, :], weight * amp[at_row, :]
     chunk = BLOCK // 3
     for first in range(0, BLOCK, chunk):
@@ -129,17 +140,18 @@
         grid_spec=pltpu.PrefetchScalarGridSpec(
             num_scalar_prefetch=1,
             grid=(slots,),
-            in_specs=[pl.BlockSpec(memory_space=pltpu.VMEM)] * len(pieces)
-            + [pl.BlockSpec((1, BLOCK, BLOCK), lambda s, *_: (s, 0, 0))],
+            in_specs=[pl.BlockSpec(memory_space=pltpu.VMEM)] * len(pieces) + [pl.BlockSpec(memory_space=pl.ANY)],
             out_specs=[pl.BlockSpec((len(places), rows, columns), lambda s, *_: (0, 0, 0)) for places in groups],
             scratch_shapes=[
                 pltpu.VMEM((PAIRS, 2 * columns), BF16),
                 pltpu.VMEM((PAIRS, 2 * columns), F32),
+                pltpu.VMEM(ladder_blocks.shape, BF16),
+                pltpu.SemaphoreType.DMA((slots, 2)),
             ],
         ),
         out_shape=[jax.ShapeDtypeStruct((len(places), rows, columns), BF16) for places in groups],
         compiler_params=pltpu.CompilerParams(
-            dimension_semantics=("arbitrary",), vmem_limit_bytes=40 * 1024 * 1024
+            dimension_semantics=("arbitrary",), vmem_limit_bytes=48 * 1024 * 1024
         ),
         cost_estimate=pl.CostEstimate(
             flops=slots * 8 * BLOCK * BLOCK * columns,

time: 70.1 us -> 72.5 us (1.034)
  other arithmetic: 1.32 us -> 4.52 us
  starting transfers between devices: 30.3 us -> 32 us
  waiting for transfers between devices: 23.4 us -> 22.1 us
  Pallas kernels: 13.5 us -> 12.4 us
    ppermute x22, waiting for transfers between devices: 16.7 us -> 14.8 us  [swap(): return lax.ppermute(value, 'tri', pairs)]
    ppermute x22, starting transfers between devices: 15.3 us -> 16.6 us  [swap(): return lax.ppermute(value, 'tri', pairs)]
    convert_element_type x1, other arithmetic: 0.26 us -> 1.57 us  [shards(): add(kept[i], came[i]).astype(BF16)[None]]
    pallas_call x1, Pallas kernels: 10.8 us -> 9.71 us  [ladder(): pl.pallas_call(functools.partial(ladder_kernel, [(mask, part) for _, mask...]
    convert_element_type x1, other arithmetic: 0.1 us -> 1.04 us  [shards(): add(real[2], real_in[2], far_x[0]).astype(BF16)[None]]
    convert_element_type x1, other arithmetic: 0.1 us -> 1.04 us  [shards(): add(imag[2], imag_in[2], far_y[0]).astype(BF16)[None]]
  transfers between devices with their start and end apart: 28 -> 28, of which waited for: 12 -> 12; matrix products, arithmetic and copies ran while one was open for 2% -> 4% of each run, Pallas kernels for 18% -> 16%
where the time goes in v10:
time: 72.5 us; the launch traced here: 72.2 us
  starting transfers between devices  32 us (44%)
  waiting for transfers between devices  22.1 us (30%)
  Pallas kernels  12.4 us (17%)
  other arithmetic  4.52 us (6%)
  local copies, waits for them, and re-layouts  1.08 us (1%)
    ppermute x22, starting transfers between devices, swap(): return lax.ppermute(value, 'tri', pairs)  16.6 us
    ppermute x6, starting transfers between devices, turn(): lax.ppermute(value, 'vp', [(order[i], order[(i + distance) % vp_size]) fo...  15.4 us
    ppermute x22, waiting for transfers between devices, swap(): return lax.ppermute(value, 'tri', pairs)  14.8 us
    pallas_call x1, Pallas kernels, ladder(): pl.pallas_call(functools.partial(ladder_kernel, [(mask, part) for _, mask...  9.71 us
    ppermute x6, waiting for transfers between devices, turn(): lax.ppermute(value, 'vp', [(order[i], order[(i + distance) % vp_size]) fo...  7.26 us
    convert_element_type x1, other arithmetic, shards(): add(kept[i], came[i]).astype(BF16)[None]  1.57 us
  transfers between devices with their start and end apart: 28, of which 12 were waited for; matrix products, arithmetic and copies ran while one was open for 4% of the time, Pallas kernels for 16%

profile of v10, /device:TPU:0, one launch (start us, length us, event | category | flops | bytes accessed | tf_op | source)
XLA Modules:
  0.0 72.2 jit_solution(16553236841782921504)
XLA Ops:
  0.0 3.0 %collective-permute-start.1 = (bf16[2,960,128]{2,1,0:T(8,128)(2,1)}, bf16[2,960,128]{2,1,0:T(8,128)(2,1)S(1)}, u32[]{:S(2)}, u32[]{:S(2)}) collective-permute-start(bf16[2,960,128]{2,1,0:T(8,128)(2,1)} %source_ref.1), channel_id=1, source_target_pairs={{0,16},{4,20},{8,24},{12,28},{16,0},{20,4},{24,8},{28,12},{1,17},{... | collective-permute-start | bytes 1474568 | tf_op jit(solution)/shard_map/ppermute | solution.py:20
  3.0 1.5 %collective-permute-start = (bf16[2,960,128]{2,1,0:T(8,128)(2,1)}, bf16[2,960,128]{2,1,0:T(8,128)(2,1)S(1)}, u32[]{:S(2)}, u32[]{:S(2)}) collective-permute-start(bf16[2,960,128]{2,1,0:T(8,128)(2,1)} %source_ref.1), channel_id=1, source_target_pairs={{0,8},{4,12},{8,0},{12,4},{16,24},{20,28},{24,16},{28,20},{1,9},{5... | collective-permute-start | bytes 1474568 | tf_op jit(solution)/shard_map/ppermute | solution.py:20
  4.5 2.6 %collective-permute-start.2 = (bf16[2,960,128]{2,1,0:T(8,128)(2,1)}, bf16[2,960,128]{2,1,0:T(8,128)(2,1)S(1)}, u32[]{:S(2)}, u32[]{:S(2)}) collective-permute-start(bf16[2,960,128]{2,1,0:T(8,128)(2,1)} %source_ref.1), channel_id=1, source_target_pairs={{0,2},{2,3},{3,1},{1,0},{4,6},{6,7},{7,5},{5,4},{8,10},{10,11},{11... | collective-permute-start | bytes 1474568 | tf_op jit(solution)/shard_map/ppermute | solution.py:277
  7.1 1.6 %collective-permute-start.3 = (bf16[960,128]{1,0:T(8,128)(2,1)}, bf16[960,128]{1,0:T(8,128)(2,1)S(1)}, u32[]{:S(2)}, u32[]{:S(2)}) collective-permute-start(bf16[960,128]{1,0:T(8,128)(2,1)} %int_ref.1), channel_id=1, source_target_pairs={{0,2},{2,3},{3,1},{1,0},{4,6},{6,7},{7,5},{5,4},{8,10},{10,11},{11... | collective-permute-start | bytes 737288 | tf_op jit(solution)/shard_map/ppermute | solution.py:277
  8.6 0.7 %pad_add_fusion.small_ref = s32[8]{0:T(128)S(1)} fusion(s32[7]{0:T(128)} %param.7, s32[1]{0:T(128)} %bitcast), kind=kLoop, calls=%fused_computation.14 | loop fusion | flops 8 | bytes 64 | tf_op jit(solution)/shard_map/concatenate | solution.py:283
  9.4 1.0 %copy-done = bf16[2,960,128]{2,1,0:T(8,128)(2,1)S(1)} copy-done((bf16[2,960,128]{2,1,0:T(8,128)(2,1)S(1)}, bf16[2,960,128]{2,1,0:T(8,128)(2,1)}, u32[]{:S(2)}) %copy-start) | copy-done | bytes 491544
  10.7 3.7 %collective-permute-done.1.refs_2_ = bf16[2,960,128]{2,1,0:T(8,128)(2,1)S(1)} collective-permute-done((bf16[2,960,128]{2,1,0:T(8,128)(2,1)}, bf16[2,960,128]{2,1,0:T(8,128)(2,1)S(1)}, u32[]{:S(2)}, u32[]{:S(2)}) %collective-permute-start.1) | collective-permute-done | bytes 491552 | tf_op jit(solution)/shard_map/ppermute | solution.py:20
  14.4 1.5 %collective-permute-done.refs_1_ = bf16[2,960,128]{2,1,0:T(8,128)(2,1)S(1)} collective-permute-done((bf16[2,960,128]{2,1,0:T(8,128)(2,1)}, bf16[2,960,128]{2,1,0:T(8,128)(2,1)S(1)}, u32[]{:S(2)}, u32[]{:S(2)}) %collective-permute-start) | collective-permute-done | bytes 491552 | tf_op jit(solution)/shard_map/ppermute | solution.py:20
  15.9 1.6 %collective-permute-start.4 = (bf16[960,128]{1,0:T(8,128)(2,1)S(1)}, bf16[960,128]{1,0:T(8,128)(2,1)S(1)}, u32[]{:S(2)}, u32[]{:S(2)}) collective-permute-start(bf16[960,128]{1,0:T(8,128)(2,1)S(1)} %slice_bitcast_fusion.1), channel_id=1, source_target_pairs={{0,8},{4,12},{8,0},{12,4},{16,24},{20,28},{24,16},{28,20},{1,9},{5... | collective-permute-start | bytes 737288 | tf_op jit(solution)/shard_map/ppermute | solution.py:20
  18.0 5.8 %collective-permute-done.3.last_ref = bf16[960,128]{1,0:T(8,128)(2,1)S(1)} collective-permute-done((bf16[960,128]{1,0:T(8,128)(2,1)}, bf16[960,128]{1,0:T(8,128)(2,1)S(1)}, u32[]{:S(2)}, u32[]{:S(2)}) %collective-permute-start.3) | collective-permute-done | bytes 245792 | tf_op jit(solution)/shard_map/ppermute | solution.py:277
  24.8 3.3 %collective-permute-start.11 = (bf16[2,960,128]{2,1,0:T(8,128)(2,1)S(1)}, bf16[2,960,128]{2,1,0:T(8,128)(2,1)S(1)}, u32[]{:S(2)}, u32[]{:S(2)}) collective-permute-start(bf16[2,960,128]{2,1,0:T(8,128)(2,1)S(1)} %collective-permute-done.2.refs_1_), channel_id=1, source_target_pairs={{0,2},{2,3},{3,1},{1,0},{4,6},{6,7},{7,5},{5,4},{8,10},{10,11},{11... | collective-permute-start | bytes 1474568 | tf_op jit(solution)/shard_map/ppermute | solution.py:277
  28.1 9.7 %ladder.1 = (bf16[3,960,128]{2,1,0:T(8,128)(2,1)S(1)}, bf16[3,960,128]{2,1,0:T(8,128)(2,1)}, bf16[2,960,128]{2,1,0:T(8,128)(2,1)S(1)}, bf16[3,960,128]{2,1,0:T(8...) custom-call(s32[8]{0:T(128)S(1)} %pad_add_fusion.small_ref, ...), custom_call_target="tpu_custom_call" | custom-call | flops 4227858432 | bytes 16121856 | tf_op jit(solution)/shard_map/ladder/pallas_call | solution.py:138
  37.8 1.0 %collective-permute-done.11.refs_2_ = bf16[2,960,128]{2,1,0:T(8,128)(2,1)S(1)} collective-permute-done((bf16[2,960,128]{2,1,0:T(8,128)(2,1)S(1)}, bf16[2,960,128]{2,1,0:T(8,128)(2,1)S(1)}, u32[]{:S(2)}, u32[]{:S(2)}) %collective-permute-start.11) | collective-permute-done | bytes 491552 | tf_op jit(solution)/shard_map/ppermute | solution.py:277
  39.3 0.6 contract.1
  39.9 2.1 %collective-permute-done.12 = bf16[3,960,128]{2,1,0:T(8,128)(2,1)S(1)} collective-permute-done((bf16[3,960,128]{2,1,0:T(8,128)(2,1)S(1)}, bf16[3,960,128]{2,1,0:T(8,128)(2,1)S(1)}, u32[]{:S(2)}, u32[]{:S(2)}) %collective-permute-start.12) | collective-permute-done | bytes 737312 | tf_op jit(solution)/shard_map/ppermute | solution.py:20
  42.3 1.6 %add_convert_fusion.2 = (bf16[1,960,128]{2,1,0:T(8,128)(2,1)S(1)}, bf16[1,960,128]{2,1,0:T(8,128)(2,1)S(1)}, bf16[1,960,128]{2,1,0:T(8,128)(2,1)S(1)}, bf16[1,960,128]{2,1,0:T(8,128)(2,1)S(1)}) fusion(bf16[3,960,128]{2,1,0:T(8,128)(2,1)S(1)} %collective-permute-done.13, bf16[3,960,128]{2,1,0:T(8,128)(2,1)} %get-tuple-element.61, ...), kind=kLoop, calls=%fused_computation.2 | loop fusion | flops 1966080 | bytes 2949120 | tf_op jit(solution)/shard_map/convert_element_type | solution.py:306
  44.1 0.5 collective-permute-start.17
  45.3 2.7 %collective-permute-start.16 = (bf16[128,128]{1,0:T(8,128)(2,1)S(1)}, bf16[128,128]{1,0:T(8,128)(2,1)S(1)}, u32[]{:S(2)}, u32[]{:S(2)}) collective-permute-start(bf16[128,128]{1,0:T(8,128)(2,1)S(1)} %get-tuple-element.89), channel_id=1, source_target_pairs={{0,3},{2,1},{3,0},{1,2},{4,7},{6,5},{7,4},{5,6},{8,11},{10,9},{11,... | collective-permute-start | bytes 98312 | tf_op jit(solution)/shard_map/ppermute | solution.py:277
  48.0 1.3 %collective-permute-start.15 = (bf16[128,128]{1,0:T(8,128)(2,1)S(1)}, bf16[128,128]{1,0:T(8,128)(2,1)S(1)}, u32[]{:S(2)}, u32[]{:S(2)}) collective-permute-start(bf16[128,128]{1,0:T(8,128)(2,1)S(1)} %get-tuple-element.90), channel_id=1, source_target_pairs={{0,1},{2,0},{3,2},{1,3},{4,5},{6,4},{7,6},{5,7},{8,9},{10,8},{11,1... | collective-permute-start | bytes 98312 | tf_op jit(solution)/shard_map/ppermute | solution.py:277
  49.4 1.3 %collective-permute-start.24 = (bf16[1,960,128]{2,1,0:T(8,128)(2,1)S(1)}, bf16[1,960,128]{2,1,0:T(8,128)(2,1)S(1)}, u32[]{:S(2)}, u32[]{:S(2)}) collective-permute-start(bf16[1,960,128]{2,1,0:T(8,128)(2,1)S(1)} %get-tuple-element.73), channel_id=1, source_target_pairs={{0,8},{4,12},{8,0},{12,4},{16,24},{20,28},{24,16},{28,20},{1,9},{5... | collective-permute-start | bytes 737288 | tf_op jit(solution)/shard_map/ppermute | solution.py:20
  51.2 1.7 %collective-permute-start.25 = (bf16[1,960,128]{2,1,0:T(8,128)(2,1)S(1)}, bf16[1,960,128]{2,1,0:T(8,128)(2,1)S(1)}, u32[]{:S(2)}, u32[]{:S(2)}) collective-permute-start(bf16[1,960,128]{2,1,0:T(8,128)(2,1)S(1)} %get-tuple-element.74), channel_id=1, source_target_pairs={{0,16},{4,20},{8,24},{12,28},{16,0},{20,4},{24,8},{28,12},{1,17},{... | collective-permute-start | bytes 737288 | tf_op jit(solution)/shard_map/ppermute | solution.py:20
  52.9 1.6 %collective-permute-start.19 = (bf16[4,128,128]{2,1,0:T(8,128)(2,1)S(1)}, bf16[4,128,128]{2,1,0:T(8,128)(2,1)S(1)}, u32[]{:S(2)}, u32[]{:S(2)}) collective-permute-start(bf16[4,128,128]{2,1,0:T(8,128)(2,1)S(1)} %pad_maximum_fusion), channel_id=1, source_target_pairs={{0,8},{4,12},{8,0},{12,4},{16,24},{20,28},{24,16},{28,20},{1,9},{5... | collective-permute-start | bytes 393224 | tf_op jit(solution)/shard_map/ppermute | solution.py:20
  54.4 1.0 %add_convert_fusion = bf16[1,960,128]{2,1,0:T(8,128)(2,1)S(1)} fusion(bf16[1,960,128]{2,1,0:T(8,128)(2,1)S(1)} %collective-permute-done.18, bf16[3,960,128]{2,1,0:T(8,128)(2,1)S(1)} %collective-permute-done.13, bf16[3,960,128]{2,1,0:T(8,128)(2,1)} %get-tuple-element.61), kind=kLoop, calls=%fused_computation | loop fusion | flops 737280 | bytes 983040 | tf_op jit(solution)/shard_map/convert_element_type | solution.py:318
  55.5 3.9 %collective-permute-start.21 = (bf16[2,960,128]{2,1,0:T(8,128)(2,1)S(1)}, bf16[2,960,128]{2,1,0:T(8,128)(2,1)S(1)}, u32[]{:S(2)}, u32[]{:S(2)}) collective-permute-start(bf16[2,960,128]{2,1,0:T(8,128)(2,1)S(1)} %collective-permute-done.11.refs_2_), channel_id=1, source_target_pairs={{0,2},{2,3},{3,1},{1,0},{4,6},{6,7},{7,5},{5,4},{8,10},{10,11},{11... | collective-permute-start | bytes 1474568 | tf_op jit(solution)/shard_map/ppermute | solution.py:277
  59.4 1.0 %add_convert_fusion.1 = bf16[1,960,128]{2,1,0:T(8,128)(2,1)S(1)} fusion(bf16[1,960,128]{2,1,0:T(8,128)(2,1)S(1)} %collective-permute-done.17, bf16[3,960,128]{2,1,0:T(8,128)(2,1)S(1)} %collective-permute-done.12, bf16[3,960,128]{2,1,0:T(8,128)(2,1)} %get-tuple-element.54), kind=kLoop, calls=%fused_computation.1 | loop fusion | flops 737280 | bytes 983040 | tf_op jit(solution)/shard_map/convert_element_type | solution.py:317
  60.6 0.6 collective-permute-start.23
  61.2 2.0 %collective-permute-start.20 = (bf16[4,128,128]{2,1,0:T(8,128)(2,1)S(1)}, bf16[4,128,128]{2,1,0:T(8,128)(2,1)S(1)}, u32[]{:S(2)}, u32[]{:S(2)}) collective-permute-start(bf16[4,128,128]{2,1,0:T(8,128)(2,1)S(1)} %add_convert_fusion.7), channel_id=1, source_target_pairs={{0,16},{4,20},{8,24},{12,28},{16,0},{20,4},{24,8},{28,12},{1,17},{... | collective-permute-start | bytes 393224 | tf_op jit(solution)/shard_map/ppermute | solution.py:20
  63.2 4.4 %collective-permute-done.22.refs_6_ = bf16[1,960,128]{2,1,0:T(8,128)(2,1)S(1)} collective-permute-done((bf16[1,960,128]{2,1,0:T(8,128)(2,1)S(1)}, bf16[1,960,128]{2,1,0:T(8,128)(2,1)S(1)}, u32[]{:S(2)}, u32[]{:S(2)}) %collective-permute-start.22) | collective-permute-done | bytes 245792 | tf_op jit(solution)/shard_map/ppermute | solution.py:20
  67.7 1.3 %collective-permute-done.20 = bf16[4,128,128]{2,1,0:T(8,128)(2,1)S(1)} collective-permute-done((bf16[4,128,128]{2,1,0:T(8,128)(2,1)S(1)}, bf16[4,128,128]{2,1,0:T(8,128)(2,1)S(1)}, u32[]{:S(2)}, u32[]{:S(2)}) %collective-permute-start.20) | collective-permute-done | bytes 131104 | tf_op jit(solution)/shard_map/ppermute | solution.py:20
  69.1 1.3 %collective-permute-done.26.other_ref = bf16[4,128,128]{2,1,0:T(8,128)(2,1)S(1)} collective-permute-done((bf16[4,128,128]{2,1,0:T(8,128)(2,1)S(1)}, bf16[4,128,128]{2,1,0:T(8,128)(2,1)S(1)}, u32[]{:S(2)}, u32[]{:S(2)}) %collective-permute-start.26) | collective-permute-done | bytes 131104 | tf_op jit(solution)/shard_map/ppermute | solution.py:20
  70.4 0.7 quadratic.1.base_ref
  71.2 1.1 %finish.1 = bf16[2,960,128]{2,1,0:T(8,128)(2,1)} custom-call(f32[2,960,128]{2,1,0:T(8,128)S(1)} %quadratic.1.base_ref, bf16[2,960,128]{2,1,0:T(8,128)(2,1)S(1)} %get-tuple-element.77.refs_0_.refs_1_, bf16[2,960,128]{2,1,0:T(8,128)(2,1)S(1)} %get-tuple-element.77.refs_0_.refs_1_, bf16[2,960,128]{2,1,0:T(8,128)(2,1)S(1)} %collective-permute-done.27.refs_2_.refs_3_, ...), custom_call_target="tpu_custom_call" | custom-call | tf_op jit(solution)/shard_map/finish/pallas_call | solution.py:251
  (44 shorter events, 4.4 us)
Async XLA Ops:
  0.0 14.4 %collective-permute-start.1 = (bf16[2,960,128]{2,1,0:T(8,128)(2,1)}, bf16[2,960,128]{2,1,0:T(8,128)(2,1)S(1)}, u32[]{:S(2)}, u32[]{:S(2)}) collective-permute-start(bf16[2,960,128]{2,1,0:T(8,128)(2,1)} %source_ref.1), channel_id=1, source_target_pairs={{0,16},{4,20},{8,24},{12,28},{16,0},{20,4},{24,8},{28,12},{1,17},{... | collective-permute-start | bytes 1474568 | tf_op jit(solution)/shard_map/ppermute | solution.py:20
  3.0 12.9 %collective-permute-start = (bf16[2,960,128]{2,1,0:T(8,128)(2,1)}, bf16[2,960,128]{2,1,0:T(8,128)(2,1)S(1)}, u32[]{:S(2)}, u32[]{:S(2)}) collective-permute-start(bf16[2,960,128]{2,1,0:T(8,128)(2,1)} %source_ref.1), channel_id=1, source_target_pairs={{0,8},{4,12},{8,0},{12,4},{16,24},{20,28},{24,16},{28,20},{1,9},{5... | collective-permute-start | bytes 1474568 | tf_op jit(solution)/shard_map/ppermute | solution.py:20
  4.5 19.3 %collective-permute-start.6 = (bf16[2,960,128]{2,1,0:T(8,128)(2,1)}, bf16[2,960,128]{2,1,0:T(8,128)(2,1)S(1)}, u32[]{:S(2)}, u32[]{:S(2)}) collective-permute-start(bf16[2,960,128]{2,1,0:T(8,128)(2,1)} %source_ref.1), channel_id=1, source_target_pairs={{0,4},{4,0},{8,12},{12,8},{16,20},{20,16},{24,28},{28,24},{1,5},{5... | collective-permute-start | bytes 1474568 | tf_op jit(solution)/shard_map/ppermute | solution.py:20
  4.5 20.4 %collective-permute-start.2 = (bf16[2,960,128]{2,1,0:T(8,128)(2,1)}, bf16[2,960,128]{2,1,0:T(8,128)(2,1)S(1)}, u32[]{:S(2)}, u32[]{:S(2)}) collective-permute-start(bf16[2,960,128]{2,1,0:T(8,128)(2,1)} %source_ref.1), channel_id=1, source_target_pairs={{0,2},{2,3},{3,1},{1,0},{4,6},{6,7},{7,5},{5,4},{8,10},{10,11},{11... | collective-permute-start | bytes 1474568 | tf_op jit(solution)/shard_map/ppermute | solution.py:277
  7.1 16.7 %collective-permute-start.3 = (bf16[960,128]{1,0:T(8,128)(2,1)}, bf16[960,128]{1,0:T(8,128)(2,1)S(1)}, u32[]{:S(2)}, u32[]{:S(2)}) collective-permute-start(bf16[960,128]{1,0:T(8,128)(2,1)} %int_ref.1), channel_id=1, source_target_pairs={{0,2},{2,3},{3,1},{1,0},{4,6},{6,7},{7,5},{5,4},{8,10},{10,11},{11... | collective-permute-start | bytes 737288 | tf_op jit(solution)/shard_map/ppermute | solution.py:277
  9.4 1.0 %copy-start = (bf16[2,960,128]{2,1,0:T(8,128)(2,1)S(1)}, bf16[2,960,128]{2,1,0:T(8,128)(2,1)}, u32[]{:S(2)}) copy-start(bf16[2,960,128]{2,1,0:T(8,128)(2,1)} %source_ref.1) | copy-start | bytes 1474564
  10.7 28.6 %copy-start.1 = (bf16[960,128]{1,0:T(8,128)(2,1)S(1)}, bf16[960,128]{1,0:T(8,128)(2,1)}, u32[]{:S(2)}) copy-start(bf16[960,128]{1,0:T(8,128)(2,1)} %int_ref.1) | copy-start | bytes 737284
  15.9 8.4 %collective-permute-start.4 = (bf16[960,128]{1,0:T(8,128)(2,1)S(1)}, bf16[960,128]{1,0:T(8,128)(2,1)S(1)}, u32[]{:S(2)}, u32[]{:S(2)}) collective-permute-start(bf16[960,128]{1,0:T(8,128)(2,1)S(1)} %slice_bitcast_fusion.1), channel_id=1, source_target_pairs={{0,8},{4,12},{8,0},{12,4},{16,24},{20,28},{24,16},{28,20},{1,9},{5... | collective-permute-start | bytes 737288 | tf_op jit(solution)/shard_map/ppermute | solution.py:20
  17.5 6.9 %collective-permute-start.5 = (bf16[960,128]{1,0:T(8,128)(2,1)S(1)}, bf16[960,128]{1,0:T(8,128)(2,1)S(1)}, u32[]{:S(2)}, u32[]{:S(2)}) collective-permute-start(bf16[960,128]{1,0:T(8,128)(2,1)S(1)} %slice_bitcast_fusion), channel_id=1, source_target_pairs={{0,16},{4,20},{8,24},{12,28},{16,0},{20,4},{24,8},{28,12},{1,17},{... | collective-permute-start | bytes 737288 | tf_op jit(solution)/shard_map/ppermute | solution.py:20
  23.8 4.3 %collective-permute-start.7 = (bf16[2,960,128]{2,1,0:T(8,128)(2,1)S(1)}, bf16[2,960,128]{2,1,0:T(8,128)(2,1)S(1)}, u32[]{:S(2)}, u32[]{:S(2)}) collective-permute-start(bf16[2,960,128]{2,1,0:T(8,128)(2,1)S(1)} %collective-permute-done.refs_1_), channel_id=1, source_target_pairs={{0,4},{4,0},{8,12},{12,8},{16,20},{20,16},{24,28},{28,24},{1,5},{5... | collective-permute-start | bytes 1474568 | tf_op jit(solution)/shard_map/ppermute | solution.py:20
  23.8 4.3 %collective-permute-start.8 = (bf16[2,960,128]{2,1,0:T(8,128)(2,1)S(1)}, bf16[2,960,128]{2,1,0:T(8,128)(2,1)S(1)}, u32[]{:S(2)}, u32[]{:S(2)}) collective-permute-start(bf16[2,960,128]{2,1,0:T(8,128)(2,1)S(1)} %collective-permute-done.1.refs_2_), channel_id=1, source_target_pairs={{0,4},{4,0},{8,12},{12,8},{16,20},{20,16},{24,28},{28,24},{1,5},{5... | collective-permute-start | bytes 1474568 | tf_op jit(solution)/shard_map/ppermute | solution.py:20
  24.3 3.8 %collective-permute-start.9 = (bf16[960,128]{1,0:T(8,128)(2,1)S(1)}, bf16[960,128]{1,0:T(8,128)(2,1)S(1)}, u32[]{:S(2)}, u32[]{:S(2)}) collective-permute-start(bf16[960,128]{1,0:T(8,128)(2,1)S(1)} %collective-permute-done.4.refs_3_), channel_id=1, source_target_pairs={{0,4},{4,0},{8,12},{12,8},{16,20},{20,16},{24,28},{28,24},{1,5},{5... | collective-permute-start | bytes 737288 | tf_op jit(solution)/shard_map/ppermute | solution.py:20
  24.4 3.7 %collective-permute-start.10 = (bf16[960,128]{1,0:T(8,128)(2,1)S(1)}, bf16[960,128]{1,0:T(8,128)(2,1)S(1)}, u32[]{:S(2)}, u32[]{:S(2)}) collective-permute-start(bf16[960,128]{1,0:T(8,128)(2,1)S(1)} %collective-permute-done.5.refs_4_), channel_id=1, source_target_pairs={{0,4},{4,0},{8,12},{12,8},{16,20},{20,16},{24,28},{28,24},{1,5},{5... | collective-permute-start | bytes 737288 | tf_op jit(solution)/shard_map/ppermute | solution.py:20
  24.8 14.0 %collective-permute-start.11 = (bf16[2,960,128]{2,1,0:T(8,128)(2,1)S(1)}, bf16[2,960,128]{2,1,0:T(8,128)(2,1)S(1)}, u32[]{:S(2)}, u32[]{:S(2)}) collective-permute-start(bf16[2,960,128]{2,1,0:T(8,128)(2,1)S(1)} %collective-permute-done.2.refs_1_), channel_id=1, source_target_pairs={{0,2},{2,3},{3,1},{1,0},{4,6},{6,7},{7,5},{5,4},{8,10},{10,11},{11... | collective-permute-start | bytes 1474568 | tf_op jit(solution)/shard_map/ppermute | solution.py:277
  38.8 3.2 %collective-permute-start.12 = (bf16[3,960,128]{2,1,0:T(8,128)(2,1)S(1)}, bf16[3,960,128]{2,1,0:T(8,128)(2,1)S(1)}, u32[]{:S(2)}, u32[]{:S(2)}) collective-permute-start(bf16[3,960,128]{2,1,0:T(8,128)(2,1)S(1)} %get-tuple-element.55), channel_id=1, source_target_pairs={{0,4},{4,0},{8,12},{12,8},{16,20},{20,16},{24,28},{28,24},{1,5},{5... | collective-permute-start | bytes 2211848 | tf_op jit(solution)/shard_map/ppermute | solution.py:20
  38.8 3.5 %collective-permute-start.13 = (bf16[3,960,128]{2,1,0:T(8,128)(2,1)}, bf16[3,960,128]{2,1,0:T(8,128)(2,1)S(1)}, u32[]{:S(2)}, u32[]{:S(2)}) collective-permute-start(bf16[3,960,128]{2,1,0:T(8,128)(2,1)} %get-tuple-element.56), channel_id=1, source_target_pairs={{0,4},{4,0},{8,12},{12,8},{16,20},{20,16},{24,28},{28,24},{1,5},{5... | collective-permute-start | bytes 2211848 | tf_op jit(solution)/shard_map/ppermute | solution.py:20
  43.9 1.4 %collective-permute-start.14 = (bf16[4,128,128]{2,1,0:T(8,128)(2,1)S(1)}, bf16[4,128,128]{2,1,0:T(8,128)(2,1)S(1)}, u32[]{:S(2)}, u32[]{:S(2)}) collective-permute-start(bf16[4,128,128]{2,1,0:T(8,128)(2,1)S(1)} %get-tuple-element.66), channel_id=1, source_target_pairs={{0,4},{4,0},{8,12},{12,8},{16,20},{20,16},{24,28},{28,24},{1,5},{5... | collective-permute-start | bytes 393224 | tf_op jit(solution)/shard_map/ppermute | solution.py:20
  44.1 8.8 %collective-permute-start.17 = (bf16[1,960,128]{2,1,0:T(8,128)(2,1)S(1)}, bf16[1,960,128]{2,1,0:T(8,128)(2,1)S(1)}, u32[]{:S(2)}, u32[]{:S(2)}) collective-permute-start(bf16[1,960,128]{2,1,0:T(8,128)(2,1)S(1)} %get-tuple-element.67), channel_id=1, source_target_pairs={{0,8},{4,12},{8,0},{12,4},{16,24},{20,28},{24,16},{28,20},{1,9},{5... | collective-permute-start | bytes 737288 | tf_op jit(solution)/shard_map/ppermute | solution.py:20
  44.6 8.2 %collective-permute-start.18 = (bf16[1,960,128]{2,1,0:T(8,128)(2,1)S(1)}, bf16[1,960,128]{2,1,0:T(8,128)(2,1)S(1)}, u32[]{:S(2)}, u32[]{:S(2)}) collective-permute-start(bf16[1,960,128]{2,1,0:T(8,128)(2,1)S(1)} %get-tuple-element.68), channel_id=1, source_target_pairs={{0,16},{4,20},{8,24},{12,28},{16,0},{20,4},{24,8},{28,12},{1,17},{... | collective-permute-start | bytes 737288 | tf_op jit(solution)/shard_map/ppermute | solution.py:20
  45.3 5.8 %collective-permute-start.16 = (bf16[128,128]{1,0:T(8,128)(2,1)S(1)}, bf16[128,128]{1,0:T(8,128)(2,1)S(1)}, u32[]{:S(2)}, u32[]{:S(2)}) collective-permute-start(bf16[128,128]{1,0:T(8,128)(2,1)S(1)} %get-tuple-element.89), channel_id=1, source_target_pairs={{0,3},{2,1},{3,0},{1,2},{4,7},{6,5},{7,4},{5,6},{8,11},{10,9},{11,... | collective-permute-start | bytes 98312 | tf_op jit(solution)/shard_map/ppermute | solution.py:277
  48.0 4.8 %collective-permute-start.15 = (bf16[128,128]{1,0:T(8,128)(2,1)S(1)}, bf16[128,128]{1,0:T(8,128)(2,1)S(1)}, u32[]{:S(2)}, u32[]{:S(2)}) collective-permute-start(bf16[128,128]{1,0:T(8,128)(2,1)S(1)} %get-tuple-element.90), channel_id=1, source_target_pairs={{0,1},{2,0},{3,2},{1,3},{4,5},{6,4},{7,6},{5,7},{8,9},{10,8},{11,1... | collective-permute-start | bytes 98312 | tf_op jit(solution)/shard_map/ppermute | solution.py:277
  49.4 11.8 %collective-permute-start.24 = (bf16[1,960,128]{2,1,0:T(8,128)(2,1)S(1)}, bf16[1,960,128]{2,1,0:T(8,128)(2,1)S(1)}, u32[]{:S(2)}, u32[]{:S(2)}) collective-permute-start(bf16[1,960,128]{2,1,0:T(8,128)(2,1)S(1)} %get-tuple-element.73), channel_id=1, source_target_pairs={{0,8},{4,12},{8,0},{12,4},{16,24},{20,28},{24,16},{28,20},{1,9},{5... | collective-permute-start | bytes 737288 | tf_op jit(solution)/shard_map/ppermute | solution.py:20
  51.2 12.0 %collective-permute-start.25 = (bf16[1,960,128]{2,1,0:T(8,128)(2,1)S(1)}, bf16[1,960,128]{2,1,0:T(8,128)(2,1)S(1)}, u32[]{:S(2)}, u32[]{:S(2)}) collective-permute-start(bf16[1,960,128]{2,1,0:T(8,128)(2,1)S(1)} %get-tuple-element.74), channel_id=1, source_target_pairs={{0,16},{4,20},{8,24},{12,28},{16,0},{20,4},{24,8},{28,12},{1,17},{... | collective-permute-start | bytes 737288 | tf_op jit(solution)/shard_map/ppermute | solution.py:20
  52.9 7.7 %collective-permute-start.19 = (bf16[4,128,128]{2,1,0:T(8,128)(2,1)S(1)}, bf16[4,128,128]{2,1,0:T(8,128)(2,1)S(1)}, u32[]{:S(2)}, u32[]{:S(2)}) collective-permute-start(bf16[4,128,128]{2,1,0:T(8,128)(2,1)S(1)} %pad_maximum_fusion), channel_id=1, source_target_pairs={{0,8},{4,12},{8,0},{12,4},{16,24},{20,28},{24,16},{28,20},{1,9},{5... | collective-permute-start | bytes 393224 | tf_op jit(solution)/shard_map/ppermute | solution.py:20
  55.5 13.5 %collective-permute-start.21 = (bf16[2,960,128]{2,1,0:T(8,128)(2,1)S(1)}, bf16[2,960,128]{2,1,0:T(8,128)(2,1)S(1)}, u32[]{:S(2)}, u32[]{:S(2)}) collective-permute-start(bf16[2,960,128]{2,1,0:T(8,128)(2,1)S(1)} %collective-permute-done.11.refs_2_), channel_id=1, source_target_pairs={{0,2},{2,3},{3,1},{1,0},{4,6},{6,7},{7,5},{5,4},{8,10},{10,11},{11... | collective-permute-start | bytes 1474568 | tf_op jit(solution)/shard_map/ppermute | solution.py:277
  60.4 7.1 %collective-permute-start.22 = (bf16[1,960,128]{2,1,0:T(8,128)(2,1)S(1)}, bf16[1,960,128]{2,1,0:T(8,128)(2,1)S(1)}, u32[]{:S(2)}, u32[]{:S(2)}) collective-permute-start(bf16[1,960,128]{2,1,0:T(8,128)(2,1)S(1)} %add_convert_fusion.1), channel_id=1, source_target_pairs={{0,16},{4,20},{8,24},{12,28},{16,0},{20,4},{24,8},{28,12},{1,17},{... | collective-permute-start | bytes 737288 | tf_op jit(solution)/shard_map/ppermute | solution.py:20
  60.6 7.1 %collective-permute-start.23 = (bf16[1,960,128]{2,1,0:T(8,128)(2,1)S(1)}, bf16[1,960,128]{2,1,0:T(8,128)(2,1)S(1)}, u32[]{:S(2)}, u32[]{:S(2)}) collective-permute-start(bf16[1,960,128]{2,1,0:T(8,128)(2,1)S(1)} %add_convert_fusion), channel_id=1, source_target_pairs={{0,8},{4,12},{8,0},{12,4},{16,24},{20,28},{24,16},{28,20},{1,9},{5... | collective-permute-start | bytes 737288 | tf_op jit(solution)/shard_map/ppermute | solution.py:20
  61.2 7.8 %collective-permute-start.20 = (bf16[4,128,128]{2,1,0:T(8,128)(2,1)S(1)}, bf16[4,128,128]{2,1,0:T(8,128)(2,1)S(1)}, u32[]{:S(2)}, u32[]{:S(2)}) collective-permute-start(bf16[4,128,128]{2,1,0:T(8,128)(2,1)S(1)} %add_convert_fusion.7), channel_id=1, source_target_pairs={{0,16},{4,20},{8,24},{12,28},{16,0},{20,4},{24,8},{28,12},{1,17},{... | collective-permute-start | bytes 393224 | tf_op jit(solution)/shard_map/ppermute | solution.py:20
  63.2 7.9 %collective-permute-start.27 = (bf16[2,960,128]{2,1,0:T(8,128)(2,1)S(1)}, bf16[2,960,128]{2,1,0:T(8,128)(2,1)S(1)}, u32[]{:S(2)}, u32[]{:S(2)}) collective-permute-start(bf16[2,960,128]{2,1,0:T(8,128)(2,1)S(1)} %get-tuple-element.78), channel_id=1, source_target_pairs={{0,4},{4,0},{8,12},{12,8},{16,20},{20,16},{24,28},{28,24},{1,5},{5... | collective-permute-start | bytes 1474568 | tf_op jit(solution)/shard_map/ppermute | solution.py:20
  69.0 1.4 %collective-permute-start.26 = (bf16[4,128,128]{2,1,0:T(8,128)(2,1)S(1)}, bf16[4,128,128]{2,1,0:T(8,128)(2,1)S(1)}, u32[]{:S(2)}, u32[]{:S(2)}) collective-permute-start(bf16[4,128,128]{2,1,0:T(8,128)(2,1)S(1)} %add_convert_fusion.6.mine_ref), channel_id=1, source_target_pairs={{0,4},{4,0},{8,12},{12,8},{16,20},{20,16},{24,28},{28,24},{1,5},{5... | collective-permute-start | bytes 393224 | tf_op jit(solution)/shard_map/ppermute | solution.py:20

commit v11 on v10

--- a/solution.py
+++ b/solution.py
@@ -151,7 +151,7 @@
         ),
         out_shape=[jax.ShapeDtypeStruct((len(places), rows, columns), BF16) for places in groups],
         compiler_params=pltpu.CompilerParams(
-            dimension_semantics=("arbitrary",), vmem_limit_bytes=48 * 1024 * 1024
+            dimension_semantics=("arbitrary",), vmem_limit_bytes=40 * 1024 * 1024
         ),
         cost_estimate=pl.CostEstimate(
             flops=slots * 8 * BLOCK * BLOCK * columns,
@@ -201,9 +201,9 @@
     )(core, integrals, back_integrals, *ring)
 
 
-def quadratic_kernel(core_ref, mine_ref, other_ref, *refs):
-    amp_ref, out_ref = refs[0], refs[-1]
-    _, rows, columns = amp_ref.shape
+def quadratic_kernel(core_ref, mine_ref, other_ref, base_ref, *refs):
+    out_ref = refs[-1]
+    _, rows, columns = base_ref.shape
     vp_size = len(refs) - 1
     core = core_ref[0]
     total = jnp.zeros((rows, 2 * columns), F32)
@@ -216,46 +216,46 @@
             [jnp.concatenate([real, imag], axis=1), jnp.concatenate([-imag, real], axis=1)], axis=0
         )
         total += jnp.dot(both, weights, preferred_element_type=F32)
-    out_ref[0] = amp_ref[0].astype(F32) + 0.25 * total[:, columns:]
-    out_ref[1] = amp_ref[1].astype(F32) - 0.25 * total[:, :columns]
-
-
-def quadratic(core, ring, mine, other):
+    out_ref[0] = (base_ref[0] + 0.25 * total[:, columns:]).astype(BF16)
+    out_ref[1] = (base_ref[1] - 0.25 * total[:, :columns]).astype(BF16)
+
+
+def quadratic(core, ring, mine, other, base):
     vmem = pl.BlockSpec(memory_space=pltpu.VMEM)
     size = ring[0].size
     return pl.pallas_call(
         quadratic_kernel,
-        in_specs=[pl.BlockSpec(memory_space=pltpu.SMEM)] + [vmem] * (2 + len(ring)),
-        out_specs=vmem,
-        out_shape=jax.ShapeDtypeStruct(ring[0].shape, F32),
-        compiler_params=pltpu.CompilerParams(vmem_limit_bytes=20 * 1024 * 1024),
-        cost_estimate=pl.CostEstimate(
-            flops=4 * len(ring) * size * ring[0].shape[2],
-            bytes_accessed=(2 * len(ring) + 4) * size,
-            transcendentals=0,
-        ),
-        name="quadratic",
-    )(core, mine, other, *ring)
-
-
-def finish_kernel(places, base_ref, *refs):
-    sums = [0.0, 0.0]
-    for ref, (_, part, place) in zip(refs, places, strict=False):
-        sums[part] = sums[part] + ref[place].astype(F32)
-    refs[-1][0] = (base_ref[0] + 0.5 * sums[1]).astype(BF16)
-    refs[-1][1] = (base_ref[1] - 0.5 * sums[0]).astype(BF16)
-
-
-def finish(base, terms):
-    vmem = pl.BlockSpec(memory_space=pltpu.VMEM)
-    return pl.pallas_call(
-        functools.partial(finish_kernel, [(None, part, place) for _, part, place in terms]),
-        in_specs=[vmem] * (1 + len(terms)),
+        in_specs=[pl.BlockSpec(memory_space=pltpu.SMEM)] + [vmem] * (3 + len(ring)),
         out_specs=vmem,
         out_shape=jax.ShapeDtypeStruct(base.shape, BF16),
         compiler_params=pltpu.CompilerParams(vmem_limit_bytes=20 * 1024 * 1024),
-        name="finish",
-    )(base, *[value for value, _, _ in terms])
+        cost_estimate=pl.CostEstimate(
+            flops=4 * len(ring) * size * base.shape[2],
+            bytes_accessed=(2 * len(ring) + 6) * size,
+            transcendentals=0,
+        ),
+        name="quadratic",
+    )(core, mine, other, base, *ring)
+
+
+def combine_kernel(places, amp_ref, *refs):
+    sums = [0.0, 0.0]
+    for ref, (part, place) in zip(refs, places, strict=False):
+        sums[part] = sums[part] + ref[place].astype(F32)
+    refs[-1][0] = amp_ref[0].astype(F32) + 0.5 * sums[1]
+    refs[-1][1] = amp_ref[1].astype(F32) - 0.5 * sums[0]
+
+
+def combine(amplitudes, terms):
+    vmem = pl.BlockSpec(memory_space=pltpu.VMEM)
+    return pl.pallas_call(
+        functools.partial(combine_kernel, [(part, place) for _, part, place in terms]),
+        in_specs=[vmem] * (1 + len(terms)),
+        out_specs=vmem,
+        out_shape=jax.ShapeDtypeStruct(amplitudes.shape, F32),
+        compiler_params=pltpu.CompilerParams(vmem_limit_bytes=20 * 1024 * 1024),
+        name="combine",
+    )(amplitudes, *[value for value, _, _ in terms])
 
 
 def scatter_plain(partial, tri_size):
@@ -312,13 +312,12 @@
         far_x, far_y = swap(far_x, tri_size, 1), swap(far_y, tri_size, 2)
         near_x, near_y = swap(near_x, tri_size, 1), swap(near_y, tri_size, 2)
         mine = shift(add(hold, swap(give, tri_size, 0)).astype(BF16))
-        mine, far_x, far_y = lax.optimization_barrier((mine, far_x, far_y))
-        last = turn(after(ring[-1], mine))
+        mine, far_x, far_y, last = lax.optimization_barrier((mine, far_x, far_y, turn(ring[-1])))
         then_y = swap(add(real[2], real_in[2], far_x[0]).astype(BF16)[None], tri_size, 2)
         then_x = swap(add(imag[2], imag_in[2], far_y[0]).astype(BF16)[None], tri_size, 1)
         mine = add(mine, swap(mine, tri_size, 1)).astype(BF16)
-        received, last, then_y, then_x, near_x, near_y = lax.optimization_barrier(
-            (swap(mine, tri_size, 2), last, then_y, then_x, near_x, near_y)
+        received, then_y, then_x, near_x, near_y = lax.optimization_barrier(
+            (swap(mine, tri_size, 2), then_y, then_x, near_x, near_y)
         )
         mine = add(mine, received).astype(BF16)
         terms = [(own, 0, 0), (own, 1, 1), (own_in, 0, 0), (own_in, 1, 1)]
@@ -329,8 +328,8 @@
         mine = shift(add(hold, swap(give, tri_size, 0)).astype(BF16))
         for bit in range(1, bits):
             mine = add(mine, swap(mine, tri_size, bit)).astype(BF16)
-    base = quadratic(core, [*ring, last], mine, swap(mine, tri_size, 0))
-    return finish(base, terms)
+    base = combine(ring[0], terms)
+    return quadratic(core, [*ring, last], mine, swap(mine, tri_size, 0), base)
 
 
 def solution(mesh):

time: 72.5 us -> 79.9 us (1.10)
  waiting for transfers between devices: 22.1 us -> 39.6 us
  starting transfers between devices: 32 us -> 26.5 us
  other arithmetic: 4.52 us -> 1.32 us
  Pallas kernels: 12.4 us -> 11 us
    ppermute x6, waiting for transfers between devices: 7.26 us -> 20 us  [turn(): lax.ppermute(value, 'vp', [(order[i], order[(i + distance) % vp_size]) fo...]
    ppermute x22, waiting for transfers between devices: 14.8 us -> 19.6 us  [swap(): return lax.ppermute(value, 'tri', pairs)]
    ppermute x6, starting transfers between devices: 15.4 us -> 12.3 us  [turn(): lax.ppermute(value, 'vp', [(order[i], order[(i + distance) % vp_size]) fo...]
    ppermute x22, starting transfers between devices: 16.6 us -> 14.3 us  [swap(): return lax.ppermute(value, 'tri', pairs)]
    pallas_call x1, Pallas kernels: 9.71 us -> 8.32 us  [ladder(): pl.pallas_call(functools.partial(ladder_kernel, [(mask, part) for _, mask...]
    convert_element_type x1, other arithmetic: 1.57 us -> 0.26 us  [shards(): add(kept[i], came[i]).astype(BF16)[None]]
    convert_element_type x1, other arithmetic: 1.04 us -> 0.1 us  [shards(): add(real[2], real_in[2], far_x[0]).astype(BF16)[None]]
    convert_element_type x1, other arithmetic: 1.04 us -> 0.1 us  [shards(): add(imag[2], imag_in[2], far_y[0]).astype(BF16)[None]]
  transfers between devices with their start and end apart: 28 -> 28, of which waited for: 12 -> 12; matrix products, arithmetic and copies ran while one was open for 4% -> 1% of each run, Pallas kernels for 16% -> 12%
where the time goes in v11:
time: 79.9 us; the launch traced here: 79.8 us
  waiting for transfers between devices  39.6 us (50%)
  starting transfers between devices  26.5 us (33%)
  Pallas kernels  11 us (14%)
  other arithmetic  1.32 us (2%)
  local copies, waits for them, and re-layouts  1.08 us (1%)
    ppermute x6, waiting for transfers between devices, turn(): lax.ppermute(value, 'vp', [(order[i], order[(i + distance) % vp_size]) fo...  20 us
    ppermute x22, waiting for transfers between devices, swap(): return lax.ppermute(value, 'tri', pairs)  19.6 us
    ppermute x22, starting transfers between devices, swap(): return lax.ppermute(value, 'tri', pairs)  14.3 us
    ppermute x6, starting transfers between devices, turn(): lax.ppermute(value, 'vp', [(order[i], order[(i + distance) % vp_size]) fo...  12.3 us
    pallas_call x1, Pallas kernels, ladder(): pl.pallas_call(functools.partial(ladder_kernel, [(mask, part) for _, mask...  8.32 us
  transfers between devices with their start and end apart: 28, of which 12 were waited for; matrix products, arithmetic and copies ran while one was open for 1% of the time, Pallas kernels for 12%

profile of v11, /device:TPU:0, one launch (start us, length us, event | category | flops | bytes accessed | tf_op | source)
XLA Modules:
  0.0 79.8 jit_solution(5889982770566037723)
XLA Ops:
  0.0 3.0 %collective-permute-start.1 = (bf16[2,960,128]{2,1,0:T(8,128)(2,1)}, bf16[2,960,128]{2,1,0:T(8,128)(2,1)S(1)}, u32[]{:S(2)}, u32[]{:S(2)}) collective-permute-start(bf16[2,960,128]{2,1,0:T(8,128)(2,1)} %source_ref.1), channel_id=1, source_target_pairs={{0,16},{4,20},{8,24},{12,28},{16,0},{20,4},{24,8},{28,12},{1,17},{... | collective-permute-start | bytes 1474568 | tf_op jit(solution)/shard_map/ppermute | solution.py:20
  3.0 1.5 %collective-permute-start = (bf16[2,960,128]{2,1,0:T(8,128)(2,1)}, bf16[2,960,128]{2,1,0:T(8,128)(2,1)S(1)}, u32[]{:S(2)}, u32[]{:S(2)}) collective-permute-start(bf16[2,960,128]{2,1,0:T(8,128)(2,1)} %source_ref.1), channel_id=1, source_target_pairs={{0,8},{4,12},{8,0},{12,4},{16,24},{20,28},{24,16},{28,20},{1,9},{5... | collective-permute-start | bytes 1474568 | tf_op jit(solution)/shard_map/ppermute | solution.py:20
  4.5 2.6 %collective-permute-start.2 = (bf16[2,960,128]{2,1,0:T(8,128)(2,1)}, bf16[2,960,128]{2,1,0:T(8,128)(2,1)S(1)}, u32[]{:S(2)}, u32[]{:S(2)}) collective-permute-start(bf16[2,960,128]{2,1,0:T(8,128)(2,1)} %source_ref.1), channel_id=1, source_target_pairs={{0,2},{2,3},{3,1},{1,0},{4,6},{6,7},{7,5},{5,4},{8,10},{10,11},{11... | collective-permute-start | bytes 1474568 | tf_op jit(solution)/shard_map/ppermute | solution.py:277
  7.1 1.6 %collective-permute-start.3 = (bf16[960,128]{1,0:T(8,128)(2,1)}, bf16[960,128]{1,0:T(8,128)(2,1)S(1)}, u32[]{:S(2)}, u32[]{:S(2)}) collective-permute-start(bf16[960,128]{1,0:T(8,128)(2,1)} %int_ref.1), channel_id=1, source_target_pairs={{0,2},{2,3},{3,1},{1,0},{4,6},{6,7},{7,5},{5,4},{8,10},{10,11},{11... | collective-permute-start | bytes 737288 | tf_op jit(solution)/shard_map/ppermute | solution.py:277
  8.6 0.7 pad_add_fusion.small_ref
  9.4 1.0 %copy-done = bf16[2,960,128]{2,1,0:T(8,128)(2,1)S(1)} copy-done((bf16[2,960,128]{2,1,0:T(8,128)(2,1)S(1)}, bf16[2,960,128]{2,1,0:T(8,128)(2,1)}, u32[]{:S(2)}) %copy-start) | copy-done | bytes 491544
  10.7 3.7 %collective-permute-done.1.refs_2_ = bf16[2,960,128]{2,1,0:T(8,128)(2,1)S(1)} collective-permute-done((bf16[2,960,128]{2,1,0:T(8,128)(2,1)}, bf16[2,960,128]{2,1,0:T(8,128)(2,1)S(1)}, u32[]{:S(2)}, u32[]{:S(2)}) %collective-permute-start.1) | collective-permute-done | bytes 491552 | tf_op jit(solution)/shard_map/ppermute | solution.py:20
  14.4 1.5 %collective-permute-done.refs_1_ = bf16[2,960,128]{2,1,0:T(8,128)(2,1)S(1)} collective-permute-done((bf16[2,960,128]{2,1,0:T(8,128)(2,1)}, bf16[2,960,128]{2,1,0:T(8,128)(2,1)S(1)}, u32[]{:S(2)}, u32[]{:S(2)}) %collective-permute-start) | collective-permute-done | bytes 491552 | tf_op jit(solution)/shard_map/ppermute | solution.py:20
  15.9 1.6 %collective-permute-start.4 = (bf16[960,128]{1,0:T(8,128)(2,1)S(1)}, bf16[960,128]{1,0:T(8,128)(2,1)S(1)}, u32[]{:S(2)}, u32[]{:S(2)}) collective-permute-start(bf16[960,128]{1,0:T(8,128)(2,1)S(1)} %slice_bitcast_fusion.1), channel_id=1, source_target_pairs={{0,8},{4,12},{8,0},{12,4},{16,24},{20,28},{24,16},{28,20},{1,9},{5... | collective-permute-start | bytes 737288 | tf_op jit(solution)/shard_map/ppermute | solution.py:20
  17.5 0.5 collective-permute-start.5
  18.0 5.8 %collective-permute-done.3.last_ref = bf16[960,128]{1,0:T(8,128)(2,1)S(1)} collective-permute-done((bf16[960,128]{1,0:T(8,128)(2,1)}, bf16[960,128]{1,0:T(8,128)(2,1)S(1)}, u32[]{:S(2)}, u32[]{:S(2)}) %collective-permute-start.3) | collective-permute-done | bytes 245792 | tf_op jit(solution)/shard_map/ppermute | solution.py:277
  23.8 0.5 collective-permute-start.8
  24.8 3.3 %collective-permute-start.11 = (bf16[2,960,128]{2,1,0:T(8,128)(2,1)S(1)}, bf16[2,960,128]{2,1,0:T(8,128)(2,1)S(1)}, u32[]{:S(2)}, u32[]{:S(2)}) collective-permute-start(bf16[2,960,128]{2,1,0:T(8,128)(2,1)S(1)} %collective-permute-done.2.refs_1_), channel_id=1, source_target_pairs={{0,2},{2,3},{3,1},{1,0},{4,6},{6,7},{7,5},{5,4},{8,10},{10,11},{11... | collective-permute-start | bytes 1474568 | tf_op jit(solution)/shard_map/ppermute | solution.py:277
  28.1 8.3 %ladder.1 = (bf16[3,960,128]{2,1,0:T(8,128)(2,1)S(1)}, bf16[3,960,128]{2,1,0:T(8,128)(2,1)S(1)}, bf16[2,960,128]{2,1,0:T(8,128)(2,1)S(1)}, bf16[3,960,128]{2,1,0...) custom-call(s32[8]{0:T(128)S(1)} %pad_add_fusion.small_ref, ...), custom_call_target="tpu_custom_call" | custom-call | flops 4227858432 | bytes 16121856 | tf_op jit(solution)/shard_map/ladder/pallas_call | solution.py:138
  36.4 2.4 %collective-permute-done.11.refs_2_ = bf16[2,960,128]{2,1,0:T(8,128)(2,1)S(1)} collective-permute-done((bf16[2,960,128]{2,1,0:T(8,128)(2,1)S(1)}, bf16[2,960,128]{2,1,0:T(8,128)(2,1)S(1)}, u32[]{:S(2)}, u32[]{:S(2)}) %collective-permute-start.11) | collective-permute-done | bytes 491552 | tf_op jit(solution)/shard_map/ppermute | solution.py:277
  38.8 0.5 collective-permute-start.13
  39.3 0.6 contract.1
  39.9 1.1 %collective-permute-done.12 = bf16[3,960,128]{2,1,0:T(8,128)(2,1)S(1)} collective-permute-done((bf16[3,960,128]{2,1,0:T(8,128)(2,1)S(1)}, bf16[3,960,128]{2,1,0:T(8,128)(2,1)S(1)}, u32[]{:S(2)}, u32[]{:S(2)}) %collective-permute-start.12) | collective-permute-done | bytes 737312 | tf_op jit(solution)/shard_map/ppermute | solution.py:20
  41.0 1.1 %collective-permute-done.13 = bf16[3,960,128]{2,1,0:T(8,128)(2,1)S(1)} collective-permute-done((bf16[3,960,128]{2,1,0:T(8,128)(2,1)S(1)}, bf16[3,960,128]{2,1,0:T(8,128)(2,1)S(1)}, u32[]{:S(2)}, u32[]{:S(2)}) %collective-permute-start.13) | collective-permute-done | bytes 737312 | tf_op jit(solution)/shard_map/ppermute | solution.py:20
  42.5 3.4 %collective-permute-start.19 = (bf16[2,960,128]{2,1,0:T(8,128)(2,1)S(1)}, bf16[2,960,128]{2,1,0:T(8,128)(2,1)S(1)}, u32[]{:S(2)}, u32[]{:S(2)}) collective-permute-start(bf16[2,960,128]{2,1,0:T(8,128)(2,1)S(1)} %collective-permute-done.11.refs_2_), channel_id=1, source_target_pairs={{0,2},{2,3},{3,1},{1,0},{4,6},{6,7},{7,5},{5,4},{8,10},{10,11},{11... | collective-permute-start | bytes 1474568 | tf_op jit(solution)/shard_map/ppermute | solution.py:277
  45.9 0.5 collective-permute-start.17
  47.0 1.4 %collective-permute-start.16 = (bf16[128,128]{1,0:T(8,128)(2,1)S(1)}, bf16[128,128]{1,0:T(8,128)(2,1)S(1)}, u32[]{:S(2)}, u32[]{:S(2)}) collective-permute-start(bf16[128,128]{1,0:T(8,128)(2,1)S(1)} %get-tuple-element.87), channel_id=1, source_target_pairs={{0,3},{2,1},{3,0},{1,2},{4,7},{6,5},{7,4},{5,6},{8,11},{10,9},{11,... | collective-permute-start | bytes 98312 | tf_op jit(solution)/shard_map/ppermute | solution.py:277
  48.5 11.4 %collective-permute-done.16 = bf16[128,128]{1,0:T(8,128)(2,1)S(1)} collective-permute-done((bf16[128,128]{1,0:T(8,128)(2,1)S(1)}, bf16[128,128]{1,0:T(8,128)(2,1)S(1)}, u32[]{:S(2)}, u32[]{:S(2)}) %collective-permute-start.16) | collective-permute-done | bytes 32800 | tf_op jit(solution)/shard_map/ppermute | solution.py:277
  59.9 0.5 collective-permute-start.24
  61.5 1.1 %collective-permute-start.20 = (bf16[4,128,128]{2,1,0:T(8,128)(2,1)S(1)}, bf16[4,128,128]{2,1,0:T(8,128)(2,1)S(1)}, u32[]{:S(2)}, u32[]{:S(2)}) collective-permute-start(bf16[4,128,128]{2,1,0:T(8,128)(2,1)S(1)} %pad_maximum_fusion), channel_id=1, source_target_pairs={{0,8},{4,12},{8,0},{12,4},{16,24},{20,28},{24,16},{28,20},{1,9},{5... | collective-permute-start | bytes 393224 | tf_op jit(solution)/shard_map/ppermute | solution.py:20
  62.7 1.6 %collective-permute-start.22 = (bf16[1,960,128]{2,1,0:T(8,128)(2,1)S(1)}, bf16[1,960,128]{2,1,0:T(8,128)(2,1)S(1)}, u32[]{:S(2)}, u32[]{:S(2)}) collective-permute-start(bf16[1,960,128]{2,1,0:T(8,128)(2,1)S(1)} %add_convert_fusion.1), channel_id=1, source_target_pairs={{0,16},{4,20},{8,24},{12,28},{16,0},{20,4},{24,8},{28,12},{1,17},{... | collective-permute-start | bytes 737288 | tf_op jit(solution)/shard_map/ppermute | solution.py:20
  64.3 1.0 %collective-permute-start.23 = (bf16[1,960,128]{2,1,0:T(8,128)(2,1)S(1)}, bf16[1,960,128]{2,1,0:T(8,128)(2,1)S(1)}, u32[]{:S(2)}, u32[]{:S(2)}) collective-permute-start(bf16[1,960,128]{2,1,0:T(8,128)(2,1)S(1)} %add_convert_fusion), channel_id=1, source_target_pairs={{0,8},{4,12},{8,0},{12,4},{16,24},{20,28},{24,16},{28,20},{1,9},{5... | collective-permute-start | bytes 737288 | tf_op jit(solution)/shard_map/ppermute | solution.py:20
  65.3 6.2 %collective-permute-done.20 = bf16[4,128,128]{2,1,0:T(8,128)(2,1)S(1)} collective-permute-done((bf16[4,128,128]{2,1,0:T(8,128)(2,1)S(1)}, bf16[4,128,128]{2,1,0:T(8,128)(2,1)S(1)}, u32[]{:S(2)}, u32[]{:S(2)}) %collective-permute-start.20) | collective-permute-done | bytes 131104 | tf_op jit(solution)/shard_map/ppermute | solution.py:20
  71.8 3.1 %collective-permute-done.22.refs_6_ = bf16[1,960,128]{2,1,0:T(8,128)(2,1)S(1)} collective-permute-done((bf16[1,960,128]{2,1,0:T(8,128)(2,1)S(1)}, bf16[1,960,128]{2,1,0:T(8,128)(2,1)S(1)}, u32[]{:S(2)}, u32[]{:S(2)}) %collective-permute-start.22) | collective-permute-done | bytes 245792 | tf_op jit(solution)/shard_map/ppermute | solution.py:20
  74.9 1.9 %collective-permute-done.21 = bf16[4,128,128]{2,1,0:T(8,128)(2,1)S(1)} collective-permute-done((bf16[4,128,128]{2,1,0:T(8,128)(2,1)S(1)}, bf16[4,128,128]{2,1,0:T(8,128)(2,1)S(1)}, u32[]{:S(2)}, u32[]{:S(2)}) %collective-permute-start.21) | collective-permute-done | bytes 131104 | tf_op jit(solution)/shard_map/ppermute | solution.py:20
  77.3 1.0 %collective-permute-done.26.other_ref = bf16[4,128,128]{2,1,0:T(8,128)(2,1)S(1)} collective-permute-done((bf16[4,128,128]{2,1,0:T(8,128)(2,1)S(1)}, bf16[4,128,128]{2,1,0:T(8,128)(2,1)S(1)}, u32[]{:S(2)}, u32[]{:S(2)}) %collective-permute-start.26) | collective-permute-done | bytes 131104 | tf_op jit(solution)/shard_map/ppermute | solution.py:20
  78.3 1.5 %quadratic.1 = bf16[2,960,128]{2,1,0:T(8,128)(2,1)} custom-call(s32[1]{0:T(128)S(6)} %and.4.core_ref, bf16[4,128,128]{2,1,0:T(8,128)(2,1)S(1)} %add_convert_fusion.6.mine_ref, bf16[4,128,128]{2,1,0:T(8,128)(2,1)S(1)} %collective-permute-done.26.other_ref, f32[2,960,128]{2,1,0:T(8,128)S(1)} %combine.1.base_ref, ...), custom_call_target="tpu_custom_call" | custom-call | flops 503316480 | bytes 3440640 | tf_op jit(solution)/shard_map/quadratic/pallas_call | solution.py:226
  (44 shorter events, 3.8 us)
Async XLA Ops:
  0.0 14.4 %collective-permute-start.1 = (bf16[2,960,128]{2,1,0:T(8,128)(2,1)}, bf16[2,960,128]{2,1,0:T(8,128)(2,1)S(1)}, u32[]{:S(2)}, u32[]{:S(2)}) collective-permute-start(bf16[2,960,128]{2,1,0:T(8,128)(2,1)} %source_ref.1), channel_id=1, source_target_pairs={{0,16},{4,20},{8,24},{12,28},{16,0},{20,4},{24,8},{28,12},{1,17},{... | collective-permute-start | bytes 1474568 | tf_op jit(solution)/shard_map/ppermute | solution.py:20
  3.0 12.9 %collective-permute-start = (bf16[2,960,128]{2,1,0:T(8,128)(2,1)}, bf16[2,960,128]{2,1,0:T(8,128)(2,1)S(1)}, u32[]{:S(2)}, u32[]{:S(2)}) collective-permute-start(bf16[2,960,128]{2,1,0:T(8,128)(2,1)} %source_ref.1), channel_id=1, source_target_pairs={{0,8},{4,12},{8,0},{12,4},{16,24},{20,28},{24,16},{28,20},{1,9},{5... | collective-permute-start | bytes 1474568 | tf_op jit(solution)/shard_map/ppermute | solution.py:20
  4.5 19.3 %collective-permute-start.6 = (bf16[2,960,128]{2,1,0:T(8,128)(2,1)}, bf16[2,960,128]{2,1,0:T(8,128)(2,1)S(1)}, u32[]{:S(2)}, u32[]{:S(2)}) collective-permute-start(bf16[2,960,128]{2,1,0:T(8,128)(2,1)} %source_ref.1), channel_id=1, source_target_pairs={{0,4},{4,0},{8,12},{12,8},{16,20},{20,16},{24,28},{28,24},{1,5},{5... | collective-permute-start | bytes 1474568 | tf_op jit(solution)/shard_map/ppermute | solution.py:20
  4.5 20.4 %collective-permute-start.2 = (bf16[2,960,128]{2,1,0:T(8,128)(2,1)}, bf16[2,960,128]{2,1,0:T(8,128)(2,1)S(1)}, u32[]{:S(2)}, u32[]{:S(2)}) collective-permute-start(bf16[2,960,128]{2,1,0:T(8,128)(2,1)} %source_ref.1), channel_id=1, source_target_pairs={{0,2},{2,3},{3,1},{1,0},{4,6},{6,7},{7,5},{5,4},{8,10},{10,11},{11... | collective-permute-start | bytes 1474568 | tf_op jit(solution)/shard_map/ppermute | solution.py:277
  7.1 16.7 %collective-permute-start.3 = (bf16[960,128]{1,0:T(8,128)(2,1)}, bf16[960,128]{1,0:T(8,128)(2,1)S(1)}, u32[]{:S(2)}, u32[]{:S(2)}) collective-permute-start(bf16[960,128]{1,0:T(8,128)(2,1)} %int_ref.1), channel_id=1, source_target_pairs={{0,2},{2,3},{3,1},{1,0},{4,6},{6,7},{7,5},{5,4},{8,10},{10,11},{11... | collective-permute-start | bytes 737288 | tf_op jit(solution)/shard_map/ppermute | solution.py:277
  9.4 1.0 %copy-start = (bf16[2,960,128]{2,1,0:T(8,128)(2,1)S(1)}, bf16[2,960,128]{2,1,0:T(8,128)(2,1)}, u32[]{:S(2)}) copy-start(bf16[2,960,128]{2,1,0:T(8,128)(2,1)} %source_ref.1) | copy-start | bytes 1474564
  10.7 28.6 %copy-start.1 = (bf16[960,128]{1,0:T(8,128)(2,1)S(1)}, bf16[960,128]{1,0:T(8,128)(2,1)}, u32[]{:S(2)}) copy-start(bf16[960,128]{1,0:T(8,128)(2,1)} %int_ref.1) | copy-start | bytes 737284
  15.9 8.4 %collective-permute-start.4 = (bf16[960,128]{1,0:T(8,128)(2,1)S(1)}, bf16[960,128]{1,0:T(8,128)(2,1)S(1)}, u32[]{:S(2)}, u32[]{:S(2)}) collective-permute-start(bf16[960,128]{1,0:T(8,128)(2,1)S(1)} %slice_bitcast_fusion.1), channel_id=1, source_target_pairs={{0,8},{4,12},{8,0},{12,4},{16,24},{20,28},{24,16},{28,20},{1,9},{5... | collective-permute-start | bytes 737288 | tf_op jit(solution)/shard_map/ppermute | solution.py:20
  17.5 6.9 %collective-permute-start.5 = (bf16[960,128]{1,0:T(8,128)(2,1)S(1)}, bf16[960,128]{1,0:T(8,128)(2,1)S(1)}, u32[]{:S(2)}, u32[]{:S(2)}) collective-permute-start(bf16[960,128]{1,0:T(8,128)(2,1)S(1)} %slice_bitcast_fusion), channel_id=1, source_target_pairs={{0,16},{4,20},{8,24},{12,28},{16,0},{20,4},{24,8},{28,12},{1,17},{... | collective-permute-start | bytes 737288 | tf_op jit(solution)/shard_map/ppermute | solution.py:20
  23.8 4.3 %collective-permute-start.7 = (bf16[2,960,128]{2,1,0:T(8,128)(2,1)S(1)}, bf16[2,960,128]{2,1,0:T(8,128)(2,1)S(1)}, u32[]{:S(2)}, u32[]{:S(2)}) collective-permute-start(bf16[2,960,128]{2,1,0:T(8,128)(2,1)S(1)} %collective-permute-done.refs_1_), channel_id=1, source_target_pairs={{0,4},{4,0},{8,12},{12,8},{16,20},{20,16},{24,28},{28,24},{1,5},{5... | collective-permute-start | bytes 1474568 | tf_op jit(solution)/shard_map/ppermute | solution.py:20
  23.8 4.3 %collective-permute-start.8 = (bf16[2,960,128]{2,1,0:T(8,128)(2,1)S(1)}, bf16[2,960,128]{2,1,0:T(8,128)(2,1)S(1)}, u32[]{:S(2)}, u32[]{:S(2)}) collective-permute-start(bf16[2,960,128]{2,1,0:T(8,128)(2,1)S(1)} %collective-permute-done.1.refs_2_), channel_id=1, source_target_pairs={{0,4},{4,0},{8,12},{12,8},{16,20},{20,16},{24,28},{28,24},{1,5},{5... | collective-permute-start | bytes 1474568 | tf_op jit(solution)/shard_map/ppermute | solution.py:20
  24.3 3.8 %collective-permute-start.9 = (bf16[960,128]{1,0:T(8,128)(2,1)S(1)}, bf16[960,128]{1,0:T(8,128)(2,1)S(1)}, u32[]{:S(2)}, u32[]{:S(2)}) collective-permute-start(bf16[960,128]{1,0:T(8,128)(2,1)S(1)} %collective-permute-done.4.refs_3_), channel_id=1, source_target_pairs={{0,4},{4,0},{8,12},{12,8},{16,20},{20,16},{24,28},{28,24},{1,5},{5... | collective-permute-start | bytes 737288 | tf_op jit(solution)/shard_map/ppermute | solution.py:20
  24.4 3.7 %collective-permute-start.10 = (bf16[960,128]{1,0:T(8,128)(2,1)S(1)}, bf16[960,128]{1,0:T(8,128)(2,1)S(1)}, u32[]{:S(2)}, u32[]{:S(2)}) collective-permute-start(bf16[960,128]{1,0:T(8,128)(2,1)S(1)} %collective-permute-done.5.refs_4_), channel_id=1, source_target_pairs={{0,4},{4,0},{8,12},{12,8},{16,20},{20,16},{24,28},{28,24},{1,5},{5... | collective-permute-start | bytes 737288 | tf_op jit(solution)/shard_map/ppermute | solution.py:20
  24.8 14.0 %collective-permute-start.11 = (bf16[2,960,128]{2,1,0:T(8,128)(2,1)S(1)}, bf16[2,960,128]{2,1,0:T(8,128)(2,1)S(1)}, u32[]{:S(2)}, u32[]{:S(2)}) collective-permute-start(bf16[2,960,128]{2,1,0:T(8,128)(2,1)S(1)} %collective-permute-done.2.refs_1_), channel_id=1, source_target_pairs={{0,2},{2,3},{3,1},{1,0},{4,6},{6,7},{7,5},{5,4},{8,10},{10,11},{11... | collective-permute-start | bytes 1474568 | tf_op jit(solution)/shard_map/ppermute | solution.py:277
  38.8 2.2 %collective-permute-start.12 = (bf16[3,960,128]{2,1,0:T(8,128)(2,1)S(1)}, bf16[3,960,128]{2,1,0:T(8,128)(2,1)S(1)}, u32[]{:S(2)}, u32[]{:S(2)}) collective-permute-start(bf16[3,960,128]{2,1,0:T(8,128)(2,1)S(1)} %get-tuple-element.54), channel_id=1, source_target_pairs={{0,4},{4,0},{8,12},{12,8},{16,20},{20,16},{24,28},{28,24},{1,5},{5... | collective-permute-start | bytes 2211848 | tf_op jit(solution)/shard_map/ppermute | solution.py:20
  38.8 3.3 %collective-permute-start.13 = (bf16[3,960,128]{2,1,0:T(8,128)(2,1)S(1)}, bf16[3,960,128]{2,1,0:T(8,128)(2,1)S(1)}, u32[]{:S(2)}, u32[]{:S(2)}) collective-permute-start(bf16[3,960,128]{2,1,0:T(8,128)(2,1)S(1)} %get-tuple-element.55), channel_id=1, source_target_pairs={{0,4},{4,0},{8,12},{12,8},{16,20},{20,16},{24,28},{28,24},{1,5},{5... | collective-permute-start | bytes 2211848 | tf_op jit(solution)/shard_map/ppermute | solution.py:20
  42.3 4.6 %collective-permute-start.14 = (bf16[4,128,128]{2,1,0:T(8,128)(2,1)S(1)}, bf16[4,128,128]{2,1,0:T(8,128)(2,1)S(1)}, u32[]{:S(2)}, u32[]{:S(2)}) collective-permute-start(bf16[4,128,128]{2,1,0:T(8,128)(2,1)S(1)} %get-tuple-element.65), channel_id=1, source_target_pairs={{0,4},{4,0},{8,12},{12,8},{16,20},{20,16},{24,28},{28,24},{1,5},{5... | collective-permute-start | bytes 393224 | tf_op jit(solution)/shard_map/ppermute | solution.py:20
  42.5 18.8 %collective-permute-start.19 = (bf16[2,960,128]{2,1,0:T(8,128)(2,1)S(1)}, bf16[2,960,128]{2,1,0:T(8,128)(2,1)S(1)}, u32[]{:S(2)}, u32[]{:S(2)}) collective-permute-start(bf16[2,960,128]{2,1,0:T(8,128)(2,1)S(1)} %collective-permute-done.11.refs_2_), channel_id=1, source_target_pairs={{0,2},{2,3},{3,1},{1,0},{4,6},{6,7},{7,5},{5,4},{8,10},{10,11},{11... | collective-permute-start | bytes 1474568 | tf_op jit(solution)/shard_map/ppermute | solution.py:277
  45.9 15.5 %collective-permute-start.17 = (bf16[1,960,128]{2,1,0:T(8,128)(2,1)S(1)}, bf16[1,960,128]{2,1,0:T(8,128)(2,1)S(1)}, u32[]{:S(2)}, u32[]{:S(2)}) collective-permute-start(bf16[1,960,128]{2,1,0:T(8,128)(2,1)S(1)} %get-tuple-element.66), channel_id=1, source_target_pairs={{0,8},{4,12},{8,0},{12,4},{16,24},{20,28},{24,16},{28,20},{1,9},{5... | collective-permute-start | bytes 737288 | tf_op jit(solution)/shard_map/ppermute | solution.py:20
  46.5 14.9 %collective-permute-start.18 = (bf16[1,960,128]{2,1,0:T(8,128)(2,1)S(1)}, bf16[1,960,128]{2,1,0:T(8,128)(2,1)S(1)}, u32[]{:S(2)}, u32[]{:S(2)}) collective-permute-start(bf16[1,960,128]{2,1,0:T(8,128)(2,1)S(1)} %get-tuple-element.67), channel_id=1, source_target_pairs={{0,16},{4,20},{8,24},{12,28},{16,0},{20,4},{24,8},{28,12},{1,17},{... | collective-permute-start | bytes 737288 | tf_op jit(solution)/shard_map/ppermute | solution.py:20
  47.0 12.8 %collective-permute-start.16 = (bf16[128,128]{1,0:T(8,128)(2,1)S(1)}, bf16[128,128]{1,0:T(8,128)(2,1)S(1)}, u32[]{:S(2)}, u32[]{:S(2)}) collective-permute-start(bf16[128,128]{1,0:T(8,128)(2,1)S(1)} %get-tuple-element.87), channel_id=1, source_target_pairs={{0,3},{2,1},{3,0},{1,2},{4,7},{6,5},{7,4},{5,6},{8,11},{10,9},{11,... | collective-permute-start | bytes 98312 | tf_op jit(solution)/shard_map/ppermute | solution.py:277
  48.5 12.4 %collective-permute-start.15 = (bf16[128,128]{1,0:T(8,128)(2,1)S(1)}, bf16[128,128]{1,0:T(8,128)(2,1)S(1)}, u32[]{:S(2)}, u32[]{:S(2)}) collective-permute-start(bf16[128,128]{1,0:T(8,128)(2,1)S(1)} %get-tuple-element.88), channel_id=1, source_target_pairs={{0,1},{2,0},{3,2},{1,3},{4,5},{6,4},{7,6},{5,7},{8,9},{10,8},{11,1... | collective-permute-start | bytes 98312 | tf_op jit(solution)/shard_map/ppermute | solution.py:277
  59.9 11.9 %collective-permute-start.24 = (bf16[1,960,128]{2,1,0:T(8,128)(2,1)S(1)}, bf16[1,960,128]{2,1,0:T(8,128)(2,1)S(1)}, u32[]{:S(2)}, u32[]{:S(2)}) collective-permute-start(bf16[1,960,128]{2,1,0:T(8,128)(2,1)S(1)} %get-tuple-element.71), channel_id=1, source_target_pairs={{0,8},{4,12},{8,0},{12,4},{16,24},{20,28},{24,16},{28,20},{1,9},{5... | collective-permute-start | bytes 737288 | tf_op jit(solution)/shard_map/ppermute | solution.py:20
  60.9 10.9 %collective-permute-start.25 = (bf16[1,960,128]{2,1,0:T(8,128)(2,1)S(1)}, bf16[1,960,128]{2,1,0:T(8,128)(2,1)S(1)}, u32[]{:S(2)}, u32[]{:S(2)}) collective-permute-start(bf16[1,960,128]{2,1,0:T(8,128)(2,1)S(1)} %get-tuple-element.72), channel_id=1, source_target_pairs={{0,16},{4,20},{8,24},{12,28},{16,0},{20,4},{24,8},{28,12},{1,17},{... | collective-permute-start | bytes 737288 | tf_op jit(solution)/shard_map/ppermute | solution.py:20
  61.5 10.0 %collective-permute-start.20 = (bf16[4,128,128]{2,1,0:T(8,128)(2,1)S(1)}, bf16[4,128,128]{2,1,0:T(8,128)(2,1)S(1)}, u32[]{:S(2)}, u32[]{:S(2)}) collective-permute-start(bf16[4,128,128]{2,1,0:T(8,128)(2,1)S(1)} %pad_maximum_fusion), channel_id=1, source_target_pairs={{0,8},{4,12},{8,0},{12,4},{16,24},{20,28},{24,16},{28,20},{1,9},{5... | collective-permute-start | bytes 393224 | tf_op jit(solution)/shard_map/ppermute | solution.py:20
  62.7 12.2 %collective-permute-start.22 = (bf16[1,960,128]{2,1,0:T(8,128)(2,1)S(1)}, bf16[1,960,128]{2,1,0:T(8,128)(2,1)S(1)}, u32[]{:S(2)}, u32[]{:S(2)}) collective-permute-start(bf16[1,960,128]{2,1,0:T(8,128)(2,1)S(1)} %add_convert_fusion.1), channel_id=1, source_target_pairs={{0,16},{4,20},{8,24},{12,28},{16,0},{20,4},{24,8},{28,12},{1,17},{... | collective-permute-start | bytes 737288 | tf_op jit(solution)/shard_map/ppermute | solution.py:20
  64.3 10.6 %collective-permute-start.23 = (bf16[1,960,128]{2,1,0:T(8,128)(2,1)S(1)}, bf16[1,960,128]{2,1,0:T(8,128)(2,1)S(1)}, u32[]{:S(2)}, u32[]{:S(2)}) collective-permute-start(bf16[1,960,128]{2,1,0:T(8,128)(2,1)S(1)} %add_convert_fusion), channel_id=1, source_target_pairs={{0,8},{4,12},{8,0},{12,4},{16,24},{20,28},{24,16},{28,20},{1,9},{5... | collective-permute-start | bytes 737288 | tf_op jit(solution)/shard_map/ppermute | solution.py:20
  71.6 5.2 %collective-permute-start.21 = (bf16[4,128,128]{2,1,0:T(8,128)(2,1)S(1)}, bf16[4,128,128]{2,1,0:T(8,128)(2,1)S(1)}, u32[]{:S(2)}, u32[]{:S(2)}) collective-permute-start(bf16[4,128,128]{2,1,0:T(8,128)(2,1)S(1)} %add_convert_fusion.7), channel_id=1, source_target_pairs={{0,16},{4,20},{8,24},{12,28},{16,0},{20,4},{24,8},{28,12},{1,17},{... | collective-permute-start | bytes 393224 | tf_op jit(solution)/shard_map/ppermute | solution.py:20
  71.7 5.2 %collective-permute-start.27 = (bf16[2,960,128]{2,1,0:T(8,128)(2,1)S(1)}, bf16[2,960,128]{2,1,0:T(8,128)(2,1)S(1)}, u32[]{:S(2)}, u32[]{:S(2)}) collective-permute-start(bf16[2,960,128]{2,1,0:T(8,128)(2,1)S(1)} %get-tuple-element.75), channel_id=1, source_target_pairs={{0,4},{4,0},{8,12},{12,8},{16,20},{20,16},{24,28},{28,24},{1,5},{5... | collective-permute-start | bytes 1474568 | tf_op jit(solution)/shard_map/ppermute | solution.py:20
  76.9 1.4 %collective-permute-start.26 = (bf16[4,128,128]{2,1,0:T(8,128)(2,1)S(1)}, bf16[4,128,128]{2,1,0:T(8,128)(2,1)S(1)}, u32[]{:S(2)}, u32[]{:S(2)}) collective-permute-start(bf16[4,128,128]{2,1,0:T(8,128)(2,1)S(1)} %add_convert_fusion.6.mine_ref), channel_id=1, source_target_pairs={{0,4},{4,0},{8,12},{12,8},{16,20},{20,16},{24,28},{28,24},{1,5},{5... | collective-permute-start | bytes 393224 | tf_op jit(solution)/shard_map/ppermute | solution.py:20

commit v12 on v11

--- a/solution.py
+++ b/solution.py
@@ -154,8 +154,8 @@
             dimension_semantics=("arbitrary",), vmem_limit_bytes=40 * 1024 * 1024
         ),
         cost_estimate=pl.CostEstimate(
-            flops=slots * 8 * BLOCK * BLOCK * columns,
-            bytes_accessed=slots * BLOCK * BLOCK * 2 + 8 * PAIRS * columns,
+            flops=slots * BLOCK * BLOCK * columns,
+            bytes_accessed=2 * PAIRS * columns,
             transcendentals=0,
         ),
         name="ladder",
@@ -279,9 +279,9 @@
     ring = [amplitudes]
     for _ in range(2, vp_size):
         ring.append(turn(ring[-1]))
-    back_integrals = turn(integrals)
+    back_integrals = turn(after(integrals, ring[1]))
     pieces, small = gather_tri(amplitudes, jnp.concatenate([me, slot_block]), tri_size)
-    small = after(small, ring[1], back_integrals)
+    small = after(small, ring[1])
     ring[0] = pieces[0][0]
 
     if tri_size == 8:
@@ -291,7 +291,7 @@
     else:
         groups = [[(mask, part) for mask in range(tri_size) for part in range(2)]]
     partials = ladder(small, pieces, ladder_blocks, groups)
-    *partials, ring[-1] = lax.optimization_barrier((*partials, ring[-1]))
+    *partials, ring[-1], back_integrals = lax.optimization_barrier((*partials, ring[-1], back_integrals))
     hold, give = contract(core, integrals, back_integrals, ring)
 
     def shift(value):
@@ -312,12 +312,13 @@
         far_x, far_y = swap(far_x, tri_size, 1), swap(far_y, tri_size, 2)
         near_x, near_y = swap(near_x, tri_size, 1), swap(near_y, tri_size, 2)
         mine = shift(add(hold, swap(give, tri_size, 0)).astype(BF16))
-        mine, far_x, far_y, last = lax.optimization_barrier((mine, far_x, far_y, turn(ring[-1])))
+        mine, far_x, far_y = lax.optimization_barrier((mine, far_x, far_y))
+        last = turn(after(ring[-1], mine))
         then_y = swap(add(real[2], real_in[2], far_x[0]).astype(BF16)[None], tri_size, 2)
         then_x = swap(add(imag[2], imag_in[2], far_y[0]).astype(BF16)[None], tri_size, 1)
         mine = add(mine, swap(mine, tri_size, 1)).astype(BF16)
-        received, then_y, then_x, near_x, near_y = lax.optimization_barrier(
-            (swap(mine, tri_size, 2), then_y, then_x, near_x, near_y)
+        received, last, then_y, then_x, near_x, near_y = lax.optimization_barrier(
+            (swap(mine, tri_size, 2), last, then_y, then_x, near_x, near_y)
         )
         mine = add(mine, received).astype(BF16)
         terms = [(own, 0, 0), (own, 1, 1), (own_in, 0, 0), (own_in, 1, 1)]

time: 79.9 us -> 74.7 us (0.935)
  waiting for transfers between devices: 39.6 us -> 30.7 us
  starting transfers between devices: 26.5 us -> 30.3 us
    ppermute x6, waiting for transfers between devices: 20 us -> 7.69 us  [turn(): lax.ppermute(value, 'vp', [(order[i], order[(i + distance) % vp_size]) fo...]
    ppermute x22, waiting for transfers between devices: 19.6 us -> 23 us  [swap(): return lax.ppermute(value, 'tri', pairs)]
    ppermute x22, starting transfers between devices: 14.3 us -> 16.5 us  [swap(): return lax.ppermute(value, 'tri', pairs)]
    ppermute x6, starting transfers between devices: 12.3 us -> 13.8 us  [turn(): lax.ppermute(value, 'vp', [(order[i], order[(i + distance) % vp_size]) fo...]
  transfers between devices with their start and end apart: 28 -> 28, of which waited for: 12 -> 12; matrix products, arithmetic and copies ran while one was open for 1% -> 1% of each run, Pallas kernels for 12% -> 13%
where the time goes in v12:
time: 74.7 us; the launch traced here: 74.5 us
  waiting for transfers between devices  30.7 us (41%)
  starting transfers between devices  30.3 us (41%)
  Pallas kernels  11 us (15%)
  other arithmetic  1.33 us (2%)
  local copies, waits for them, and re-layouts  1.08 us (1%)
    ppermute x22, waiting for transfers between devices, swap(): return lax.ppermute(value, 'tri', pairs)  23 us
    ppermute x22, starting transfers between devices, swap(): return lax.ppermute(value, 'tri', pairs)  16.5 us
    ppermute x6, starting transfers between devices, turn(): lax.ppermute(value, 'vp', [(order[i], order[(i + distance) % vp_size]) fo...  13.8 us
    pallas_call x1, Pallas kernels, ladder(): pl.pallas_call(functools.partial(ladder_kernel, [(mask, part) for _, mask...  8.32 us
    ppermute x6, waiting for transfers between devices, turn(): lax.ppermute(value, 'vp', [(order[i], order[(i + distance) % vp_size]) fo...  7.69 us
  transfers between devices with their start and end apart: 28, of which 12 were waited for; matrix products, arithmetic and copies ran while one was open for 1% of the time, Pallas kernels for 13%

profile of v12, /device:TPU:0, one launch (start us, length us, event | category | flops | bytes accessed | tf_op | source)
XLA Modules:
  0.0 74.5 jit_solution(218222897587112085)
XLA Ops:
  0.0 2.9 %collective-permute-start = (bf16[2,960,128]{2,1,0:T(8,128)(2,1)}, bf16[2,960,128]{2,1,0:T(8,128)(2,1)S(1)}, u32[]{:S(2)}, u32[]{:S(2)}) collective-permute-start(bf16[2,960,128]{2,1,0:T(8,128)(2,1)} %source_ref.1), channel_id=1, source_target_pairs={{0,8},{4,12},{8,0},{12,4},{16,24},{20,28},{24,16},{28,20},{1,9},{5... | collective-permute-start | bytes 1474568 | tf_op jit(solution)/shard_map/ppermute | solution.py:20
  2.9 1.5 %collective-permute-start.1 = (bf16[2,960,128]{2,1,0:T(8,128)(2,1)}, bf16[2,960,128]{2,1,0:T(8,128)(2,1)S(1)}, u32[]{:S(2)}, u32[]{:S(2)}) collective-permute-start(bf16[2,960,128]{2,1,0:T(8,128)(2,1)} %source_ref.1), channel_id=1, source_target_pairs={{0,16},{4,20},{8,24},{12,28},{16,0},{20,4},{24,8},{28,12},{1,17},{... | collective-permute-start | bytes 1474568 | tf_op jit(solution)/shard_map/ppermute | solution.py:20
  4.5 2.6 %collective-permute-start.2 = (bf16[2,960,128]{2,1,0:T(8,128)(2,1)}, bf16[2,960,128]{2,1,0:T(8,128)(2,1)S(1)}, u32[]{:S(2)}, u32[]{:S(2)}) collective-permute-start(bf16[2,960,128]{2,1,0:T(8,128)(2,1)} %source_ref.1), channel_id=1, source_target_pairs={{0,2},{2,3},{3,1},{1,0},{4,6},{6,7},{7,5},{5,4},{8,10},{10,11},{11... | collective-permute-start | bytes 1474568 | tf_op jit(solution)/shard_map/ppermute | solution.py:277
  7.1 0.7 pad_add_fusion.small_ref
  7.8 1.0 %copy-done = bf16[2,960,128]{2,1,0:T(8,128)(2,1)S(1)} copy-done((bf16[2,960,128]{2,1,0:T(8,128)(2,1)S(1)}, bf16[2,960,128]{2,1,0:T(8,128)(2,1)}, u32[]{:S(2)}) %copy-start) | copy-done | bytes 491544
  9.1 5.2 %collective-permute-done.refs_1_ = bf16[2,960,128]{2,1,0:T(8,128)(2,1)S(1)} collective-permute-done((bf16[2,960,128]{2,1,0:T(8,128)(2,1)}, bf16[2,960,128]{2,1,0:T(8,128)(2,1)S(1)}, u32[]{:S(2)}, u32[]{:S(2)}) %collective-permute-start) | collective-permute-done | bytes 491552 | tf_op jit(solution)/shard_map/ppermute | solution.py:20
  14.4 1.5 %collective-permute-done.1.refs_2_ = bf16[2,960,128]{2,1,0:T(8,128)(2,1)S(1)} collective-permute-done((bf16[2,960,128]{2,1,0:T(8,128)(2,1)}, bf16[2,960,128]{2,1,0:T(8,128)(2,1)S(1)}, u32[]{:S(2)}, u32[]{:S(2)}) %collective-permute-start.1) | collective-permute-done | bytes 491552 | tf_op jit(solution)/shard_map/ppermute | solution.py:20
  16.3 1.8 %collective-permute-start.4 = (bf16[960,128]{1,0:T(8,128)(2,1)S(1)}, bf16[960,128]{1,0:T(8,128)(2,1)S(1)}, u32[]{:S(2)}, u32[]{:S(2)}) collective-permute-start(bf16[960,128]{1,0:T(8,128)(2,1)S(1)} %slice_bitcast_fusion), channel_id=1, source_target_pairs={{0,16},{4,20},{8,24},{12,28},{16,0},{20,4},{24,8},{28,12},{1,17},{... | collective-permute-start | bytes 737288 | tf_op jit(solution)/shard_map/ppermute | solution.py:20
  18.6 3.8 %collective-permute-done.3.refs_3_ = bf16[960,128]{1,0:T(8,128)(2,1)S(1)} collective-permute-done((bf16[960,128]{1,0:T(8,128)(2,1)S(1)}, bf16[960,128]{1,0:T(8,128)(2,1)S(1)}, u32[]{:S(2)}, u32[]{:S(2)}) %collective-permute-start.3) | collective-permute-done | bytes 245792 | tf_op jit(solution)/shard_map/ppermute | solution.py:20
  22.4 2.6 %collective-permute-start.10 = (bf16[2,960,128]{2,1,0:T(8,128)(2,1)S(1)}, bf16[2,960,128]{2,1,0:T(8,128)(2,1)S(1)}, u32[]{:S(2)}, u32[]{:S(2)}) collective-permute-start(bf16[2,960,128]{2,1,0:T(8,128)(2,1)S(1)} %collective-permute-done.2.refs_1_), channel_id=1, source_target_pairs={{0,2},{2,3},{3,1},{1,0},{4,6},{6,7},{7,5},{5,4},{8,10},{10,11},{11... | collective-permute-start | bytes 1474568 | tf_op jit(solution)/shard_map/ppermute | solution.py:277
  25.3 1.6 %collective-permute-start.11 = (bf16[960,128]{1,0:T(8,128)(2,1)}, bf16[960,128]{1,0:T(8,128)(2,1)S(1)}, u32[]{:S(2)}, u32[]{:S(2)}) collective-permute-start(bf16[960,128]{1,0:T(8,128)(2,1)} %int_ref.1), channel_id=1, source_target_pairs={{0,2},{2,3},{3,1},{1,0},{4,6},{6,7},{7,5},{5,4},{8,10},{10,11},{11... | collective-permute-start | bytes 737288 | tf_op jit(solution)/shard_map/ppermute | solution.py:277
  26.8 8.3 %ladder.1 = (bf16[3,960,128]{2,1,0:T(8,128)(2,1)S(1)}, bf16[3,960,128]{2,1,0:T(8,128)(2,1)S(1)}, bf16[2,960,128]{2,1,0:T(8,128)(2,1)S(1)}, bf16[3,960,128]{2,1,0...) custom-call(s32[8]{0:T(128)S(1)} %pad_add_fusion.small_ref, ...), custom_call_target="tpu_custom_call" | custom-call | flops 528482304 | bytes 1966080 | tf_op jit(solution)/shard_map/ladder/pallas_call | solution.py:138
  35.2 6.4 %collective-permute-done.11.last_ref = bf16[960,128]{1,0:T(8,128)(2,1)S(1)} collective-permute-done((bf16[960,128]{1,0:T(8,128)(2,1)}, bf16[960,128]{1,0:T(8,128)(2,1)S(1)}, u32[]{:S(2)}, u32[]{:S(2)}) %collective-permute-start.11) | collective-permute-done | bytes 245792 | tf_op jit(solution)/shard_map/ppermute | solution.py:277
  42.6 1.1 %collective-permute-done.12 = bf16[3,960,128]{2,1,0:T(8,128)(2,1)S(1)} collective-permute-done((bf16[3,960,128]{2,1,0:T(8,128)(2,1)S(1)}, bf16[3,960,128]{2,1,0:T(8,128)(2,1)S(1)}, u32[]{:S(2)}, u32[]{:S(2)}) %collective-permute-start.12) | collective-permute-done | bytes 737312 | tf_op jit(solution)/shard_map/ppermute | solution.py:20
  43.8 1.1 %collective-permute-done.13 = bf16[3,960,128]{2,1,0:T(8,128)(2,1)S(1)} collective-permute-done((bf16[3,960,128]{2,1,0:T(8,128)(2,1)S(1)}, bf16[3,960,128]{2,1,0:T(8,128)(2,1)S(1)}, u32[]{:S(2)}, u32[]{:S(2)}) %collective-permute-start.13) | collective-permute-done | bytes 737312 | tf_op jit(solution)/shard_map/ppermute | solution.py:20
  45.3 0.6 collective-permute-start.17
  45.9 1.5 %collective-permute-start.18 = (bf16[1,960,128]{2,1,0:T(8,128)(2,1)S(1)}, bf16[1,960,128]{2,1,0:T(8,128)(2,1)S(1)}, u32[]{:S(2)}, u32[]{:S(2)}) collective-permute-start(bf16[1,960,128]{2,1,0:T(8,128)(2,1)S(1)} %get-tuple-element.72), channel_id=1, source_target_pairs={{0,16},{4,20},{8,24},{12,28},{16,0},{20,4},{24,8},{28,12},{1,17},{... | collective-permute-start | bytes 737288 | tf_op jit(solution)/shard_map/ppermute | solution.py:20
  47.5 2.3 %collective-permute-start.15 = (bf16[128,128]{1,0:T(8,128)(2,1)S(1)}, bf16[128,128]{1,0:T(8,128)(2,1)S(1)}, u32[]{:S(2)}, u32[]{:S(2)}) collective-permute-start(bf16[128,128]{1,0:T(8,128)(2,1)S(1)} %get-tuple-element.94), channel_id=1, source_target_pairs={{0,1},{2,0},{3,2},{1,3},{4,5},{6,4},{7,6},{5,7},{8,9},{10,8},{11,1... | collective-permute-start | bytes 98312 | tf_op jit(solution)/shard_map/ppermute | solution.py:277
  49.8 2.5 %collective-permute-start.16 = (bf16[128,128]{1,0:T(8,128)(2,1)S(1)}, bf16[128,128]{1,0:T(8,128)(2,1)S(1)}, u32[]{:S(2)}, u32[]{:S(2)}) collective-permute-start(bf16[128,128]{1,0:T(8,128)(2,1)S(1)} %get-tuple-element.93), channel_id=1, source_target_pairs={{0,3},{2,1},{3,0},{1,2},{4,7},{6,5},{7,4},{5,6},{8,11},{10,9},{11,... | collective-permute-start | bytes 98312 | tf_op jit(solution)/shard_map/ppermute | solution.py:277
  52.3 1.4 %collective-permute-start.24 = (bf16[1,960,128]{2,1,0:T(8,128)(2,1)S(1)}, bf16[1,960,128]{2,1,0:T(8,128)(2,1)S(1)}, u32[]{:S(2)}, u32[]{:S(2)}) collective-permute-start(bf16[1,960,128]{2,1,0:T(8,128)(2,1)S(1)} %get-tuple-element.77), channel_id=1, source_target_pairs={{0,8},{4,12},{8,0},{12,4},{16,24},{20,28},{24,16},{28,20},{1,9},{5... | collective-permute-start | bytes 737288 | tf_op jit(solution)/shard_map/ppermute | solution.py:20
  54.2 1.3 %collective-permute-done.16 = bf16[128,128]{1,0:T(8,128)(2,1)S(1)} collective-permute-done((bf16[128,128]{1,0:T(8,128)(2,1)S(1)}, bf16[128,128]{1,0:T(8,128)(2,1)S(1)}, u32[]{:S(2)}, u32[]{:S(2)}) %collective-permute-start.16) | collective-permute-done | bytes 32800 | tf_op jit(solution)/shard_map/ppermute | solution.py:277
  55.6 1.5 %collective-permute-start.19 = (bf16[4,128,128]{2,1,0:T(8,128)(2,1)S(1)}, bf16[4,128,128]{2,1,0:T(8,128)(2,1)S(1)}, u32[]{:S(2)}, u32[]{:S(2)}) collective-permute-start(bf16[4,128,128]{2,1,0:T(8,128)(2,1)S(1)} %pad_maximum_fusion), channel_id=1, source_target_pairs={{0,8},{4,12},{8,0},{12,4},{16,24},{20,28},{24,16},{28,20},{1,9},{5... | collective-permute-start | bytes 393224 | tf_op jit(solution)/shard_map/ppermute | solution.py:20
  57.1 0.7 collective-permute-start.23
  57.8 2.3 %collective-permute-start.21 = (bf16[2,960,128]{2,1,0:T(8,128)(2,1)S(1)}, bf16[2,960,128]{2,1,0:T(8,128)(2,1)S(1)}, u32[]{:S(2)}, u32[]{:S(2)}) collective-permute-start(bf16[2,960,128]{2,1,0:T(8,128)(2,1)S(1)} %collective-permute-done.10.refs_2_), channel_id=1, source_target_pairs={{0,2},{2,3},{3,1},{1,0},{4,6},{6,7},{7,5},{5,4},{8,10},{10,11},{11... | collective-permute-start | bytes 1474568 | tf_op jit(solution)/shard_map/ppermute | solution.py:277
  60.2 3.8 %collective-permute-done.19 = bf16[4,128,128]{2,1,0:T(8,128)(2,1)S(1)} collective-permute-done((bf16[4,128,128]{2,1,0:T(8,128)(2,1)S(1)}, bf16[4,128,128]{2,1,0:T(8,128)(2,1)S(1)}, u32[]{:S(2)}, u32[]{:S(2)}) %collective-permute-start.19) | collective-permute-done | bytes 131104 | tf_op jit(solution)/shard_map/ppermute | solution.py:20
  64.0 0.6 collective-permute-start.22
  64.6 1.5 %collective-permute-start.20 = (bf16[4,128,128]{2,1,0:T(8,128)(2,1)S(1)}, bf16[4,128,128]{2,1,0:T(8,128)(2,1)S(1)}, u32[]{:S(2)}, u32[]{:S(2)}) collective-permute-start(bf16[4,128,128]{2,1,0:T(8,128)(2,1)S(1)} %add_convert_fusion.7), channel_id=1, source_target_pairs={{0,16},{4,20},{8,24},{12,28},{16,0},{20,4},{24,8},{28,12},{1,17},{... | collective-permute-start | bytes 393224 | tf_op jit(solution)/shard_map/ppermute | solution.py:20
  66.1 1.3 %collective-permute-done.23.refs_7_ = bf16[1,960,128]{2,1,0:T(8,128)(2,1)S(1)} collective-permute-done((bf16[1,960,128]{2,1,0:T(8,128)(2,1)S(1)}, bf16[1,960,128]{2,1,0:T(8,128)(2,1)S(1)}, u32[]{:S(2)}, u32[]{:S(2)}) %collective-permute-start.23) | collective-permute-done | bytes 245792 | tf_op jit(solution)/shard_map/ppermute | solution.py:20
  67.5 2.7 %collective-permute-done.22.refs_6_ = bf16[1,960,128]{2,1,0:T(8,128)(2,1)S(1)} collective-permute-done((bf16[1,960,128]{2,1,0:T(8,128)(2,1)S(1)}, bf16[1,960,128]{2,1,0:T(8,128)(2,1)S(1)}, u32[]{:S(2)}, u32[]{:S(2)}) %collective-permute-start.22) | collective-permute-done | bytes 245792 | tf_op jit(solution)/shard_map/ppermute | solution.py:20
  70.2 1.4 %collective-permute-done.20 = bf16[4,128,128]{2,1,0:T(8,128)(2,1)S(1)} collective-permute-done((bf16[4,128,128]{2,1,0:T(8,128)(2,1)S(1)}, bf16[4,128,128]{2,1,0:T(8,128)(2,1)S(1)}, u32[]{:S(2)}, u32[]{:S(2)}) %collective-permute-start.20) | collective-permute-done | bytes 131104 | tf_op jit(solution)/shard_map/ppermute | solution.py:20
  72.1 1.0 %collective-permute-done.26.other_ref = bf16[4,128,128]{2,1,0:T(8,128)(2,1)S(1)} collective-permute-done((bf16[4,128,128]{2,1,0:T(8,128)(2,1)S(1)}, bf16[4,128,128]{2,1,0:T(8,128)(2,1)S(1)}, u32[]{:S(2)}, u32[]{:S(2)}) %collective-permute-start.26) | collective-permute-done | bytes 131104 | tf_op jit(solution)/shard_map/ppermute | solution.py:20
  73.0 1.5 %quadratic.1 = bf16[2,960,128]{2,1,0:T(8,128)(2,1)} custom-call(s32[1]{0:T(128)S(6)} %and.4.core_ref, bf16[4,128,128]{2,1,0:T(8,128)(2,1)S(1)} %add_convert_fusion.6.mine_ref, bf16[4,128,128]{2,1,0:T(8,128)(2,1)S(1)} %collective-permute-done.26.other_ref, f32[2,960,128]{2,1,0:T(8,128)S(1)} %combine.1.base_ref, ...), custom_call_target="tpu_custom_call" | custom-call | flops 503316480 | bytes 3440640 | tf_op jit(solution)/shard_map/quadratic/pallas_call | solution.py:226
  (44 shorter events, 4.4 us)
Async XLA Ops:
  0.0 14.4 %collective-permute-start = (bf16[2,960,128]{2,1,0:T(8,128)(2,1)}, bf16[2,960,128]{2,1,0:T(8,128)(2,1)S(1)}, u32[]{:S(2)}, u32[]{:S(2)}) collective-permute-start(bf16[2,960,128]{2,1,0:T(8,128)(2,1)} %source_ref.1), channel_id=1, source_target_pairs={{0,8},{4,12},{8,0},{12,4},{16,24},{20,28},{24,16},{28,20},{1,9},{5... | collective-permute-start | bytes 1474568 | tf_op jit(solution)/shard_map/ppermute | solution.py:20
  2.9 12.9 %collective-permute-start.1 = (bf16[2,960,128]{2,1,0:T(8,128)(2,1)}, bf16[2,960,128]{2,1,0:T(8,128)(2,1)S(1)}, u32[]{:S(2)}, u32[]{:S(2)}) collective-permute-start(bf16[2,960,128]{2,1,0:T(8,128)(2,1)} %source_ref.1), channel_id=1, source_target_pairs={{0,16},{4,20},{8,24},{12,28},{16,0},{20,4},{24,8},{28,12},{1,17},{... | collective-permute-start | bytes 1474568 | tf_op jit(solution)/shard_map/ppermute | solution.py:20
  4.5 13.6 %collective-permute-start.2 = (bf16[2,960,128]{2,1,0:T(8,128)(2,1)}, bf16[2,960,128]{2,1,0:T(8,128)(2,1)S(1)}, u32[]{:S(2)}, u32[]{:S(2)}) collective-permute-start(bf16[2,960,128]{2,1,0:T(8,128)(2,1)} %source_ref.1), channel_id=1, source_target_pairs={{0,2},{2,3},{3,1},{1,0},{4,6},{6,7},{7,5},{5,4},{8,10},{10,11},{11... | collective-permute-start | bytes 1474568 | tf_op jit(solution)/shard_map/ppermute | solution.py:277
  7.0 15.4 %collective-permute-start.5 = (bf16[2,960,128]{2,1,0:T(8,128)(2,1)}, bf16[2,960,128]{2,1,0:T(8,128)(2,1)S(1)}, u32[]{:S(2)}, u32[]{:S(2)}) collective-permute-start(bf16[2,960,128]{2,1,0:T(8,128)(2,1)} %source_ref.1), channel_id=1, source_target_pairs={{0,4},{4,0},{8,12},{12,8},{16,20},{20,16},{24,28},{28,24},{1,5},{5... | collective-permute-start | bytes 1474568 | tf_op jit(solution)/shard_map/ppermute | solution.py:20
  7.8 1.0 %copy-start = (bf16[2,960,128]{2,1,0:T(8,128)(2,1)S(1)}, bf16[2,960,128]{2,1,0:T(8,128)(2,1)}, u32[]{:S(2)}) copy-start(bf16[2,960,128]{2,1,0:T(8,128)(2,1)} %source_ref.1) | copy-start | bytes 1474564
  8.8 33.2 %copy-start.1 = (bf16[960,128]{1,0:T(8,128)(2,1)S(1)}, bf16[960,128]{1,0:T(8,128)(2,1)}, u32[]{:S(2)}) copy-start(bf16[960,128]{1,0:T(8,128)(2,1)} %int_ref.1) | copy-start | bytes 737284
  15.9 6.6 %collective-permute-start.3 = (bf16[960,128]{1,0:T(8,128)(2,1)S(1)}, bf16[960,128]{1,0:T(8,128)(2,1)S(1)}, u32[]{:S(2)}, u32[]{:S(2)}) collective-permute-start(bf16[960,128]{1,0:T(8,128)(2,1)S(1)} %slice_bitcast_fusion.1), channel_id=1, source_target_pairs={{0,8},{4,12},{8,0},{12,4},{16,24},{20,28},{24,16},{28,20},{1,9},{5... | collective-permute-start | bytes 737288 | tf_op jit(solution)/shard_map/ppermute | solution.py:20
  16.3 8.7 %collective-permute-start.4 = (bf16[960,128]{1,0:T(8,128)(2,1)S(1)}, bf16[960,128]{1,0:T(8,128)(2,1)S(1)}, u32[]{:S(2)}, u32[]{:S(2)}) collective-permute-start(bf16[960,128]{1,0:T(8,128)(2,1)S(1)} %slice_bitcast_fusion), channel_id=1, source_target_pairs={{0,16},{4,20},{8,24},{12,28},{16,0},{20,4},{24,8},{28,12},{1,17},{... | collective-permute-start | bytes 737288 | tf_op jit(solution)/shard_map/ppermute | solution.py:20
  18.1 8.8 %collective-permute-start.6 = (bf16[2,960,128]{2,1,0:T(8,128)(2,1)S(1)}, bf16[2,960,128]{2,1,0:T(8,128)(2,1)S(1)}, u32[]{:S(2)}, u32[]{:S(2)}) collective-permute-start(bf16[2,960,128]{2,1,0:T(8,128)(2,1)S(1)} %collective-permute-done.refs_1_), channel_id=1, source_target_pairs={{0,4},{4,0},{8,12},{12,8},{16,20},{20,16},{24,28},{28,24},{1,5},{5... | collective-permute-start | bytes 1474568 | tf_op jit(solution)/shard_map/ppermute | solution.py:20
  18.1 8.8 %collective-permute-start.7 = (bf16[2,960,128]{2,1,0:T(8,128)(2,1)S(1)}, bf16[2,960,128]{2,1,0:T(8,128)(2,1)S(1)}, u32[]{:S(2)}, u32[]{:S(2)}) collective-permute-start(bf16[2,960,128]{2,1,0:T(8,128)(2,1)S(1)} %collective-permute-done.1.refs_2_), channel_id=1, source_target_pairs={{0,4},{4,0},{8,12},{12,8},{16,20},{20,16},{24,28},{28,24},{1,5},{5... | collective-permute-start | bytes 1474568 | tf_op jit(solution)/shard_map/ppermute | solution.py:20
  22.4 2.8 %collective-permute-start.8 = (bf16[960,128]{1,0:T(8,128)(2,1)S(1)}, bf16[960,128]{1,0:T(8,128)(2,1)S(1)}, u32[]{:S(2)}, u32[]{:S(2)}) collective-permute-start(bf16[960,128]{1,0:T(8,128)(2,1)S(1)} %collective-permute-done.3.refs_3_), channel_id=1, source_target_pairs={{0,4},{4,0},{8,12},{12,8},{16,20},{20,16},{24,28},{28,24},{1,5},{5... | collective-permute-start | bytes 737288 | tf_op jit(solution)/shard_map/ppermute | solution.py:20
  22.4 19.1 %collective-permute-start.10 = (bf16[2,960,128]{2,1,0:T(8,128)(2,1)S(1)}, bf16[2,960,128]{2,1,0:T(8,128)(2,1)S(1)}, u32[]{:S(2)}, u32[]{:S(2)}) collective-permute-start(bf16[2,960,128]{2,1,0:T(8,128)(2,1)S(1)} %collective-permute-done.2.refs_1_), channel_id=1, source_target_pairs={{0,2},{2,3},{3,1},{1,0},{4,6},{6,7},{7,5},{5,4},{8,10},{10,11},{11... | collective-permute-start | bytes 1474568 | tf_op jit(solution)/shard_map/ppermute | solution.py:277
  25.0 1.8 %collective-permute-start.9 = (bf16[960,128]{1,0:T(8,128)(2,1)S(1)}, bf16[960,128]{1,0:T(8,128)(2,1)S(1)}, u32[]{:S(2)}, u32[]{:S(2)}) collective-permute-start(bf16[960,128]{1,0:T(8,128)(2,1)S(1)} %collective-permute-done.4.refs_4_), channel_id=1, source_target_pairs={{0,4},{4,0},{8,12},{12,8},{16,20},{20,16},{24,28},{28,24},{1,5},{5... | collective-permute-start | bytes 737288 | tf_op jit(solution)/shard_map/ppermute | solution.py:20
  25.3 16.3 %collective-permute-start.11 = (bf16[960,128]{1,0:T(8,128)(2,1)}, bf16[960,128]{1,0:T(8,128)(2,1)S(1)}, u32[]{:S(2)}, u32[]{:S(2)}) collective-permute-start(bf16[960,128]{1,0:T(8,128)(2,1)} %int_ref.1), channel_id=1, source_target_pairs={{0,2},{2,3},{3,1},{1,0},{4,6},{6,7},{7,5},{5,4},{8,10},{10,11},{11... | collective-permute-start | bytes 737288 | tf_op jit(solution)/shard_map/ppermute | solution.py:277
  41.5 2.2 %collective-permute-start.12 = (bf16[3,960,128]{2,1,0:T(8,128)(2,1)S(1)}, bf16[3,960,128]{2,1,0:T(8,128)(2,1)S(1)}, u32[]{:S(2)}, u32[]{:S(2)}) collective-permute-start(bf16[3,960,128]{2,1,0:T(8,128)(2,1)S(1)} %get-tuple-element.58), channel_id=1, source_target_pairs={{0,4},{4,0},{8,12},{12,8},{16,20},{20,16},{24,28},{28,24},{1,5},{5... | collective-permute-start | bytes 2211848 | tf_op jit(solution)/shard_map/ppermute | solution.py:20
  41.6 3.3 %collective-permute-start.13 = (bf16[3,960,128]{2,1,0:T(8,128)(2,1)S(1)}, bf16[3,960,128]{2,1,0:T(8,128)(2,1)S(1)}, u32[]{:S(2)}, u32[]{:S(2)}) collective-permute-start(bf16[3,960,128]{2,1,0:T(8,128)(2,1)S(1)} %get-tuple-element.59), channel_id=1, source_target_pairs={{0,4},{4,0},{8,12},{12,8},{16,20},{20,16},{24,28},{28,24},{1,5},{5... | collective-permute-start | bytes 2211848 | tf_op jit(solution)/shard_map/ppermute | solution.py:20
  45.1 2.3 %collective-permute-start.14 = (bf16[4,128,128]{2,1,0:T(8,128)(2,1)S(1)}, bf16[4,128,128]{2,1,0:T(8,128)(2,1)S(1)}, u32[]{:S(2)}, u32[]{:S(2)}) collective-permute-start(bf16[4,128,128]{2,1,0:T(8,128)(2,1)S(1)} %get-tuple-element.70), channel_id=1, source_target_pairs={{0,4},{4,0},{8,12},{12,8},{16,20},{20,16},{24,28},{28,24},{1,5},{5... | collective-permute-start | bytes 393224 | tf_op jit(solution)/shard_map/ppermute | solution.py:20
  45.3 10.3 %collective-permute-start.17 = (bf16[1,960,128]{2,1,0:T(8,128)(2,1)S(1)}, bf16[1,960,128]{2,1,0:T(8,128)(2,1)S(1)}, u32[]{:S(2)}, u32[]{:S(2)}) collective-permute-start(bf16[1,960,128]{2,1,0:T(8,128)(2,1)S(1)} %get-tuple-element.71), channel_id=1, source_target_pairs={{0,8},{4,12},{8,0},{12,4},{16,24},{20,28},{24,16},{28,20},{1,9},{5... | collective-permute-start | bytes 737288 | tf_op jit(solution)/shard_map/ppermute | solution.py:20
  45.9 9.7 %collective-permute-start.18 = (bf16[1,960,128]{2,1,0:T(8,128)(2,1)S(1)}, bf16[1,960,128]{2,1,0:T(8,128)(2,1)S(1)}, u32[]{:S(2)}, u32[]{:S(2)}) collective-permute-start(bf16[1,960,128]{2,1,0:T(8,128)(2,1)S(1)} %get-tuple-element.72), channel_id=1, source_target_pairs={{0,16},{4,20},{8,24},{12,28},{16,0},{20,4},{24,8},{28,12},{1,17},{... | collective-permute-start | bytes 737288 | tf_op jit(solution)/shard_map/ppermute | solution.py:20
  47.5 6.2 %collective-permute-start.15 = (bf16[128,128]{1,0:T(8,128)(2,1)S(1)}, bf16[128,128]{1,0:T(8,128)(2,1)S(1)}, u32[]{:S(2)}, u32[]{:S(2)}) collective-permute-start(bf16[128,128]{1,0:T(8,128)(2,1)S(1)} %get-tuple-element.94), channel_id=1, source_target_pairs={{0,1},{2,0},{3,2},{1,3},{4,5},{6,4},{7,6},{5,7},{8,9},{10,8},{11,1... | collective-permute-start | bytes 98312 | tf_op jit(solution)/shard_map/ppermute | solution.py:277
  49.8 5.7 %collective-permute-start.16 = (bf16[128,128]{1,0:T(8,128)(2,1)S(1)}, bf16[128,128]{1,0:T(8,128)(2,1)S(1)}, u32[]{:S(2)}, u32[]{:S(2)}) collective-permute-start(bf16[128,128]{1,0:T(8,128)(2,1)S(1)} %get-tuple-element.93), channel_id=1, source_target_pairs={{0,3},{2,1},{3,0},{1,2},{4,7},{6,5},{7,4},{5,6},{8,11},{10,9},{11,... | collective-permute-start | bytes 98312 | tf_op jit(solution)/shard_map/ppermute | solution.py:277
  52.3 12.3 %collective-permute-start.24 = (bf16[1,960,128]{2,1,0:T(8,128)(2,1)S(1)}, bf16[1,960,128]{2,1,0:T(8,128)(2,1)S(1)}, u32[]{:S(2)}, u32[]{:S(2)}) collective-permute-start(bf16[1,960,128]{2,1,0:T(8,128)(2,1)S(1)} %get-tuple-element.77), channel_id=1, source_target_pairs={{0,8},{4,12},{8,0},{12,4},{16,24},{20,28},{24,16},{28,20},{1,9},{5... | collective-permute-start | bytes 737288 | tf_op jit(solution)/shard_map/ppermute | solution.py:20
  53.7 12.4 %collective-permute-start.25 = (bf16[1,960,128]{2,1,0:T(8,128)(2,1)S(1)}, bf16[1,960,128]{2,1,0:T(8,128)(2,1)S(1)}, u32[]{:S(2)}, u32[]{:S(2)}) collective-permute-start(bf16[1,960,128]{2,1,0:T(8,128)(2,1)S(1)} %get-tuple-element.78), channel_id=1, source_target_pairs={{0,16},{4,20},{8,24},{12,28},{16,0},{20,4},{24,8},{28,12},{1,17},{... | collective-permute-start | bytes 737288 | tf_op jit(solution)/shard_map/ppermute | solution.py:20
  55.6 8.4 %collective-permute-start.19 = (bf16[4,128,128]{2,1,0:T(8,128)(2,1)S(1)}, bf16[4,128,128]{2,1,0:T(8,128)(2,1)S(1)}, u32[]{:S(2)}, u32[]{:S(2)}) collective-permute-start(bf16[4,128,128]{2,1,0:T(8,128)(2,1)S(1)} %pad_maximum_fusion), channel_id=1, source_target_pairs={{0,8},{4,12},{8,0},{12,4},{16,24},{20,28},{24,16},{28,20},{1,9},{5... | collective-permute-start | bytes 393224 | tf_op jit(solution)/shard_map/ppermute | solution.py:20
  57.1 10.3 %collective-permute-start.23 = (bf16[1,960,128]{2,1,0:T(8,128)(2,1)S(1)}, bf16[1,960,128]{2,1,0:T(8,128)(2,1)S(1)}, u32[]{:S(2)}, u32[]{:S(2)}) collective-permute-start(bf16[1,960,128]{2,1,0:T(8,128)(2,1)S(1)} %add_convert_fusion), channel_id=1, source_target_pairs={{0,8},{4,12},{8,0},{12,4},{16,24},{20,28},{24,16},{28,20},{1,9},{5... | collective-permute-start | bytes 737288 | tf_op jit(solution)/shard_map/ppermute | solution.py:20
  57.8 13.8 %collective-permute-start.21 = (bf16[2,960,128]{2,1,0:T(8,128)(2,1)S(1)}, bf16[2,960,128]{2,1,0:T(8,128)(2,1)S(1)}, u32[]{:S(2)}, u32[]{:S(2)}) collective-permute-start(bf16[2,960,128]{2,1,0:T(8,128)(2,1)S(1)} %collective-permute-done.10.refs_2_), channel_id=1, source_target_pairs={{0,2},{2,3},{3,1},{1,0},{4,6},{6,7},{7,5},{5,4},{8,10},{10,11},{11... | collective-permute-start | bytes 1474568 | tf_op jit(solution)/shard_map/ppermute | solution.py:277
  64.0 6.2 %collective-permute-start.22 = (bf16[1,960,128]{2,1,0:T(8,128)(2,1)S(1)}, bf16[1,960,128]{2,1,0:T(8,128)(2,1)S(1)}, u32[]{:S(2)}, u32[]{:S(2)}) collective-permute-start(bf16[1,960,128]{2,1,0:T(8,128)(2,1)S(1)} %add_convert_fusion.1), channel_id=1, source_target_pairs={{0,16},{4,20},{8,24},{12,28},{16,0},{20,4},{24,8},{28,12},{1,17},{... | collective-permute-start | bytes 737288 | tf_op jit(solution)/shard_map/ppermute | solution.py:20
  64.6 7.0 %collective-permute-start.20 = (bf16[4,128,128]{2,1,0:T(8,128)(2,1)S(1)}, bf16[4,128,128]{2,1,0:T(8,128)(2,1)S(1)}, u32[]{:S(2)}, u32[]{:S(2)}) collective-permute-start(bf16[4,128,128]{2,1,0:T(8,128)(2,1)S(1)} %add_convert_fusion.7), channel_id=1, source_target_pairs={{0,16},{4,20},{8,24},{12,28},{16,0},{20,4},{24,8},{28,12},{1,17},{... | collective-permute-start | bytes 393224 | tf_op jit(solution)/shard_map/ppermute | solution.py:20
  66.1 5.6 %collective-permute-start.27 = (bf16[2,960,128]{2,1,0:T(8,128)(2,1)S(1)}, bf16[2,960,128]{2,1,0:T(8,128)(2,1)S(1)}, u32[]{:S(2)}, u32[]{:S(2)}) collective-permute-start(bf16[2,960,128]{2,1,0:T(8,128)(2,1)S(1)} %get-tuple-element.81), channel_id=1, source_target_pairs={{0,4},{4,0},{8,12},{12,8},{16,20},{20,16},{24,28},{28,24},{1,5},{5... | collective-permute-start | bytes 1474568 | tf_op jit(solution)/shard_map/ppermute | solution.py:20
  71.6 1.4 %collective-permute-start.26 = (bf16[4,128,128]{2,1,0:T(8,128)(2,1)S(1)}, bf16[4,128,128]{2,1,0:T(8,128)(2,1)S(1)}, u32[]{:S(2)}, u32[]{:S(2)}) collective-permute-start(bf16[4,128,128]{2,1,0:T(8,128)(2,1)S(1)} %add_convert_fusion.6.mine_ref), channel_id=1, source_target_pairs={{0,4},{4,0},{8,12},{12,8},{16,20},{20,16},{24,28},{28,24},{1,5},{5... | collective-permute-start | bytes 393224 | tf_op jit(solution)/shard_map/ppermute | solution.py:20

commit v13 on v12

--- a/solution.py
+++ b/solution.py
@@ -279,9 +279,9 @@
     ring = [amplitudes]
     for _ in range(2, vp_size):
         ring.append(turn(ring[-1]))
-    back_integrals = turn(after(integrals, ring[1]))
+    back_integrals = turn(integrals)
     pieces, small = gather_tri(amplitudes, jnp.concatenate([me, slot_block]), tri_size)
-    small = after(small, ring[1])
+    small = after(small, ring[1], back_integrals)
     ring[0] = pieces[0][0]
 
     if tri_size == 8:
@@ -291,7 +291,7 @@
     else:
         groups = [[(mask, part) for mask in range(tri_size) for part in range(2)]]
     partials = ladder(small, pieces, ladder_blocks, groups)
-    *partials, ring[-1], back_integrals = lax.optimization_barrier((*partials, ring[-1], back_integrals))
+    *partials, ring[-1] = lax.optimization_barrier((*partials, ring[-1]))
     hold, give = contract(core, integrals, back_integrals, ring)
 
     def shift(value):

time: 74.7 us -> 68.7 us (0.920)
  waiting for transfers between devices: 30.7 us -> 23.8 us
  starting transfers between devices: 30.3 us -> 31.2 us
    ppermute x22, waiting for transfers between devices: 23 us -> 17 us  [swap(): return lax.ppermute(value, 'tri', pairs)]
    ppermute x6, starting transfers between devices: 13.8 us -> 15.4 us  [turn(): lax.ppermute(value, 'vp', [(order[i], order[(i + distance) % vp_size]) fo...]
    ppermute x6, waiting for transfers between devices: 7.69 us -> 6.8 us  [turn(): lax.ppermute(value, 'vp', [(order[i], order[(i + distance) % vp_size]) fo...]
  transfers between devices with their start and end apart: 28 -> 28, of which waited for: 12 -> 14; matrix products, arithmetic and copies ran while one was open for 1% -> 2% of each run, Pallas kernels for 13% -> 14%
where the time goes in v13:
time: 68.7 us; the launch traced here: 68.6 us
  starting transfers between devices  31.2 us (45%)
  waiting for transfers between devices  23.8 us (35%)
  Pallas kernels  11 us (16%)
  other arithmetic  1.32 us (2%)
  local copies, waits for them, and re-layouts  1.08 us (2%)
    ppermute x22, waiting for transfers between devices, swap(): return lax.ppermute(value, 'tri', pairs)  17 us
    ppermute x22, starting transfers between devices, swap(): return lax.ppermute(value, 'tri', pairs)  15.9 us
    ppermute x6, starting transfers between devices, turn(): lax.ppermute(value, 'vp', [(order[i], order[(i + distance) % vp_size]) fo...  15.4 us
    pallas_call x1, Pallas kernels, ladder(): pl.pallas_call(functools.partial(ladder_kernel, [(mask, part) for _, mask...  8.31 us
    ppermute x6, waiting for transfers between devices, turn(): lax.ppermute(value, 'vp', [(order[i], order[(i + distance) % vp_size]) fo...  6.8 us
    pallas_call x1, Pallas kernels, quadratic(): pl.pallas_call(quadratic_kernel, in_specs=[pl.BlockSpec(memory_space=pltp...  1.49 us
  transfers between devices with their start and end apart: 28, of which 14 were waited for; matrix products, arithmetic and copies ran while one was open for 2% of the time, Pallas kernels for 14%

profile of v13, /device:TPU:0, one launch (start us, length us, event | category | flops | bytes accessed | tf_op | source)
XLA Modules:
  0.0 68.6 jit_solution(3296543306030096385)
XLA Ops:
  0.0 3.0 %collective-permute-start.1 = (bf16[2,960,128]{2,1,0:T(8,128)(2,1)}, bf16[2,960,128]{2,1,0:T(8,128)(2,1)S(1)}, u32[]{:S(2)}, u32[]{:S(2)}) collective-permute-start(bf16[2,960,128]{2,1,0:T(8,128)(2,1)} %source_ref.1), channel_id=1, source_target_pairs={{0,16},{4,20},{8,24},{12,28},{16,0},{20,4},{24,8},{28,12},{1,17},{... | collective-permute-start | bytes 1474568 | tf_op jit(solution)/shard_map/ppermute | solution.py:20
  3.0 1.5 %collective-permute-start = (bf16[2,960,128]{2,1,0:T(8,128)(2,1)}, bf16[2,960,128]{2,1,0:T(8,128)(2,1)S(1)}, u32[]{:S(2)}, u32[]{:S(2)}) collective-permute-start(bf16[2,960,128]{2,1,0:T(8,128)(2,1)} %source_ref.1), channel_id=1, source_target_pairs={{0,8},{4,12},{8,0},{12,4},{16,24},{20,28},{24,16},{28,20},{1,9},{5... | collective-permute-start | bytes 1474568 | tf_op jit(solution)/shard_map/ppermute | solution.py:20
  4.5 2.6 %collective-permute-start.2 = (bf16[2,960,128]{2,1,0:T(8,128)(2,1)}, bf16[2,960,128]{2,1,0:T(8,128)(2,1)S(1)}, u32[]{:S(2)}, u32[]{:S(2)}) collective-permute-start(bf16[2,960,128]{2,1,0:T(8,128)(2,1)} %source_ref.1), channel_id=1, source_target_pairs={{0,2},{2,3},{3,1},{1,0},{4,6},{6,7},{7,5},{5,4},{8,10},{10,11},{11... | collective-permute-start | bytes 1474568 | tf_op jit(solution)/shard_map/ppermute | solution.py:277
  7.1 1.6 %collective-permute-start.3 = (bf16[960,128]{1,0:T(8,128)(2,1)}, bf16[960,128]{1,0:T(8,128)(2,1)S(1)}, u32[]{:S(2)}, u32[]{:S(2)}) collective-permute-start(bf16[960,128]{1,0:T(8,128)(2,1)} %int_ref.1), channel_id=1, source_target_pairs={{0,2},{2,3},{3,1},{1,0},{4,6},{6,7},{7,5},{5,4},{8,10},{10,11},{11... | collective-permute-start | bytes 737288 | tf_op jit(solution)/shard_map/ppermute | solution.py:277
  8.6 0.7 %pad_add_fusion.small_ref = s32[8]{0:T(128)S(1)} fusion(s32[7]{0:T(128)} %param.7, s32[1]{0:T(128)} %bitcast), kind=kLoop, calls=%fused_computation.14 | loop fusion | flops 8 | bytes 64 | tf_op jit(solution)/shard_map/concatenate | solution.py:283
  9.4 1.0 %copy-done = bf16[2,960,128]{2,1,0:T(8,128)(2,1)S(1)} copy-done((bf16[2,960,128]{2,1,0:T(8,128)(2,1)S(1)}, bf16[2,960,128]{2,1,0:T(8,128)(2,1)}, u32[]{:S(2)}) %copy-start) | copy-done | bytes 491544
  10.7 3.7 %collective-permute-done.1.refs_2_ = bf16[2,960,128]{2,1,0:T(8,128)(2,1)S(1)} collective-permute-done((bf16[2,960,128]{2,1,0:T(8,128)(2,1)}, bf16[2,960,128]{2,1,0:T(8,128)(2,1)S(1)}, u32[]{:S(2)}, u32[]{:S(2)}) %collective-permute-start.1) | collective-permute-done | bytes 491552 | tf_op jit(solution)/shard_map/ppermute | solution.py:20
  14.4 1.5 %collective-permute-done.refs_1_ = bf16[2,960,128]{2,1,0:T(8,128)(2,1)S(1)} collective-permute-done((bf16[2,960,128]{2,1,0:T(8,128)(2,1)}, bf16[2,960,128]{2,1,0:T(8,128)(2,1)S(1)}, u32[]{:S(2)}, u32[]{:S(2)}) %collective-permute-start) | collective-permute-done | bytes 491552 | tf_op jit(solution)/shard_map/ppermute | solution.py:20
  15.9 1.6 %collective-permute-start.4 = (bf16[960,128]{1,0:T(8,128)(2,1)S(1)}, bf16[960,128]{1,0:T(8,128)(2,1)S(1)}, u32[]{:S(2)}, u32[]{:S(2)}) collective-permute-start(bf16[960,128]{1,0:T(8,128)(2,1)S(1)} %slice_bitcast_fusion.1), channel_id=1, source_target_pairs={{0,8},{4,12},{8,0},{12,4},{16,24},{20,28},{24,16},{28,20},{1,9},{5... | collective-permute-start | bytes 737288 | tf_op jit(solution)/shard_map/ppermute | solution.py:20
  18.0 5.8 %collective-permute-done.3.last_ref = bf16[960,128]{1,0:T(8,128)(2,1)S(1)} collective-permute-done((bf16[960,128]{1,0:T(8,128)(2,1)}, bf16[960,128]{1,0:T(8,128)(2,1)S(1)}, u32[]{:S(2)}, u32[]{:S(2)}) %collective-permute-start.3) | collective-permute-done | bytes 245792 | tf_op jit(solution)/shard_map/ppermute | solution.py:277
  23.8 0.5 collective-permute-start.8
  24.3 3.3 %collective-permute-start.11 = (bf16[2,960,128]{2,1,0:T(8,128)(2,1)S(1)}, bf16[2,960,128]{2,1,0:T(8,128)(2,1)S(1)}, u32[]{:S(2)}, u32[]{:S(2)}) collective-permute-start(bf16[2,960,128]{2,1,0:T(8,128)(2,1)S(1)} %collective-permute-done.2.refs_1_), channel_id=1, source_target_pairs={{0,2},{2,3},{3,1},{1,0},{4,6},{6,7},{7,5},{5,4},{8,10},{10,11},{11... | collective-permute-start | bytes 1474568 | tf_op jit(solution)/shard_map/ppermute | solution.py:277
  28.1 1.0 %collective-permute-done.9.refs_8_ = bf16[960,128]{1,0:T(8,128)(2,1)S(1)} collective-permute-done((bf16[960,128]{1,0:T(8,128)(2,1)S(1)}, bf16[960,128]{1,0:T(8,128)(2,1)S(1)}, u32[]{:S(2)}, u32[]{:S(2)}) %collective-permute-start.9) | collective-permute-done | bytes 245792 | tf_op jit(solution)/shard_map/ppermute | solution.py:20
  29.5 8.3 %ladder.1 = (bf16[3,960,128]{2,1,0:T(8,128)(2,1)S(1)}, bf16[3,960,128]{2,1,0:T(8,128)(2,1)S(1)}, bf16[2,960,128]{2,1,0:T(8,128)(2,1)S(1)}, bf16[3,960,128]{2,1,0...) custom-call(s32[8]{0:T(128)S(1)} %pad_add_fusion.small_ref, ...), custom_call_target="tpu_custom_call" | custom-call | flops 528482304 | bytes 1966080 | tf_op jit(solution)/shard_map/ladder/pallas_call | solution.py:138
  37.8 0.5 collective-permute-done.11.refs_2_
  38.8 0.6 contract.1
  39.4 1.1 %collective-permute-done.12 = bf16[3,960,128]{2,1,0:T(8,128)(2,1)S(1)} collective-permute-done((bf16[3,960,128]{2,1,0:T(8,128)(2,1)S(1)}, bf16[3,960,128]{2,1,0:T(8,128)(2,1)S(1)}, u32[]{:S(2)}, u32[]{:S(2)}) %collective-permute-start.12) | collective-permute-done | bytes 737312 | tf_op jit(solution)/shard_map/ppermute | solution.py:20
  40.5 1.1 %collective-permute-done.13 = bf16[3,960,128]{2,1,0:T(8,128)(2,1)S(1)} collective-permute-done((bf16[3,960,128]{2,1,0:T(8,128)(2,1)S(1)}, bf16[3,960,128]{2,1,0:T(8,128)(2,1)S(1)}, u32[]{:S(2)}, u32[]{:S(2)}) %collective-permute-start.13) | collective-permute-done | bytes 737312 | tf_op jit(solution)/shard_map/ppermute | solution.py:20
  42.0 0.5 collective-permute-start.17
  43.3 2.7 %collective-permute-start.16 = (bf16[128,128]{1,0:T(8,128)(2,1)S(1)}, bf16[128,128]{1,0:T(8,128)(2,1)S(1)}, u32[]{:S(2)}, u32[]{:S(2)}) collective-permute-start(bf16[128,128]{1,0:T(8,128)(2,1)S(1)} %get-tuple-element.89), channel_id=1, source_target_pairs={{0,3},{2,1},{3,0},{1,2},{4,7},{6,5},{7,4},{5,6},{8,11},{10,9},{11,... | collective-permute-start | bytes 98312 | tf_op jit(solution)/shard_map/ppermute | solution.py:277
  46.0 1.3 %collective-permute-start.15 = (bf16[128,128]{1,0:T(8,128)(2,1)S(1)}, bf16[128,128]{1,0:T(8,128)(2,1)S(1)}, u32[]{:S(2)}, u32[]{:S(2)}) collective-permute-start(bf16[128,128]{1,0:T(8,128)(2,1)S(1)} %get-tuple-element.90), channel_id=1, source_target_pairs={{0,1},{2,0},{3,2},{1,3},{4,5},{6,4},{7,6},{5,7},{8,9},{10,8},{11,1... | collective-permute-start | bytes 98312 | tf_op jit(solution)/shard_map/ppermute | solution.py:277
  47.3 1.3 %collective-permute-start.24 = (bf16[1,960,128]{2,1,0:T(8,128)(2,1)S(1)}, bf16[1,960,128]{2,1,0:T(8,128)(2,1)S(1)}, u32[]{:S(2)}, u32[]{:S(2)}) collective-permute-start(bf16[1,960,128]{2,1,0:T(8,128)(2,1)S(1)} %get-tuple-element.73), channel_id=1, source_target_pairs={{0,8},{4,12},{8,0},{12,4},{16,24},{20,28},{24,16},{28,20},{1,9},{5... | collective-permute-start | bytes 737288 | tf_op jit(solution)/shard_map/ppermute | solution.py:20
  49.1 1.7 %collective-permute-start.25 = (bf16[1,960,128]{2,1,0:T(8,128)(2,1)S(1)}, bf16[1,960,128]{2,1,0:T(8,128)(2,1)S(1)}, u32[]{:S(2)}, u32[]{:S(2)}) collective-permute-start(bf16[1,960,128]{2,1,0:T(8,128)(2,1)S(1)} %get-tuple-element.74), channel_id=1, source_target_pairs={{0,16},{4,20},{8,24},{12,28},{16,0},{20,4},{24,8},{28,12},{1,17},{... | collective-permute-start | bytes 737288 | tf_op jit(solution)/shard_map/ppermute | solution.py:20
  50.8 1.6 %collective-permute-start.19 = (bf16[4,128,128]{2,1,0:T(8,128)(2,1)S(1)}, bf16[4,128,128]{2,1,0:T(8,128)(2,1)S(1)}, u32[]{:S(2)}, u32[]{:S(2)}) collective-permute-start(bf16[4,128,128]{2,1,0:T(8,128)(2,1)S(1)} %pad_maximum_fusion), channel_id=1, source_target_pairs={{0,8},{4,12},{8,0},{12,4},{16,24},{20,28},{24,16},{28,20},{1,9},{5... | collective-permute-start | bytes 393224 | tf_op jit(solution)/shard_map/ppermute | solution.py:20
  52.5 3.9 %collective-permute-start.21 = (bf16[2,960,128]{2,1,0:T(8,128)(2,1)S(1)}, bf16[2,960,128]{2,1,0:T(8,128)(2,1)S(1)}, u32[]{:S(2)}, u32[]{:S(2)}) collective-permute-start(bf16[2,960,128]{2,1,0:T(8,128)(2,1)S(1)} %collective-permute-done.11.refs_2_), channel_id=1, source_target_pairs={{0,2},{2,3},{3,1},{1,0},{4,6},{6,7},{7,5},{5,4},{8,10},{10,11},{11... | collective-permute-start | bytes 1474568 | tf_op jit(solution)/shard_map/ppermute | solution.py:277
  56.6 1.7 %collective-permute-done.19 = bf16[4,128,128]{2,1,0:T(8,128)(2,1)S(1)} collective-permute-done((bf16[4,128,128]{2,1,0:T(8,128)(2,1)S(1)}, bf16[4,128,128]{2,1,0:T(8,128)(2,1)S(1)}, u32[]{:S(2)}, u32[]{:S(2)}) %collective-permute-start.19) | collective-permute-done | bytes 131104 | tf_op jit(solution)/shard_map/ppermute | solution.py:20
  58.3 0.5 collective-permute-start.23
  58.9 1.3 %collective-permute-start.20 = (bf16[4,128,128]{2,1,0:T(8,128)(2,1)S(1)}, bf16[4,128,128]{2,1,0:T(8,128)(2,1)S(1)}, u32[]{:S(2)}, u32[]{:S(2)}) collective-permute-start(bf16[4,128,128]{2,1,0:T(8,128)(2,1)S(1)} %add_convert_fusion.7), channel_id=1, source_target_pairs={{0,16},{4,20},{8,24},{12,28},{16,0},{20,4},{24,8},{28,12},{1,17},{... | collective-permute-start | bytes 393224 | tf_op jit(solution)/shard_map/ppermute | solution.py:20
  60.2 4.0 %collective-permute-done.22.refs_6_ = bf16[1,960,128]{2,1,0:T(8,128)(2,1)S(1)} collective-permute-done((bf16[1,960,128]{2,1,0:T(8,128)(2,1)S(1)}, bf16[1,960,128]{2,1,0:T(8,128)(2,1)S(1)}, u32[]{:S(2)}, u32[]{:S(2)}) %collective-permute-start.22) | collective-permute-done | bytes 245792 | tf_op jit(solution)/shard_map/ppermute | solution.py:20
  64.2 1.4 %collective-permute-done.23.refs_7_ = bf16[1,960,128]{2,1,0:T(8,128)(2,1)S(1)} collective-permute-done((bf16[1,960,128]{2,1,0:T(8,128)(2,1)S(1)}, bf16[1,960,128]{2,1,0:T(8,128)(2,1)S(1)}, u32[]{:S(2)}, u32[]{:S(2)}) %collective-permute-start.23) | collective-permute-done | bytes 245792 | tf_op jit(solution)/shard_map/ppermute | solution.py:20
  66.1 1.0 %collective-permute-done.26.other_ref = bf16[4,128,128]{2,1,0:T(8,128)(2,1)S(1)} collective-permute-done((bf16[4,128,128]{2,1,0:T(8,128)(2,1)S(1)}, bf16[4,128,128]{2,1,0:T(8,128)(2,1)S(1)}, u32[]{:S(2)}, u32[]{:S(2)}) %collective-permute-start.26) | collective-permute-done | bytes 131104 | tf_op jit(solution)/shard_map/ppermute | solution.py:20
  67.1 1.5 %quadratic.1 = bf16[2,960,128]{2,1,0:T(8,128)(2,1)} custom-call(s32[1]{0:T(128)S(6)} %and.4.core_ref, bf16[4,128,128]{2,1,0:T(8,128)(2,1)S(1)} %add_convert_fusion.6.mine_ref, bf16[4,128,128]{2,1,0:T(8,128)(2,1)S(1)} %collective-permute-done.26.other_ref, f32[2,960,128]{2,1,0:T(8,128)S(1)} %combine.1.base_ref, ...), custom_call_target="tpu_custom_call" | custom-call | flops 503316480 | bytes 3440640 | tf_op jit(solution)/shard_map/quadratic/pallas_call | solution.py:226
  (44 shorter events, 4.7 us)
Async XLA Ops:
  0.0 14.4 %collective-permute-start.1 = (bf16[2,960,128]{2,1,0:T(8,128)(2,1)}, bf16[2,960,128]{2,1,0:T(8,128)(2,1)S(1)}, u32[]{:S(2)}, u32[]{:S(2)}) collective-permute-start(bf16[2,960,128]{2,1,0:T(8,128)(2,1)} %source_ref.1), channel_id=1, source_target_pairs={{0,16},{4,20},{8,24},{12,28},{16,0},{20,4},{24,8},{28,12},{1,17},{... | collective-permute-start | bytes 1474568 | tf_op jit(solution)/shard_map/ppermute | solution.py:20
  3.0 12.9 %collective-permute-start = (bf16[2,960,128]{2,1,0:T(8,128)(2,1)}, bf16[2,960,128]{2,1,0:T(8,128)(2,1)S(1)}, u32[]{:S(2)}, u32[]{:S(2)}) collective-permute-start(bf16[2,960,128]{2,1,0:T(8,128)(2,1)} %source_ref.1), channel_id=1, source_target_pairs={{0,8},{4,12},{8,0},{12,4},{16,24},{20,28},{24,16},{28,20},{1,9},{5... | collective-permute-start | bytes 1474568 | tf_op jit(solution)/shard_map/ppermute | solution.py:20
  4.5 19.3 %collective-permute-start.6 = (bf16[2,960,128]{2,1,0:T(8,128)(2,1)}, bf16[2,960,128]{2,1,0:T(8,128)(2,1)S(1)}, u32[]{:S(2)}, u32[]{:S(2)}) collective-permute-start(bf16[2,960,128]{2,1,0:T(8,128)(2,1)} %source_ref.1), channel_id=1, source_target_pairs={{0,4},{4,0},{8,12},{12,8},{16,20},{20,16},{24,28},{28,24},{1,5},{5... | collective-permute-start | bytes 1474568 | tf_op jit(solution)/shard_map/ppermute | solution.py:20
  4.5 19.8 %collective-permute-start.2 = (bf16[2,960,128]{2,1,0:T(8,128)(2,1)}, bf16[2,960,128]{2,1,0:T(8,128)(2,1)S(1)}, u32[]{:S(2)}, u32[]{:S(2)}) collective-permute-start(bf16[2,960,128]{2,1,0:T(8,128)(2,1)} %source_ref.1), channel_id=1, source_target_pairs={{0,2},{2,3},{3,1},{1,0},{4,6},{6,7},{7,5},{5,4},{8,10},{10,11},{11... | collective-permute-start | bytes 1474568 | tf_op jit(solution)/shard_map/ppermute | solution.py:277
  7.1 16.7 %collective-permute-start.3 = (bf16[960,128]{1,0:T(8,128)(2,1)}, bf16[960,128]{1,0:T(8,128)(2,1)S(1)}, u32[]{:S(2)}, u32[]{:S(2)}) collective-permute-start(bf16[960,128]{1,0:T(8,128)(2,1)} %int_ref.1), channel_id=1, source_target_pairs={{0,2},{2,3},{3,1},{1,0},{4,6},{6,7},{7,5},{5,4},{8,10},{10,11},{11... | collective-permute-start | bytes 737288 | tf_op jit(solution)/shard_map/ppermute | solution.py:277
  9.4 1.0 %copy-start = (bf16[2,960,128]{2,1,0:T(8,128)(2,1)S(1)}, bf16[2,960,128]{2,1,0:T(8,128)(2,1)}, u32[]{:S(2)}) copy-start(bf16[2,960,128]{2,1,0:T(8,128)(2,1)} %source_ref.1) | copy-start | bytes 1474564
  10.4 28.4 %copy-start.1 = (bf16[960,128]{1,0:T(8,128)(2,1)S(1)}, bf16[960,128]{1,0:T(8,128)(2,1)}, u32[]{:S(2)}) copy-start(bf16[960,128]{1,0:T(8,128)(2,1)} %int_ref.1) | copy-start | bytes 737284
  15.9 11.7 %collective-permute-start.4 = (bf16[960,128]{1,0:T(8,128)(2,1)S(1)}, bf16[960,128]{1,0:T(8,128)(2,1)S(1)}, u32[]{:S(2)}, u32[]{:S(2)}) collective-permute-start(bf16[960,128]{1,0:T(8,128)(2,1)S(1)} %slice_bitcast_fusion.1), channel_id=1, source_target_pairs={{0,8},{4,12},{8,0},{12,4},{16,24},{20,28},{24,16},{28,20},{1,9},{5... | collective-permute-start | bytes 737288 | tf_op jit(solution)/shard_map/ppermute | solution.py:20
  17.5 10.1 %collective-permute-start.5 = (bf16[960,128]{1,0:T(8,128)(2,1)S(1)}, bf16[960,128]{1,0:T(8,128)(2,1)S(1)}, u32[]{:S(2)}, u32[]{:S(2)}) collective-permute-start(bf16[960,128]{1,0:T(8,128)(2,1)S(1)} %slice_bitcast_fusion), channel_id=1, source_target_pairs={{0,16},{4,20},{8,24},{12,28},{16,0},{20,4},{24,8},{28,12},{1,17},{... | collective-permute-start | bytes 737288 | tf_op jit(solution)/shard_map/ppermute | solution.py:20
  23.8 5.7 %collective-permute-start.7 = (bf16[2,960,128]{2,1,0:T(8,128)(2,1)S(1)}, bf16[2,960,128]{2,1,0:T(8,128)(2,1)S(1)}, u32[]{:S(2)}, u32[]{:S(2)}) collective-permute-start(bf16[2,960,128]{2,1,0:T(8,128)(2,1)S(1)} %collective-permute-done.refs_1_), channel_id=1, source_target_pairs={{0,4},{4,0},{8,12},{12,8},{16,20},{20,16},{24,28},{28,24},{1,5},{5... | collective-permute-start | bytes 1474568 | tf_op jit(solution)/shard_map/ppermute | solution.py:20
  23.8 5.7 %collective-permute-start.8 = (bf16[2,960,128]{2,1,0:T(8,128)(2,1)S(1)}, bf16[2,960,128]{2,1,0:T(8,128)(2,1)S(1)}, u32[]{:S(2)}, u32[]{:S(2)}) collective-permute-start(bf16[2,960,128]{2,1,0:T(8,128)(2,1)S(1)} %collective-permute-done.1.refs_2_), channel_id=1, source_target_pairs={{0,4},{4,0},{8,12},{12,8},{16,20},{20,16},{24,28},{28,24},{1,5},{5... | collective-permute-start | bytes 1474568 | tf_op jit(solution)/shard_map/ppermute | solution.py:20
  24.3 14.0 %collective-permute-start.11 = (bf16[2,960,128]{2,1,0:T(8,128)(2,1)S(1)}, bf16[2,960,128]{2,1,0:T(8,128)(2,1)S(1)}, u32[]{:S(2)}, u32[]{:S(2)}) collective-permute-start(bf16[2,960,128]{2,1,0:T(8,128)(2,1)S(1)} %collective-permute-done.2.refs_1_), channel_id=1, source_target_pairs={{0,2},{2,3},{3,1},{1,0},{4,6},{6,7},{7,5},{5,4},{8,10},{10,11},{11... | collective-permute-start | bytes 1474568 | tf_op jit(solution)/shard_map/ppermute | solution.py:277
  27.6 1.5 %collective-permute-start.9 = (bf16[960,128]{1,0:T(8,128)(2,1)S(1)}, bf16[960,128]{1,0:T(8,128)(2,1)S(1)}, u32[]{:S(2)}, u32[]{:S(2)}) collective-permute-start(bf16[960,128]{1,0:T(8,128)(2,1)S(1)} %collective-permute-done.4.refs_3_), channel_id=1, source_target_pairs={{0,4},{4,0},{8,12},{12,8},{16,20},{20,16},{24,28},{28,24},{1,5},{5... | collective-permute-start | bytes 737288 | tf_op jit(solution)/shard_map/ppermute | solution.py:20
  27.6 1.9 %collective-permute-start.10 = (bf16[960,128]{1,0:T(8,128)(2,1)S(1)}, bf16[960,128]{1,0:T(8,128)(2,1)S(1)}, u32[]{:S(2)}, u32[]{:S(2)}) collective-permute-start(bf16[960,128]{1,0:T(8,128)(2,1)S(1)} %collective-permute-done.5.refs_4_), channel_id=1, source_target_pairs={{0,4},{4,0},{8,12},{12,8},{16,20},{20,16},{24,28},{28,24},{1,5},{5... | collective-permute-start | bytes 737288 | tf_op jit(solution)/shard_map/ppermute | solution.py:20
  38.3 2.2 %collective-permute-start.12 = (bf16[3,960,128]{2,1,0:T(8,128)(2,1)S(1)}, bf16[3,960,128]{2,1,0:T(8,128)(2,1)S(1)}, u32[]{:S(2)}, u32[]{:S(2)}) collective-permute-start(bf16[3,960,128]{2,1,0:T(8,128)(2,1)S(1)} %get-tuple-element.55), channel_id=1, source_target_pairs={{0,4},{4,0},{8,12},{12,8},{16,20},{20,16},{24,28},{28,24},{1,5},{5... | collective-permute-start | bytes 2211848 | tf_op jit(solution)/shard_map/ppermute | solution.py:20
  38.3 3.3 %collective-permute-start.13 = (bf16[3,960,128]{2,1,0:T(8,128)(2,1)S(1)}, bf16[3,960,128]{2,1,0:T(8,128)(2,1)S(1)}, u32[]{:S(2)}, u32[]{:S(2)}) collective-permute-start(bf16[3,960,128]{2,1,0:T(8,128)(2,1)S(1)} %get-tuple-element.56), channel_id=1, source_target_pairs={{0,4},{4,0},{8,12},{12,8},{16,20},{20,16},{24,28},{28,24},{1,5},{5... | collective-permute-start | bytes 2211848 | tf_op jit(solution)/shard_map/ppermute | solution.py:20
  41.8 1.4 %collective-permute-start.14 = (bf16[4,128,128]{2,1,0:T(8,128)(2,1)S(1)}, bf16[4,128,128]{2,1,0:T(8,128)(2,1)S(1)}, u32[]{:S(2)}, u32[]{:S(2)}) collective-permute-start(bf16[4,128,128]{2,1,0:T(8,128)(2,1)S(1)} %get-tuple-element.66), channel_id=1, source_target_pairs={{0,4},{4,0},{8,12},{12,8},{16,20},{20,16},{24,28},{28,24},{1,5},{5... | collective-permute-start | bytes 393224 | tf_op jit(solution)/shard_map/ppermute | solution.py:20
  42.0 8.8 %collective-permute-start.17 = (bf16[1,960,128]{2,1,0:T(8,128)(2,1)S(1)}, bf16[1,960,128]{2,1,0:T(8,128)(2,1)S(1)}, u32[]{:S(2)}, u32[]{:S(2)}) collective-permute-start(bf16[1,960,128]{2,1,0:T(8,128)(2,1)S(1)} %get-tuple-element.67), channel_id=1, source_target_pairs={{0,8},{4,12},{8,0},{12,4},{16,24},{20,28},{24,16},{28,20},{1,9},{5... | collective-permute-start | bytes 737288 | tf_op jit(solution)/shard_map/ppermute | solution.py:20
  42.6 8.2 %collective-permute-start.18 = (bf16[1,960,128]{2,1,0:T(8,128)(2,1)S(1)}, bf16[1,960,128]{2,1,0:T(8,128)(2,1)S(1)}, u32[]{:S(2)}, u32[]{:S(2)}) collective-permute-start(bf16[1,960,128]{2,1,0:T(8,128)(2,1)S(1)} %get-tuple-element.68), channel_id=1, source_target_pairs={{0,16},{4,20},{8,24},{12,28},{16,0},{20,4},{24,8},{28,12},{1,17},{... | collective-permute-start | bytes 737288 | tf_op jit(solution)/shard_map/ppermute | solution.py:20
  43.3 5.8 %collective-permute-start.16 = (bf16[128,128]{1,0:T(8,128)(2,1)S(1)}, bf16[128,128]{1,0:T(8,128)(2,1)S(1)}, u32[]{:S(2)}, u32[]{:S(2)}) collective-permute-start(bf16[128,128]{1,0:T(8,128)(2,1)S(1)} %get-tuple-element.89), channel_id=1, source_target_pairs={{0,3},{2,1},{3,0},{1,2},{4,7},{6,5},{7,4},{5,6},{8,11},{10,9},{11,... | collective-permute-start | bytes 98312 | tf_op jit(solution)/shard_map/ppermute | solution.py:277
  46.0 4.8 %collective-permute-start.15 = (bf16[128,128]{1,0:T(8,128)(2,1)S(1)}, bf16[128,128]{1,0:T(8,128)(2,1)S(1)}, u32[]{:S(2)}, u32[]{:S(2)}) collective-permute-start(bf16[128,128]{1,0:T(8,128)(2,1)S(1)} %get-tuple-element.90), channel_id=1, source_target_pairs={{0,1},{2,0},{3,2},{1,3},{4,5},{6,4},{7,6},{5,7},{8,9},{10,8},{11,1... | collective-permute-start | bytes 98312 | tf_op jit(solution)/shard_map/ppermute | solution.py:277
  47.3 11.6 %collective-permute-start.24 = (bf16[1,960,128]{2,1,0:T(8,128)(2,1)S(1)}, bf16[1,960,128]{2,1,0:T(8,128)(2,1)S(1)}, u32[]{:S(2)}, u32[]{:S(2)}) collective-permute-start(bf16[1,960,128]{2,1,0:T(8,128)(2,1)S(1)} %get-tuple-element.73), channel_id=1, source_target_pairs={{0,8},{4,12},{8,0},{12,4},{16,24},{20,28},{24,16},{28,20},{1,9},{5... | collective-permute-start | bytes 737288 | tf_op jit(solution)/shard_map/ppermute | solution.py:20
  49.1 11.1 %collective-permute-start.25 = (bf16[1,960,128]{2,1,0:T(8,128)(2,1)S(1)}, bf16[1,960,128]{2,1,0:T(8,128)(2,1)S(1)}, u32[]{:S(2)}, u32[]{:S(2)}) collective-permute-start(bf16[1,960,128]{2,1,0:T(8,128)(2,1)S(1)} %get-tuple-element.74), channel_id=1, source_target_pairs={{0,16},{4,20},{8,24},{12,28},{16,0},{20,4},{24,8},{28,12},{1,17},{... | collective-permute-start | bytes 737288 | tf_op jit(solution)/shard_map/ppermute | solution.py:20
  50.8 7.5 %collective-permute-start.19 = (bf16[4,128,128]{2,1,0:T(8,128)(2,1)S(1)}, bf16[4,128,128]{2,1,0:T(8,128)(2,1)S(1)}, u32[]{:S(2)}, u32[]{:S(2)}) collective-permute-start(bf16[4,128,128]{2,1,0:T(8,128)(2,1)S(1)} %pad_maximum_fusion), channel_id=1, source_target_pairs={{0,8},{4,12},{8,0},{12,4},{16,24},{20,28},{24,16},{28,20},{1,9},{5... | collective-permute-start | bytes 393224 | tf_op jit(solution)/shard_map/ppermute | solution.py:20
  52.5 13.2 %collective-permute-start.21 = (bf16[2,960,128]{2,1,0:T(8,128)(2,1)S(1)}, bf16[2,960,128]{2,1,0:T(8,128)(2,1)S(1)}, u32[]{:S(2)}, u32[]{:S(2)}) collective-permute-start(bf16[2,960,128]{2,1,0:T(8,128)(2,1)S(1)} %collective-permute-done.11.refs_2_), channel_id=1, source_target_pairs={{0,2},{2,3},{3,1},{1,0},{4,6},{6,7},{7,5},{5,4},{8,10},{10,11},{11... | collective-permute-start | bytes 1474568 | tf_op jit(solution)/shard_map/ppermute | solution.py:277
  56.5 7.7 %collective-permute-start.22 = (bf16[1,960,128]{2,1,0:T(8,128)(2,1)S(1)}, bf16[1,960,128]{2,1,0:T(8,128)(2,1)S(1)}, u32[]{:S(2)}, u32[]{:S(2)}) collective-permute-start(bf16[1,960,128]{2,1,0:T(8,128)(2,1)S(1)} %add_convert_fusion.1), channel_id=1, source_target_pairs={{0,16},{4,20},{8,24},{12,28},{16,0},{20,4},{24,8},{28,12},{1,17},{... | collective-permute-start | bytes 737288 | tf_op jit(solution)/shard_map/ppermute | solution.py:20
  58.3 7.3 %collective-permute-start.23 = (bf16[1,960,128]{2,1,0:T(8,128)(2,1)S(1)}, bf16[1,960,128]{2,1,0:T(8,128)(2,1)S(1)}, u32[]{:S(2)}, u32[]{:S(2)}) collective-permute-start(bf16[1,960,128]{2,1,0:T(8,128)(2,1)S(1)} %add_convert_fusion), channel_id=1, source_target_pairs={{0,8},{4,12},{8,0},{12,4},{16,24},{20,28},{24,16},{28,20},{1,9},{5... | collective-permute-start | bytes 737288 | tf_op jit(solution)/shard_map/ppermute | solution.py:20
  58.9 6.7 %collective-permute-start.20 = (bf16[4,128,128]{2,1,0:T(8,128)(2,1)S(1)}, bf16[4,128,128]{2,1,0:T(8,128)(2,1)S(1)}, u32[]{:S(2)}, u32[]{:S(2)}) collective-permute-start(bf16[4,128,128]{2,1,0:T(8,128)(2,1)S(1)} %add_convert_fusion.7), channel_id=1, source_target_pairs={{0,16},{4,20},{8,24},{12,28},{16,0},{20,4},{24,8},{28,12},{1,17},{... | collective-permute-start | bytes 393224 | tf_op jit(solution)/shard_map/ppermute | solution.py:20
  60.2 5.6 %collective-permute-start.27 = (bf16[2,960,128]{2,1,0:T(8,128)(2,1)S(1)}, bf16[2,960,128]{2,1,0:T(8,128)(2,1)S(1)}, u32[]{:S(2)}, u32[]{:S(2)}) collective-permute-start(bf16[2,960,128]{2,1,0:T(8,128)(2,1)S(1)} %get-tuple-element.77), channel_id=1, source_target_pairs={{0,4},{4,0},{8,12},{12,8},{16,20},{20,16},{24,28},{28,24},{1,5},{5... | collective-permute-start | bytes 1474568 | tf_op jit(solution)/shard_map/ppermute | solution.py:20
  65.7 1.4 %collective-permute-start.26 = (bf16[4,128,128]{2,1,0:T(8,128)(2,1)S(1)}, bf16[4,128,128]{2,1,0:T(8,128)(2,1)S(1)}, u32[]{:S(2)}, u32[]{:S(2)}) collective-permute-start(bf16[4,128,128]{2,1,0:T(8,128)(2,1)S(1)} %add_convert_fusion.6.mine_ref), channel_id=1, source_target_pairs={{0,4},{4,0},{8,12},{12,8},{16,20},{20,16},{24,28},{28,24},{1,5},{5... | collective-permute-start | bytes 393224 | tf_op jit(solution)/shard_map/ppermute | solution.py:20

commit v14 on v13

--- a/solution.py
+++ b/solution.py
@@ -285,9 +285,8 @@
     ring[0] = pieces[0][0]
 
     if tri_size == 8:
-        real_order, imag_order = (2, 6, 4), (4, 6, 2)
-        groups = [[(mask | 1, 0) for mask in real_order], [(mask | 1, 1) for mask in imag_order], [(1, 0), (1, 1)]]
-        groups += [[(mask, 0) for mask in real_order], [(mask, 1) for mask in imag_order], [(0, 0), (0, 1)]]
+        far, rest, mine = [(6, 0), (6, 1)], [(2, 0), (4, 1), (4, 0), (2, 1)], [(0, 0), (0, 1)]
+        groups = [[(mask | 1, part) for mask, part in places] for places in (far, rest, mine)] + [far, rest, mine]
     else:
         groups = [[(mask, part) for mask in range(tri_size) for part in range(2)]]
     partials = ladder(small, pieces, ladder_blocks, groups)
@@ -299,23 +298,21 @@
         return jnp.stack([value[0], *moved, value[vp_size - 1]])
 
     if tri_size == 8:
-        real, imag, own = partials[3:]
-        real_in, imag_in, own_in = (swap(value, tri_size, 0) for value in partials[:3])
-        real_in, imag_in, hold, give = lax.optimization_barrier((real_in, imag_in, hold, give))
-        far_x, far_y, near_x, near_y = (
-            add(kept[i], came[i]).astype(BF16)[None]
-            for i, kept, came in ((1, real, real_in), (1, imag, imag_in), (0, real, real_in), (0, imag, imag_in))
-        )
-        far_x, far_y, near_x, near_y, hold, give = lax.optimization_barrier(
-            (far_x, far_y, near_x, near_y, hold, give)
-        )
+        far, rest, own = partials[3:]
+        far_in, rest_in, own_in = (swap(value, tri_size, 0) for value in partials[:3])
+        far_in, hold, give = lax.optimization_barrier((far_in, hold, give))
+        far_x, far_y = (add(far[i], far_in[i]).astype(BF16)[None] for i in range(2))
+        far_x, far_y, hold, give = lax.optimization_barrier((far_x, far_y, hold, give))
+        near_x, near_y = (add(rest[i], rest_in[i]).astype(BF16)[None] for i in range(2))
         far_x, far_y = swap(far_x, tri_size, 1), swap(far_y, tri_size, 2)
+        mine = add(hold, swap(give, tri_size, 0)).astype(BF16)
+        near_x, near_y, mine = lax.optimization_barrier((near_x, near_y, mine))
         near_x, near_y = swap(near_x, tri_size, 1), swap(near_y, tri_size, 2)
-        mine = shift(add(hold, swap(give, tri_size, 0)).astype(BF16))
+        mine = shift(mine)
         mine, far_x, far_y = lax.optimization_barrier((mine, far_x, far_y))
         last = turn(after(ring[-1], mine))
-        then_y = swap(add(real[2], real_in[2], far_x[0]).astype(BF16)[None], tri_size, 2)
-        then_x = swap(add(imag[2], imag_in[2], far_y[0]).astype(BF16)[None], tri_size, 1)
+        then_y = swap(add(rest[2], rest_in[2], far_x[0]).astype(BF16)[None], tri_size, 2)
+        then_x = swap(add(rest[3], rest_in[3], far_y[0]).astype(BF16)[None], tri_size, 1)
         mine = add(mine, swap(mine, tri_size, 1)).astype(BF16)
         received, last, then_y, then_x, near_x, near_y = lax.optimization_barrier(
             (swap(mine, tri_size, 2), last, then_y, then_x, near_x, near_y)

time: 68.7 us -> 69.8 us (1.016)
  waiting for transfers between devices: 23.8 us -> 24.6 us
where the time goes in v14:
time: 69.8 us; the launch traced here: 69.7 us
  starting transfers between devices  31.6 us (45%)
  waiting for transfers between devices  24.6 us (35%)
  Pallas kernels  11 us (16%)
  other arithmetic  1.32 us (2%)
  local copies, waits for them, and re-layouts  1.08 us (2%)
    ppermute x22, waiting for transfers between devices, swap(): return lax.ppermute(value, 'tri', pairs)  17.6 us
    ppermute x22, starting transfers between devices, swap(): return lax.ppermute(value, 'tri', pairs)  16.4 us
    ppermute x6, starting transfers between devices, turn(): lax.ppermute(value, 'vp', [(order[i], order[(i + distance) % vp_size]) fo...  15.2 us
    pallas_call x1, Pallas kernels, ladder(): pl.pallas_call(functools.partial(ladder_kernel, [(mask, part) for _, mask...  8.27 us
    ppermute x6, waiting for transfers between devices, turn(): lax.ppermute(value, 'vp', [(order[i], order[(i + distance) % vp_size]) fo...  6.92 us
    pallas_call x1, Pallas kernels, quadratic(): pl.pallas_call(quadratic_kernel, in_specs=[pl.BlockSpec(memory_space=pltp...  1.49 us
  transfers between devices with their start and end apart: 28, of which 14 were waited for; matrix products, arithmetic and copies ran while one was open for 2% of the time, Pallas kernels for 14%

profile of v14, /device:TPU:0, one launch (start us, length us, event | category | flops | bytes accessed | tf_op | source)
XLA Modules:
  0.0 69.7 jit_solution(9308043224101499368)
XLA Ops:
  0.0 3.0 %collective-permute-start.1 = (bf16[2,960,128]{2,1,0:T(8,128)(2,1)}, bf16[2,960,128]{2,1,0:T(8,128)(2,1)S(1)}, u32[]{:S(2)}, u32[]{:S(2)}) collective-permute-start(bf16[2,960,128]{2,1,0:T(8,128)(2,1)} %source_ref.1), channel_id=1, source_target_pairs={{0,16},{4,20},{8,24},{12,28},{16,0},{20,4},{24,8},{28,12},{1,17},{... | collective-permute-start | bytes 1474568 | tf_op jit(solution)/shard_map/ppermute | solution.py:20
  3.0 1.5 %collective-permute-start = (bf16[2,960,128]{2,1,0:T(8,128)(2,1)}, bf16[2,960,128]{2,1,0:T(8,128)(2,1)S(1)}, u32[]{:S(2)}, u32[]{:S(2)}) collective-permute-start(bf16[2,960,128]{2,1,0:T(8,128)(2,1)} %source_ref.1), channel_id=1, source_target_pairs={{0,8},{4,12},{8,0},{12,4},{16,24},{20,28},{24,16},{28,20},{1,9},{5... | collective-permute-start | bytes 1474568 | tf_op jit(solution)/shard_map/ppermute | solution.py:20
  4.5 2.6 %collective-permute-start.2 = (bf16[2,960,128]{2,1,0:T(8,128)(2,1)}, bf16[2,960,128]{2,1,0:T(8,128)(2,1)S(1)}, u32[]{:S(2)}, u32[]{:S(2)}) collective-permute-start(bf16[2,960,128]{2,1,0:T(8,128)(2,1)} %source_ref.1), channel_id=1, source_target_pairs={{0,2},{2,3},{3,1},{1,0},{4,6},{6,7},{7,5},{5,4},{8,10},{10,11},{11... | collective-permute-start | bytes 1474568 | tf_op jit(solution)/shard_map/ppermute | solution.py:277
  7.1 1.6 %collective-permute-start.3 = (bf16[960,128]{1,0:T(8,128)(2,1)}, bf16[960,128]{1,0:T(8,128)(2,1)S(1)}, u32[]{:S(2)}, u32[]{:S(2)}) collective-permute-start(bf16[960,128]{1,0:T(8,128)(2,1)} %int_ref.1), channel_id=1, source_target_pairs={{0,2},{2,3},{3,1},{1,0},{4,6},{6,7},{7,5},{5,4},{8,10},{10,11},{11... | collective-permute-start | bytes 737288 | tf_op jit(solution)/shard_map/ppermute | solution.py:277
  8.6 0.7 %pad_add_fusion.small_ref = s32[8]{0:T(128)S(1)} fusion(s32[7]{0:T(128)} %param.7, s32[1]{0:T(128)} %bitcast), kind=kLoop, calls=%fused_computation.14 | loop fusion | flops 8 | bytes 64 | tf_op jit(solution)/shard_map/concatenate | solution.py:283
  9.4 1.0 %copy-done = bf16[2,960,128]{2,1,0:T(8,128)(2,1)S(1)} copy-done((bf16[2,960,128]{2,1,0:T(8,128)(2,1)S(1)}, bf16[2,960,128]{2,1,0:T(8,128)(2,1)}, u32[]{:S(2)}) %copy-start) | copy-done | bytes 491544
  10.7 3.7 %collective-permute-done.1.refs_2_ = bf16[2,960,128]{2,1,0:T(8,128)(2,1)S(1)} collective-permute-done((bf16[2,960,128]{2,1,0:T(8,128)(2,1)}, bf16[2,960,128]{2,1,0:T(8,128)(2,1)S(1)}, u32[]{:S(2)}, u32[]{:S(2)}) %collective-permute-start.1) | collective-permute-done | bytes 491552 | tf_op jit(solution)/shard_map/ppermute | solution.py:20
  14.4 1.5 %collective-permute-done.refs_1_ = bf16[2,960,128]{2,1,0:T(8,128)(2,1)S(1)} collective-permute-done((bf16[2,960,128]{2,1,0:T(8,128)(2,1)}, bf16[2,960,128]{2,1,0:T(8,128)(2,1)S(1)}, u32[]{:S(2)}, u32[]{:S(2)}) %collective-permute-start) | collective-permute-done | bytes 491552 | tf_op jit(solution)/shard_map/ppermute | solution.py:20
  15.9 1.6 %collective-permute-start.4 = (bf16[960,128]{1,0:T(8,128)(2,1)S(1)}, bf16[960,128]{1,0:T(8,128)(2,1)S(1)}, u32[]{:S(2)}, u32[]{:S(2)}) collective-permute-start(bf16[960,128]{1,0:T(8,128)(2,1)S(1)} %slice_bitcast_fusion.1), channel_id=1, source_target_pairs={{0,8},{4,12},{8,0},{12,4},{16,24},{20,28},{24,16},{28,20},{1,9},{5... | collective-permute-start | bytes 737288 | tf_op jit(solution)/shard_map/ppermute | solution.py:20
  18.0 5.8 %collective-permute-done.3.last_ref = bf16[960,128]{1,0:T(8,128)(2,1)S(1)} collective-permute-done((bf16[960,128]{1,0:T(8,128)(2,1)}, bf16[960,128]{1,0:T(8,128)(2,1)S(1)}, u32[]{:S(2)}, u32[]{:S(2)}) %collective-permute-start.3) | collective-permute-done | bytes 245792 | tf_op jit(solution)/shard_map/ppermute | solution.py:277
  23.8 0.5 collective-permute-start.8
  24.3 3.3 %collective-permute-start.11 = (bf16[2,960,128]{2,1,0:T(8,128)(2,1)S(1)}, bf16[2,960,128]{2,1,0:T(8,128)(2,1)S(1)}, u32[]{:S(2)}, u32[]{:S(2)}) collective-permute-start(bf16[2,960,128]{2,1,0:T(8,128)(2,1)S(1)} %collective-permute-done.2.refs_1_), channel_id=1, source_target_pairs={{0,2},{2,3},{3,1},{1,0},{4,6},{6,7},{7,5},{5,4},{8,10},{10,11},{11... | collective-permute-start | bytes 1474568 | tf_op jit(solution)/shard_map/ppermute | solution.py:277
  28.1 1.0 %collective-permute-done.9.refs_8_ = bf16[960,128]{1,0:T(8,128)(2,1)S(1)} collective-permute-done((bf16[960,128]{1,0:T(8,128)(2,1)S(1)}, bf16[960,128]{1,0:T(8,128)(2,1)S(1)}, u32[]{:S(2)}, u32[]{:S(2)}) %collective-permute-start.9) | collective-permute-done | bytes 245792 | tf_op jit(solution)/shard_map/ppermute | solution.py:20
  29.5 8.3 %ladder.1 = (bf16[2,960,128]{2,1,0:T(8,128)(2,1)S(1)}, bf16[4,960,128]{2,1,0:T(8,128)(2,1)S(1)}, bf16[2,960,128]{2,1,0:T(8,128)(2,1)S(1)}, bf16[2,960,128]{2,1,0...) custom-call(s32[8]{0:T(128)S(1)} %pad_add_fusion.small_ref, ...), custom_call_target="tpu_custom_call" | custom-call | flops 528482304 | bytes 1966080 | tf_op jit(solution)/shard_map/ladder/pallas_call | solution.py:138
  37.7 0.5 collective-permute-done.11.refs_2_
  38.8 0.6 contract.1
  39.4 0.8 %collective-permute-done.13 = bf16[2,960,128]{2,1,0:T(8,128)(2,1)S(1)} collective-permute-done((bf16[2,960,128]{2,1,0:T(8,128)(2,1)S(1)}, bf16[2,960,128]{2,1,0:T(8,128)(2,1)S(1)}, u32[]{:S(2)}, u32[]{:S(2)}) %collective-permute-start.13) | collective-permute-done | bytes 491552 | tf_op jit(solution)/shard_map/ppermute | solution.py:20
  40.5 0.5 collective-permute-start.17
  42.0 2.7 %collective-permute-start.16 = (bf16[128,128]{1,0:T(8,128)(2,1)S(1)}, bf16[128,128]{1,0:T(8,128)(2,1)S(1)}, u32[]{:S(2)}, u32[]{:S(2)}) collective-permute-start(bf16[128,128]{1,0:T(8,128)(2,1)S(1)} %get-tuple-element.91), channel_id=1, source_target_pairs={{0,3},{2,1},{3,0},{1,2},{4,7},{6,5},{7,4},{5,6},{8,11},{10,9},{11,... | collective-permute-start | bytes 98312 | tf_op jit(solution)/shard_map/ppermute | solution.py:277
  44.6 1.3 %collective-permute-start.15 = (bf16[128,128]{1,0:T(8,128)(2,1)S(1)}, bf16[128,128]{1,0:T(8,128)(2,1)S(1)}, u32[]{:S(2)}, u32[]{:S(2)}) collective-permute-start(bf16[128,128]{1,0:T(8,128)(2,1)S(1)} %get-tuple-element.92), channel_id=1, source_target_pairs={{0,1},{2,0},{3,2},{1,3},{4,5},{6,4},{7,6},{5,7},{8,9},{10,8},{11,1... | collective-permute-start | bytes 98312 | tf_op jit(solution)/shard_map/ppermute | solution.py:277
  46.0 1.3 %collective-permute-start.24 = (bf16[1,960,128]{2,1,0:T(8,128)(2,1)S(1)}, bf16[1,960,128]{2,1,0:T(8,128)(2,1)S(1)}, u32[]{:S(2)}, u32[]{:S(2)}) collective-permute-start(bf16[1,960,128]{2,1,0:T(8,128)(2,1)S(1)} %get-tuple-element.73), channel_id=1, source_target_pairs={{0,8},{4,12},{8,0},{12,4},{16,24},{20,28},{24,16},{28,20},{1,9},{5... | collective-permute-start | bytes 737288 | tf_op jit(solution)/shard_map/ppermute | solution.py:20
  47.8 1.6 %collective-permute-start.25 = (bf16[1,960,128]{2,1,0:T(8,128)(2,1)S(1)}, bf16[1,960,128]{2,1,0:T(8,128)(2,1)S(1)}, u32[]{:S(2)}, u32[]{:S(2)}) collective-permute-start(bf16[1,960,128]{2,1,0:T(8,128)(2,1)S(1)} %get-tuple-element.74), channel_id=1, source_target_pairs={{0,16},{4,20},{8,24},{12,28},{16,0},{20,4},{24,8},{28,12},{1,17},{... | collective-permute-start | bytes 737288 | tf_op jit(solution)/shard_map/ppermute | solution.py:20
  49.5 1.5 %collective-permute-start.19 = (bf16[4,128,128]{2,1,0:T(8,128)(2,1)S(1)}, bf16[4,128,128]{2,1,0:T(8,128)(2,1)S(1)}, u32[]{:S(2)}, u32[]{:S(2)}) collective-permute-start(bf16[4,128,128]{2,1,0:T(8,128)(2,1)S(1)} %pad_maximum_fusion), channel_id=1, source_target_pairs={{0,8},{4,12},{8,0},{12,4},{16,24},{20,28},{24,16},{28,20},{1,9},{5... | collective-permute-start | bytes 393224 | tf_op jit(solution)/shard_map/ppermute | solution.py:20
  51.0 3.7 %collective-permute-start.21 = (bf16[2,960,128]{2,1,0:T(8,128)(2,1)S(1)}, bf16[2,960,128]{2,1,0:T(8,128)(2,1)S(1)}, u32[]{:S(2)}, u32[]{:S(2)}) collective-permute-start(bf16[2,960,128]{2,1,0:T(8,128)(2,1)S(1)} %collective-permute-done.11.refs_2_), channel_id=1, source_target_pairs={{0,2},{2,3},{3,1},{1,0},{4,6},{6,7},{7,5},{5,4},{8,10},{10,11},{11... | collective-permute-start | bytes 1474568 | tf_op jit(solution)/shard_map/ppermute | solution.py:277
  55.4 2.3 %collective-permute-done.19 = bf16[4,128,128]{2,1,0:T(8,128)(2,1)S(1)} collective-permute-done((bf16[4,128,128]{2,1,0:T(8,128)(2,1)S(1)}, bf16[4,128,128]{2,1,0:T(8,128)(2,1)S(1)}, u32[]{:S(2)}, u32[]{:S(2)}) %collective-permute-start.19) | collective-permute-done | bytes 131104 | tf_op jit(solution)/shard_map/ppermute | solution.py:20
  57.7 1.0 %collective-permute-start.22 = (bf16[1,960,128]{2,1,0:T(8,128)(2,1)S(1)}, bf16[1,960,128]{2,1,0:T(8,128)(2,1)S(1)}, u32[]{:S(2)}, u32[]{:S(2)}) collective-permute-start(bf16[1,960,128]{2,1,0:T(8,128)(2,1)S(1)} %get-tuple-element.84), channel_id=1, source_target_pairs={{0,16},{4,20},{8,24},{12,28},{16,0},{20,4},{24,8},{28,12},{1,17},{... | collective-permute-start | bytes 737288 | tf_op jit(solution)/shard_map/ppermute | solution.py:20
  58.7 1.1 %collective-permute-start.20 = (bf16[4,128,128]{2,1,0:T(8,128)(2,1)S(1)}, bf16[4,128,128]{2,1,0:T(8,128)(2,1)S(1)}, u32[]{:S(2)}, u32[]{:S(2)}) collective-permute-start(bf16[4,128,128]{2,1,0:T(8,128)(2,1)S(1)} %add_convert_fusion.7), channel_id=1, source_target_pairs={{0,16},{4,20},{8,24},{12,28},{16,0},{20,4},{24,8},{28,12},{1,17},{... | collective-permute-start | bytes 393224 | tf_op jit(solution)/shard_map/ppermute | solution.py:20
  59.8 2.2 %collective-permute-done.23.refs_7_ = bf16[1,960,128]{2,1,0:T(8,128)(2,1)S(1)} collective-permute-done((bf16[1,960,128]{2,1,0:T(8,128)(2,1)S(1)}, bf16[1,960,128]{2,1,0:T(8,128)(2,1)S(1)}, u32[]{:S(2)}, u32[]{:S(2)}) %collective-permute-start.23) | collective-permute-done | bytes 245792 | tf_op jit(solution)/shard_map/ppermute | solution.py:20
  62.1 3.2 %collective-permute-done.22.refs_6_ = bf16[1,960,128]{2,1,0:T(8,128)(2,1)S(1)} collective-permute-done((bf16[1,960,128]{2,1,0:T(8,128)(2,1)S(1)}, bf16[1,960,128]{2,1,0:T(8,128)(2,1)S(1)}, u32[]{:S(2)}, u32[]{:S(2)}) %collective-permute-start.22) | collective-permute-done | bytes 245792 | tf_op jit(solution)/shard_map/ppermute | solution.py:20
  65.3 1.4 %collective-permute-done.20 = bf16[4,128,128]{2,1,0:T(8,128)(2,1)S(1)} collective-permute-done((bf16[4,128,128]{2,1,0:T(8,128)(2,1)S(1)}, bf16[4,128,128]{2,1,0:T(8,128)(2,1)S(1)}, u32[]{:S(2)}, u32[]{:S(2)}) %collective-permute-start.20) | collective-permute-done | bytes 131104 | tf_op jit(solution)/shard_map/ppermute | solution.py:20
  67.2 1.0 %collective-permute-done.26.other_ref = bf16[4,128,128]{2,1,0:T(8,128)(2,1)S(1)} collective-permute-done((bf16[4,128,128]{2,1,0:T(8,128)(2,1)S(1)}, bf16[4,128,128]{2,1,0:T(8,128)(2,1)S(1)}, u32[]{:S(2)}, u32[]{:S(2)}) %collective-permute-start.26) | collective-permute-done | bytes 131104 | tf_op jit(solution)/shard_map/ppermute | solution.py:20
  68.2 1.5 %quadratic.1 = bf16[2,960,128]{2,1,0:T(8,128)(2,1)} custom-call(s32[1]{0:T(128)S(6)} %and.4.core_ref, bf16[4,128,128]{2,1,0:T(8,128)(2,1)S(1)} %add_convert_fusion.6.mine_ref, bf16[4,128,128]{2,1,0:T(8,128)(2,1)S(1)} %collective-permute-done.26.other_ref, f32[2,960,128]{2,1,0:T(8,128)S(1)} %combine.1.base_ref, ...), custom_call_target="tpu_custom_call" | custom-call | flops 503316480 | bytes 3440640 | tf_op jit(solution)/shard_map/quadratic/pallas_call | solution.py:226
  (44 shorter events, 5.2 us)
Async XLA Ops:
  0.0 14.4 %collective-permute-start.1 = (bf16[2,960,128]{2,1,0:T(8,128)(2,1)}, bf16[2,960,128]{2,1,0:T(8,128)(2,1)S(1)}, u32[]{:S(2)}, u32[]{:S(2)}) collective-permute-start(bf16[2,960,128]{2,1,0:T(8,128)(2,1)} %source_ref.1), channel_id=1, source_target_pairs={{0,16},{4,20},{8,24},{12,28},{16,0},{20,4},{24,8},{28,12},{1,17},{... | collective-permute-start | bytes 1474568 | tf_op jit(solution)/shard_map/ppermute | solution.py:20
  3.0 12.9 %collective-permute-start = (bf16[2,960,128]{2,1,0:T(8,128)(2,1)}, bf16[2,960,128]{2,1,0:T(8,128)(2,1)S(1)}, u32[]{:S(2)}, u32[]{:S(2)}) collective-permute-start(bf16[2,960,128]{2,1,0:T(8,128)(2,1)} %source_ref.1), channel_id=1, source_target_pairs={{0,8},{4,12},{8,0},{12,4},{16,24},{20,28},{24,16},{28,20},{1,9},{5... | collective-permute-start | bytes 1474568 | tf_op jit(solution)/shard_map/ppermute | solution.py:20
  4.5 19.3 %collective-permute-start.6 = (bf16[2,960,128]{2,1,0:T(8,128)(2,1)}, bf16[2,960,128]{2,1,0:T(8,128)(2,1)S(1)}, u32[]{:S(2)}, u32[]{:S(2)}) collective-permute-start(bf16[2,960,128]{2,1,0:T(8,128)(2,1)} %source_ref.1), channel_id=1, source_target_pairs={{0,4},{4,0},{8,12},{12,8},{16,20},{20,16},{24,28},{28,24},{1,5},{5... | collective-permute-start | bytes 1474568 | tf_op jit(solution)/shard_map/ppermute | solution.py:20
  4.5 19.8 %collective-permute-start.2 = (bf16[2,960,128]{2,1,0:T(8,128)(2,1)}, bf16[2,960,128]{2,1,0:T(8,128)(2,1)S(1)}, u32[]{:S(2)}, u32[]{:S(2)}) collective-permute-start(bf16[2,960,128]{2,1,0:T(8,128)(2,1)} %source_ref.1), channel_id=1, source_target_pairs={{0,2},{2,3},{3,1},{1,0},{4,6},{6,7},{7,5},{5,4},{8,10},{10,11},{11... | collective-permute-start | bytes 1474568 | tf_op jit(solution)/shard_map/ppermute | solution.py:277
  7.1 16.7 %collective-permute-start.3 = (bf16[960,128]{1,0:T(8,128)(2,1)}, bf16[960,128]{1,0:T(8,128)(2,1)S(1)}, u32[]{:S(2)}, u32[]{:S(2)}) collective-permute-start(bf16[960,128]{1,0:T(8,128)(2,1)} %int_ref.1), channel_id=1, source_target_pairs={{0,2},{2,3},{3,1},{1,0},{4,6},{6,7},{7,5},{5,4},{8,10},{10,11},{11... | collective-permute-start | bytes 737288 | tf_op jit(solution)/shard_map/ppermute | solution.py:277
  9.4 1.0 %copy-start = (bf16[2,960,128]{2,1,0:T(8,128)(2,1)S(1)}, bf16[2,960,128]{2,1,0:T(8,128)(2,1)}, u32[]{:S(2)}) copy-start(bf16[2,960,128]{2,1,0:T(8,128)(2,1)} %source_ref.1) | copy-start | bytes 1474564
  10.4 28.4 %copy-start.1 = (bf16[960,128]{1,0:T(8,128)(2,1)S(1)}, bf16[960,128]{1,0:T(8,128)(2,1)}, u32[]{:S(2)}) copy-start(bf16[960,128]{1,0:T(8,128)(2,1)} %int_ref.1) | copy-start | bytes 737284
  15.9 11.7 %collective-permute-start.4 = (bf16[960,128]{1,0:T(8,128)(2,1)S(1)}, bf16[960,128]{1,0:T(8,128)(2,1)S(1)}, u32[]{:S(2)}, u32[]{:S(2)}) collective-permute-start(bf16[960,128]{1,0:T(8,128)(2,1)S(1)} %slice_bitcast_fusion.1), channel_id=1, source_target_pairs={{0,8},{4,12},{8,0},{12,4},{16,24},{20,28},{24,16},{28,20},{1,9},{5... | collective-permute-start | bytes 737288 | tf_op jit(solution)/shard_map/ppermute | solution.py:20
  17.5 10.1 %collective-permute-start.5 = (bf16[960,128]{1,0:T(8,128)(2,1)S(1)}, bf16[960,128]{1,0:T(8,128)(2,1)S(1)}, u32[]{:S(2)}, u32[]{:S(2)}) collective-permute-start(bf16[960,128]{1,0:T(8,128)(2,1)S(1)} %slice_bitcast_fusion), channel_id=1, source_target_pairs={{0,16},{4,20},{8,24},{12,28},{16,0},{20,4},{24,8},{28,12},{1,17},{... | collective-permute-start | bytes 737288 | tf_op jit(solution)/shard_map/ppermute | solution.py:20
  23.8 5.7 %collective-permute-start.7 = (bf16[2,960,128]{2,1,0:T(8,128)(2,1)S(1)}, bf16[2,960,128]{2,1,0:T(8,128)(2,1)S(1)}, u32[]{:S(2)}, u32[]{:S(2)}) collective-permute-start(bf16[2,960,128]{2,1,0:T(8,128)(2,1)S(1)} %collective-permute-done.refs_1_), channel_id=1, source_target_pairs={{0,4},{4,0},{8,12},{12,8},{16,20},{20,16},{24,28},{28,24},{1,5},{5... | collective-permute-start | bytes 1474568 | tf_op jit(solution)/shard_map/ppermute | solution.py:20
  23.8 5.7 %collective-permute-start.8 = (bf16[2,960,128]{2,1,0:T(8,128)(2,1)S(1)}, bf16[2,960,128]{2,1,0:T(8,128)(2,1)S(1)}, u32[]{:S(2)}, u32[]{:S(2)}) collective-permute-start(bf16[2,960,128]{2,1,0:T(8,128)(2,1)S(1)} %collective-permute-done.1.refs_2_), channel_id=1, source_target_pairs={{0,4},{4,0},{8,12},{12,8},{16,20},{20,16},{24,28},{28,24},{1,5},{5... | collective-permute-start | bytes 1474568 | tf_op jit(solution)/shard_map/ppermute | solution.py:20
  24.3 14.0 %collective-permute-start.11 = (bf16[2,960,128]{2,1,0:T(8,128)(2,1)S(1)}, bf16[2,960,128]{2,1,0:T(8,128)(2,1)S(1)}, u32[]{:S(2)}, u32[]{:S(2)}) collective-permute-start(bf16[2,960,128]{2,1,0:T(8,128)(2,1)S(1)} %collective-permute-done.2.refs_1_), channel_id=1, source_target_pairs={{0,2},{2,3},{3,1},{1,0},{4,6},{6,7},{7,5},{5,4},{8,10},{10,11},{11... | collective-permute-start | bytes 1474568 | tf_op jit(solution)/shard_map/ppermute | solution.py:277
  27.6 1.5 %collective-permute-start.9 = (bf16[960,128]{1,0:T(8,128)(2,1)S(1)}, bf16[960,128]{1,0:T(8,128)(2,1)S(1)}, u32[]{:S(2)}, u32[]{:S(2)}) collective-permute-start(bf16[960,128]{1,0:T(8,128)(2,1)S(1)} %collective-permute-done.4.refs_3_), channel_id=1, source_target_pairs={{0,4},{4,0},{8,12},{12,8},{16,20},{20,16},{24,28},{28,24},{1,5},{5... | collective-permute-start | bytes 737288 | tf_op jit(solution)/shard_map/ppermute | solution.py:20
  27.6 1.9 %collective-permute-start.10 = (bf16[960,128]{1,0:T(8,128)(2,1)S(1)}, bf16[960,128]{1,0:T(8,128)(2,1)S(1)}, u32[]{:S(2)}, u32[]{:S(2)}) collective-permute-start(bf16[960,128]{1,0:T(8,128)(2,1)S(1)} %collective-permute-done.5.refs_4_), channel_id=1, source_target_pairs={{0,4},{4,0},{8,12},{12,8},{16,20},{20,16},{24,28},{28,24},{1,5},{5... | collective-permute-start | bytes 737288 | tf_op jit(solution)/shard_map/ppermute | solution.py:20
  38.3 1.9 %collective-permute-start.13 = (bf16[2,960,128]{2,1,0:T(8,128)(2,1)S(1)}, bf16[2,960,128]{2,1,0:T(8,128)(2,1)S(1)}, u32[]{:S(2)}, u32[]{:S(2)}) collective-permute-start(bf16[2,960,128]{2,1,0:T(8,128)(2,1)S(1)} %get-tuple-element.57), channel_id=1, source_target_pairs={{0,4},{4,0},{8,12},{12,8},{16,20},{20,16},{24,28},{28,24},{1,5},{5... | collective-permute-start | bytes 1474568 | tf_op jit(solution)/shard_map/ppermute | solution.py:20
  38.3 3.5 %collective-permute-start.12 = (bf16[4,960,128]{2,1,0:T(8,128)(2,1)S(1)}, bf16[4,960,128]{2,1,0:T(8,128)(2,1)S(1)}, u32[]{:S(2)}, u32[]{:S(2)}) collective-permute-start(bf16[4,960,128]{2,1,0:T(8,128)(2,1)S(1)} %get-tuple-element.55), channel_id=1, source_target_pairs={{0,4},{4,0},{8,12},{12,8},{16,20},{20,16},{24,28},{28,24},{1,5},{5... | collective-permute-start | bytes 2949128 | tf_op jit(solution)/shard_map/ppermute | solution.py:20
  40.3 1.5 %collective-permute-start.14 = (bf16[4,128,128]{2,1,0:T(8,128)(2,1)S(1)}, bf16[4,128,128]{2,1,0:T(8,128)(2,1)S(1)}, u32[]{:S(2)}, u32[]{:S(2)}) collective-permute-start(bf16[4,128,128]{2,1,0:T(8,128)(2,1)S(1)} %get-tuple-element.65), channel_id=1, source_target_pairs={{0,4},{4,0},{8,12},{12,8},{16,20},{20,16},{24,28},{28,24},{1,5},{5... | collective-permute-start | bytes 393224 | tf_op jit(solution)/shard_map/ppermute | solution.py:20
  40.5 9.0 %collective-permute-start.17 = (bf16[1,960,128]{2,1,0:T(8,128)(2,1)S(1)}, bf16[1,960,128]{2,1,0:T(8,128)(2,1)S(1)}, u32[]{:S(2)}, u32[]{:S(2)}) collective-permute-start(bf16[1,960,128]{2,1,0:T(8,128)(2,1)S(1)} %get-tuple-element.67), channel_id=1, source_target_pairs={{0,8},{4,12},{8,0},{12,4},{16,24},{20,28},{24,16},{28,20},{1,9},{5... | collective-permute-start | bytes 737288 | tf_op jit(solution)/shard_map/ppermute | solution.py:20
  41.0 8.4 %collective-permute-start.18 = (bf16[1,960,128]{2,1,0:T(8,128)(2,1)S(1)}, bf16[1,960,128]{2,1,0:T(8,128)(2,1)S(1)}, u32[]{:S(2)}, u32[]{:S(2)}) collective-permute-start(bf16[1,960,128]{2,1,0:T(8,128)(2,1)S(1)} %get-tuple-element.68), channel_id=1, source_target_pairs={{0,16},{4,20},{8,24},{12,28},{16,0},{20,4},{24,8},{28,12},{1,17},{... | collective-permute-start | bytes 737288 | tf_op jit(solution)/shard_map/ppermute | solution.py:20
  42.0 5.8 %collective-permute-start.16 = (bf16[128,128]{1,0:T(8,128)(2,1)S(1)}, bf16[128,128]{1,0:T(8,128)(2,1)S(1)}, u32[]{:S(2)}, u32[]{:S(2)}) collective-permute-start(bf16[128,128]{1,0:T(8,128)(2,1)S(1)} %get-tuple-element.91), channel_id=1, source_target_pairs={{0,3},{2,1},{3,0},{1,2},{4,7},{6,5},{7,4},{5,6},{8,11},{10,9},{11,... | collective-permute-start | bytes 98312 | tf_op jit(solution)/shard_map/ppermute | solution.py:277
  44.6 4.8 %collective-permute-start.15 = (bf16[128,128]{1,0:T(8,128)(2,1)S(1)}, bf16[128,128]{1,0:T(8,128)(2,1)S(1)}, u32[]{:S(2)}, u32[]{:S(2)}) collective-permute-start(bf16[128,128]{1,0:T(8,128)(2,1)S(1)} %get-tuple-element.92), channel_id=1, source_target_pairs={{0,1},{2,0},{3,2},{1,3},{4,5},{6,4},{7,6},{5,7},{8,9},{10,8},{11,1... | collective-permute-start | bytes 98312 | tf_op jit(solution)/shard_map/ppermute | solution.py:277
  46.0 12.7 %collective-permute-start.24 = (bf16[1,960,128]{2,1,0:T(8,128)(2,1)S(1)}, bf16[1,960,128]{2,1,0:T(8,128)(2,1)S(1)}, u32[]{:S(2)}, u32[]{:S(2)}) collective-permute-start(bf16[1,960,128]{2,1,0:T(8,128)(2,1)S(1)} %get-tuple-element.73), channel_id=1, source_target_pairs={{0,8},{4,12},{8,0},{12,4},{16,24},{20,28},{24,16},{28,20},{1,9},{5... | collective-permute-start | bytes 737288 | tf_op jit(solution)/shard_map/ppermute | solution.py:20
  47.8 12.0 %collective-permute-start.25 = (bf16[1,960,128]{2,1,0:T(8,128)(2,1)S(1)}, bf16[1,960,128]{2,1,0:T(8,128)(2,1)S(1)}, u32[]{:S(2)}, u32[]{:S(2)}) collective-permute-start(bf16[1,960,128]{2,1,0:T(8,128)(2,1)S(1)} %get-tuple-element.74), channel_id=1, source_target_pairs={{0,16},{4,20},{8,24},{12,28},{16,0},{20,4},{24,8},{28,12},{1,17},{... | collective-permute-start | bytes 737288 | tf_op jit(solution)/shard_map/ppermute | solution.py:20
  49.5 8.2 %collective-permute-start.19 = (bf16[4,128,128]{2,1,0:T(8,128)(2,1)S(1)}, bf16[4,128,128]{2,1,0:T(8,128)(2,1)S(1)}, u32[]{:S(2)}, u32[]{:S(2)}) collective-permute-start(bf16[4,128,128]{2,1,0:T(8,128)(2,1)S(1)} %pad_maximum_fusion), channel_id=1, source_target_pairs={{0,8},{4,12},{8,0},{12,4},{16,24},{20,28},{24,16},{28,20},{1,9},{5... | collective-permute-start | bytes 393224 | tf_op jit(solution)/shard_map/ppermute | solution.py:20
  51.0 15.7 %collective-permute-start.21 = (bf16[2,960,128]{2,1,0:T(8,128)(2,1)S(1)}, bf16[2,960,128]{2,1,0:T(8,128)(2,1)S(1)}, u32[]{:S(2)}, u32[]{:S(2)}) collective-permute-start(bf16[2,960,128]{2,1,0:T(8,128)(2,1)S(1)} %collective-permute-done.11.refs_2_), channel_id=1, source_target_pairs={{0,2},{2,3},{3,1},{1,0},{4,6},{6,7},{7,5},{5,4},{8,10},{10,11},{11... | collective-permute-start | bytes 1474568 | tf_op jit(solution)/shard_map/ppermute | solution.py:277
  54.9 7.1 %collective-permute-start.23 = (bf16[1,960,128]{2,1,0:T(8,128)(2,1)S(1)}, bf16[1,960,128]{2,1,0:T(8,128)(2,1)S(1)}, u32[]{:S(2)}, u32[]{:S(2)}) collective-permute-start(bf16[1,960,128]{2,1,0:T(8,128)(2,1)S(1)} %get-tuple-element.83), channel_id=1, source_target_pairs={{0,8},{4,12},{8,0},{12,4},{16,24},{20,28},{24,16},{28,20},{1,9},{5... | collective-permute-start | bytes 737288 | tf_op jit(solution)/shard_map/ppermute | solution.py:20
  57.7 7.6 %collective-permute-start.22 = (bf16[1,960,128]{2,1,0:T(8,128)(2,1)S(1)}, bf16[1,960,128]{2,1,0:T(8,128)(2,1)S(1)}, u32[]{:S(2)}, u32[]{:S(2)}) collective-permute-start(bf16[1,960,128]{2,1,0:T(8,128)(2,1)S(1)} %get-tuple-element.84), channel_id=1, source_target_pairs={{0,16},{4,20},{8,24},{12,28},{16,0},{20,4},{24,8},{28,12},{1,17},{... | collective-permute-start | bytes 737288 | tf_op jit(solution)/shard_map/ppermute | solution.py:20
  58.7 8.0 %collective-permute-start.20 = (bf16[4,128,128]{2,1,0:T(8,128)(2,1)S(1)}, bf16[4,128,128]{2,1,0:T(8,128)(2,1)S(1)}, u32[]{:S(2)}, u32[]{:S(2)}) collective-permute-start(bf16[4,128,128]{2,1,0:T(8,128)(2,1)S(1)} %add_convert_fusion.7), channel_id=1, source_target_pairs={{0,16},{4,20},{8,24},{12,28},{16,0},{20,4},{24,8},{28,12},{1,17},{... | collective-permute-start | bytes 393224 | tf_op jit(solution)/shard_map/ppermute | solution.py:20
  59.8 7.0 %collective-permute-start.27 = (bf16[2,960,128]{2,1,0:T(8,128)(2,1)S(1)}, bf16[2,960,128]{2,1,0:T(8,128)(2,1)S(1)}, u32[]{:S(2)}, u32[]{:S(2)}) collective-permute-start(bf16[2,960,128]{2,1,0:T(8,128)(2,1)S(1)} %get-tuple-element.77), channel_id=1, source_target_pairs={{0,4},{4,0},{8,12},{12,8},{16,20},{20,16},{24,28},{28,24},{1,5},{5... | collective-permute-start | bytes 1474568 | tf_op jit(solution)/shard_map/ppermute | solution.py:20
  66.7 1.4 %collective-permute-start.26 = (bf16[4,128,128]{2,1,0:T(8,128)(2,1)S(1)}, bf16[4,128,128]{2,1,0:T(8,128)(2,1)S(1)}, u32[]{:S(2)}, u32[]{:S(2)}) collective-permute-start(bf16[4,128,128]{2,1,0:T(8,128)(2,1)S(1)} %add_convert_fusion.6.mine_ref), channel_id=1, source_target_pairs={{0,4},{4,0},{8,12},{12,8},{16,20},{20,16},{24,28},{28,24},{1,5},{5... | collective-permute-start | bytes 393224 | tf_op jit(solution)/shard_map/ppermute | solution.py:20
